TPU v7x, 32 devices: a whole 2x2x4 slice. The times are simulated.
32 devices in a mesh: ctx: 4 (over z), shard: 8 (over y, x, core).
Axes of the slice: x: 2, y: 2, z: 4, core: 2. Of those that a mesh axis runs over, the one named last changes fastest.
Arguments:
- tokens: bfloat16 [8, 512, 2048], P('shard', 'ctx'), may hold values from -6 to 6
- cotangent: bfloat16 [8, 512, 2048], P('shard', 'ctx'), may hold values from -6 to 6
- block_order: int32 [8], replicated, may hold values from 0 to 7, each once
- routes: int32 [8, 512, 8], P('shard', 'ctx'), may hold values from 0 to 31, all different within a row; in each aligned block of 128 rows (0 to 127, 128 to 255, ..., all dimensions but the last counted through in order) at most 40 rows name the same one
- attn_gain: float32 [2048], replicated, may hold values from 0.1 to 1.9
- w_query: bfloat16 [2048, 4096], P('shard'), may hold values from -0.125 to 0.125
- key_weight: bfloat16 [2048, 512], P('shard'), may hold values from -0.125 to 0.125
- value_weight: bfloat16 [2048, 512], P('shard'), may hold values from -0.125 to 0.125
- query_gain: float32 [128], replicated, may hold values from 0.1 to 1.9
- key_gain: float32 [128], replicated, may hold values from 0.1 to 1.9
- w_out: bfloat16 [4096, 2048], P('shard'), may hold values from -1.5 to 1.5
- ffn_gain: float32 [2048], replicated, may hold values from 0.1 to 1.9
- w_router: bfloat16 [2048, 32], P('shard'), may hold values from -0.0625 to 0.0625
- w_gate: bfloat16 [32, 2048, 768], P(('ctx', 'shard')), may hold values from -0.125 to 0.125
- w_up: bfloat16 [32, 2048, 768], P(('ctx', 'shard')), may hold values from -0.125 to 0.125
- w_down: bfloat16 [32, 768, 2048], P(('ctx', 'shard')), may hold values from -0.625 to 0.625
Outputs:
- mixed: bfloat16 [8, 512, 2048], P('shard', 'ctx')
- grad_tokens: float32 [8, 512, 2048], P('shard', 'ctx')
- grad_attn_gain: float32 [2048], replicated
- grad_w_query: float32 [2048, 4096], P('shard')
- grad_w_key: float32 [2048, 512], P('shard')
- grad_w_value: float32 [2048, 512], P('shard')
- grad_query_gain: float32 [128], replicated
- grad_key_gain: float32 [128], replicated
- grad_w_out: float32 [4096, 2048], P('shard')
- grad_ffn_gain: float32 [2048], replicated
- grad_w_router: float32 [2048, 32], P('shard')
- grad_w_gate: float32 [32, 2048, 768], P(('ctx', 'shard'))
- grad_w_up: float32 [32, 2048, 768], P(('ctx', 'shard'))
- grad_w_down: float32 [32, 768, 2048], P(('ctx', 'shard'))
Inputs may be any that keep to these rules, and one draw needn't show every extreme that they name: Slot j of every sequence's storage holds causal block block_order[j]; each of the 8 blocks once. `routes`: each token names 8 different experts; among the 128 rows of one device (aligned blocks of a sequence's storage) no expert is named by more than 40 rows, a bound that some block reaches.
All inputs are finite; a program needn't handle non-finite values.
Results may differ from a plain program's by a relative error of at most 0.028.
Values may be sent and summed in bfloat16 or wider, within the bound.
A program may use at most 384 MiB of HBM per device.

v0:
```python
import math

import jax
import jax.numpy as jnp
from jax import lax
from jax.sharding import PartitionSpec as P

QUERY_HEADS = 32
KEY_VALUE_HEADS = 4
HEAD_DIM = 128


epsilon = 1e-06
rope_base = 1000000.0


def rms_scale(hidden, gain):
    return hidden * lax.rsqrt(jnp.mean(hidden * hidden, axis=-1, keepdims=True) + epsilon) * gain


def rotate(headwise, places):
    half_size = headwise.shape[-1] // 2
    frequency = rope_base ** (-jnp.arange(half_size, dtype=jnp.float32) * 2.0 / headwise.shape[-1])
    angles = places.astype(jnp.float32)[:, None] * frequency[None, :]
    cosine = jnp.cos(angles)[:, None, :]
    sine = jnp.sin(angles)[:, None, :]
    former = headwise[..., :half_size]
    latter = headwise[..., half_size:]
    return jnp.concatenate(
        [former * cosine - latter * sine, latter * cosine + former * sine], axis=-1
    )


def head_prep(pre_rows, gain, places):
    headwise = pre_rows.reshape(pre_rows.shape[0], -1, HEAD_DIM)
    return rotate(rms_scale(headwise, gain), places).reshape(pre_rows.shape)


def place_of(row_ids, order, block_rows):
    block_ids = jnp.arange(order.shape[0], dtype=jnp.int32)
    owner_block = row_ids // block_rows
    picked_block = jnp.sum(
        jnp.where(owner_block[:, None] == block_ids[None, :], order[None, :], 0), axis=1
    )
    return picked_block * block_rows + row_ids % block_rows


def contract_rows(left, right):
    return lax.dot_general(
        left, right, (((0,), (0,)), ((), ())), preferred_element_type=jnp.float32
    )


def contract_cols(left, right):
    return lax.dot_general(
        left, right, (((1,), (1,)), ((), ())), preferred_element_type=jnp.float32
    )


def over_blocks(update_fn, running, split_parts, first_row):
    row_count = split_parts[0].shape[0]
    sub_rows = math.gcd(row_count, 512)
    block_total = row_count // sub_rows
    if block_total == 1:
        return update_fn(running, split_parts, first_row)
    stacked = tuple(
        (piece.reshape((block_total, sub_rows) + piece.shape[1:]) for piece in split_parts)
    )

    def advance(state, item):
        return (update_fn(state, item[1], first_row + item[0] * sub_rows), None)

    final, unused = lax.scan(advance, running, (jnp.arange(block_total, dtype=jnp.int32), stacked))
    return final


def weight_terms_of(left_in, left_two, left_attn, factor_qkv, factor_logits, factor_proj):
    part_one = contract_rows(left_in, factor_qkv)
    part_two = contract_rows(left_two, factor_logits)
    part_three = contract_rows(left_attn, factor_proj)
    return jnp.concatenate([part_one, part_two, part_three.reshape(left_in.shape[1], -1)], axis=1)


def shards(
    tokens,
    cotangent,
    block_order,
    routes,
    attn_gain,
    w_query,
    key_weight,
    value_weight,
    query_gain,
    key_gain,
    w_out,
    ffn_gain,
    w_router,
    w_gate,
    w_up,
    w_down,
):
    rows_per_shard = tokens.shape[1]
    model_width = tokens.shape[2]
    block_rows = rows_per_shard // 2
    ctx_count = lax.axis_size("ctx")
    shard_count = lax.axis_size("shard")
    experts = ctx_count * shard_count
    query_groups = QUERY_HEADS // KEY_VALUE_HEADS
    score_scale = HEAD_DIM ** (-0.5)
    top_count = routes.shape[2]
    capacity = rows_per_shard * top_count // experts + max(
        rows_per_shard * top_count // (4 * experts), 1
    )
    sequence_length = rows_per_shard * ctx_count
    inputs = tokens[0].astype(jnp.float32)
    upstream = cotangent[0].astype(jnp.float32)
    route_rows = routes[0]
    query_all, key_all, value_all, router_all, out_all = (
        lax.all_gather(w_query, "shard", axis=0, tiled=True),
        lax.all_gather(key_weight, "shard", axis=0, tiled=True),
        lax.all_gather(value_weight, "shard", axis=0, tiled=True),
        lax.all_gather(w_router, "shard", axis=0, tiled=True),
        lax.all_gather(w_out, "shard", axis=0, tiled=True),
    )
    normed = rms_scale(inputs, attn_gain)
    normed_b = normed.astype(jnp.bfloat16)
    query_pre = jnp.dot(normed_b, query_all, preferred_element_type=jnp.float32)
    key_pre = jnp.dot(normed_b, key_all, preferred_element_type=jnp.float32)
    value_b = jnp.dot(normed_b, value_all, preferred_element_type=jnp.float32).astype(jnp.bfloat16)
    row_ids = lax.axis_index("ctx") * rows_per_shard + jnp.arange(rows_per_shard, dtype=jnp.int32)
    q_places = place_of(row_ids, block_order, block_rows)
    query_batch = head_prep(query_pre, query_gain, q_places).astype(jnp.bfloat16)
    key_b = head_prep(key_pre, key_gain, q_places).astype(jnp.bfloat16)
    headed_queries = query_batch.reshape(rows_per_shard, KEY_VALUE_HEADS, query_groups, HEAD_DIM)

    def scores_for(split_parts, first_row):
        key_row_block = split_parts[0].reshape(-1, KEY_VALUE_HEADS, HEAD_DIM)
        value_row_block = split_parts[1].reshape(-1, KEY_VALUE_HEADS, HEAD_DIM)
        row_count = key_row_block.shape[0]
        k_places = place_of(
            first_row + jnp.arange(row_count, dtype=jnp.int32), block_order, block_rows
        )
        raw_scores = (
            jnp.einsum(
                "tkgd,pkd->kgtp", headed_queries, key_row_block, preferred_element_type=jnp.float32
            )
            * score_scale
        )
        masked = jnp.where((k_places[None, :] <= q_places[:, None])[None, None], raw_scores, -1e30)
        return (masked, key_row_block, value_row_block)

    def attend_block(running, split_parts, first_row):
        running_max, denominator, weighted = running
        masked, key_row_block, value_row_block = scores_for(split_parts, first_row)
        new_max = jnp.maximum(running_max, jnp.max(masked, axis=-1))
        factor = jnp.exp(running_max - new_max)
        exp_scores = jnp.exp(masked - new_max[..., None])
        denominator = denominator * factor + jnp.sum(exp_scores, axis=-1)
        update = jnp.einsum(
            "kgtp,pkd->tkgd",
            exp_scores.astype(jnp.bfloat16),
            value_row_block,
            preferred_element_type=jnp.float32,
        )
        weighted = weighted * jnp.transpose(factor, (2, 0, 1))[..., None] + update
        return (new_max, denominator, weighted)

    start_state = (
        jnp.full((KEY_VALUE_HEADS, query_groups, rows_per_shard), -1e30, jnp.float32),
        jnp.zeros((KEY_VALUE_HEADS, query_groups, rows_per_shard), jnp.float32),
        jnp.zeros((rows_per_shard, KEY_VALUE_HEADS, query_groups, HEAD_DIM), jnp.float32),
    )
    running_max, denominator, weighted = over_blocks(
        attend_block,
        start_state,
        (
            lax.all_gather(key_b, "ctx", axis=0, tiled=True),
            lax.all_gather(value_b, "ctx", axis=0, tiled=True),
        ),
        jnp.int32(0),
    )
    attn_f32 = weighted / jnp.transpose(denominator, (2, 0, 1))[..., None]
    log_total = running_max + jnp.log(denominator)
    attn_b = attn_f32.reshape(rows_per_shard, QUERY_HEADS * HEAD_DIM).astype(jnp.bfloat16)
    middle = inputs + jnp.dot(attn_b, out_all, preferred_element_type=jnp.float32)
    normed_two = rms_scale(middle, ffn_gain)
    second_b = normed_two.astype(jnp.bfloat16)
    logits = jnp.dot(second_b, router_all, preferred_element_type=jnp.float32)
    chosen_mask = route_rows[:, :, None] == jnp.arange(experts, dtype=jnp.int32)[None, None, :]
    picked_logits = jnp.sum(jnp.where(chosen_mask, logits[:, None, :], 0.0), axis=-1)
    gate_weights = jax.nn.softmax(picked_logits, axis=-1)
    flat_routes = route_rows.reshape(-1)
    one_hot = (flat_routes[:, None] == jnp.arange(experts, dtype=jnp.int32)[None, :]).astype(
        jnp.int32
    )
    slot_index = jnp.sum(jnp.cumsum(one_hot, axis=0) * one_hot, axis=1) - 1
    target_rows = flat_routes * capacity + slot_index
    spread_rows = jnp.broadcast_to(
        second_b[:, None, :], (rows_per_shard, top_count, model_width)
    ).reshape(-1, model_width)
    send_rows = (
        jnp.zeros((experts * capacity, model_width), jnp.bfloat16).at[target_rows].set(spread_rows)
    )
    received = lax.all_to_all(
        send_rows.reshape(experts, capacity, model_width),
        ("ctx", "shard"),
        split_axis=0,
        concat_axis=0,
        tiled=True,
    ).reshape(experts * capacity, model_width)
    gate_pre = jnp.dot(received, w_gate[0], preferred_element_type=jnp.float32)
    up_pre = jnp.dot(received, w_up[0], preferred_element_type=jnp.float32)
    activated = jax.nn.silu(gate_pre)
    hidden_b = (activated * up_pre).astype(jnp.bfloat16)
    expert_out = jnp.dot(hidden_b, w_down[0], preferred_element_type=jnp.float32).astype(
        jnp.bfloat16
    )
    returned = lax.all_to_all(
        expert_out.reshape(experts, capacity, model_width),
        ("ctx", "shard"),
        split_axis=0,
        concat_axis=0,
        tiled=True,
    ).reshape(experts * capacity, model_width)
    chosen_out = (
        returned[target_rows].astype(jnp.float32).reshape(rows_per_shard, top_count, model_width)
    )
    mixture = jnp.einsum("tk,tkd->td", gate_weights, chosen_out)
    mixed = (middle + mixture).astype(jnp.bfloat16)
    grad_gates = jnp.einsum("tkd,td->tk", chosen_out, upstream)
    back_rows = (
        (gate_weights[:, :, None] * upstream[:, None, :])
        .astype(jnp.bfloat16)
        .reshape(-1, model_width)
    )
    back_send = (
        jnp.zeros((experts * capacity, model_width), jnp.bfloat16).at[target_rows].set(back_rows)
    )
    grad_expert = lax.all_to_all(
        back_send.reshape(experts, capacity, model_width),
        ("ctx", "shard"),
        split_axis=0,
        concat_axis=0,
        tiled=True,
    ).reshape(experts * capacity, model_width)
    grad_w_down = contract_rows(hidden_b, grad_expert)
    grad_hidden = contract_cols(grad_expert, w_down[0])
    sigmoid_g = jax.nn.sigmoid(gate_pre)
    silu_slope = sigmoid_g * (1.0 + gate_pre * (1.0 - sigmoid_g))
    grad_gate_pre = (grad_hidden * up_pre * silu_slope).astype(jnp.bfloat16)
    grad_up_pre = (grad_hidden * activated).astype(jnp.bfloat16)
    grad_w_gate = contract_rows(received, grad_gate_pre)
    grad_w_up = contract_rows(received, grad_up_pre)
    grad_received = contract_cols(grad_gate_pre, w_gate[0]) + contract_cols(grad_up_pre, w_up[0])
    grad_back = (
        lax.all_to_all(
            grad_received.reshape(experts, capacity, model_width).astype(jnp.bfloat16),
            ("ctx", "shard"),
            split_axis=0,
            concat_axis=0,
            tiled=True,
        )
        .astype(jnp.float32)
        .reshape(experts * capacity, model_width)
    )
    grad_second = jnp.sum(
        grad_back[target_rows].reshape(rows_per_shard, top_count, model_width), axis=1
    )
    grad_picked = gate_weights * (
        grad_gates - jnp.sum(gate_weights * grad_gates, axis=-1, keepdims=True)
    )
    grad_logits_b = jnp.sum(jnp.where(chosen_mask, grad_picked[:, :, None], 0.0), axis=1).astype(
        jnp.bfloat16
    )
    grad_second = grad_second + contract_cols(grad_logits_b, router_all)
    prepared, norm_two_back = jax.vjp(rms_scale, middle, ffn_gain)
    grad_middle_part, grad_ffn_gain = norm_two_back(grad_second)
    grad_middle = upstream + grad_middle_part
    grad_proj_b = grad_middle.astype(jnp.bfloat16)
    gradient_attention_batch = contract_cols(grad_proj_b, out_all).astype(jnp.bfloat16)
    gradient_per_head = gradient_attention_batch.reshape(
        rows_per_shard, KEY_VALUE_HEADS, query_groups, HEAD_DIM
    )
    row_dots = jnp.transpose(
        jnp.sum(gradient_per_head.astype(jnp.float32) * attn_f32, axis=-1), (1, 2, 0)
    )

    def back_block(running, split_parts, first_row):
        grad_query, gradient_key_matrix, gradient_value_matrix = running
        masked, key_row_block, value_row_block = scores_for(split_parts, first_row)
        row_count = key_row_block.shape[0]
        exp_scores = jnp.exp(masked - log_total[..., None])
        grad_value_piece = jnp.einsum(
            "kgtp,tkgd->pkd",
            exp_scores.astype(jnp.bfloat16),
            gradient_per_head,
            preferred_element_type=jnp.float32,
        )
        grad_weights = jnp.einsum(
            "tkgd,pkd->kgtp", gradient_per_head, value_row_block, preferred_element_type=jnp.float32
        )
        grad_scores = (exp_scores * (grad_weights - row_dots[..., None])).astype(jnp.bfloat16)
        grad_query = grad_query + score_scale * jnp.einsum(
            "kgtp,pkd->tkgd", grad_scores, key_row_block, preferred_element_type=jnp.float32
        )
        grad_key_piece = score_scale * jnp.einsum(
            "kgtp,tkgd->pkd", grad_scores, headed_queries, preferred_element_type=jnp.float32
        )
        gradient_key_matrix = lax.dynamic_update_slice_in_dim(
            gradient_key_matrix,
            lax.dynamic_slice_in_dim(gradient_key_matrix, first_row, row_count, 0) + grad_key_piece,
            first_row,
            0,
        )
        gradient_value_matrix = lax.dynamic_update_slice_in_dim(
            gradient_value_matrix,
            lax.dynamic_slice_in_dim(gradient_value_matrix, first_row, row_count, 0)
            + grad_value_piece,
            first_row,
            0,
        )
        return (grad_query, gradient_key_matrix, gradient_value_matrix)

    back_state = (
        jnp.zeros((rows_per_shard, KEY_VALUE_HEADS, query_groups, HEAD_DIM), jnp.float32),
        jnp.zeros((sequence_length, KEY_VALUE_HEADS, HEAD_DIM), jnp.float32),
        jnp.zeros((sequence_length, KEY_VALUE_HEADS, HEAD_DIM), jnp.float32),
    )
    grad_query, gradient_key_matrix, gradient_value_matrix = over_blocks(
        back_block,
        back_state,
        (
            lax.all_gather(key_b, "ctx", axis=0, tiled=True),
            lax.all_gather(value_b, "ctx", axis=0, tiled=True),
        ),
        jnp.int32(0),
    )
    grad_key_rows, grad_value_rows = (
        lax.psum_scatter(
            gradient_key_matrix.reshape(sequence_length, KEY_VALUE_HEADS * HEAD_DIM).astype(
                jnp.bfloat16
            ),
            "ctx",
            scatter_dimension=0,
            tiled=True,
        ).astype(jnp.float32),
        lax.psum_scatter(
            gradient_value_matrix.reshape(sequence_length, KEY_VALUE_HEADS * HEAD_DIM).astype(
                jnp.bfloat16
            ),
            "ctx",
            scatter_dimension=0,
            tiled=True,
        ).astype(jnp.float32),
    )

    def prep_both(query_in, key_in, query_g, key_g):
        return (head_prep(query_in, query_g, q_places), head_prep(key_in, key_g, q_places))

    prepared, prep_back = jax.vjp(prep_both, query_pre, key_pre, query_gain, key_gain)
    grad_query_pre, grad_key_pre, grad_query_gain, grad_key_gain = prep_back(
        (grad_query.reshape(rows_per_shard, QUERY_HEADS * HEAD_DIM), grad_key_rows)
    )
    grad_query_b = grad_query_pre.astype(jnp.bfloat16)
    grad_key_b = grad_key_pre.astype(jnp.bfloat16)
    grad_value_b = grad_value_rows.astype(jnp.bfloat16)
    grad_normed = (
        contract_cols(grad_query_b, query_all)
        + contract_cols(grad_key_b, key_all)
        + contract_cols(grad_value_b, value_all)
    )
    prepared, norm_one_back = jax.vjp(rms_scale, inputs, attn_gain)
    grad_input_part, grad_attn_gain = norm_one_back(grad_normed)
    grad_tokens = grad_middle + grad_input_part
    grad_attn_gain, grad_query_gain, grad_key_gain, grad_ffn_gain = lax.psum(
        (grad_attn_gain, grad_query_gain, grad_key_gain, grad_ffn_gain), ("ctx", "shard")
    )
    projected = jnp.concatenate([grad_query_b, grad_key_b, grad_value_b], axis=1)
    partial_rows = lax.psum_scatter(
        weight_terms_of(normed_b, second_b, attn_b, projected, grad_logits_b, grad_proj_b).astype(
            jnp.bfloat16
        ),
        "shard",
        scatter_dimension=0,
        tiled=True,
    )
    summed = lax.psum(partial_rows, "ctx").astype(jnp.float32)
    width_q = QUERY_HEADS * HEAD_DIM
    key_width = KEY_VALUE_HEADS * HEAD_DIM
    grad_w_query = summed[:, :width_q]
    grad_w_key = summed[:, width_q : width_q + key_width]
    grad_w_value = summed[:, width_q + key_width : width_q + 2 * key_width]
    grad_w_router = summed[:, width_q + 2 * key_width : width_q + 2 * key_width + experts]
    grad_w_out = summed[:, width_q + 2 * key_width + experts :].reshape(-1, model_width)
    return (
        mixed[None],
        grad_tokens[None],
        grad_attn_gain,
        grad_w_query,
        grad_w_key,
        grad_w_value,
        grad_query_gain,
        grad_key_gain,
        grad_w_out,
        grad_ffn_gain,
        grad_w_router,
        grad_w_gate[None],
        grad_w_up[None],
        grad_w_down[None],
    )


def solution(mesh):
    return jax.shard_map(
        shards,
        mesh=mesh,
        in_specs=(
            P("shard", "ctx", None),
            P("shard", "ctx", None),
            P(),
            P("shard", "ctx", None),
            P(),
            P("shard", None),
            P("shard", None),
            P("shard", None),
            P(),
            P(),
            P("shard", None),
            P(),
            P("shard", None),
            P(("ctx", "shard"), None, None),
            P(("ctx", "shard"), None, None),
            P(("ctx", "shard"), None, None),
        ),
        out_specs=(
            P("shard", "ctx", None),
            P("shard", "ctx", None),
            P(),
            P("shard", None),
            P("shard", None),
            P("shard", None),
            P(),
            P(),
            P("shard", None),
            P(),
            P("shard", None),
            P(("ctx", "shard"), None, None),
            P(("ctx", "shard"), None, None),
            P(("ctx", "shard"), None, None),
        ),
        check_vma=False,
    )
```

profile of v0, /device:TPU:0, one launch (start us, length us, event | category | flops | bytes accessed | tf_op | source)
XLA Modules:
  0.0 1440.8 jit_solution(4678029707110974427)
XLA Ops:
  10.6 9.0 reduce-window.6
  22.5 18.2 %all-gather.5.cloned.1.call-done = bf16[2048,512]{1,0:T(8,128)(2,1)} async-done(((bf16[256,512]{1,0:T(8,128)(2,1)}), bf16[2048,512]{1,0:T(8,128)(2,1)}) %all-gather.5.cloned.1.call-update) | async-done | bytes 2097168 | tf_op jit(solution)/shard_map/all_gather | solution.py:120
  44.6 25.9 %all-gather.9.cloned.1.call-done = bf16[2048,512]{1,0:T(8,128)(2,1)} async-done(((bf16[256,512]{1,0:T(8,128)(2,1)}), bf16[2048,512]{1,0:T(8,128)(2,1)}) %all-gather.9.cloned.1.call-update) | async-done | bytes 2097168 | tf_op jit(solution)/shard_map/all_gather | solution.py:121
  72.7 16.4 %all_gather.27 = bf16[512,512]{1,0:T(8,128)(2,1)} all-gather(bf16[128,512]{1,0:T(8,128)(2,1)S(1)} %convolution_convert_fusion.5), channel_id=1, replica_groups=mesh['ctx'=4,'shard'=8] {'ctx'}, dimensions={0}, use_global_device_ids=true | all-gather | bytes 655360 | tf_op jit(solution)/shard_map/all_gather | solution.py:178
  94.5 16.2 %all_gather.24 = bf16[512,512]{0,1:T(8,128)(2,1)} all-gather(bf16[128,512]{0,1:T(8,128)(2,1)S(1)} %bitcast.287), channel_id=1, replica_groups=mesh['ctx'=4,'shard'=8] {'ctx'}, dimensions={0}, use_global_device_ids=true | all-gather | bytes 655360 | tf_op jit(solution)/shard_map/all_gather | solution.py:177
  110.8 51.5 %all-gather.7.cloned.1.call-done = bf16[2048,4096]{1,0:T(8,128)(2,1)} async-done(((bf16[256,4096]{1,0:T(8,128)(2,1)}), bf16[2048,4096]{1,0:T(8,128)(2,1)}) %all-gather.7.cloned.1.call-update) | async-done | bytes 16777232 | tf_op jit(solution)/shard_map/all_gather | solution.py:119
  162.3 22.1 %copy.109 = bf16[4096,2048]{1,0:T(8,128)(2,1)} copy(bf16[4096,2048]{0,1:T(8,128)(2,1)} %bitcast.257) | data formatting | bytes 33554432 | tf_op jit(solution)/shard_map/dot_general | solution.py:127
  184.4 8.4 multiply_reduce_fusion.3
  202.5 51.4 %all-gather.11.cloned.1.call-done = bf16[4096,2048]{1,0:T(8,128)(2,1)} async-done(((bf16[512,2048]{1,0:T(8,128)(2,1)}), bf16[4096,2048]{1,0:T(8,128)(2,1)}) %all-gather.11.cloned.1.call-update) | async-done | bytes 16777232 | tf_op jit(solution)/shard_map/all_gather | solution.py:123
  253.9 8.6 multiply_reduce_fusion.6
  264.4 10.3 scatter_custom_fusion
  274.7 120.7 %all_to_all.20 = bf16[32,40,2048]{2,1,0:T(8,128)(2,1)S(1)} all-to-all(bf16[32,40,2048]{2,1,0:T(8,128)(2,1)} %bitcast.259), channel_id=1, replica_groups=mesh['ctx'=4,'shard'=8] {'ctx','shard'}, dimensions={0} | all-to-all | bytes 10485760 | tf_op jit(solution)/shard_map/all_to_all | solution.py:204
  416.3 38.7 %all_gather.29 = bf16[2048,32]{0,1:T(8,128)(2,1)S(1)} all-gather(bf16[256,32]{0,1:T(8,128)(2,1)S(1)} %copy-done.48), channel_id=1, replica_groups=mesh['ctx'=4,'shard'=8] {'shard'}, dimensions={0}, use_global_device_ids=true | all-gather | bytes 147456 | tf_op jit(solution)/shard_map/all_gather | solution.py:122
  458.6 74.5 %all-to-all-done.1 = bf16[32,40,2048]{2,1,0:T(8,128)(2,1)} async-done(((bf16[32,40,2048]{2,1,0:T(8,128)(2,1)}), bf16[32,40,2048]{2,1,0:T(8,128)(2,1)}, u32[]{:S(2)}, u32[]{:S(2)}) %all-to-all-start.1) | async-done | bytes 5242912 | tf_op jit(solution)/shard_map/all_to_all | solution.py:218
  533.1 12.2 gather_fusion
  550.6 10.5 scatter_custom_fusion.1
  561.1 120.0 %all_to_all.21 = bf16[32,40,2048]{2,1,0:T(8,128)(2,1)S(1)} all-to-all(bf16[32,40,2048]{2,1,0:T(8,128)(2,1)} %bitcast.258), channel_id=1, replica_groups=mesh['ctx'=4,'shard'=8] {'ctx','shard'}, dimensions={0} | all-to-all | bytes 10485760 | tf_op jit(solution)/shard_map/all_to_all | solution.py:239
  709.2 110.9 %all-to-all-done.3 = bf16[32,40,2048]{2,1,0:T(8,128)(2,1)} async-done(((bf16[32,40,2048]{2,1,0:T(8,128)(2,1)}), bf16[32,40,2048]{2,1,0:T(8,128)(2,1)}, u32[]{:S(2)}, u32[]{:S(2)}) %all-to-all-start.3) | async-done | bytes 5242912 | tf_op jit(solution)/shard_map/all_to_all | solution.py:256
  820.0 8.0 bitcast_convert_fusion
  828.0 13.1 gather_fusion.1
  849.3 8.2 convolution_convert_fusion.1
  857.5 11.4 convolution_convert_fusion.3
  887.9 24.6 %reshape.494 = bf16[2048,4096]{1,0:T(8,128)(2,1)} reshape(bf16[4096,2048]{1,0:T(8,128)(2,1)} %convolution_convert_fusion.1) | data formatting | bytes 33554432 | tf_op jit(solution)/shard_map/reshape | solution.py:81
  923.4 14.8 %reduce-scatter.12.cloned.1.call-done = bf16[128,512]{1,0:T(8,128)(2,1)} async-done(((bf16[512,512]{1,0:T(8,128)(2,1)}), bf16[128,512]{1,0:T(8,128)(2,1)}) %reduce-scatter.12.cloned.1.call-update) | async-done | bytes 131088
  939.3 11.4 convolution_convert_fusion
  950.7 63.8 %concatenate.18 = bf16[2048,9248]{1,0:T(8,128)(2,1)} concatenate(bf16[2048,5120]{1,0:T(8,128)(2,1)} %convolution_convert_fusion, bf16[2048,32]{1,0:T(8,128)(2,1)S(1)} %copy-done.25, bf16[2048,4096]{1,0:T(8,128)(2,1)} %reshape.494), dimensions={1} | concatenate | bytes 75759616 | tf_op jit(solution)/shard_map/concatenate | solution.py:81
  1014.5 226.1 %reduce-scatter.8.cloned.1.call-done = bf16[256,9248]{1,0:T(8,128)(2,1)} async-done(((bf16[2048,9248]{1,0:T(8,128)(2,1)}), bf16[256,9248]{1,0:T(8,128)(2,1)}) %reduce-scatter.8.cloned.1.call-update) | async-done | bytes 4734992 | tf_op jit(solution)/shard_map/reduce_scatter | solution.py:379
  1240.7 9.0 convolution_bitcast_fusion.2
  1249.7 8.8 convolution_bitcast_fusion.1
  1264.8 11.6 fusion.122
  1280.1 47.9 %all-reduce.4 = (f32[2048]{0:T(1024)}, f32[128]{0:T(128)}, f32[128]{0:T(128)}, f32[2048]{0:T(1024)}) all-reduce(f32[2048]{0:T(1024)S(1)} %get-tuple-element.88, f32[128]{0:T(128)S(1)} %copy-done.56, f32[128]{0:T(128)S(1)} %copy-done.57, f32[2048]{0:T(1024)S(1)} %copy-done.45), channel_id=1, replica_groups=mesh['ctx'=4,'shard'=8] {'ctx','shard'}, use_global_device_ids=true, to_apply=%region_27.28 | all-reduce | flops 4352 | bytes 34816 | tf_op jit(solution)/shard_map/psum | solution.py:375
  1329.2 89.0 %all-reduce.7.cloned.1.call-done = bf16[256,9248]{1,0:T(8,128)(2,1)} async-done(((bf16[256,9248]{1,0:T(8,128)(2,1)}), bf16[256,9248]{1,0:T(8,128)(2,1)}) %all-reduce.7.cloned.1.call-update) | async-done | bytes 4734992 | tf_op jit(solution)/shard_map/psum | solution.py:387
  (273 shorter events, 151.9 us)
Async XLA Ops:
  7.2 399.3 %copy-start = (bf16[1,768,2048]{2,1,0:T(8,128)(2,1)S(1)}, bf16[1,768,2048]{2,1,0:T(8,128)(2,1)}, u32[]{:S(2)}) copy-start(bf16[1,768,2048]{2,1,0:T(8,128)(2,1)} %param.31) | copy-start | bytes 9437188
  7.2 12.8 copy-start.60
  7.2 33.4 %all-gather.5.cloned.1.call-start = ((), (), s32[]{:S(2)}) async-start(), calls=%async_computation.7 | async-start | bytes 2359296 | tf_op jit(solution)/shard_map/all_gather | solution.py:120
  8.0 62.5 %all-gather.9.cloned.1.call-start = ((), (), s32[]{:S(2)}) async-start(), calls=%async_computation.9 | async-start | bytes 2359296 | tf_op jit(solution)/shard_map/all_gather | solution.py:121
  8.7 153.6 %all-gather.7.cloned.1.call-start = ((), (), s32[]{:S(2)}) async-start(), calls=%async_computation.8 | async-start | bytes 18874368 | tf_op jit(solution)/shard_map/all_gather | solution.py:119
  9.4 61.0 %copy-start.35 = (f32[2048]{0:T(1024)S(1)}, f32[2048]{0:T(1024)}, u32[]{:S(2)}) copy-start(f32[2048]{0:T(1024)} %param.20) | copy-start | bytes 24580
  9.4 244.4 %all-gather.11.cloned.1.call-start = ((), (), s32[]{:S(2)}) async-start(), calls=%async_computation.10 | async-start | bytes 18874368 | tf_op jit(solution)/shard_map/all_gather | solution.py:123
  22.0 162.4 %copy-start.46 = (f32[128]{0:T(128)}, f32[128]{0:T(128)S(1)}, u32[]{:S(2)}) copy-start(f32[128]{0:T(128)S(1)} %fusion.108) | copy-start | bytes 1540
  22.3 171.0 %copy-start.28 = (f32[128,64]{0,1:T(8,128)}, f32[128,64]{0,1:T(8,128)S(1)}, u32[]{:S(2)}) copy-start(f32[128,64]{0,1:T(8,128)S(1)} %get-tuple-element.118) | copy-start | bytes 98308
  22.3 171.0 %copy-start.30 = (f32[128,64]{0,1:T(8,128)}, f32[128,64]{0,1:T(8,128)S(1)}, u32[]{:S(2)}) copy-start(f32[128,64]{0,1:T(8,128)S(1)} %get-tuple-element.119) | copy-start | bytes 98308
  44.6 49.8 %copy-start.52 = (f32[128]{0:T(128)S(1)}, f32[128]{0:T(128)}, u32[]{:S(2)}) copy-start(f32[128]{0:T(128)} %param.25) | copy-start | bytes 1540
  93.7 90.7 %copy-start.50 = (f32[128,4]{0,1:T(4,128)}, f32[128,4]{0,1:T(4,128)S(1)}, u32[]{:S(2)}) copy-start(f32[128,4]{0,1:T(4,128)S(1)} %get-tuple-element.120) | copy-start | bytes 6148
  253.9 9.6 copy-start.41
  274.7 120.7 %copy-start.61 = (bf16[1,2048,768]{2,1,0:T(8,128)(2,1)S(1)}, bf16[1,2048,768]{2,1,0:T(8,128)(2,1)}, u32[]{:S(2)}) copy-start(bf16[1,2048,768]{2,1,0:T(8,128)(2,1)} %param.29) | copy-start | bytes 9437188
  412.5 120.6 %all-to-all-start.1 = ((bf16[32,40,2048]{2,1,0:T(8,128)(2,1)}), bf16[32,40,2048]{2,1,0:T(8,128)(2,1)}, u32[]{:S(2)}, u32[]{:S(2)}) async-start(bf16[32,40,2048]{2,1,0:T(8,128)(2,1)} %bitcast.279), calls=%async_computation.1 | async-start | bytes 10485760 | tf_op jit(solution)/shard_map/all_to_all | solution.py:218
  561.1 120.1 %copy-start.68 = (f32[1280,768]{1,0:T(8,128)S(1)}, f32[1280,768]{1,0:T(8,128)}, u32[]{:S(2)}) copy-start(f32[1280,768]{1,0:T(8,128)} %copy-done.67) | copy-start | bytes 11796484
  561.1 120.1 %copy-start.72 = (f32[1280,768]{1,0:T(8,128)S(1)}, f32[1280,768]{1,0:T(8,128)}, u32[]{:S(2)}) copy-start(f32[1280,768]{1,0:T(8,128)} %get-tuple-element.131) | copy-start | bytes 11796484
  699.4 120.6 %all-to-all-start.3 = ((bf16[32,40,2048]{2,1,0:T(8,128)(2,1)}), bf16[32,40,2048]{2,1,0:T(8,128)(2,1)}, u32[]{:S(2)}, u32[]{:S(2)}) async-start(bf16[32,40,2048]{2,1,0:T(8,128)(2,1)} %bitcast.278), calls=%async_computation.3 | async-start | bytes 10485760 | tf_op jit(solution)/shard_map/all_to_all | solution.py:256
  703.3 217.5 %reduce-scatter.10.cloned.1.call-start = ((), (), s32[]{:S(2)}) async-start(), calls=%async_computation.13 | async-start | bytes 655360
  886.8 51.4 %reduce-scatter.12.cloned.1.call-start = ((), (), s32[]{:S(2)}) async-start(), calls=%async_computation.14 | async-start | bytes 655360
  887.9 24.6 %copy-start.19 = (bf16[512,512]{0,1:T(8,128)(2,1)S(1)}, bf16[512,512]{0,1:T(8,128)(2,1)}, u32[]{:S(2)}) copy-start(bf16[512,512]{0,1:T(8,128)(2,1)} %all_gather.24) | copy-start | bytes 1572868
  917.5 21.8 %copy-start.5 = (bf16[1,128,2048]{2,1,0:T(8,128)(2,1)S(1)}, bf16[1,128,2048]{2,1,0:T(8,128)(2,1)}, u32[]{:S(2)}) copy-start(bf16[1,128,2048]{2,1,0:T(8,128)(2,1)} %param.16) | copy-start | bytes 1572868
  917.5 21.8 %copy-start.36 = (f32[2048]{0:T(1024)S(1)}, f32[2048]{0:T(1024)}, u32[]{:S(2)}) copy-start(f32[2048]{0:T(1024)} %param.20) | copy-start | bytes 24580
  917.5 21.8 %copy-start.47 = (f32[128]{0:T(128)S(1)}, f32[128]{0:T(128)}, u32[]{:S(2)}) copy-start(f32[128]{0:T(128)} %copy-done.46) | copy-start | bytes 1540
  917.5 323.1 %reduce-scatter.8.cloned.1.call-start = ((), (), s32[]{:S(2)}) async-start(), calls=%async_computation.11 | async-start | bytes 43057152 | tf_op jit(solution)/shard_map/reduce_scatter | solution.py:379
  939.3 11.4 copy-start.25
  1014.5 226.2 %copy-start.70 = (bf16[1280,768]{1,0:T(8,128)(2,1)S(1)}, bf16[1280,768]{1,0:T(8,128)(2,1)}, u32[]{:S(2)}) copy-start(bf16[1280,768]{1,0:T(8,128)(2,1)} %copy-done.69) | copy-start | bytes 5898244
  1014.5 403.8 %all-reduce.7.cloned.1.call-start = ((), (), s32[]{:S(2)}) async-start(), calls=%async_computation.12 | async-start | bytes 9568256 | tf_op jit(solution)/shard_map/psum | solution.py:387
  1240.7 9.0 copy-start.71
  1240.7 17.8 %slice-start = ((s8[5242880]{0:T(1024)(128)(4,1)}), s8[4194304]{0:T(1024)(128)(4,1)S(1)}, s32[]{:S(2)}) async-start(s8[5242880]{0:T(1024)(128)(4,1)} %bitcast.275), calls=%async_computation.15 | async-start | bytes 8388608
  1276.4 51.5 %copy-start.59 = (f32[128]{0:T(128)S(1)}, f32[128]{0:T(128)}, u32[]{:S(2)}) copy-start(f32[128]{0:T(128)} %copy-done.58) | copy-start | bytes 1540
  1276.4 51.5 %copy-start.7 = (f32[128,2048]{1,0:T(8,128)S(1)}, f32[128,2048]{1,0:T(8,128)}, u32[]{:S(2)}) copy-start(f32[128,2048]{1,0:T(8,128)} %copy-done.6) | copy-start | bytes 3145732
  (53 other events, 214.8 us)
Sparse Core Ops, SparseCore 0:
  9.9 30.6 all-gather.4
  42.5 27.8 all-gather.8
  72.4 89.8 all-gather.6
  164.0 89.8 all-gather.10
  886.9 20.5 reduce-scatter.9
  917.6 20.5 reduce-scatter.11
  1014.6 226.0 reduce-scatter.7
  1243.2 175.0 all-reduce.6
where the time goes:
time: 1450 us; the launch traced here: 1440 us
  waiting for transfers between devices  665 us (46%)
  blocking collectives  360 us (25%)
  local copies, waits for them, and re-layouts  180 us (12%)
  matrix products  159 us (11%)
  other arithmetic  53.5 us (4%)
  between operations  15.7 us (1%)
    reduce_scatter x1, waiting for transfers between devices, shards(): lax.psum_scatter(weight_terms_of(normed_b, second_b, attn_b, projected, g...  226 us
    all_to_all x1, blocking collectives, shards(): lax.all_to_all(send_rows.reshape(experts, capacity, model_width), ('ctx',...  121 us
    all_to_all x1, blocking collectives, shards(): lax.all_to_all(back_send.reshape(experts, capacity, model_width), ('ctx',...  120 us
    all_to_all x1, waiting for transfers between devices, shards(): lax.all_to_all(grad_received.reshape(experts, capacity, model_width).asty...  111 us
    psum x1, waiting for transfers between devices, shards(): summed = lax.psum(partial_rows, 'ctx').astype(jnp.float32)  89 us
    all_to_all x1, waiting for transfers between devices, shards(): lax.all_to_all(expert_out.reshape(experts, capacity, model_width), ('ctx'...  74.5 us
    concatenate x1, local copies, waits for them, and re-layouts, weight_terms_of(): jnp.concatenate([part_one, part_two, part_three.reshape(left_in.shape[1],...  63.8 us
    all_gather x1, waiting for transfers between devices, shards(): lax.all_gather(w_query, 'shard', axis=0, tiled=True)  51.5 us
  transfers between devices with their start and end apart: 10, of which 9 were waited for; matrix products, arithmetic and copies ran while one was open for 10% of the time, Pallas kernels for 0%

commit v1 on v0

v1 whole, which is shorter than its diff:
```python
import jax
import jax.numpy as jnp
from jax import lax
from jax.sharding import PartitionSpec as P

QUERY_HEADS = 32
KEY_VALUE_HEADS = 4
HEAD_DIM = 128

epsilon = 1e-06
rope_base = 1000000.0
BF = jnp.bfloat16
F32 = jnp.float32


def rms_scale(hidden, gain):
    return hidden * lax.rsqrt(jnp.mean(hidden * hidden, axis=-1, keepdims=True) + epsilon) * gain


def rotate(headwise, places):
    half_size = headwise.shape[-1] // 2
    frequency = rope_base ** (-jnp.arange(half_size, dtype=F32) * 2.0 / headwise.shape[-1])
    angles = places.astype(F32)[:, None] * frequency[None, :]
    cosine = jnp.cos(angles)[:, None, :]
    sine = jnp.sin(angles)[:, None, :]
    former = headwise[..., :half_size]
    latter = headwise[..., half_size:]
    return jnp.concatenate(
        [former * cosine - latter * sine, latter * cosine + former * sine], axis=-1
    )


def place_of(row_ids, order, block_rows):
    block_ids = jnp.arange(order.shape[0], dtype=jnp.int32)
    owner_block = row_ids // block_rows
    picked_block = jnp.sum(
        jnp.where(owner_block[:, None] == block_ids[None, :], order[None, :], 0), axis=1
    )
    return picked_block * block_rows + row_ids % block_rows


def dot(left, right):
    return jnp.dot(left, right, preferred_element_type=F32)


def contract_rows(left, right):
    return lax.dot_general(left, right, (((0,), (0,)), ((), ())), preferred_element_type=F32)


def contract_cols(left, right):
    return lax.dot_general(left, right, (((1,), (1,)), ((), ())), preferred_element_type=F32)


def gather_shard(x):
    return lax.all_gather(x, "shard", axis=0, tiled=True)


def scatter_shard(x):
    return lax.psum_scatter(x, "shard", scatter_dimension=0, tiled=True)


def exchange_shard(x):
    return lax.all_to_all(x, "shard", split_axis=0, concat_axis=0, tiled=True)


def gather_ctx(x):
    return lax.all_gather(x, "ctx", axis=0, tiled=False)


def scatter_ctx(x):
    return lax.psum_scatter(x, "ctx", scatter_dimension=0, tiled=False)


def shards(
    tokens,
    cotangent,
    block_order,
    routes,
    attn_gain,
    w_query,
    key_weight,
    value_weight,
    query_gain,
    key_gain,
    w_out,
    ffn_gain,
    w_router,
    w_gate,
    w_up,
    w_down,
):
    rows = tokens.shape[1]
    width = tokens.shape[2]
    ctx_count = lax.axis_size("ctx")
    shard_count = lax.axis_size("shard")
    my_ctx = lax.axis_index("ctx")
    my_shard = lax.axis_index("shard")
    experts = ctx_count * shard_count
    block_rows = rows // 2
    heads = QUERY_HEADS // shard_count
    head_cols = heads * HEAD_DIM
    sharers = shard_count // KEY_VALUE_HEADS
    score_scale = HEAD_DIM ** (-0.5)
    top_count = routes.shape[2]
    capacity = rows * top_count // experts + max(rows * top_count // (4 * experts), 1)
    sequence = rows * ctx_count
    plane = rows * shard_count
    wrows = width // shard_count

    inputs = tokens[0].astype(F32)
    upstream_b = cotangent[0]
    upstream = upstream_b.astype(F32)

    kv_kind = [key_weight, value_weight]
    extra = [
        kv_kind[(s % sharers) % 2][:, (s // sharers) * HEAD_DIM : (s // sharers + 1) * HEAD_DIM]
        for s in range(shard_count)
    ]
    send_w = jnp.stack(
        [
            jnp.concatenate([w_query[:, s * head_cols : (s + 1) * head_cols], extra[s]], axis=1)
            for s in range(shard_count)
        ]
    )
    w_mine = exchange_shard(send_w).reshape(width, head_cols + HEAD_DIM)

    normed = rms_scale(inputs, attn_gain)
    normed_b = normed.astype(BF)
    normed_all = gather_shard(normed_b)

    routes_all = lax.all_gather(routes[0], ("ctx", "shard"), axis=0, tiled=False).reshape(
        ctx_count, shard_count, rows, top_count
    )
    named = jnp.sum(
        (routes_all[..., None] == jnp.arange(experts, dtype=jnp.int32)).astype(BF), axis=3
    )
    earlier = (
        jnp.arange(rows, dtype=jnp.int32)[:, None] > jnp.arange(rows, dtype=jnp.int32)[None, :]
    ).astype(BF)
    slots = jnp.arange(capacity, dtype=F32)

    def places_in(mask):
        rank = jnp.einsum("tu,...un->...tn", earlier, mask, preferred_element_type=F32)
        pick = jnp.where(mask > 0, rank, -1.0)
        return (jnp.swapaxes(pick, -1, -2)[..., None, :] == slots[:, None]).astype(BF)

    my_rows = lax.dynamic_index_in_dim(named, my_shard, 1, keepdims=False)
    my_rows = lax.dynamic_slice_in_dim(my_rows, my_ctx * shard_count, shard_count, 2)
    pick_send = places_in(my_rows)
    mine = lax.dynamic_slice_in_dim(named, my_ctx * shard_count + my_shard, 1, 3)
    pick_here = places_in(mine)[:, :, 0]
    chosen_here = jnp.einsum(
        "cbqt,cbte->bcqe", pick_here, named, preferred_element_type=F32
    ).reshape(-1, experts)

    def dispatch(rows_b):
        every = gather_ctx(rows_b)
        sent = jnp.einsum("bsqt,btd->sbqd", pick_send, every, preferred_element_type=F32)
        return exchange_shard(sent.astype(BF).reshape(shard_count, ctx_count * capacity, -1)).reshape(
            shard_count * ctx_count * capacity, -1
        )

    def combine(slot_rows):
        back = exchange_shard(slot_rows.reshape(shard_count, ctx_count * capacity, -1))
        back = back.reshape(shard_count, ctx_count, capacity, -1)
        part = jnp.einsum("bsqt,sbqd->btd", pick_send, back, preferred_element_type=F32)
        return scatter_ctx(part.astype(BF)).astype(F32)

    grad_expert_rows = dispatch(upstream_b)

    qkv = dot(normed_all, w_mine)
    query_pre = qkv[:, :head_cols].reshape(shard_count, rows, heads, HEAD_DIM)
    row_ids = my_ctx * rows + jnp.arange(rows, dtype=jnp.int32)
    q_places = place_of(row_ids, block_order, block_rows)
    k_places = place_of(jnp.arange(sequence, dtype=jnp.int32), block_order, block_rows)
    sees = k_places[None, :] <= q_places[:, None]

    def prep(pre, gain):
        shape = pre.shape
        flat = pre.reshape(-1, rows, shape[-2], HEAD_DIM)
        return jax.vmap(lambda v: rotate(rms_scale(v, gain), q_places))(flat).reshape(shape)

    queries = prep(query_pre, query_gain).astype(BF)
    my_place = lax.rem(my_shard, sharers)
    is_key = lax.rem(my_place, 2) == 0
    part_count = sharers // 2
    kv_pre = qkv[:, head_cols:]
    key_roped = prep(kv_pre.reshape(shard_count, rows, 1, HEAD_DIM), key_gain).reshape(plane, HEAD_DIM)
    kv_b = jnp.where(is_key, key_roped, kv_pre).astype(BF)
    groups = [
        [g * sharers + i for i in range(sharers)] for g in range(KEY_VALUE_HEADS)
    ]
    kv_pair = lax.all_gather(kv_b, "shard", axis=0, tiled=False, axis_index_groups=groups)[:2]
    kv_all = gather_ctx(kv_pair)
    kv_all = kv_all.reshape(ctx_count, 2, shard_count, rows, HEAD_DIM)
    kv_all = jnp.transpose(kv_all, (1, 2, 0, 3, 4)).reshape(2, shard_count, sequence, HEAD_DIM)
    keys, values = kv_all[0], kv_all[1]

    scores = (
        jnp.einsum("sthd,spd->shtp", queries, keys, preferred_element_type=F32) * score_scale
    )
    scores = jnp.where(sees, scores, -1e30)
    top = jnp.max(scores, axis=-1, keepdims=True)
    raised = jnp.exp(scores - top)
    total = jnp.sum(raised, axis=-1, keepdims=True)
    probs = raised / total
    probs_b = probs.astype(BF)
    attn_f32 = jnp.einsum("shtp,spd->sthd", probs_b, values, preferred_element_type=F32)
    attn_b = attn_f32.astype(BF)
    attn_rows = attn_b.reshape(plane, head_cols)
    proj = scatter_shard(dot(attn_rows, w_out).astype(BF))
    middle = inputs + proj.astype(F32)

    normed_two = rms_scale(middle, ffn_gain)
    second_b = normed_two.astype(BF)
    router_all = gather_shard(w_router)
    logits = dot(second_b, router_all)
    chosen = jnp.sum(
        (routes[0][:, :, None] == jnp.arange(experts, dtype=jnp.int32)).astype(F32), axis=1
    )

    def gates_of(log, mask):
        masked = jnp.where(mask > 0, log, -1e30)
        peak = jnp.max(masked, axis=-1, keepdims=True)
        risen = jnp.exp(masked - peak) * mask
        return risen / jnp.maximum(jnp.sum(risen, axis=-1, keepdims=True), 1e-30)

    gates = gates_of(logits, chosen)

    received = dispatch(second_b)
    my_expert = my_ctx * shard_count + my_shard
    slot_gates = lax.dynamic_slice_in_dim(
        gates_of(dot(received, router_all), chosen_here), my_expert, 1, 1
    )
    gate_pre = dot(received, w_gate[0])
    up_pre = dot(received, w_up[0])
    activated = jax.nn.silu(gate_pre)
    hidden_b = (activated * up_pre).astype(BF)
    expert_out = dot(hidden_b, w_down[0]).astype(BF)
    expert_out_f = expert_out.astype(F32)
    mixed = (middle + combine((slot_gates * expert_out_f).astype(BF))).astype(BF)
    upstream_rows = grad_expert_rows.astype(F32)
    slot_dot = jnp.sum(expert_out_f * upstream_rows, axis=1, keepdims=True)
    grad_expert = (slot_gates * upstream_rows).astype(BF)
    grad_w_down = contract_rows(hidden_b, grad_expert)
    grad_hidden = contract_cols(grad_expert, w_down[0])
    sigmoid_g = jax.nn.sigmoid(gate_pre)
    silu_slope = sigmoid_g * (1.0 + gate_pre * (1.0 - sigmoid_g))
    grad_gate_pre = (grad_hidden * up_pre * silu_slope).astype(BF)
    grad_up_pre = (grad_hidden * activated).astype(BF)
    grad_w_gate = contract_rows(received, grad_gate_pre)
    grad_w_up = contract_rows(received, grad_up_pre)
    grad_received = contract_cols(grad_gate_pre, w_gate[0]) + contract_cols(grad_up_pre, w_up[0])

    tail_cols = -(-2 * experts // 128) * 128
    coarse = slot_dot.astype(BF).astype(F32)
    fine = slot_dot - coarse
    column = jnp.arange(tail_cols, dtype=jnp.int32)[None, :]
    tail = jnp.where(column == my_expert, coarse, 0.0) + jnp.where(
        column == experts + my_expert, fine, 0.0
    )
    back = combine(jnp.concatenate([grad_received, tail], axis=1).astype(BF))
    grad_second = back[:, :width]
    grad_gates = back[:, width : width + experts] + back[:, width + experts : width + 2 * experts]
    grad_logits_b = (
        gates * (grad_gates - jnp.sum(gates * grad_gates, axis=-1, keepdims=True))
    ).astype(BF)
    grad_w_router_part = contract_rows(second_b, grad_logits_b)
    grad_second = grad_second + contract_cols(grad_logits_b, router_all)
    unused, norm_two_back = jax.vjp(rms_scale, middle, ffn_gain)
    grad_middle_part, grad_ffn_gain = norm_two_back(grad_second)
    grad_middle = upstream + grad_middle_part
    grad_proj_b = grad_middle.astype(BF)

    grad_proj_all = gather_shard(grad_proj_b)
    grad_attn = contract_cols(grad_proj_all, w_out).astype(BF)
    grad_w_out = lax.psum(contract_rows(attn_rows, grad_proj_all).astype(BF), "ctx").astype(F32)
    grad_heads = grad_attn.reshape(shard_count, rows, heads, HEAD_DIM)
    delta = jnp.transpose(jnp.sum(grad_heads.astype(F32) * attn_f32, axis=-1), (0, 2, 1))[..., None]
    grad_probs = jnp.einsum("sthd,spd->shtp", grad_heads, values, preferred_element_type=F32)
    grad_scores = (probs * (grad_probs - delta)).astype(BF)
    grad_query = score_scale * jnp.einsum(
        "shtp,spd->sthd", grad_scores, keys, preferred_element_type=F32
    )
    grad_keys = score_scale * jnp.einsum(
        "shtp,sthd->spd", grad_scores, queries, preferred_element_type=F32
    )
    grad_values = jnp.einsum("shtp,sthd->spd", probs_b, grad_heads, preferred_element_type=F32)
    grad_kv = jnp.stack([grad_keys, grad_values]).astype(BF)
    grad_kv = grad_kv.reshape(2, shard_count, ctx_count, rows, HEAD_DIM)
    grad_kv = scatter_ctx(jnp.transpose(grad_kv, (2, 0, 1, 3, 4)))
    grad_kv = grad_kv.reshape(2, part_count, plane // part_count, HEAD_DIM)
    grad_kv = jnp.transpose(grad_kv, (1, 0, 2, 3)).reshape(sharers, plane // part_count, HEAD_DIM)
    grad_kv = lax.psum_scatter(
        grad_kv, "shard", scatter_dimension=0, tiled=False, axis_index_groups=groups
    ).astype(F32)
    first = (my_place // 2) * (plane // part_count)

    unused, query_back = jax.vjp(prep, query_pre, query_gain)
    grad_query_pre, grad_query_gain = query_back(grad_query)
    parts_k = (shard_count // part_count, rows, 1, HEAD_DIM)
    kv_mine = lax.dynamic_slice_in_dim(kv_pre, first, plane // part_count, 0)
    unused, key_back = jax.vjp(prep, kv_mine.reshape(parts_k), key_gain)
    grad_key_pre, grad_key_gain = key_back(grad_kv.reshape(parts_k))
    grad_key_gain = jnp.where(is_key, grad_key_gain, 0.0)
    grad_kv_b = jnp.where(is_key, grad_key_pre.reshape(-1, HEAD_DIM), grad_kv).astype(BF)
    if part_count > 1:
        grad_kv_full = lax.dynamic_update_slice_in_dim(
            jnp.zeros((plane, HEAD_DIM), BF), grad_kv_b, first, 0
        )
    else:
        grad_kv_full = grad_kv_b
    grad_pre = jnp.concatenate(
        [grad_query_pre.reshape(plane, head_cols).astype(BF), grad_kv_full], axis=1
    )
    grad_normed = scatter_shard(contract_cols(grad_pre, w_mine).astype(BF)).astype(F32)
    unused, norm_one_back = jax.vjp(rms_scale, inputs, attn_gain)
    grad_input_part, grad_attn_gain = norm_one_back(grad_normed)
    grad_tokens = grad_middle + grad_input_part
    grad_attn_gain, grad_query_gain, grad_key_gain, grad_ffn_gain = lax.psum(
        (grad_attn_gain, grad_query_gain, grad_key_gain, grad_ffn_gain), ("ctx", "shard")
    )

    grad_w = contract_rows(normed_all, grad_pre).astype(BF)
    router_cols = -(-experts // 128) * 128
    router_part = jnp.pad(grad_w_router_part, ((0, 0), (0, router_cols - experts))).astype(BF)
    packed = jnp.concatenate([grad_w, router_part], axis=1).reshape(shard_count, wrows, -1)
    packed = exchange_shard(packed)
    queries_part = jnp.transpose(packed[:, :, :head_cols], (1, 0, 2)).reshape(wrows, -1)
    kinds = packed[:, :, head_cols : head_cols + HEAD_DIM].astype(F32)
    kinds = jnp.sum(kinds.reshape(KEY_VALUE_HEADS, part_count, 2, wrows, HEAD_DIM), axis=1)
    kinds = jnp.transpose(kinds, (2, 1, 0, 3)).reshape(wrows, -1).astype(BF)
    router_sum = jnp.sum(packed[:, :, head_cols + HEAD_DIM :].astype(F32), axis=0).astype(BF)
    summed = lax.psum(jnp.concatenate([queries_part, kinds, router_sum], axis=1), "ctx").astype(F32)
    width_q = QUERY_HEADS * HEAD_DIM
    key_width = KEY_VALUE_HEADS * HEAD_DIM
    grad_w_query = summed[:, :width_q]
    grad_w_key = summed[:, width_q : width_q + key_width]
    grad_w_value = summed[:, width_q + key_width : width_q + 2 * key_width]
    grad_w_router = summed[:, width_q + 2 * key_width : width_q + 2 * key_width + experts]
    return (
        mixed[None],
        grad_tokens[None],
        grad_attn_gain,
        grad_w_query,
        grad_w_key,
        grad_w_value,
        grad_query_gain,
        grad_key_gain,
        grad_w_out,
        grad_ffn_gain,
        grad_w_router,
        grad_w_gate[None],
        grad_w_up[None],
        grad_w_down[None],
    )


def solution(mesh):
    rows = P("shard", "ctx", None)
    matrix = P("shard", None)
    expert = P(("ctx", "shard"), None, None)
    return jax.shard_map(
        shards,
        mesh=mesh,
        in_specs=(
            rows, rows, P(), rows, P(), matrix, matrix, matrix, P(), P(), matrix, P(), matrix,
            expert, expert, expert,
        ),
        out_specs=(
            rows, rows, P(), matrix, matrix, matrix, P(), P(), matrix, P(), matrix,
            expert, expert, expert,
        ),
        check_vma=False,
    )
```

time: 1450 us -> 1050 us (0.72)
  waiting for transfers between devices: 665 us -> 431 us
  local copies, waits for them, and re-layouts: 180 us -> 59.8 us
  blocking collectives: 360 us -> 295 us
    all_to_all x2 -> x4, waiting for transfers between devices: 185 us -> 83.3 us  [exchange_shard(): return lax.all_to_all(x, 'shard', split_axis=0, concat_axis=0, tiled=True)]
    reduce_scatter x1 -> x6, waiting for transfers between devices: 226 us -> 131 us  [the longest x3 81.1 us: scatter_ctx(): return lax.psum_scatter(x, 'ctx', scatter_dimension=0, tiled=False)]
    all_to_all x2, blocking collectives: 241 us -> 147 us  [exchange_shard(): return lax.all_to_all(x, 'shard', split_axis=0, concat_axis=0, tiled=True)]
    concatenate x1 -> x0, local copies, waits for them, and re-layouts: 63.8 us -> none  [weight_terms_of(): jnp.concatenate([part_one, part_two, part_three.reshape(left_in.shape[1],...]
    all_gather x3, blocking collectives: 71.3 us -> 104 us  [the longest x1 58.8 us: gather_shard(): return lax.all_gather(x, 'shard', axis=0, tiled=True)]
    all_gather x4 -> x5, waiting for transfers between devices: 147 us -> 116 us  [the longest x3 80.3 us: gather_ctx(): return lax.all_gather(x, 'ctx', axis=0, tiled=False)]
    gather x2 -> x0, local copies, waits for them, and re-layouts: 25.3 us -> none  [the longest x1 13.1 us: shards(): grad_back[target_rows].reshape(rows_per_shard, top_count, model_width)]
    dot_general x3 -> x1, local copies, waits for them, and re-layouts: 26.1 us -> 1.14 us  [shards(): jnp.einsum('cbqt,cbte->bcqe', pick_here, named, preferred_element_type=F32)]
  transfers between devices with their start and end apart: 10 -> 16, of which waited for: 9 -> 11; matrix products, arithmetic and copies ran while one was open for 10% -> 12% of each run, Pallas kernels for 0% -> 0%
where the time goes in v1:
time: 1050 us; the launch traced here: 1040 us
  waiting for transfers between devices  431 us (41%)
  blocking collectives  295 us (28%)
  matrix products  160 us (15%)
  other arithmetic  61.8 us (6%)
  local copies, waits for them, and re-layouts  59.8 us (6%)
  starting transfers between devices  20.9 us (2%)
  between operations  15.5 us (1%)
    all_to_all x2, blocking collectives, exchange_shard(): return lax.all_to_all(x, 'shard', split_axis=0, concat_axis=0, tiled=True)  147 us
    psum x1, waiting for transfers between devices, shards(): lax.psum(jnp.concatenate([queries_part, kinds, router_sum], axis=1), 'ctx')  98.8 us
    all_to_all x4, waiting for transfers between devices, exchange_shard(): return lax.all_to_all(x, 'shard', split_axis=0, concat_axis=0, tiled=True)  83.3 us
    reduce_scatter x3, waiting for transfers between devices, scatter_ctx(): return lax.psum_scatter(x, 'ctx', scatter_dimension=0, tiled=False)  81.1 us
    all_gather x3, waiting for transfers between devices, gather_ctx(): return lax.all_gather(x, 'ctx', axis=0, tiled=False)  80.3 us
    all_gather x1, blocking collectives, gather_shard(): return lax.all_gather(x, 'shard', axis=0, tiled=True)  58.8 us
    reduce_scatter x2, waiting for transfers between devices, scatter_shard(): return lax.psum_scatter(x, 'shard', scatter_dimension=0, tiled=True)  50.2 us
    psum x1, blocking collectives, shards(): lax.psum((grad_attn_gain, grad_query_gain, grad_key_gain, grad_ffn_gain),...  44.2 us
  transfers between devices with their start and end apart: 16, of which 11 were waited for; matrix products, arithmetic and copies ran while one was open for 12% of the time, Pallas kernels for 0%

profile of v1, /device:TPU:0, one launch (start us, length us, event | category | flops | bytes accessed | tf_op | source)
XLA Modules:
  0.0 1043.6 jit_solution(16036504361294056862)
XLA Ops:
  20.5 5.3 all-to-all-start
  26.3 44.5 %all-to-all-done = bf16[8,256,640]{2,1,0:T(8,128)(2,1)} async-done(((bf16[8,256,640]{2,1,0:T(8,128)(2,1)}), bf16[8,256,640]{2,1,0:T(8,128)(2,1)}, u32[]{:S(2)}, u32[]{:S(2)}) %all-to-all-start) | async-done | bytes 2621472 | tf_op jit(solution)/shard_map/all_to_all | solution.py:63
  70.8 6.0 fusion.125
  97.5 30.8 %all-gather.15.cloned.1.call-done = bf16[8,1024,128]{2,1,0:T(8,128)(2,1)} async-done(((bf16[2,1024,128]{2,1,0:T(8,128)(2,1)}), bf16[8,1024,128]{2,1,0:T(8,128)(2,1)}) %all-gather.15.cloned.1.call-update) | async-done | bytes 2097168 | tf_op jit(solution)/shard_map/all_gather | solution.py:67
  131.5 8.4 fusion.122
  153.4 50.2 %reduce-scatter.7.cloned.1.call-done = bf16[128,2048]{1,0:T(8,128)(2,1)} async-done(((bf16[1024,2048]{1,0:T(8,128)(2,1)}), bf16[128,2048]{1,0:T(8,128)(2,1)}) %reduce-scatter.7.cloned.1.call-update) | async-done | bytes 524304 | tf_op jit(solution)/shard_map/reduce_scatter | solution.py:59
  207.3 42.5 %all_gather.38 = s32[32,128,8]{1,2,0:T(8,128)S(1)} all-gather(s32[1,128,8]{1,2,0:T(8,128)S(1)} %copy-done.42), channel_id=1, replica_groups=mesh['ctx'=4,'shard'=8] {'ctx','shard'}, dimensions={0}, use_global_device_ids=true | all-gather | bytes 135168 | tf_op jit(solution)/shard_map/all_gather | solution.py:131
  264.9 46.9 %all-gather.11.cloned.1.call-done = bf16[4,128,2048]{2,1,0:T(8,128)(2,1)} async-done(((bf16[1,128,2048]{2,1,0:T(8,128)(2,1)}), bf16[4,128,2048]{2,1,0:T(8,128)(2,1)}) %all-gather.11.cloned.1.call-update) | async-done | bytes 2097168 | tf_op jit(solution)/shard_map/all_gather | solution.py:67
  317.6 7.0 all-to-all-done.1
  334.5 58.8 %all_gather.41 = bf16[2048,32]{0,1:T(8,128)(2,1)S(1)} all-gather(bf16[256,32]{0,1:T(8,128)(2,1)S(1)} %copy-done.41), channel_id=1, replica_groups=mesh['ctx'=4,'shard'=8] {'shard'}, dimensions={0}, use_global_device_ids=true | all-gather | bytes 147456 | tf_op jit(solution)/shard_map/all_gather | solution.py:55
  397.7 9.8 fusion.32
  407.5 8.7 fusion.36
  421.1 7.3 multiply_convert_fusion
  428.4 9.0 fusion.34
  437.4 9.3 fusion.4
  446.8 9.8 add_convert_fusion
  457.6 66.3 %all_to_all.30 = bf16[8,160,2176]{2,1,0:T(8,128)(2,1)S(1)} all-to-all(bf16[8,160,2176]{2,1,0:T(8,128)(2,1)S(1)} %pad_maximum_fusion), channel_id=1, replica_groups=mesh['ctx'=4,'shard'=8] {'shard'}, dimensions={0} | all-to-all | bytes 11141120 | tf_op jit(solution)/shard_map/all_to_all | solution.py:63
  527.7 42.2 %reduce-scatter.11.cloned.1.call-done = bf16[1,128,2176]{2,1,0:T(8,128)(2,1)} async-done(((bf16[4,128,2176]{2,1,0:T(8,128)(2,1)}), bf16[1,128,2176]{2,1,0:T(8,128)(2,1)}) %reduce-scatter.11.cloned.1.call-update) | async-done | bytes 557072 | tf_op jit(solution)/shard_map/reduce_scatter | solution.py:71
  574.1 36.2 %all-gather.13.cloned.1.call-done = bf16[1024,2048]{1,0:T(8,128)(2,1)} async-done(((bf16[128,2048]{1,0:T(8,128)(2,1)}), bf16[1024,2048]{1,0:T(8,128)(2,1)}) %all-gather.13.cloned.1.call-update) | async-done | bytes 4194320 | tf_op jit(solution)/shard_map/all_gather | solution.py:55
  610.3 6.2 convolution_convert_fusion.6
  639.7 38.9 %reduce-scatter.13.cloned.1.call-done = bf16[1,2,8,128,128]{4,3,2,1,0:T(8,128)(2,1)} async-done(((bf16[4,2,8,128,128]{4,3,2,1,0:T(8,128)(2,1)}), bf16[1,2,8,128,128]{4,3,2,1,0:T(8,128)(2,1)}) %reduce-scatter.13.cloned.1.call-update) | async-done | bytes 524304 | tf_op jit(solution)/shard_map/reduce_scatter | solution.py:71
  694.3 7.5 convolution_convert_fusion.1
  702.0 80.8 %all_to_all.31 = bf16[8,160,2048]{2,1,0:T(8,128)(2,1)S(1)} all-to-all(bf16[8,160,2048]{2,1,0:T(8,128)(2,1)} %bitcast.317), channel_id=1, replica_groups=mesh['ctx'=4,'shard'=8] {'shard'}, dimensions={0} | all-to-all | bytes 10485760 | tf_op jit(solution)/shard_map/all_to_all | solution.py:63
  786.8 5.6 convolution_convert_fusion.3
  799.5 5.9 convolution_convert_fusion.4
  805.4 31.8 %all-to-all-done.5 = bf16[8,256,768]{1,2,0:T(8,128)(2,1)} async-done(((bf16[8,256,768]{1,2,0:T(8,128)(2,1)}), bf16[8,256,768]{1,2,0:T(8,128)(2,1)}, u32[]{:S(2)}, u32[]{:S(2)}) %all-to-all-start.5) | async-done | bytes 3145760 | tf_op jit(solution)/shard_map/all_to_all | solution.py:63
  842.0 10.3 convolution_bitcast_fusion.1
  852.3 8.8 convolution_bitcast_fusion.2
  861.2 6.2 convolution_bitcast_fusion
  869.0 44.2 %all-reduce.5 = (f32[2048]{0:T(1024)}, f32[128]{0:T(128)}, f32[128]{0:T(128)}, f32[2048]{0:T(1024)}) all-reduce(f32[2048]{0:T(1024)S(1)} %get-tuple-element.104, f32[128]{0:T(128)S(1)} %get-tuple-element.98, f32[128]{0:T(128)S(1)} %broadcast_select_fusion, ...), channel_id=1, replica_groups=mesh['ctx'=4,'shard'=8] {'ctx','shard'}, use_global_device_ids=true, to_apply=%region_28.29 | all-reduce | flops 4352 | bytes 34816 | tf_op jit(solution)/shard_map/psum | solution.py:320
  916.5 98.8 %all-reduce.9.cloned.1.call-done = (bf16[256,5248]{0,1:T(8,128)(2,1)}, bf16[512,2048]{1,0:T(8,128)(2,1)}) async-done(((bf16[256,5248]{0,1:T(8,128)(2,1)}, bf16[512,2048]{1,0:T(8,128)(2,1)}), (bf16[256,5248]{0,1:T(8,128)(2,1)}, bf16[512,2048]{1,0:T(8,128)(2,1)})) %all-reduce.9.cloned.1.call-update) | async-done | bytes 4784144 | tf_op jit(solution)/shard_map/psum | solution.py:334
  1022.6 5.6 copy.241
  (301 shorter events, 178.6 us)
Async XLA Ops:
  7.2 412.6 %copy-start = (bf16[1,768,2048]{2,1,0:T(8,128)(2,1)S(1)}, bf16[1,768,2048]{2,1,0:T(8,128)(2,1)}, u32[]{:S(2)}) copy-start(bf16[1,768,2048]{2,1,0:T(8,128)(2,1)} %param.31) | copy-start | bytes 9437188
  7.2 63.6 %all-gather.9.cloned.1.call-start = ((), (), s32[]{:S(2)}) async-start(), calls=%async_computation.12 | async-start | bytes 4718592 | tf_op jit(solution)/shard_map/all_gather | solution.py:55
  20.5 50.3 %all-to-all-start = ((bf16[8,256,640]{2,1,0:T(8,128)(2,1)}), bf16[8,256,640]{2,1,0:T(8,128)(2,1)}, u32[]{:S(2)}, u32[]{:S(2)}) async-start(bf16[8,256,640]{2,1,0:T(8,128)(2,1)} %fusion.74), calls=%async_computation | async-start | bytes 5242880 | tf_op jit(solution)/shard_map/all_to_all | solution.py:63
  25.8 102.5 %all-gather.15.cloned.1.call-start = ((), (), s32[]{:S(2)}) async-start(), calls=%async_computation.21 | async-start | bytes 2621440 | tf_op jit(solution)/shard_map/all_gather | solution.py:67
  81.3 122.3 %reduce-scatter.7.cloned.1.call-start = ((), (), s32[]{:S(2)}) async-start(), calls=%async_computation.13 | async-start | bytes 4718592 | tf_op jit(solution)/shard_map/reduce_scatter | solution.py:59
  153.4 51.7 %copy-start.36 = (f32[2048]{0:T(1024)S(1)}, f32[2048]{0:T(1024)}, u32[]{:S(2)}) copy-start(f32[2048]{0:T(1024)} %param.27) | copy-start | bytes 24580
  153.4 54.0 %copy-start.42 = (s32[1,128,8]{1,2,0:T(8,128)S(1)}, s32[1,128,8]{1,2,0:T(8,128)}, u32[]{:S(2)}) copy-start(s32[1,128,8]{1,2,0:T(8,128)} %param.19) | copy-start | bytes 12292
  153.4 100.3 %all-gather.17.cloned.1.call-start = ((), (), s32[]{:S(2)}) async-start(), calls=%async_computation.22 | async-start | bytes 2621440 | tf_op jit(solution)/shard_map/all_gather | solution.py:67
  205.1 44.7 %copy-start.60 = (f32[128]{0:T(128)}, f32[128]{0:T(128)S(1)}, u32[]{:S(2)}) copy-start(f32[128]{0:T(128)S(1)} %multiply_reduce_fusion.5) | copy-start | bytes 1540
  205.1 44.7 %copy-start.45 = (f32[128]{0:T(128)}, f32[128]{0:T(128)S(1)}, u32[]{:S(2)}) copy-start(f32[128]{0:T(128)S(1)} %fusion.105) | copy-start | bytes 1540
  259.6 65.0 %all-to-all-start.1 = ((bf16[8,160,2048]{2,1,0:T(8,128)(2,1)}), bf16[8,160,2048]{2,1,0:T(8,128)(2,1)}, u32[]{:S(2)}, u32[]{:S(2)}) async-start(bf16[8,160,2048]{2,1,0:T(8,128)(2,1)} %bitcast.311), calls=%async_computation.2 | async-start | bytes 10485760 | tf_op jit(solution)/shard_map/all_to_all | solution.py:63
  264.3 47.4 %all-gather.11.cloned.1.call-start = ((), (), s32[]{:S(2)}) async-start(), calls=%async_computation.15 | async-start | bytes 2621440 | tf_op jit(solution)/shard_map/all_gather | solution.py:67
  324.6 91.5 %all-to-all-start.3 = ((bf16[8,160,2048]{2,1,0:T(8,128)(2,1)}), bf16[8,160,2048]{2,1,0:T(8,128)(2,1)}, u32[]{:S(2)}, u32[]{:S(2)}) async-start(bf16[8,160,2048]{2,1,0:T(8,128)(2,1)} %bitcast.310), calls=%async_computation.5 | async-start | bytes 10485760 | tf_op jit(solution)/shard_map/all_to_all | solution.py:63
  329.5 240.4 %reduce-scatter.11.cloned.1.call-start = ((), (), s32[]{:S(2)}) async-start(), calls=%async_computation.16 | async-start | bytes 2785280 | tf_op jit(solution)/shard_map/reduce_scatter | solution.py:71
  526.7 45.3 %copy-start.3 = (bf16[1,128,2048]{2,1,0:T(8,128)(2,1)S(1)}, bf16[1,128,2048]{2,1,0:T(8,128)(2,1)}, u32[]{:S(2)}) copy-start(bf16[1,128,2048]{2,1,0:T(8,128)(2,1)} %param.16) | copy-start | bytes 1572868
  526.7 45.3 %copy-start.5 = (bf16[128,2048]{1,0:T(8,128)(2,1)S(1)}, bf16[128,2048]{1,0:T(8,128)(2,1)}, u32[]{:S(2)}) copy-start(bf16[128,2048]{1,0:T(8,128)(2,1)} %reduce-scatter.7.cloned.1.call-done) | copy-start | bytes 1572868
  526.7 45.3 %copy-start.46 = (f32[128]{0:T(128)S(1)}, f32[128]{0:T(128)}, u32[]{:S(2)}) copy-start(f32[128]{0:T(128)} %copy-done.45) | copy-start | bytes 1540
  526.7 83.6 %all-gather.13.cloned.1.call-start = ((), (), s32[]{:S(2)}) async-start(), calls=%async_computation.17 | async-start | bytes 4718592 | tf_op jit(solution)/shard_map/all_gather | solution.py:55
  527.5 45.2 %copy-start.61 = (f32[128]{0:T(128)S(1)}, f32[128]{0:T(128)}, u32[]{:S(2)}) copy-start(f32[128]{0:T(128)} %copy-done.60) | copy-start | bytes 1540
  527.5 45.2 %copy-start.10 = (bf16[1,128,2048]{2,1,0:T(8,128)(2,1)S(1)}, bf16[1,128,2048]{2,1,0:T(8,128)(2,1)}, u32[]{:S(2)}) copy-start(bf16[1,128,2048]{2,1,0:T(8,128)(2,1)} %param.17) | copy-start | bytes 1572868
  527.7 45.0 %copy-start.54 = (f32[128]{0:T(128)}, f32[128]{0:T(128)S(1)}, u32[]{:S(2)}) copy-start(f32[128]{0:T(128)S(1)} %broadcast_maximum_fusion.1) | copy-start | bytes 1540
  574.0 104.6 %reduce-scatter.13.cloned.1.call-start = ((), (), s32[]{:S(2)}) async-start(), calls=%async_computation.18 | async-start | bytes 2621440 | tf_op jit(solution)/shard_map/reduce_scatter | solution.py:71
  634.5 55.1 %reduce-scatter.15.cloned.1.call-start = ((), (), s32[]{:S(2)}) async-start(), calls=%async_computation.19 | async-start | bytes 786432 | tf_op jit(solution)/shard_map/reduce_scatter | solution.py:294
  678.6 188.8 %reduce-scatter.17.cloned.1.call-start = ((), (), s32[]{:S(2)}) async-start(), calls=%async_computation.20 | async-start | bytes 4718592 | tf_op jit(solution)/shard_map/reduce_scatter | solution.py:59
  701.9 211.4 %reduce-scatter.9.cloned.1.call-start = ((), (), s32[]{:S(2)}) async-start(), calls=%async_computation.14 | async-start | bytes 2621440 | tf_op jit(solution)/shard_map/reduce_scatter | solution.py:71
  794.7 42.5 %all-to-all-start.5 = ((bf16[8,256,768]{1,2,0:T(8,128)(2,1)}), bf16[8,256,768]{1,2,0:T(8,128)(2,1)}, u32[]{:S(2)}, u32[]{:S(2)}) async-start(bf16[8,256,768]{1,2,0:T(8,128)(2,1)} %bitcast.312), calls=%async_computation.11 | async-start | bytes 6291456 | tf_op jit(solution)/shard_map/all_to_all | solution.py:63
  799.3 216.0 %all-reduce.9.cloned.1.call-start = ((), (), s32[]{:S(2)}) async-start(), calls=%async_computation.23 | async-start | bytes 9568256 | tf_op jit(solution)/shard_map/psum | solution.py:334
  861.1 52.1 %copy-start.59 = (f32[128]{0:T(128)S(1)}, f32[128]{0:T(128)}, u32[]{:S(2)}) copy-start(f32[128]{0:T(128)} %copy-done.58) | copy-start | bytes 1540
  861.1 52.2 %copy-start.11 = (bf16[1,128,2048]{2,1,0:T(8,128)(2,1)S(1)}, bf16[1,128,2048]{2,1,0:T(8,128)(2,1)}, u32[]{:S(2)}) copy-start(bf16[1,128,2048]{2,1,0:T(8,128)(2,1)} %param.17) | copy-start | bytes 1572868
  861.1 52.2 %copy-start.14 = (f32[128,2048]{1,0:T(8,128)S(1)}, f32[128,2048]{1,0:T(8,128)}, u32[]{:S(2)}) copy-start(f32[128,2048]{1,0:T(8,128)} %copy-done.13) | copy-start | bytes 3145732
  861.2 52.2 %copy-start.47 = (f32[128]{0:T(128)S(1)}, f32[128]{0:T(128)}, u32[]{:S(2)}) copy-start(f32[128]{0:T(128)} %copy-done.45) | copy-start | bytes 1540
  861.2 52.2 %copy-start.53 = (f32[128]{0:T(128)S(1)}, f32[128]{0:T(128)}, u32[]{:S(2)}) copy-start(f32[128]{0:T(128)} %copy-done.52) | copy-start | bytes 1540
  (57 other events, 324.9 us)
Sparse Core Ops, SparseCore 0:
  11.9 58.6 all-gather.8
  81.4 46.8 all-gather.14
  153.5 50.0 reduce-scatter.6
  207.4 46.2 all-gather.16
  266.5 45.2 all-gather.10
  526.8 43.0 reduce-scatter.10
  574.1 36.1 all-gather.12
  634.7 43.8 reduce-scatter.12
  680.8 7.2 reduce-scatter.14
  702.0 79.9 reduce-scatter.16
  785.6 42.2 reduce-scatter.8
  842.1 173.1 all-reduce.8

commit v2 on v1

--- a/solution.py
+++ b/solution.py
@@ -1,7 +1,574 @@
+import functools
+
 import jax
 import jax.numpy as jnp
 from jax import lax
+from jax.experimental import pallas as pl
+from jax.experimental.pallas import tpu as pltpu
 from jax.sharding import PartitionSpec as P
+
+BF = jnp.bfloat16
+F32 = jnp.float32
+MESH = pl.DeviceIdType.MESH
+ANY = pl.BlockSpec(memory_space=pl.ANY)
+VMEM = pl.BlockSpec(memory_space=pltpu.VMEM)
+DMA = pltpu.SemaphoreType.DMA
+
+
+def push(src, dst, send_sem, recv_sem, **where):
+    return pltpu.make_async_remote_copy(
+        src_ref=src, dst_ref=dst, send_sem=send_sem, recv_sem=recv_sem,
+        device_id=where, device_id_type=MESH,
+    )
+
+
+def greet(shard_peers, ctx_peers):
+    barrier = pltpu.get_barrier_semaphore()
+    for peer in shard_peers:
+        pl.semaphore_signal(barrier, inc=1, device_id={"shard": peer}, device_id_type=MESH)
+    for peer in ctx_peers:
+        pl.semaphore_signal(barrier, inc=1, device_id={"ctx": peer}, device_id_type=MESH)
+    pl.semaphore_wait(barrier, len(shard_peers) + len(ctx_peers))
+
+
+def here(ctx_count, shard_count):
+    c, s = lax.axis_index("ctx"), lax.axis_index("shard")
+    parity = lax.rem(s, 2)
+    sibling = s + 1 - 2 * parity
+    others = [lax.rem(s + d, shard_count) for d in range(1, shard_count)]
+    layers = [lax.rem(c + d, ctx_count) for d in range(1, ctx_count)]
+    return c, s, parity, sibling, others, layers
+
+
+def call(body, outs, in_specs, scratch, ident, args, mib=48, out_specs=None):
+    return pl.pallas_call(
+        body,
+        out_shape=outs,
+        in_specs=in_specs,
+        out_specs=out_specs if out_specs is not None else [ANY] * len(outs),
+        scratch_shapes=scratch,
+        compiler_params=pltpu.CompilerParams(
+            collective_id=ident, has_side_effects=True, vmem_limit_bytes=mib * 2**20
+        ),
+    )(*args)
+
+
+def start_body(n_ctx, n_shard, rows, wsend, routes, router, cot,
+               rows_all, w_all, routes_all, router_all, cot_all,
+               local, ss_row, rs_row, ss_fwd, rs_fwd, ss_w, rs_w, ss_rt, rs_rt, ss_ro, rs_ro,
+               ss_z, rs_z, ss_rz, rs_rz):
+    c, s, parity, sibling, others, layers = here(n_ctx, n_shard)
+    greet(others, layers)
+    chips = n_shard // 2
+    copies = [
+        pltpu.make_async_copy(rows, rows_all.at[s], local.at[0]),
+        pltpu.make_async_copy(wsend.at[s], w_all.at[s], local.at[1]),
+        pltpu.make_async_copy(routes, routes_all.at[c, s], local.at[2]),
+        pltpu.make_async_copy(router, router_all.at[s], local.at[3]),
+        pltpu.make_async_copy(cot, cot_all.at[c], local.at[4]),
+    ]
+    for item in copies:
+        item.start()
+    waits = []
+    near = []
+    for i, peer in enumerate(others):
+        item = push(routes, routes_all.at[c, s], ss_ro.at[i], rs_ro.at[i], shard=peer)
+        item.start()
+        near.append(item)
+    first = []
+    for d in range(1, chips):
+        item = push(rows, rows_all.at[s], ss_row.at[d], rs_row.at[d], shard=lax.rem(s + 2 * d, n_shard))
+        item.start()
+        first.append(item)
+    item = push(rows, rows_all.at[s], ss_fwd.at[0], rs_fwd.at[0], shard=sibling)
+    item.start()
+    waits.append(item)
+    for i, layer in enumerate(layers):
+        item = push(cot, cot_all.at[c], ss_z.at[i], rs_z.at[i], ctx=layer)
+        item.start()
+        waits.append(item)
+    for i, peer in enumerate(others):
+        item = push(wsend.at[peer], w_all.at[s], ss_w.at[i], rs_w.at[i], shard=peer)
+        item.start()
+        waits.append(item)
+        item = push(router, router_all.at[s], ss_rt.at[i], rs_rt.at[i], shard=peer)
+        item.start()
+        waits.append(item)
+    copies[2].wait()
+    for item in near:
+        item.wait()
+    for i, layer in enumerate(layers):
+        item = push(routes_all.at[c], routes_all.at[c], ss_rz.at[i], rs_rz.at[i], ctx=layer)
+        item.start()
+        waits.append(item)
+    for d in range(1, chips):
+        first[d - 1].wait()
+        origin = lax.rem(s + n_shard - 2 * d, n_shard)
+        item = push(rows_all.at[origin], rows_all.at[origin], ss_fwd.at[d], rs_fwd.at[d], shard=sibling)
+        item.start()
+        waits.append(item)
+    for i in (0, 1, 3, 4):
+        copies[i].wait()
+    for item in waits:
+        item.wait()
+
+
+def start(n_ctx, n_shard, rows, wsend, routes, router, cot):
+    n, z = n_shard, n_ctx
+    shapes = [
+        (n,) + rows.shape, wsend.shape, (z, n) + routes.shape, (n,) + router.shape, (z,) + cot.shape,
+    ]
+    kinds = [rows.dtype, wsend.dtype, routes.dtype, router.dtype, cot.dtype]
+    sems = [DMA((5,))] + [DMA((n // 2,))] * 4 + [DMA((n - 1,))] * 6 + [DMA((z - 1,))] * 4
+    return call(
+        functools.partial(start_body, z, n),
+        [jax.ShapeDtypeStruct(a, b) for a, b in zip(shapes, kinds)],
+        [ANY] * 5, sems, 0, (rows, wsend, routes, router, cot),
+    )
+
+
+def spread_body(n_shard, rows, rows_all, local, ss_row, rs_row, ss_fwd, rs_fwd):
+    c, s, parity, sibling, others, layers = here(1, n_shard)
+    chips = n_shard // 2
+    mates = [lax.rem(s + 2 * d, n_shard) for d in range(1, chips)]
+    greet(mates + [sibling], [])
+    mine = pltpu.make_async_copy(rows, rows_all.at[s], local)
+    mine.start()
+    first, waits = [], []
+    for d in range(1, chips):
+        item = push(rows, rows_all.at[s], ss_row.at[d], rs_row.at[d], shard=mates[d - 1])
+        item.start()
+        first.append(item)
+    item = push(rows, rows_all.at[s], ss_fwd.at[0], rs_fwd.at[0], shard=sibling)
+    item.start()
+    waits.append(item)
+    for d in range(1, chips):
+        first[d - 1].wait()
+        origin = lax.rem(s + n_shard - 2 * d, n_shard)
+        item = push(rows_all.at[origin], rows_all.at[origin], ss_fwd.at[d], rs_fwd.at[d], shard=sibling)
+        item.start()
+        waits.append(item)
+    mine.wait()
+    for item in waits:
+        item.wait()
+
+
+def spread(n_shard, rows, ident):
+    return call(
+        functools.partial(spread_body, n_shard),
+        [jax.ShapeDtypeStruct((n_shard,) + rows.shape, rows.dtype)],
+        [ANY], [DMA] + [DMA((n_shard // 2,))] * 4, ident, (rows,),
+    )[0]
+
+
+def key_body(n_ctx, n_shard, mine, kv, local, ss_z, rs_z, ss_f, rs_f):
+    c, s, parity, sibling, others, layers = here(n_ctx, n_shard)
+    greet([sibling], layers)
+    own = pltpu.make_async_copy(mine, kv.at[parity, :, c], local)
+    own.start()
+    far = []
+    for i, layer in enumerate(layers):
+        item = push(mine, kv.at[parity, :, c], ss_z.at[i], rs_z.at[i], ctx=layer)
+        item.start()
+        far.append(item)
+    waits = []
+    item = push(mine, kv.at[parity, :, c], ss_f.at[0], rs_f.at[0], shard=sibling)
+    item.start()
+    waits.append(item)
+    for i in range(n_ctx - 1):
+        far[i].wait()
+        origin = lax.rem(c + n_ctx - 1 - i, n_ctx)
+        item = push(kv.at[parity, :, origin], kv.at[parity, :, origin], ss_f.at[i + 1], rs_f.at[i + 1], shard=sibling)
+        item.start()
+        waits.append(item)
+    own.wait()
+    for item in waits:
+        item.wait()
+
+
+def key_exchange(n_ctx, n_shard, mine, ident):
+    n, rows, width = mine.shape
+    return call(
+        functools.partial(key_body, n_ctx, n_shard),
+        [jax.ShapeDtypeStruct((2, n, n_ctx, rows, width), mine.dtype)],
+        [ANY], [DMA] + [DMA((n_ctx - 1,))] * 2 + [DMA((n_ctx,))] * 2, ident, (mine,),
+    )[0]
+
+
+def key_back_body(n_ctx, n_shard, parts, out, sib, zsend, zrecv, ss_s, rs_s, ss_z, rs_z):
+    c, s, parity, sibling, others, layers = here(n_ctx, n_shard)
+    greet([sibling], layers)
+    waits = []
+    order = layers + [c]
+    near = []
+    for i, layer in enumerate(order):
+        item = push(parts.at[1 - parity, :, layer], sib.at[i], ss_s.at[i], rs_s.at[i], shard=sibling)
+        item.start()
+        near.append(item)
+    far = []
+    for i, layer in enumerate(layers):
+        near[i].wait()
+        zsend[i] = (parts[parity, :, layer].astype(F32) + sib[i].astype(F32)).astype(BF)
+        item = push(zsend.at[i], zrecv.at[i], ss_z.at[i], rs_z.at[i], ctx=layer)
+        item.start()
+        far.append(item)
+    near[n_ctx - 1].wait()
+    total = parts[parity, :, c].astype(F32) + sib[n_ctx - 1].astype(F32)
+    for i in range(n_ctx - 1):
+        far[i].wait()
+        total = total + zrecv[i].astype(F32)
+    out[...] = total
+
+
+def key_back(n_ctx, n_shard, parts, ident):
+    block = (parts.shape[1], parts.shape[3], parts.shape[4])
+    return call(
+        functools.partial(key_back_body, n_ctx, n_shard),
+        [jax.ShapeDtypeStruct(block, F32)],
+        [VMEM],
+        [
+            pltpu.VMEM((n_ctx,) + block, BF), pltpu.VMEM((n_ctx - 1,) + block, BF),
+            pltpu.VMEM((n_ctx - 1,) + block, BF),
+        ] + [DMA((n_ctx,))] * 2 + [DMA((n_ctx - 1,))] * 2,
+        ident, (parts,), out_specs=[VMEM],
+    )[0]
+
+
+def product_body(n_shard, tile, flip, left, right, out, part, to_sib, sib, to_chip, got,
+                 ss_s, rs_s, ss_c, rs_c):
+    c, s, parity, sibling, others, layers = here(1, n_shard)
+    chips = n_shard // 2
+    chip = lax.div(s, 2)
+    mates = [lax.rem(s + 2 * d, n_shard) for d in range(1, chips)]
+    greet(mates + [sibling], [])
+    rows, width = out.shape
+    order = list(range(1, chips)) + [0]
+    near = [None] * chips
+    for d in order:
+        first = pl.multiple_of(lax.rem(chip + d, chips) * (2 * rows), 2 * rows)
+
+        @pl.loop(0, width // tile)
+        def _(j):
+            cols = pl.ds(pl.multiple_of(j * tile, tile), tile)
+            if flip:
+                value = lax.dot_general(left[pl.ds(first, 2 * rows), :], right[cols, :],
+                                        (((1,), (1,)), ((), ())), preferred_element_type=F32)
+            else:
+                value = jnp.dot(left[pl.ds(first, 2 * rows), :], right[:, cols],
+                                preferred_element_type=F32)
+            part[d, :, :, cols] = value.reshape(2, rows, tile)
+
+        to_sib[d] = part[d, 1 - parity].astype(BF)
+        near[d] = push(to_sib.at[d], sib.at[d], ss_s.at[d], rs_s.at[d], shard=sibling)
+        near[d].start()
+    far = []
+    for d in range(1, chips):
+        near[d].wait()
+        to_chip[d - 1] = (part[d, parity] + sib[d].astype(F32)).astype(BF)
+        item = push(to_chip.at[d - 1], got.at[d - 1], ss_c.at[d - 1], rs_c.at[d - 1], shard=mates[d - 1])
+        item.start()
+        far.append(item)
+    near[0].wait()
+    out[...] = part[0, parity] + sib[0].astype(F32)
+    for d in range(1, chips):
+        far[d - 1].wait()
+        out[...] += got[d - 1].astype(F32)
+
+
+def product_scatter(n_shard, left, right, flip, ident):
+    rows = left.shape[0] // n_shard
+    width = right.shape[0] if flip else right.shape[1]
+    chips = n_shard // 2
+    return call(
+        functools.partial(product_body, n_shard, 512, flip),
+        [jax.ShapeDtypeStruct((rows, width), F32)],
+        [VMEM, VMEM],
+        [
+            pltpu.VMEM((chips, 2, rows, width), F32), pltpu.VMEM((chips, rows, width), BF),
+            pltpu.VMEM((chips, rows, width), BF), pltpu.VMEM((chips - 1, rows, width), BF),
+            pltpu.VMEM((chips - 1, rows, width), BF),
+        ] + [DMA((chips,))] * 2 + [DMA((chips - 1,))] * 2,
+        ident, (left, right), mib=56, out_specs=[VMEM],
+    )[0]
+
+
+def finish_body(n_ctx, n_shard, q_cols, weights, router, gains, q_out, kv_out, router_out, gains_out,
+                pieces, landing, acc, total, router_in, router_mid, router_far, gains_in, gains_mid, gains_far, local,
+                ss_w, rs_w, ss_i, rs_i, ss_o, rs_o, ss_q, ss_k, ss_r, rs_r, ss_g, rs_g, ss_h, rs_h, ss_t, rs_t):
+    c, s, parity, sibling, others, layers = here(n_ctx, n_shard)
+    half = n_ctx // 2
+    left = c < half
+    depth = jnp.where(left, c, n_ctx - 1 - c)
+    inner = jnp.where(left, c + 1, c - 1)
+    outer = jnp.clip(jnp.where(left, c - 1, c + 1), 0, n_ctx - 1)
+    middle = depth == half - 1
+    inside = depth > 0
+    greet(others, layers)
+    waits = []
+    sends = [None]
+    mine = pltpu.make_async_copy(gains, gains_in.at[s], local)
+    mine.start()
+    for i, peer in enumerate(others):
+        item = push(weights.at[peer], pieces.at[i + 1], ss_w.at[i], rs_w.at[i], shard=peer)
+        item.start()
+        sends.append(item)
+        item = push(router.at[peer], router_in.at[i], ss_r.at[i], rs_r.at[i], shard=peer)
+        item.start()
+        waits.append(item)
+        item = push(gains, gains_in.at[s], ss_g.at[i], rs_g.at[i], shard=peer)
+        item.start()
+        waits.append(item)
+
+    def inward(j):
+        at = jnp.where(middle, 1, 0)
+        return push(acc.at[j], landing.at[at, j], ss_i.at[j], rs_i.at[at, j], ctx=inner)
+
+    def outward(j):
+        return push(total.at[j], landing.at[1, j], ss_o.at[j], rs_i.at[1, j], ctx=outer)
+
+    def arrived(which, j):
+        push(acc.at[j], landing.at[which, j], ss_i.at[j], rs_i.at[which, j], ctx=inner).wait_recv()
+
+    def out_copies(j):
+        source = lax.rem(s + n_shard - j, n_shard)
+        cols = pl.ds(pl.multiple_of(source * q_cols, q_cols), q_cols)
+        return (
+            pltpu.make_async_copy(total.at[j, :, pl.ds(0, q_cols)], q_out.at[:, cols], ss_q.at[j]),
+            pltpu.make_async_copy(total.at[j, :, pl.ds(q_cols, 128)], kv_out.at[source], ss_k.at[j]),
+        )
+
+    def first_half(j):
+        if j == 0:
+            own = weights[s]
+        else:
+            sends[j].wait()
+            own = pieces[j]
+
+        @pl.when(inside)
+        def _():
+            arrived(0, j)
+            acc[j] = (own.astype(F32) + landing[0, j].astype(F32)).astype(BF)
+
+        @pl.when(jnp.logical_not(inside))
+        def _():
+            acc[j] = own
+
+        inward(j).start()
+
+    def second_half(j):
+        arrived(1, j)
+
+        @pl.when(middle)
+        def _():
+            total[j] = (acc[j].astype(F32) + landing[1, j].astype(F32)).astype(BF)
+
+        @pl.when(jnp.logical_not(middle))
+        def _():
+            total[j] = landing[1, j]
+
+        @pl.when(inside)
+        def _():
+            outward(j).start()
+
+        for item in out_copies(j):
+            item.start()
+
+    lag = 2
+    for j in range(n_shard + lag):
+        if j < n_shard:
+            first_half(j)
+        if j >= lag:
+            second_half(j - lag)
+        if j == lag:
+            for item in waits:
+                item.wait()
+            mine.wait()
+            gains_mid[...] = gains_in[0]
+            for i in range(1, n_shard):
+                gains_mid[...] += gains_in[i]
+            router_mid[...] = router[s].astype(F32)
+            for i in range(n_shard - 1):
+                router_mid[...] += router_in[i].astype(F32)
+            for i, layer in enumerate(layers):
+                push(gains_mid, gains_far.at[c], ss_h.at[i], rs_h.at[i], ctx=layer).start()
+                push(router_mid, router_far.at[c], ss_t.at[i], rs_t.at[i], ctx=layer).start()
+            mine = pltpu.make_async_copy(gains_mid, gains_far.at[c], local)
+            mine.start()
+    mine.wait()
+    mine = pltpu.make_async_copy(router_mid, router_far.at[c], local)
+    mine.start()
+    for i, layer in enumerate(layers):
+        push(gains_mid, gains_far.at[c], ss_h.at[i], rs_h.at[i], ctx=layer).wait()
+        push(router_mid, router_far.at[c], ss_t.at[i], rs_t.at[i], ctx=layer).wait()
+    mine.wait()
+    gains_out[...] = gains_far[0]
+    router_out[...] = router_far[0]
+    for i in range(1, n_ctx):
+        gains_out[...] += gains_far[i]
+        router_out[...] += router_far[i]
+    for j in range(n_shard):
+        inward(j).wait_send()
+
+        @pl.when(inside)
+        def _():
+            outward(j).wait_send()
+
+        for item in out_copies(j):
+            item.wait()
+
+
+def finish(n_ctx, n_shard, q_cols, weights, router, gains, ident):
+    n, rows, cols = weights.shape
+    gain_rows = gains.shape[0]
+    router_shape = router.shape[1:]
+    return call(
+        functools.partial(finish_body, n_ctx, n, q_cols),
+        [
+            jax.ShapeDtypeStruct((rows, n * q_cols), BF), jax.ShapeDtypeStruct((n, rows, 128), BF),
+            jax.ShapeDtypeStruct(router_shape, F32), jax.ShapeDtypeStruct(gains.shape, F32),
+        ],
+        [VMEM] * 3,
+        [
+            pltpu.VMEM((n, rows, cols), BF), pltpu.VMEM((2, n, rows, cols), BF),
+            pltpu.VMEM((n, rows, cols), BF), pltpu.VMEM((n, rows, cols), BF),
+            pltpu.VMEM((n - 1,) + router_shape, BF), pltpu.VMEM(router_shape, F32),
+            pltpu.VMEM((n_ctx,) + router_shape, F32), pltpu.VMEM((n, gain_rows, 128), F32),
+            pltpu.VMEM((gain_rows, 128), F32), pltpu.VMEM((n_ctx, gain_rows, 128), F32), DMA,
+            DMA((n - 1,)), DMA((n - 1,)), DMA((n,)), DMA((2, n)), DMA((n,)), DMA((1,)),
+            DMA((n,)), DMA((n,)), DMA((n - 1,)), DMA((n - 1,)), DMA((n - 1,)), DMA((n - 1,)),
+            DMA((n_ctx - 1,)), DMA((n_ctx - 1,)), DMA((n_ctx - 1,)), DMA((n_ctx - 1,)),
+        ],
+        ident, (weights, router, gains), mib=56, out_specs=[ANY, ANY, VMEM, VMEM],
+    )
+
+
+def flip_bits(index, mask):
+    result = index
+    bit = 1
+    while bit <= mask:
+        if mask & bit:
+            result = result + bit - 2 * bit * lax.rem(lax.div(index, bit), 2)
+        bit *= 2
+    return result
+
+
+def dispatch_body(n_ctx, n_shard, group, tile, rows, picks, recv, zrows, ready, local,
+                  ss_z, rs_z, ss_x, rs_x):
+    c, s, parity, sibling, others, layers = here(n_ctx, n_shard)
+    greet(others, layers)
+    count, width = rows.shape
+    groups = n_ctx // group
+    own = pltpu.make_async_copy(rows, zrows.at[c], local.at[0])
+    own.start()
+    far = []
+    for d in range(1, n_ctx):
+        item = push(rows, zrows.at[c], ss_z.at[d], rs_z.at[d], ctx=flip_bits(c, d))
+        item.start()
+        far.append(item)
+    waits = []
+    for k in range(groups):
+        at = flip_bits(lax.div(c, group), k)
+        if k == 0:
+            own.wait()
+        for d in range(max(k * group, 1), (k + 1) * group):
+            far[d - 1].wait()
+        first = pl.multiple_of(at * group, group)
+
+        @pl.loop(0, width // tile)
+        def _(j):
+            cols = pl.ds(pl.multiple_of(j * tile, tile), tile)
+            block = zrows[pl.ds(first, group), :, cols].reshape(group * count, tile)
+            value = jnp.dot(picks[at], block, preferred_element_type=F32).astype(BF)
+            ready[k, :, :, cols] = value.reshape(n_shard, -1, tile)
+
+        for i, peer in enumerate(others):
+            item = push(ready.at[k, peer], recv.at[s, at], ss_x.at[k, i], rs_x.at[k, i], shard=peer)
+            item.start()
+            waits.append(item)
+        item = pltpu.make_async_copy(ready.at[k, s], recv.at[s, at], local.at[k + 1])
+        item.start()
+        waits.append(item)
+    for item in waits:
+        item.wait()
+
+
+def dispatch_rows(n_ctx, n_shard, group, rows, picks, ident):
+    groups, slots = picks.shape[0], picks.shape[1] // n_shard
+    count, width = rows.shape
+    return call(
+        functools.partial(dispatch_body, n_ctx, n_shard, group, 512),
+        [jax.ShapeDtypeStruct((n_shard, groups, slots, width), BF)],
+        [VMEM, VMEM],
+        [
+            pltpu.VMEM((n_ctx, count, width), BF), pltpu.VMEM((groups, n_shard, slots, width), BF),
+            DMA((groups + 1,)), DMA((n_ctx,)), DMA((n_ctx,)),
+            DMA((groups, n_shard - 1)), DMA((groups, n_shard - 1)),
+        ],
+        ident, (rows, picks), mib=56,
+    )[0]
+
+
+def combine_body(n_ctx, n_shard, group, tile, rows, picks, out, land, value, zsend, zrecv, local,
+                 ss_x, rs_x, ss_z, rs_z):
+    c, s, parity, sibling, others, layers = here(n_ctx, n_shard)
+    greet(others, layers)
+    count, width = out.shape
+    groups = n_ctx // group
+    near = {}
+    for k in reversed(range(groups)):
+        at = flip_bits(lax.div(c, group), k)
+        near[k] = []
+        for i, peer in enumerate(others):
+            item = push(rows.at[peer, at], land.at[k, s], ss_x.at[k, i], rs_x.at[k, i], shard=peer)
+            item.start()
+            near[k].append(item)
+        item = pltpu.make_async_copy(rows.at[s, at], land.at[k, s], local.at[k])
+        item.start()
+        near[k].append(item)
+    far = []
+    for k in reversed(range(groups)):
+        at = flip_bits(lax.div(c, group), k)
+        for item in near[k]:
+            item.wait()
+
+        @pl.loop(0, width // tile)
+        def _(j):
+            cols = pl.ds(pl.multiple_of(j * tile, tile), tile)
+            block = land[k, :, :, cols].reshape(-1, tile)
+            value[:, cols] = jnp.dot(picks[at], block, preferred_element_type=F32)
+
+        for d in range(k * group, (k + 1) * group):
+            place = lax.rem(flip_bits(c, d), group)
+            block = value[pl.ds(pl.multiple_of(place * count, count), count), :]
+            if d == 0:
+                out[...] = block
+            else:
+                zsend[d - 1] = block.astype(BF)
+                item = push(zsend.at[d - 1], zrecv.at[d - 1], ss_z.at[d], rs_z.at[d], ctx=flip_bits(c, d))
+                item.start()
+                far.append((d, item))
+    for d, item in far:
+        item.wait()
+        out[...] += zrecv[d - 1].astype(F32)
+
+
+def combine_rows(n_ctx, n_shard, group, rows, picks, ident):
+    groups, slots, width = rows.shape[1:]
+    count = picks.shape[1] // group
+    tile = 128 * max(t for t in range(1, 9) if (width // 128) % t == 0)
+    return call(
+        functools.partial(combine_body, n_ctx, n_shard, group, tile),
+        [jax.ShapeDtypeStruct((count, width), F32)],
+        [VMEM, VMEM],
+        [
+            pltpu.VMEM((groups, n_shard, slots, width), BF), pltpu.VMEM((group * count, width), F32),
+            pltpu.VMEM((n_ctx - 1, count, width), BF), pltpu.VMEM((n_ctx - 1, count, width), BF),
+            DMA((groups,)), DMA((groups, n_shard - 1)), DMA((groups, n_shard - 1)),
+            DMA((n_ctx,)), DMA((n_ctx,)),
+        ],
+        ident, (rows, picks), mib=56, out_specs=[VMEM],
+    )[0]
+
 
 QUERY_HEADS = 32
 KEY_VALUE_HEADS = 4
@@ -9,8 +576,6 @@
 
 epsilon = 1e-06
 rope_base = 1000000.0
-BF = jnp.bfloat16
-F32 = jnp.float32
 
 
 def rms_scale(hidden, gain):
@@ -49,14 +614,6 @@
 
 def contract_cols(left, right):
     return lax.dot_general(left, right, (((1,), (1,)), ((), ())), preferred_element_type=F32)
-
-
-def gather_shard(x):
-    return lax.all_gather(x, "shard", axis=0, tiled=True)
-
-
-def scatter_shard(x):
-    return lax.psum_scatter(x, "shard", scatter_dimension=0, tiled=True)
 
 
 def exchange_shard(x):
@@ -122,15 +679,16 @@
             for s in range(shard_count)
         ]
     )
-    w_mine = exchange_shard(send_w).reshape(width, head_cols + HEAD_DIM)
-
     normed = rms_scale(inputs, attn_gain)
     normed_b = normed.astype(BF)
-    normed_all = gather_shard(normed_b)
-
-    routes_all = lax.all_gather(routes[0], ("ctx", "shard"), axis=0, tiled=False).reshape(
-        ctx_count, shard_count, rows, top_count
-    )
+    normed_all, w_mine, routes_all, router_all, upstream_z = start(
+        ctx_count, shard_count, normed_b, send_w, routes[0].T, w_router.T, upstream_b
+    )
+    normed_all = normed_all.reshape(plane, width)
+    w_mine = w_mine.reshape(width, head_cols + HEAD_DIM)
+    routes_all = jnp.swapaxes(routes_all, 2, 3)
+    router_all = jnp.swapaxes(router_all, 1, 2).reshape(width, experts)
+
     named = jnp.sum(
         (routes_all[..., None] == jnp.arange(experts, dtype=jnp.int32)).astype(BF), axis=3
     )
@@ -153,20 +711,24 @@
         "cbqt,cbte->bcqe", pick_here, named, preferred_element_type=F32
     ).reshape(-1, experts)
 
-    def dispatch(rows_b):
-        every = gather_ctx(rows_b)
-        sent = jnp.einsum("bsqt,btd->sbqd", pick_send, every, preferred_element_type=F32)
-        return exchange_shard(sent.astype(BF).reshape(shard_count, ctx_count * capacity, -1)).reshape(
-            shard_count * ctx_count * capacity, -1
-        )
-
-    def combine(slot_rows):
-        back = exchange_shard(slot_rows.reshape(shard_count, ctx_count * capacity, -1))
-        back = back.reshape(shard_count, ctx_count, capacity, -1)
-        part = jnp.einsum("bsqt,sbqd->btd", pick_send, back, preferred_element_type=F32)
-        return scatter_ctx(part.astype(BF)).astype(F32)
-
-    grad_expert_rows = dispatch(upstream_b)
+    group = 1
+    while group * capacity % 16:
+        group *= 2
+    groups = ctx_count // group
+    by_group = jnp.swapaxes(pick_send.reshape(groups, group, shard_count, capacity, rows), 1, 2)
+    same = jnp.eye(group, dtype=BF)
+    picks = (by_group[:, :, :, :, None, :] * same[None, None, :, None, :, None]).reshape(
+        groups, shard_count * group * capacity, group * rows
+    )
+    picks_t = jnp.swapaxes(picks, 1, 2)
+    slot_rows = shard_count * ctx_count * capacity
+    block_shape = (shard_count, groups, group * capacity)
+
+    sent_up = jnp.einsum(
+        "nkr,nrd->nkd", picks, upstream_z.reshape(groups, group * rows, width), preferred_element_type=F32
+    ).astype(BF)
+    sent_up = jnp.swapaxes(sent_up.reshape((groups, shard_count, group * capacity, width)), 0, 1)
+    upstream_rows = exchange_shard(sent_up).reshape(slot_rows, width).astype(F32)
 
     qkv = dot(normed_all, w_mine)
     query_pre = qkv[:, :head_cols].reshape(shard_count, rows, heads, HEAD_DIM)
@@ -187,13 +749,8 @@
     kv_pre = qkv[:, head_cols:]
     key_roped = prep(kv_pre.reshape(shard_count, rows, 1, HEAD_DIM), key_gain).reshape(plane, HEAD_DIM)
     kv_b = jnp.where(is_key, key_roped, kv_pre).astype(BF)
-    groups = [
-        [g * sharers + i for i in range(sharers)] for g in range(KEY_VALUE_HEADS)
-    ]
-    kv_pair = lax.all_gather(kv_b, "shard", axis=0, tiled=False, axis_index_groups=groups)[:2]
-    kv_all = gather_ctx(kv_pair)
-    kv_all = kv_all.reshape(ctx_count, 2, shard_count, rows, HEAD_DIM)
-    kv_all = jnp.transpose(kv_all, (1, 2, 0, 3, 4)).reshape(2, shard_count, sequence, HEAD_DIM)
+    kv_all = key_exchange(ctx_count, shard_count, kv_b.reshape(shard_count, rows, HEAD_DIM), 1)
+    kv_all = kv_all.reshape(2, shard_count, sequence, HEAD_DIM)
     keys, values = kv_all[0], kv_all[1]
 
     scores = (
@@ -208,12 +765,10 @@
     attn_f32 = jnp.einsum("shtp,spd->sthd", probs_b, values, preferred_element_type=F32)
     attn_b = attn_f32.astype(BF)
     attn_rows = attn_b.reshape(plane, head_cols)
-    proj = scatter_shard(dot(attn_rows, w_out).astype(BF))
-    middle = inputs + proj.astype(F32)
+    middle = inputs + product_scatter(shard_count, attn_rows, w_out, False, 2)
 
     normed_two = rms_scale(middle, ffn_gain)
     second_b = normed_two.astype(BF)
-    router_all = gather_shard(w_router)
     logits = dot(second_b, router_all)
     chosen = jnp.sum(
         (routes[0][:, :, None] == jnp.arange(experts, dtype=jnp.int32)).astype(F32), axis=1
@@ -227,7 +782,7 @@
 
     gates = gates_of(logits, chosen)
 
-    received = dispatch(second_b)
+    received = dispatch_rows(ctx_count, shard_count, group, second_b, picks, 3).reshape(slot_rows, width)
     my_expert = my_ctx * shard_count + my_shard
     slot_gates = lax.dynamic_slice_in_dim(
         gates_of(dot(received, router_all), chosen_here), my_expert, 1, 1
@@ -238,8 +793,15 @@
     hidden_b = (activated * up_pre).astype(BF)
     expert_out = dot(hidden_b, w_down[0]).astype(BF)
     expert_out_f = expert_out.astype(F32)
-    mixed = (middle + combine((slot_gates * expert_out_f).astype(BF))).astype(BF)
-    upstream_rows = grad_expert_rows.astype(F32)
+    mix_back = exchange_shard((slot_gates * expert_out_f).astype(BF).reshape(block_shape + (width,)))
+    mix_part = jnp.einsum(
+        "nrsk,snkd->nrd",
+        picks_t.reshape(groups, group * rows, shard_count, group * capacity),
+        mix_back,
+        preferred_element_type=F32,
+    ).astype(BF)
+    mixture = scatter_ctx(mix_part.reshape(ctx_count, rows, width)).astype(F32)
+    mixed = (middle + mixture).astype(BF)
     slot_dot = jnp.sum(expert_out_f * upstream_rows, axis=1, keepdims=True)
     grad_expert = (slot_gates * upstream_rows).astype(BF)
     grad_w_down = contract_rows(hidden_b, grad_expert)
@@ -259,20 +821,23 @@
     tail = jnp.where(column == my_expert, coarse, 0.0) + jnp.where(
         column == experts + my_expert, fine, 0.0
     )
-    back = combine(jnp.concatenate([grad_received, tail], axis=1).astype(BF))
+    back_rows = jnp.concatenate([grad_received, tail], axis=1).astype(BF)
+    back = combine_rows(
+        ctx_count, shard_count, group, back_rows.reshape(block_shape + (width + tail_cols,)), picks_t, 4
+    )
     grad_second = back[:, :width]
     grad_gates = back[:, width : width + experts] + back[:, width + experts : width + 2 * experts]
     grad_logits_b = (
         gates * (grad_gates - jnp.sum(gates * grad_gates, axis=-1, keepdims=True))
     ).astype(BF)
-    grad_w_router_part = contract_rows(second_b, grad_logits_b)
+    router_part = contract_rows(grad_logits_b, second_b).astype(BF)
     grad_second = grad_second + contract_cols(grad_logits_b, router_all)
     unused, norm_two_back = jax.vjp(rms_scale, middle, ffn_gain)
     grad_middle_part, grad_ffn_gain = norm_two_back(grad_second)
     grad_middle = upstream + grad_middle_part
     grad_proj_b = grad_middle.astype(BF)
 
-    grad_proj_all = gather_shard(grad_proj_b)
+    grad_proj_all = spread(shard_count, grad_proj_b, 5).reshape(plane, width)
     grad_attn = contract_cols(grad_proj_all, w_out).astype(BF)
     grad_w_out = lax.psum(contract_rows(attn_rows, grad_proj_all).astype(BF), "ctx").astype(F32)
     grad_heads = grad_attn.reshape(shard_count, rows, heads, HEAD_DIM)
@@ -287,57 +852,43 @@
     )
     grad_values = jnp.einsum("shtp,sthd->spd", probs_b, grad_heads, preferred_element_type=F32)
     grad_kv = jnp.stack([grad_keys, grad_values]).astype(BF)
-    grad_kv = grad_kv.reshape(2, shard_count, ctx_count, rows, HEAD_DIM)
-    grad_kv = scatter_ctx(jnp.transpose(grad_kv, (2, 0, 1, 3, 4)))
-    grad_kv = grad_kv.reshape(2, part_count, plane // part_count, HEAD_DIM)
-    grad_kv = jnp.transpose(grad_kv, (1, 0, 2, 3)).reshape(sharers, plane // part_count, HEAD_DIM)
-    grad_kv = lax.psum_scatter(
-        grad_kv, "shard", scatter_dimension=0, tiled=False, axis_index_groups=groups
-    ).astype(F32)
-    first = (my_place // 2) * (plane // part_count)
-
+    grad_kv = key_back(
+        ctx_count, shard_count, grad_kv.reshape(2, shard_count, ctx_count, rows, HEAD_DIM), 6
+    )
     unused, query_back = jax.vjp(prep, query_pre, query_gain)
     grad_query_pre, grad_query_gain = query_back(grad_query)
-    parts_k = (shard_count // part_count, rows, 1, HEAD_DIM)
-    kv_mine = lax.dynamic_slice_in_dim(kv_pre, first, plane // part_count, 0)
-    unused, key_back = jax.vjp(prep, kv_mine.reshape(parts_k), key_gain)
-    grad_key_pre, grad_key_gain = key_back(grad_kv.reshape(parts_k))
+    kv_shape = (shard_count, rows, 1, HEAD_DIM)
+    unused, key_prep_back = jax.vjp(prep, kv_pre.reshape(kv_shape), key_gain)
+    grad_key_pre, grad_key_gain = key_prep_back(grad_kv.reshape(kv_shape))
     grad_key_gain = jnp.where(is_key, grad_key_gain, 0.0)
-    grad_kv_b = jnp.where(is_key, grad_key_pre.reshape(-1, HEAD_DIM), grad_kv).astype(BF)
-    if part_count > 1:
-        grad_kv_full = lax.dynamic_update_slice_in_dim(
-            jnp.zeros((plane, HEAD_DIM), BF), grad_kv_b, first, 0
-        )
-    else:
-        grad_kv_full = grad_kv_b
+    grad_kv_full = jnp.where(
+        is_key, grad_key_pre.reshape(plane, HEAD_DIM), grad_kv.reshape(plane, HEAD_DIM)
+    ).astype(BF)
     grad_pre = jnp.concatenate(
         [grad_query_pre.reshape(plane, head_cols).astype(BF), grad_kv_full], axis=1
     )
-    grad_normed = scatter_shard(contract_cols(grad_pre, w_mine).astype(BF)).astype(F32)
+    grad_normed = product_scatter(shard_count, grad_pre, w_mine, True, 7)
     unused, norm_one_back = jax.vjp(rms_scale, inputs, attn_gain)
     grad_input_part, grad_attn_gain = norm_one_back(grad_normed)
     grad_tokens = grad_middle + grad_input_part
-    grad_attn_gain, grad_query_gain, grad_key_gain, grad_ffn_gain = lax.psum(
-        (grad_attn_gain, grad_query_gain, grad_key_gain, grad_ffn_gain), ("ctx", "shard")
-    )
-
-    grad_w = contract_rows(normed_all, grad_pre).astype(BF)
-    router_cols = -(-experts // 128) * 128
-    router_part = jnp.pad(grad_w_router_part, ((0, 0), (0, router_cols - experts))).astype(BF)
-    packed = jnp.concatenate([grad_w, router_part], axis=1).reshape(shard_count, wrows, -1)
-    packed = exchange_shard(packed)
-    queries_part = jnp.transpose(packed[:, :, :head_cols], (1, 0, 2)).reshape(wrows, -1)
-    kinds = packed[:, :, head_cols : head_cols + HEAD_DIM].astype(F32)
-    kinds = jnp.sum(kinds.reshape(KEY_VALUE_HEADS, part_count, 2, wrows, HEAD_DIM), axis=1)
-    kinds = jnp.transpose(kinds, (2, 1, 0, 3)).reshape(wrows, -1).astype(BF)
-    router_sum = jnp.sum(packed[:, :, head_cols + HEAD_DIM :].astype(F32), axis=0).astype(BF)
-    summed = lax.psum(jnp.concatenate([queries_part, kinds, router_sum], axis=1), "ctx").astype(F32)
-    width_q = QUERY_HEADS * HEAD_DIM
-    key_width = KEY_VALUE_HEADS * HEAD_DIM
-    grad_w_query = summed[:, :width_q]
-    grad_w_key = summed[:, width_q : width_q + key_width]
-    grad_w_value = summed[:, width_q + key_width : width_q + 2 * key_width]
-    grad_w_router = summed[:, width_q + 2 * key_width : width_q + 2 * key_width + experts]
+    gains = jnp.concatenate([grad_attn_gain, grad_ffn_gain, grad_query_gain, grad_key_gain])
+    gain_rows = -(-gains.shape[0] // 1024) * 8
+    gains = jnp.pad(gains, (0, gain_rows * 128 - gains.shape[0])).reshape(gain_rows, 128)
+
+    grad_w = contract_rows(normed_all, grad_pre).astype(BF).reshape(shard_count, wrows, -1)
+    router_parts = jnp.swapaxes(router_part.reshape(experts, shard_count, wrows), 0, 1)
+    q_sum, kv_sum, router_sum, gains = finish(
+        ctx_count, shard_count, head_cols, grad_w, router_parts, gains, 8
+    )
+    gains = gains.reshape(-1)
+    grad_attn_gain, grad_ffn_gain = gains[:width], gains[width : 2 * width]
+    grad_query_gain = gains[2 * width : 2 * width + HEAD_DIM]
+    grad_key_gain = gains[2 * width + HEAD_DIM : 2 * width + 2 * HEAD_DIM]
+    grad_w_query = q_sum.astype(F32)
+    kinds = kv_sum.astype(F32).reshape(KEY_VALUE_HEADS, part_count, 2, wrows, HEAD_DIM)
+    kinds = jnp.transpose(jnp.sum(kinds, axis=1), (1, 2, 0, 3)).reshape(2, wrows, -1)
+    grad_w_key, grad_w_value = kinds[0], kinds[1]
+    grad_w_router = router_sum.T
     return (
         mixed[None],
         grad_tokens[None],

time: 1050 us -> 865 us (0.82)
  Pallas kernels: 0 us -> 580 us
  waiting for transfers between devices: 431 us -> 0.04 us
  blocking collectives: 295 us -> 0 us
  matrix products: 160 us -> 131 us
  starting transfers between devices: 20.9 us -> 9.85 us
    pallas_call x0 -> x9, Pallas kernels: none -> 580 us  [call(): pl.pallas_call(body, out_shape=outs, in_specs=in_specs, out_specs=out_spe...]
    all_to_all x2 -> x0, blocking collectives: 147 us -> none  [exchange_shard(): return lax.all_to_all(x, 'shard', split_axis=0, concat_axis=0, tiled=True)]
    all_gather x5 -> x0, waiting for transfers between devices: 116 us -> none  [the longest x3 80.3 us: gather_ctx(): return lax.all_gather(x, 'ctx', axis=0, tiled=False)]
    all_gather x3 -> x0, blocking collectives: 104 us -> none  [the longest x1 58.8 us: gather_shard(): return lax.all_gather(x, 'shard', axis=0, tiled=True)]
    psum x1, waiting for transfers between devices: 98.8 us -> 0.01 us  [shards(): lax.psum(contract_rows(attn_rows, grad_proj_all).astype(BF), 'ctx')]
    all_to_all x4 -> x2, waiting for transfers between devices: 83.3 us -> 0.01 us  [exchange_shard(): return lax.all_to_all(x, 'shard', split_axis=0, concat_axis=0, tiled=True)]
    reduce_scatter x3 -> x1, waiting for transfers between devices: 81.1 us -> 0.01 us  [scatter_ctx(): return lax.psum_scatter(x, 'ctx', scatter_dimension=0, tiled=False)]
    reduce_scatter x3 -> x0, waiting for transfers between devices: 50.2 us -> none  [the longest x2 50.2 us: scatter_shard(): return lax.psum_scatter(x, 'shard', scatter_dimension=0, tiled=True)]
  transfers between devices with their start and end apart: 16 -> 4, of which waited for: 11 -> 0; matrix products, arithmetic and copies ran while one was open for 12% -> 22% of each run, Pallas kernels for 0% -> 61%
where the time goes in v2:
time: 865 us; the launch traced here: 857 us
  Pallas kernels  580 us (67%)
  matrix products  131 us (15%)
  other arithmetic  63.7 us (7%)
  local copies, waits for them, and re-layouts  56.9 us (7%)
  between operations  15.5 us (2%)
  starting transfers between devices  9.85 us (1%)
    pallas_call x9, Pallas kernels, call(): pl.pallas_call(body, out_shape=outs, in_specs=in_specs, out_specs=out_spe...  580 us
    dot_general x6, matrix products, dot(): return jnp.dot(left, right, preferred_element_type=F32)  37.7 us
    dot_general x6, matrix products, contract_rows(): lax.dot_general(left, right, (((0,), (0,)), ((), ())), preferred_element_...  31.1 us
    dot_general x5, matrix products, contract_cols(): lax.dot_general(left, right, (((1,), (1,)), ((), ())), preferred_element_...  27.2 us
    unnamed x162, local copies, waits for them, and re-layouts  18.4 us
  transfers between devices with their start and end apart: 4, of which 0 were waited for; matrix products, arithmetic and copies ran while one was open for 22% of the time, Pallas kernels for 61%

profile of v2, /device:TPU:0, one launch (start us, length us, event | category | flops | bytes accessed | tf_op | source)
XLA Modules:
  0.0 857.0 jit_solution(16777358216612663343)
XLA Ops:
  17.5 58.2 %shard_map.263 = (bf16[8,128,2048]{2,1,0:T(8,128)(2,1)}, bf16[8,256,640]{2,1,0:T(8,128)(2,1)S(1)}, s32[4,8,8,128]{3,2,1,0:T(8,128)S(1)}, bf16[8,32,256]{2,1,0:T(8,128)(2,1)S(1)}, bf16[4,128,2048]{2,1,0:T(8,128)(2,1)S(1)}) custom-call(bf16[128,2048]{1,0:T(8,128)(2,1)S(1)} %fusion.37.rows, bf16[8,256,640]{2,1,0:T(8,128)(2,1)} %copy-done.26, ...), custom_call_target="tpu_custom_call" | custom-call | tf_op jit(solution)/shard_map/pallas_call | solution.py:44
  93.0 4.8 all-to-all-start.1
  100.4 6.0 fusion.104
  116.1 23.6 %shard_map.264 = bf16[2,8,4,128,128]{4,3,2,1,0:T(8,128)(2,1)S(1)} custom-call(bf16[8,128,128]{2,1,0:T(8,128)(2,1)S(1)} %bitcast.312), custom_call_target="tpu_custom_call" | custom-call | tf_op jit(solution)/shard_map/pallas_call | solution.py:44
  153.4 8.4 fusion.101
  161.8 4.5 fusion.15
  174.0 35.7 %shard_map.265 = f32[128,2048]{1,0:T(8,128)} custom-call(bf16[1024,512]{1,0:T(8,128)(2,1)} %bitcast.339, bf16[512,2048]{1,0:T(8,128)(2,1)} %right.1), custom_call_target="tpu_custom_call" | custom-call | tf_op jit(solution)/shard_map/pallas_call | solution.py:44
  224.8 90.7 %shard_map.266 = bf16[8,2,80,2048]{3,2,1,0:T(8,128)(2,1)} custom-call(bf16[128,2048]{1,0:T(8,128)(2,1)} %multiply_convert_fusion.3.rows, bf16[2,640,256]{2,1,0:T(8,128)(2,1)} %copy.212.picks), custom_call_target="tpu_custom_call" | custom-call | tf_op jit(solution)/shard_map/pallas_call | solution.py:44
  315.5 4.2 fusion.102
  321.7 9.8 %fusion.22 = f32[1280,768]{1,0:T(8,128)} fusion(bf16[1280,2048]{1,0:T(8,128)(2,1)} %bitcast.319, bf16[1,2048,768]{2,1,0:T(8,128)(2,1)} %param.30), kind=kOutput, calls=%fused_computation.43 | convolution fusion | flops 4026531840 | bytes 12320768 | tf_op jit(solution)/shard_map/dot_general | solution.py:608
  331.5 6.2 fusion.26
  342.5 7.3 multiply_convert_fusion
  349.8 10.0 %fusion.4 = (bf16[1280,2048]{1,0:T(8,128)(2,1)}, f32[1280]{0:T(1024)S(1)}, bf16[1280,2048]{1,0:T(8,128)(2,1)}) fusion(bf16[8,2,80,2048]{3,2,1,0:T(8,128)(2,1)} %all-to-all-done.1, f32[1280]{0:T(1024)S(1)} %divide_reduce_fusion, bf16[1280,768]{1,0:T(8,128)(2,1)S(1)} %get-tuple-element.50, bf16[1,768,2048]{2,1,0:T(8,128)(2,1)S(1)} %copy-done), kind=kOutput, calls=%fused_computation.8 | convolution fusion | flops 4050123520 | bytes 20850688 | tf_op jit(solution)/shard_map/dot_general | solution.py:608
  359.9 4.9 all-to-all-start
  365.0 8.6 fusion.24
  373.5 7.1 add_convert_fusion
  384.1 120.8 %shard_map.267 = f32[128,2176]{1,0:T(8,128)} custom-call(bf16[8,2,80,2176]{3,2,1,0:T(8,128)(2,1)} %pad_maximum_fusion.rows, bf16[2,256,640]{2,1,0:T(8,128)(2,1)} %fusion.143.picks), custom_call_target="tpu_custom_call" | custom-call | tf_op jit(solution)/shard_map/pallas_call | solution.py:44
  508.3 30.1 %shard_map.268 = bf16[8,128,2048]{2,1,0:T(8,128)(2,1)S(1)} custom-call(bf16[128,2048]{1,0:T(8,128)(2,1)S(1)} %fusion.90.rows), custom_call_target="tpu_custom_call" | custom-call | tf_op jit(solution)/shard_map/pallas_call | solution.py:44
  544.1 3.6 bitcast_convert_fusion.1
  548.9 4.9 fusion.6
  556.0 23.5 %shard_map.269 = f32[8,128,128]{2,1,0:T(8,128)S(1)} custom-call(bf16[2,8,4,128,128]{4,3,2,1,0:T(8,128)(2,1)S(1)} %pad_maximum_fusion.1.parts), custom_call_target="tpu_custom_call" | custom-call | tf_op jit(solution)/shard_map/pallas_call | solution.py:44
  579.5 3.7 convolution_convert_fusion.3
  584.5 3.6 multiply_bitcast_fusion
  602.3 36.3 %shard_map.270 = f32[128,2048]{1,0:T(8,128)} custom-call(bf16[1024,640]{1,0:T(8,128)(2,1)} %pad_maximum_fusion.2.left, bf16[2048,640]{1,0:T(8,128)(2,1)} %bitcast.310), custom_call_target="tpu_custom_call" | custom-call | tf_op jit(solution)/shard_map/pallas_call | solution.py:44
  640.3 4.8 convolution_convert_fusion.2
  645.1 5.7 bitcast_convert_fusion
  651.4 160.9 %shard_map.271 = (bf16[256,4096]{1,0:T(8,128)(2,1)}, bf16[8,256,128]{2,1,0:T(8,128)(2,1)}, f32[32,256]{1,0:T(8,128)}, f32[40,128]{1,0:T(8,128)}) custom-call(bf16[8,256,640]{2,1,0:T(8,128)(2,1)} %bitcast.342, bf16[8,32,256]{2,1,0:T(8,128)(2,1)} %bitcast.359, f32[40,128]{1,0:T(8,128)} %fusion.65.gains), custom_call_target="tpu_custom_call" | custom-call | tf_op jit(solution)/shard_map/pallas_call | solution.py:44
  819.7 8.8 %convolution_bitcast_fusion.1 = f32[1,2048,768]{2,1,0:T(8,128)} fusion(bf16[1280,2048]{1,0:T(8,128)(2,1)} %bitcast.320, bf16[1280,768]{1,0:T(8,128)(2,1)S(1)} %copy-done.71), kind=kOutput, calls=%fused_computation.35 | convolution fusion | flops 4026531840 | bytes 13500416 | tf_op jit(solution)/shard_map/dot_general | solution.py:612
  828.5 6.4 convolution_bitcast_fusion.2
  834.9 6.2 convolution_bitcast_fusion
  841.1 4.3 convert_element_type.222
  845.4 3.9 fusion.41
  (289 shorter events, 124.2 us)
Async XLA Ops:
  7.2 334.0 %copy-start = (bf16[1,768,2048]{2,1,0:T(8,128)(2,1)S(1)}, bf16[1,768,2048]{2,1,0:T(8,128)(2,1)}, u32[]{:S(2)}) copy-start(bf16[1,768,2048]{2,1,0:T(8,128)(2,1)} %param.31) | copy-start | bytes 9437188
  93.0 244.7 %all-to-all-start.1 = ((bf16[8,2,80,2048]{3,2,1,0:T(8,128)(2,1)}), bf16[8,2,80,2048]{3,2,1,0:T(8,128)(2,1)}, u32[]{:S(2)}, u32[]{:S(2)}) async-start(bf16[8,2,80,2048]{3,2,1,0:T(8,128)(2,1)} %bitcast.327), calls=%async_computation.2 | async-start | bytes 10485760 | tf_op jit(solution)/shard_map/all_to_all | solution.py:620
  174.0 35.7 %copy-start.14 = (bf16[1,128,2048]{2,1,0:T(8,128)(2,1)S(1)}, bf16[1,128,2048]{2,1,0:T(8,128)(2,1)}, u32[]{:S(2)}) copy-start(bf16[1,128,2048]{2,1,0:T(8,128)(2,1)} %param.16) | copy-start | bytes 1572868
  212.6 10.0 %copy-start.44 = (f32[2048]{0:T(1024)S(1)}, f32[2048]{0:T(1024)}, u32[]{:S(2)}) copy-start(f32[2048]{0:T(1024)} %param.27) | copy-start | bytes 24580
  224.8 90.7 %copy-start.30 = (bf16[8,4,8,256]{3,2,0,1:T(8,128)(2,1)S(1)}, bf16[8,4,8,256]{3,2,0,1:T(8,128)(2,1)}, u32[]{:S(2)}) copy-start(bf16[8,4,8,256]{3,2,0,1:T(8,128)(2,1)} %copy.257) | copy-start | bytes 393220
  319.9 11.6 %slice-start = ((s8[5242880]{0:T(1024)(128)(4,1)}), s8[4194304]{0:T(1024)(128)(4,1)S(1)}, s32[]{:S(2)}) async-start(s8[5242880]{0:T(1024)(128)(4,1)} %bitcast.321), calls=%async_computation.5 | async-start | bytes 8388608
  321.6 9.8 %slice-start.1 = ((s8[5242880]{0:T(1024)(128)(4,1)}), s8[1048576]{0:T(1024)(128)(4,1)S(1)}, s32[]{:S(2)}) async-start(s8[5242880]{0:T(1024)(128)(4,1)} %bitcast.321), calls=%async_computation.6 | async-start | bytes 2097152
  321.7 9.8 %copy-start.62 = (bf16[1,2048,768]{2,1,0:T(8,128)(2,1)S(1)}, bf16[1,2048,768]{2,1,0:T(8,128)(2,1)}, u32[]{:S(2)}) copy-start(bf16[1,2048,768]{2,1,0:T(8,128)(2,1)} %param.29) | copy-start | bytes 9437188
  349.8 10.0 %copy-start.65 = (bf16[1280,768]{1,0:T(8,128)(2,1)}, bf16[1280,768]{1,0:T(8,128)(2,1)S(1)}, u32[]{:S(2)}) copy-start(bf16[1280,768]{1,0:T(8,128)(2,1)S(1)} %get-tuple-element.50) | copy-start | bytes 5898244
  359.9 285.1 %all-to-all-start = ((bf16[8,2,80,2048]{3,2,1,0:T(8,128)(2,1)}), bf16[8,2,80,2048]{3,2,1,0:T(8,128)(2,1)}, u32[]{:S(2)}, u32[]{:S(2)}) async-start(bf16[8,2,80,2048]{3,2,1,0:T(8,128)(2,1)} %bitcast.329), calls=%async_computation | async-start | bytes 10485760 | tf_op jit(solution)/shard_map/all_to_all | solution.py:620
  364.9 476.2 %all-reduce.7.cloned.1.call-start = ((), (), s32[]{:S(2)}) async-start(), calls=%async_computation.4 | async-start | bytes 4194304 | tf_op jit(solution)/shard_map/psum | solution.py:842
  364.9 8.6 %copy-start.64 = (bf16[1,2048,768]{2,1,0:T(8,128)(2,1)S(1)}, bf16[1,2048,768]{2,1,0:T(8,128)(2,1)}, u32[]{:S(2)}) copy-start(bf16[1,2048,768]{2,1,0:T(8,128)(2,1)} %param.30) | copy-start | bytes 9437188
  365.0 8.6 %copy-start.70 = (bf16[1280,768]{1,0:T(8,128)(2,1)S(1)}, bf16[1280,768]{1,0:T(8,128)(2,1)}, u32[]{:S(2)}) copy-start(bf16[1280,768]{1,0:T(8,128)(2,1)} %get-tuple-element.48) | copy-start | bytes 5898244
  384.1 121.9 %copy-start.12 = (f32[128,2048]{1,0:T(8,128)S(1)}, f32[128,2048]{1,0:T(8,128)}, u32[]{:S(2)}) copy-start(f32[128,2048]{1,0:T(8,128)} %get-tuple-element.45) | copy-start | bytes 3145732
  384.1 121.9 %copy-start.31 = (bf16[8,4,8,256]{3,2,0,1:T(8,128)(2,1)S(1)}, bf16[8,4,8,256]{3,2,0,1:T(8,128)(2,1)}, u32[]{:S(2)}) copy-start(bf16[8,4,8,256]{3,2,0,1:T(8,128)(2,1)} %copy.257) | copy-start | bytes 393220
  384.1 122.0 %copy-start.52 = (f32[128]{0:T(128)S(1)}, f32[128]{0:T(128)}, u32[]{:S(2)}) copy-start(f32[128]{0:T(128)} %copy-done.51) | copy-start | bytes 1540
  384.1 123.8 %copy-start.60 = (f32[128]{0:T(128)S(1)}, f32[128]{0:T(128)}, u32[]{:S(2)}) copy-start(f32[128]{0:T(128)} %get-tuple-element.44) | copy-start | bytes 1540
  507.9 30.5 %copy-start.23 = (f32[128,2048]{1,0:T(8,128)}, f32[128,2048]{1,0:T(8,128)S(1)}, u32[]{:S(2)}) copy-start(f32[128,2048]{1,0:T(8,128)S(1)} %get-tuple-element.102) | copy-start | bytes 3145732
  508.3 32.2 %copy-start.28 = (bf16[512,2048]{1,0:T(8,128)(2,1)S(1)}, bf16[512,2048]{1,0:T(8,128)(2,1)}, u32[]{:S(2)}) copy-start(bf16[512,2048]{1,0:T(8,128)(2,1)} %right.1) | copy-start | bytes 6291460
  555.8 23.7 %copy-start.5 = (bf16[8,128,2048]{2,1,0:T(8,128)(2,1)S(1)}, bf16[8,128,2048]{2,1,0:T(8,128)(2,1)}, u32[]{:S(2)}) copy-start(bf16[8,128,2048]{2,1,0:T(8,128)(2,1)} %copy-done.4) | copy-start | bytes 12582916
  555.8 23.7 %copy-start.22 = (bf16[8,128,4,128]{3,2,1,0:T(4,128)(2,1)S(1)}, bf16[8,128,4,128]{3,2,1,0:T(4,128)(2,1)}, u32[]{:S(2)}) copy-start(bf16[8,128,4,128]{3,2,1,0:T(4,128)(2,1)} %copy.203) | copy-start | bytes 3145732
  583.3 262.1 %reduce-scatter.2.cloned.1.call-start = ((), (), s32[]{:S(2)}) async-start(), calls=%async_computation.3 | async-start | bytes 2621440 | tf_op jit(solution)/shard_map/reduce_scatter | solution.py:628
  602.3 36.3 %copy-start.15 = (bf16[1,128,2048]{2,1,0:T(8,128)(2,1)S(1)}, bf16[1,128,2048]{2,1,0:T(8,128)(2,1)}, u32[]{:S(2)}) copy-start(bf16[1,128,2048]{2,1,0:T(8,128)(2,1)} %param.16) | copy-start | bytes 1572868
  602.3 36.3 %copy-start.43 = (f32[2048]{0:T(1024)S(1)}, f32[2048]{0:T(1024)}, u32[]{:S(2)}) copy-start(f32[2048]{0:T(1024)} %param.20) | copy-start | bytes 24580
  602.3 36.3 %copy-start.50 = (f32[128]{0:T(128)S(1)}, f32[128]{0:T(128)}, u32[]{:S(2)}) copy-start(f32[128]{0:T(128)} %copy-done.49) | copy-start | bytes 1540
  602.3 38.0 %copy-start.61 = (bf16[8,128,2048]{2,1,0:T(8,128)(2,1)S(1)}, bf16[8,128,2048]{2,1,0:T(8,128)(2,1)}, u32[]{:S(2)}) copy-start(bf16[8,128,2048]{2,1,0:T(8,128)(2,1)} %get-tuple-element.23) | copy-start | bytes 12582916
  815.9 12.6 %slice-start.2 = ((s8[5242880]{0:T(1024)(128)(4,1)}), s8[4194304]{0:T(1024)(128)(4,1)S(1)}, s32[]{:S(2)}) async-start(s8[5242880]{0:T(1024)(128)(4,1)} %bitcast.324), calls=%async_computation.7 | async-start | bytes 8388608
  819.7 8.8 %slice-start.3 = ((s8[5242880]{0:T(1024)(128)(4,1)}), s8[1048576]{0:T(1024)(128)(4,1)S(1)}, s32[]{:S(2)}) async-start(s8[5242880]{0:T(1024)(128)(4,1)} %bitcast.324), calls=%async_computation.8 | async-start | bytes 2097152
  819.7 8.8 %copy-start.69 = (bf16[1280,768]{1,0:T(8,128)(2,1)S(1)}, bf16[1280,768]{1,0:T(8,128)(2,1)}, u32[]{:S(2)}) copy-start(bf16[1280,768]{1,0:T(8,128)(2,1)} %get-tuple-element.49) | copy-start | bytes 5898244
  819.7 15.2 %slice-start.4 = ((s8[5242880]{0:T(1024)(128)(4,1)}), s8[4194304]{0:T(1024)(128)(4,1)S(1)}, s32[]{:S(2)}) async-start(s8[5242880]{0:T(1024)(128)(4,1)} %bitcast.365), calls=%async_computation.9 | async-start | bytes 8388608
  828.5 6.4 slice-start.5
  841.1 8.8 %copy-start.1 = (bf16[1,768,2048]{2,1,0:T(8,128)(2,1)S(1)}, bf16[1,768,2048]{2,1,0:T(8,128)(2,1)}, u32[]{:S(2)}) copy-start(bf16[1,768,2048]{2,1,0:T(8,128)(2,1)} %param.31) | copy-start | bytes 9437188
  (50 other events, 136.4 us)
Sparse Core Ops, SparseCore 0:
  583.4 97.7 all-reduce.6
  683.5 61.1 reduce-scatter.1

commit v3 on v2

--- a/solution.py
+++ b/solution.py
@@ -13,6 +13,7 @@
 ANY = pl.BlockSpec(memory_space=pl.ANY)
 VMEM = pl.BlockSpec(memory_space=pltpu.VMEM)
 DMA = pltpu.SemaphoreType.DMA
+epsilon = 1e-06
 
 
 def push(src, dst, send_sem, recv_sem, **where):
@@ -38,6 +39,69 @@
     others = [lax.rem(s + d, shard_count) for d in range(1, shard_count)]
     layers = [lax.rem(c + d, ctx_count) for d in range(1, ctx_count)]
     return c, s, parity, sibling, others, layers
+
+
+def flip_bits(index, mask):
+    result = index
+    bit = 1
+    while bit <= mask:
+        if mask & bit:
+            result = result + bit - 2 * bit * lax.rem(lax.div(index, bit), 2)
+        bit *= 2
+    return result
+
+
+def lowest(d):
+    return d & -d
+
+
+class Fan:
+    def __init__(self, n_ctx, c, block, ss, rs, near_first):
+        self.n_ctx, self.c, self.block, self.ss, self.rs, self.near_first = n_ctx, c, block, ss, rs, near_first
+        self.items = {}
+
+    def send(self, d, src):
+        bits = [b for b in (1, 2, 4, 8, 16) if b < (lowest(d) or self.n_ctx)]
+        for b in bits if self.near_first else reversed(bits):
+            item = push(src, self.block(d), self.ss.at[d | b], self.rs.at[d | b], ctx=flip_bits(self.c, b))
+            item.start()
+            self.items[d | b] = item
+
+    def arrival(self, d):
+        self.items[d].wait_recv()
+        if lowest(d) > 1:
+            self.send(d, self.block(d))
+
+    def order(self):
+        return sorted(range(1, self.n_ctx), key=lambda d: (bin(d).count("1"), d if self.near_first else -d))
+
+    def drain(self):
+        for d in range(1, self.n_ctx):
+            self.items[d].wait_send()
+
+
+class Fold:
+    def __init__(self, c, sent, received, ss, rs):
+        self.c, self.sent, self.received, self.ss, self.rs = c, sent, received, ss, rs
+        self.items = {}
+
+    def take(self, d, value):
+        for b in (1, 2, 4, 8, 16):
+            if b < lowest(d) or (d == 0 and b in self.items):
+                self.items[d | b].wait_recv()
+                value = value + self.received[(d | b) - 1].astype(F32)
+        return value
+
+    def give(self, d, value):
+        self.sent[d - 1] = value.astype(BF)
+        item = push(self.sent.at[d - 1], self.received.at[d - 1], self.ss.at[d], self.rs.at[d],
+                    ctx=flip_bits(self.c, lowest(d)))
+        item.start()
+        self.items[d] = item
+
+    def drain(self):
+        for item in self.items.values():
+            item.wait_send()
 
 
 def call(body, outs, in_specs, scratch, ident, args, mib=48, out_specs=None):
@@ -83,10 +147,8 @@
     item = push(rows, rows_all.at[s], ss_fwd.at[0], rs_fwd.at[0], shard=sibling)
     item.start()
     waits.append(item)
-    for i, layer in enumerate(layers):
-        item = push(cot, cot_all.at[c], ss_z.at[i], rs_z.at[i], ctx=layer)
-        item.start()
-        waits.append(item)
+    fan = Fan(n_ctx, c, lambda d: cot_all.at[flip_bits(c, d)], ss_z, rs_z, False)
+    fan.send(0, cot)
     for i, peer in enumerate(others):
         item = push(wsend.at[peer], w_all.at[s], ss_w.at[i], rs_w.at[i], shard=peer)
         item.start()
@@ -107,6 +169,9 @@
         item = push(rows_all.at[origin], rows_all.at[origin], ss_fwd.at[d], rs_fwd.at[d], shard=sibling)
         item.start()
         waits.append(item)
+    for d in fan.order():
+        fan.arrival(d)
+    fan.drain()
     for i in (0, 1, 3, 4):
         copies[i].wait()
     for item in waits:
@@ -119,7 +184,7 @@
         (n,) + rows.shape, wsend.shape, (z, n) + routes.shape, (n,) + router.shape, (z,) + cot.shape,
     ]
     kinds = [rows.dtype, wsend.dtype, routes.dtype, router.dtype, cot.dtype]
-    sems = [DMA((5,))] + [DMA((n // 2,))] * 4 + [DMA((n - 1,))] * 6 + [DMA((z - 1,))] * 4
+    sems = [DMA((5,))] + [DMA((n // 2,))] * 4 + [DMA((n - 1,))] * 6 + [DMA((z,))] * 4
     return call(
         functools.partial(start_body, z, n),
         [jax.ShapeDtypeStruct(a, b) for a, b in zip(shapes, kinds)],
@@ -166,21 +231,19 @@
     greet([sibling], layers)
     own = pltpu.make_async_copy(mine, kv.at[parity, :, c], local)
     own.start()
-    far = []
-    for i, layer in enumerate(layers):
-        item = push(mine, kv.at[parity, :, c], ss_z.at[i], rs_z.at[i], ctx=layer)
-        item.start()
-        far.append(item)
+    fan = Fan(n_ctx, c, lambda d: kv.at[parity, :, flip_bits(c, d)], ss_z, rs_z, False)
+    fan.send(0, mine)
     waits = []
     item = push(mine, kv.at[parity, :, c], ss_f.at[0], rs_f.at[0], shard=sibling)
     item.start()
     waits.append(item)
-    for i in range(n_ctx - 1):
-        far[i].wait()
-        origin = lax.rem(c + n_ctx - 1 - i, n_ctx)
-        item = push(kv.at[parity, :, origin], kv.at[parity, :, origin], ss_f.at[i + 1], rs_f.at[i + 1], shard=sibling)
+    for d in fan.order():
+        fan.arrival(d)
+        block = kv.at[parity, :, flip_bits(c, d)]
+        item = push(block, block, ss_f.at[d], rs_f.at[d], shard=sibling)
         item.start()
         waits.append(item)
+    fan.drain()
     own.wait()
     for item in waits:
         item.wait()
@@ -191,33 +254,32 @@
     return call(
         functools.partial(key_body, n_ctx, n_shard),
         [jax.ShapeDtypeStruct((2, n, n_ctx, rows, width), mine.dtype)],
-        [ANY], [DMA] + [DMA((n_ctx - 1,))] * 2 + [DMA((n_ctx,))] * 2, ident, (mine,),
+        [ANY], [DMA] + [DMA((n_ctx,))] * 4, ident, (mine,),
     )[0]
 
 
 def key_back_body(n_ctx, n_shard, parts, out, sib, zsend, zrecv, ss_s, rs_s, ss_z, rs_z):
     c, s, parity, sibling, others, layers = here(n_ctx, n_shard)
     greet([sibling], layers)
-    waits = []
-    order = layers + [c]
-    near = []
-    for i, layer in enumerate(order):
-        item = push(parts.at[1 - parity, :, layer], sib.at[i], ss_s.at[i], rs_s.at[i], shard=sibling)
-        item.start()
-        near.append(item)
-    far = []
-    for i, layer in enumerate(layers):
-        near[i].wait()
-        zsend[i] = (parts[parity, :, layer].astype(F32) + sib[i].astype(F32)).astype(BF)
-        item = push(zsend.at[i], zrecv.at[i], ss_z.at[i], rs_z.at[i], ctx=layer)
-        item.start()
-        far.append(item)
-    near[n_ctx - 1].wait()
-    total = parts[parity, :, c].astype(F32) + sib[n_ctx - 1].astype(F32)
-    for i in range(n_ctx - 1):
-        far[i].wait()
-        total = total + zrecv[i].astype(F32)
-    out[...] = total
+    order = list(range(1, n_ctx)) + [0]
+    near = {}
+    for d in order:
+        block = parts.at[1 - parity, :, lax.rem(c + d, n_ctx)]
+        near[d] = push(block, sib.at[d], ss_s.at[d], rs_s.at[d], shard=sibling)
+        near[d].start()
+    far = {}
+    for d in order:
+        near[d].wait()
+        layer = lax.rem(c + d, n_ctx)
+        value = parts[parity, :, layer].astype(F32) + sib[d].astype(F32)
+        if d:
+            zsend[d - 1] = value.astype(BF)
+            far[d] = push(zsend.at[d - 1], zrecv.at[d - 1], ss_z.at[d], rs_z.at[d], ctx=layer)
+            far[d].start()
+    for d in range(1, n_ctx):
+        far[d].wait()
+        value = value + zrecv[d - 1].astype(F32)
+    out[...] = value
 
 
 def key_back(n_ctx, n_shard, parts, ident):
@@ -229,7 +291,7 @@
         [
             pltpu.VMEM((n_ctx,) + block, BF), pltpu.VMEM((n_ctx - 1,) + block, BF),
             pltpu.VMEM((n_ctx - 1,) + block, BF),
-        ] + [DMA((n_ctx,))] * 2 + [DMA((n_ctx - 1,))] * 2,
+        ] + [DMA((n_ctx,))] * 4,
         ident, (parts,), out_specs=[VMEM],
     )[0]
 
@@ -292,164 +354,243 @@
     )[0]
 
 
-def finish_body(n_ctx, n_shard, q_cols, weights, router, gains, q_out, kv_out, router_out, gains_out,
-                pieces, landing, acc, total, router_in, router_mid, router_far, gains_in, gains_mid, gains_far, local,
-                ss_w, rs_w, ss_i, rs_i, ss_o, rs_o, ss_q, ss_k, ss_r, rs_r, ss_g, rs_g, ss_h, rs_h, ss_t, rs_t):
+def finish_body(n_ctx, n_shard, q_cols, tile,
+                weights, wide, router, gains, left, right, tokens, gain,
+                q_out, kv_out, wide_out, router_out, gains_out, rows_out,
+                wide_landing, wide_acc, wide_total, ss_wi, rs_wi, ss_wo, ss_wc, pieces, landing, acc, total, router_in, router_mid, router_far,
+                gains_own, gains_in, gains_mid, gains_far, pair, own_part, to_sib, sib, to_chip, got,
+                local, ss_w, rs_w, ss_i, rs_i, ss_o, ss_q, ss_k, ss_r, rs_r, ss_g, rs_g, ss_h, rs_h,
+                ss_t, rs_t, ss_s, rs_s, ss_c, rs_c):
     c, s, parity, sibling, others, layers = here(n_ctx, n_shard)
     half = n_ctx // 2
-    left = c < half
-    depth = jnp.where(left, c, n_ctx - 1 - c)
-    inner = jnp.where(left, c + 1, c - 1)
-    outer = jnp.clip(jnp.where(left, c - 1, c + 1), 0, n_ctx - 1)
+    chips = n_shard // 2
+    chip = lax.div(s, 2)
+    mates = [lax.rem(s + 2 * d, n_shard) for d in range(1, chips)]
+    left_side = c < half
+    depth = jnp.where(left_side, c, n_ctx - 1 - c)
+    inner = jnp.where(left_side, c + 1, c - 1)
+    outer = jnp.clip(jnp.where(left_side, c - 1, c + 1), 0, n_ctx - 1)
     middle = depth == half - 1
     inside = depth > 0
+    rows, width = rows_out.shape
     greet(others, layers)
-    waits = []
-    sends = [None]
-    mine = pltpu.make_async_copy(gains, gains_in.at[s], local)
-    mine.start()
+    sends, small = [None], []
     for i, peer in enumerate(others):
         item = push(weights.at[peer], pieces.at[i + 1], ss_w.at[i], rs_w.at[i], shard=peer)
         item.start()
         sends.append(item)
+    for i, peer in enumerate(others):
         item = push(router.at[peer], router_in.at[i], ss_r.at[i], rs_r.at[i], shard=peer)
         item.start()
-        waits.append(item)
-        item = push(gains, gains_in.at[s], ss_g.at[i], rs_g.at[i], shard=peer)
-        item.start()
-        waits.append(item)
-
-    def inward(j):
-        at = jnp.where(middle, 1, 0)
-        return push(acc.at[j], landing.at[at, j], ss_i.at[j], rs_i.at[at, j], ctx=inner)
-
-    def outward(j):
-        return push(total.at[j], landing.at[1, j], ss_o.at[j], rs_i.at[1, j], ctx=outer)
-
-    def arrived(which, j):
-        push(acc.at[j], landing.at[which, j], ss_i.at[j], rs_i.at[which, j], ctx=inner).wait_recv()
-
-    def out_copies(j):
+        small.append(item)
+
+    def out_copies(j, ref):
         source = lax.rem(s + n_shard - j, n_shard)
         cols = pl.ds(pl.multiple_of(source * q_cols, q_cols), q_cols)
         return (
-            pltpu.make_async_copy(total.at[j, :, pl.ds(0, q_cols)], q_out.at[:, cols], ss_q.at[j]),
-            pltpu.make_async_copy(total.at[j, :, pl.ds(q_cols, 128)], kv_out.at[source], ss_k.at[j]),
+            pltpu.make_async_copy(ref.at[:, pl.ds(0, q_cols)], q_out.at[:, cols], ss_q.at[j]),
+            pltpu.make_async_copy(ref.at[:, pl.ds(q_cols, 128)], kv_out.at[source], ss_k.at[j]),
         )
 
-    def first_half(j):
-        if j == 0:
-            own = weights[s]
-        else:
-            sends[j].wait()
-            own = pieces[j]
-
-        @pl.when(inside)
-        def _():
-            arrived(0, j)
-            acc[j] = (own.astype(F32) + landing[0, j].astype(F32)).astype(BF)
-
-        @pl.when(jnp.logical_not(inside))
-        def _():
-            acc[j] = own
-
-        inward(j).start()
-
-    def second_half(j):
-        arrived(1, j)
-
-        @pl.when(middle)
-        def _():
-            total[j] = (acc[j].astype(F32) + landing[1, j].astype(F32)).astype(BF)
-
-        @pl.when(jnp.logical_not(middle))
-        def _():
-            total[j] = landing[1, j]
-
-        @pl.when(inside)
-        def _():
-            outward(j).start()
-
-        for item in out_copies(j):
+    def wide_copies(j, ref):
+        return (pltpu.make_async_copy(ref, wide_out.at[j], ss_wc.at[j]),)
+
+    class Line:
+        def __init__(self, ready, own, acc, landing, total, ss_i, rs_i, ss_o, copies):
+            self.ready, self.own, self.acc, self.landing, self.total = ready, own, acc, landing, total
+            self.ss_i, self.rs_i, self.ss_o, self.copies = ss_i, rs_i, ss_o, copies
+
+        def inward(self, j, ref):
+            at = jnp.where(middle, 1, 0)
+            return push(ref, self.landing.at[at, j], self.ss_i.at[j], self.rs_i.at[at, j], ctx=inner)
+
+        def outward(self, j):
+            return push(self.total.at[j], self.landing.at[1, j], self.ss_o.at[j], self.rs_i.at[1, j], ctx=outer)
+
+        def arrived(self, which, j):
+            push(self.acc.at[j], self.landing.at[which, j], self.ss_i.at[j], self.rs_i.at[which, j],
+                 ctx=inner).wait_recv()
+
+        def outermost(self, j):
+            @pl.when(jnp.logical_not(inside))
+            def _():
+                self.ready(j)
+                self.inward(j, self.own(j)).start()
+
+        def first_half(self, j):
+            @pl.when(inside)
+            def _():
+                self.ready(j)
+                self.arrived(0, j)
+                self.acc[j] = (self.own(j)[...].astype(F32) + self.landing[0, j].astype(F32)).astype(BF)
+                self.inward(j, self.acc.at[j]).start()
+
+        def second_half(self, j):
+            self.arrived(1, j)
+
+            @pl.when(middle)
+            def _():
+                self.total[j] = (self.acc[j].astype(F32) + self.landing[1, j].astype(F32)).astype(BF)
+
+            @pl.when(jnp.logical_not(middle))
+            def _():
+                self.total[j] = self.landing[1, j]
+
+            @pl.when(inside)
+            def _():
+                self.outward(j).start()
+
+            for item in self.copies(j, self.total.at[j]):
+                item.start()
+
+        def drain(self, j):
+            self.inward(j, self.acc.at[j]).wait_send()
+
+            @pl.when(inside)
+            def _():
+                self.outward(j).wait_send()
+
+            for item in self.copies(j, self.total.at[j]):
+                item.wait()
+
+    line = Line(lambda j: sends[j].wait() if j else None, lambda j: pieces.at[j] if j else weights.at[s],
+                acc, landing, total, ss_i, rs_i, ss_o, out_copies)
+    wide_line = Line(lambda j: None, lambda j: wide.at[j], wide_acc, wide_landing, wide_total,
+                     ss_wi, rs_wi, ss_wo, wide_copies)
+    wides = wide.shape[0]
+    steps = [(wide_line, j) for j in range(wides)] + [(line, j) for j in range(n_shard)]
+
+    near, far = {}, {}
+
+    def product(d):
+        first = pl.multiple_of(lax.rem(chip + d, chips) * (2 * rows), 2 * rows)
+
+        @pl.loop(0, width // tile)
+        def _(j):
+            cols = pl.ds(pl.multiple_of(j * tile, tile), tile)
+            value = lax.dot_general(left[pl.ds(first, 2 * rows), :], right[cols, :],
+                                    (((1,), (1,)), ((), ())), preferred_element_type=F32)
+            pair[...] = value.reshape(2, rows, tile)
+            own_part[d, :, cols] = pair[parity]
+            to_sib[d, :, cols] = pair[1 - parity].astype(BF)
+
+        near[d] = push(to_sib.at[d], sib.at[d], ss_s.at[d], rs_s.at[d], shard=sibling)
+        near[d].start()
+
+    def chip_sum(d):
+        near[d].wait()
+        to_chip[d - 1] = (own_part[d] + sib[d].astype(F32)).astype(BF)
+        far[d] = push(to_chip.at[d - 1], got.at[d - 1], ss_c.at[d - 1], rs_c.at[d - 1], shard=mates[d - 1])
+        far[d].start()
+
+    gain_sends = []
+
+    def last_sum():
+        near[0].wait()
+        grad = own_part[0] + sib[0].astype(F32)
+        for d in range(1, chips):
+            far[d].wait()
+            grad = grad + got[d - 1].astype(F32)
+        x = tokens[...].astype(F32)
+        scale = lax.rsqrt(jnp.mean(x * x, axis=-1, keepdims=True) + epsilon)
+        unit = x * scale
+        scaled = grad * gain[...]
+        rows_out[...] = scale * (scaled - unit * jnp.mean(scaled * unit, axis=-1, keepdims=True))
+        gains_own[...] = gains[...]
+        gains_own[0:1] = jnp.sum(grad * unit, axis=0, keepdims=True)
+        mine = pltpu.make_async_copy(gains_own, gains_in.at[s], local.at[0])
+        mine.start()
+        gain_sends.append(mine)
+        for i, peer in enumerate(others):
+            item = push(gains_own, gains_in.at[s], ss_g.at[i], rs_g.at[i], shard=peer)
             item.start()
-
-    lag = 2
-    for j in range(n_shard + lag):
-        if j < n_shard:
-            first_half(j)
-        if j >= lag:
-            second_half(j - lag)
-        if j == lag:
-            for item in waits:
-                item.wait()
-            mine.wait()
-            gains_mid[...] = gains_in[0]
-            for i in range(1, n_shard):
-                gains_mid[...] += gains_in[i]
-            router_mid[...] = router[s].astype(F32)
-            for i in range(n_shard - 1):
-                router_mid[...] += router_in[i].astype(F32)
-            for i, layer in enumerate(layers):
-                push(gains_mid, gains_far.at[c], ss_h.at[i], rs_h.at[i], ctx=layer).start()
-                push(router_mid, router_far.at[c], ss_t.at[i], rs_t.at[i], ctx=layer).start()
-            mine = pltpu.make_async_copy(gains_mid, gains_far.at[c], local)
-            mine.start()
-    mine.wait()
-    mine = pltpu.make_async_copy(router_mid, router_far.at[c], local)
-    mine.start()
-    for i, layer in enumerate(layers):
-        push(gains_mid, gains_far.at[c], ss_h.at[i], rs_h.at[i], ctx=layer).wait()
-        push(router_mid, router_far.at[c], ss_t.at[i], rs_t.at[i], ctx=layer).wait()
-    mine.wait()
-    gains_out[...] = gains_far[0]
-    router_out[...] = router_far[0]
-    for i in range(1, n_ctx):
-        gains_out[...] += gains_far[i]
-        router_out[...] += router_far[i]
-    for j in range(n_shard):
-        inward(j).wait_send()
-
-        @pl.when(inside)
-        def _():
-            outward(j).wait_send()
-
-        for item in out_copies(j):
+            gain_sends.append(item)
+
+    def small_plane():
+        for item in small + gain_sends:
             item.wait()
-
-
-def finish(n_ctx, n_shard, q_cols, weights, router, gains, ident):
+        gains_mid[...] = gains_in[0]
+        for i in range(1, n_shard):
+            gains_mid[...] += gains_in[i]
+        router_mid[...] = router[s].astype(F32)
+        for i in range(n_shard - 1):
+            router_mid[...] += router_in[i].astype(F32)
+        for i, layer in enumerate(layers):
+            push(gains_mid, gains_far.at[c], ss_h.at[i], rs_h.at[i], ctx=layer).start()
+            push(router_mid, router_far.at[c], ss_t.at[i], rs_t.at[i], ctx=layer).start()
+        pltpu.make_async_copy(gains_mid, gains_far.at[c], local.at[1]).start()
+        pltpu.make_async_copy(router_mid, router_far.at[c], local.at[2]).start()
+
+    def small_all():
+        pltpu.make_async_copy(gains_mid, gains_far.at[c], local.at[1]).wait()
+        pltpu.make_async_copy(router_mid, router_far.at[c], local.at[2]).wait()
+        for i, layer in enumerate(layers):
+            push(gains_mid, gains_far.at[c], ss_h.at[i], rs_h.at[i], ctx=layer).wait()
+            push(router_mid, router_far.at[c], ss_t.at[i], rs_t.at[i], ctx=layer).wait()
+        gains_out[...] = gains_far[0]
+        router_out[...] = router_far[0]
+        for i in range(1, n_ctx):
+            gains_out[...] += gains_far[i]
+            router_out[...] += router_far[i]
+
+    lag, ahead = 2, 6
+    for which, j in steps[:ahead]:
+        which.outermost(j)
+    for d in list(range(1, chips)) + [0]:
+        product(d)
+    side = [functools.partial(chip_sum, d) for d in range(1, chips)] + [last_sum, small_plane]
+    for n in range(len(steps) + lag):
+        if n + ahead < len(steps):
+            steps[n + ahead][0].outermost(steps[n + ahead][1])
+        if n < len(steps):
+            steps[n][0].first_half(steps[n][1])
+        if n >= lag:
+            steps[n - lag][0].second_half(steps[n - lag][1])
+        if n >= 2 and side:
+            side.pop(0)()
+    for job in side:
+        job()
+    small_all()
+    for which, j in steps:
+        which.drain(j)
+
+
+def finish(n_ctx, n_shard, q_cols, weights, wide, router, gains, left, right, tokens, gain, ident):
     n, rows, cols = weights.shape
-    gain_rows = gains.shape[0]
     router_shape = router.shape[1:]
+    count, width = tokens.shape
+    chips = n // 2
+    tile = 512
+    wides = wide.shape[0]
     return call(
-        functools.partial(finish_body, n_ctx, n, q_cols),
+        functools.partial(finish_body, n_ctx, n, q_cols, tile),
         [
             jax.ShapeDtypeStruct((rows, n * q_cols), BF), jax.ShapeDtypeStruct((n, rows, 128), BF),
+            jax.ShapeDtypeStruct(wide.shape, BF),
             jax.ShapeDtypeStruct(router_shape, F32), jax.ShapeDtypeStruct(gains.shape, F32),
+            jax.ShapeDtypeStruct((count, width), F32),
         ],
-        [VMEM] * 3,
+        [VMEM] * 8,
         [
+            pltpu.VMEM((2,) + wide.shape, BF), pltpu.VMEM(wide.shape, BF), pltpu.VMEM(wide.shape, BF),
+            DMA((wides,)), DMA((2, wides)), DMA((wides,)), DMA((wides,)),
             pltpu.VMEM((n, rows, cols), BF), pltpu.VMEM((2, n, rows, cols), BF),
             pltpu.VMEM((n, rows, cols), BF), pltpu.VMEM((n, rows, cols), BF),
             pltpu.VMEM((n - 1,) + router_shape, BF), pltpu.VMEM(router_shape, F32),
-            pltpu.VMEM((n_ctx,) + router_shape, F32), pltpu.VMEM((n, gain_rows, 128), F32),
-            pltpu.VMEM((gain_rows, 128), F32), pltpu.VMEM((n_ctx, gain_rows, 128), F32), DMA,
-            DMA((n - 1,)), DMA((n - 1,)), DMA((n,)), DMA((2, n)), DMA((n,)), DMA((1,)),
+            pltpu.VMEM((n_ctx,) + router_shape, F32),
+            pltpu.VMEM(gains.shape, F32), pltpu.VMEM((n,) + gains.shape, F32),
+            pltpu.VMEM(gains.shape, F32), pltpu.VMEM((n_ctx,) + gains.shape, F32),
+            pltpu.VMEM((2, count, tile), F32), pltpu.VMEM((chips, count, width), F32),
+            pltpu.VMEM((chips, count, width), BF), pltpu.VMEM((chips, count, width), BF),
+            pltpu.VMEM((chips - 1, count, width), BF), pltpu.VMEM((chips - 1, count, width), BF),
+            DMA((3,)), DMA((n - 1,)), DMA((n - 1,)), DMA((n,)), DMA((2, n)), DMA((n,)),
             DMA((n,)), DMA((n,)), DMA((n - 1,)), DMA((n - 1,)), DMA((n - 1,)), DMA((n - 1,)),
             DMA((n_ctx - 1,)), DMA((n_ctx - 1,)), DMA((n_ctx - 1,)), DMA((n_ctx - 1,)),
+            DMA((chips,)), DMA((chips,)), DMA((chips - 1,)), DMA((chips - 1,)),
         ],
-        ident, (weights, router, gains), mib=56, out_specs=[ANY, ANY, VMEM, VMEM],
-    )
-
-
-def flip_bits(index, mask):
-    result = index
-    bit = 1
-    while bit <= mask:
-        if mask & bit:
-            result = result + bit - 2 * bit * lax.rem(lax.div(index, bit), 2)
-        bit *= 2
-    return result
+        ident, (weights, wide, router, gains, left, right, tokens, gain), mib=60,
+        out_specs=[ANY, ANY, ANY, VMEM, VMEM, VMEM],
+    )
 
 
 def dispatch_body(n_ctx, n_shard, group, tile, rows, picks, recv, zrows, ready, local,
@@ -460,18 +601,18 @@
     groups = n_ctx // group
     own = pltpu.make_async_copy(rows, zrows.at[c], local.at[0])
     own.start()
-    far = []
-    for d in range(1, n_ctx):
-        item = push(rows, zrows.at[c], ss_z.at[d], rs_z.at[d], ctx=flip_bits(c, d))
-        item.start()
-        far.append(item)
+    fan = Fan(n_ctx, c, lambda d: zrows.at[flip_bits(c, d)], ss_z, rs_z, True)
+    fan.send(0, rows)
     waits = []
+    seen = set()
     for k in range(groups):
         at = flip_bits(lax.div(c, group), k)
         if k == 0:
             own.wait()
-        for d in range(max(k * group, 1), (k + 1) * group):
-            far[d - 1].wait()
+        for d in fan.order():
+            if d < (k + 1) * group and d not in seen:
+                fan.arrival(d)
+                seen.add(d)
         first = pl.multiple_of(at * group, group)
 
         @pl.loop(0, width // tile)
@@ -488,6 +629,7 @@
         item = pltpu.make_async_copy(ready.at[k, s], recv.at[s, at], local.at[k + 1])
         item.start()
         waits.append(item)
+    fan.drain()
     for item in waits:
         item.wait()
 
@@ -508,11 +650,12 @@
     )[0]
 
 
-def combine_body(n_ctx, n_shard, group, tile, rows, picks, out, land, value, zsend, zrecv, local,
-                 ss_x, rs_x, ss_z, rs_z):
+def combine_body(n_ctx, n_shard, group, tile, rows, mix, picks, out, mix_out, land, value, zsend, zrecv,
+                 msend, mrecv, mix_kept, local, ss_x, rs_x, ss_z, rs_z, ss_m, rs_m):
     c, s, parity, sibling, others, layers = here(n_ctx, n_shard)
     greet(others, layers)
     count, width = out.shape
+    mix_width = mix_out.shape[1]
     groups = n_ctx // group
     near = {}
     for k in reversed(range(groups)):
@@ -525,49 +668,68 @@
         item = pltpu.make_async_copy(rows.at[s, at], land.at[k, s], local.at[k])
         item.start()
         near[k].append(item)
-    far = []
+
+    def local_sums(k, block_of, step, last):
+        at = flip_bits(lax.div(c, group), k)
+
+        @pl.loop(0, last // step)
+        def _(j):
+            cols = pl.ds(pl.multiple_of(j * step, step), step)
+            value[:, cols] = jnp.dot(picks[at], block_of(at, cols), preferred_element_type=F32)
+
+    def part(d, last):
+        place = lax.rem(flip_bits(c, d), group)
+        return value[pl.ds(pl.multiple_of(place * count, count), count), pl.ds(0, last)]
+
+    def in_group(k):
+        return sorted(range(k * group, (k + 1) * group), key=lambda d: (lowest(d) or n_ctx, d))
+
+    mix_fold = Fold(c, msend, mrecv, ss_m, rs_m)
     for k in reversed(range(groups)):
-        at = flip_bits(lax.div(c, group), k)
+        local_sums(k, lambda at, cols: mix[:, at, :, cols].reshape(picks.shape[2], -1), 512, mix_width)
+        for d in in_group(k):
+            if lowest(d) == 1:
+                mix_fold.give(d, part(d, mix_width))
+            else:
+                mix_kept[d // 2] = part(d, mix_width)
+    fold = Fold(c, zsend, zrecv, ss_z, rs_z)
+    for k in reversed(range(groups)):
         for item in near[k]:
             item.wait()
-
-        @pl.loop(0, width // tile)
-        def _(j):
-            cols = pl.ds(pl.multiple_of(j * tile, tile), tile)
-            block = land[k, :, :, cols].reshape(-1, tile)
-            value[:, cols] = jnp.dot(picks[at], block, preferred_element_type=F32)
-
-        for d in range(k * group, (k + 1) * group):
-            place = lax.rem(flip_bits(c, d), group)
-            block = value[pl.ds(pl.multiple_of(place * count, count), count), :]
-            if d == 0:
-                out[...] = block
-            else:
-                zsend[d - 1] = block.astype(BF)
-                item = push(zsend.at[d - 1], zrecv.at[d - 1], ss_z.at[d], rs_z.at[d], ctx=flip_bits(c, d))
-                item.start()
-                far.append((d, item))
-    for d, item in far:
-        item.wait()
-        out[...] += zrecv[d - 1].astype(F32)
-
-
-def combine_rows(n_ctx, n_shard, group, rows, picks, ident):
+        local_sums(k, lambda at, cols: land[k, :, :, cols].reshape(picks.shape[2], -1), tile, width)
+        for d in in_group(k):
+            if lowest(d) == 1:
+                fold.give(d, part(d, width))
+        for d in in_group(k):
+            if lowest(d) != 1:
+                if d:
+                    mix_fold.give(d, mix_fold.take(d, mix_kept[d // 2]))
+                    fold.give(d, fold.take(d, part(d, width)))
+                else:
+                    mix_out[...] = mix_fold.take(0, mix_kept[0])
+                    out[...] = fold.take(0, part(0, width))
+    mix_fold.drain()
+    fold.drain()
+
+
+def combine_rows(n_ctx, n_shard, group, rows, mix, picks, ident):
     groups, slots, width = rows.shape[1:]
+    mix_width = mix.shape[3]
     count = picks.shape[1] // group
     tile = 128 * max(t for t in range(1, 9) if (width // 128) % t == 0)
     return call(
         functools.partial(combine_body, n_ctx, n_shard, group, tile),
-        [jax.ShapeDtypeStruct((count, width), F32)],
-        [VMEM, VMEM],
+        [jax.ShapeDtypeStruct((count, width), F32), jax.ShapeDtypeStruct((count, mix_width), F32)],
+        [VMEM, VMEM, VMEM],
         [
             pltpu.VMEM((groups, n_shard, slots, width), BF), pltpu.VMEM((group * count, width), F32),
             pltpu.VMEM((n_ctx - 1, count, width), BF), pltpu.VMEM((n_ctx - 1, count, width), BF),
-            DMA((groups,)), DMA((groups, n_shard - 1)), DMA((groups, n_shard - 1)),
-            DMA((n_ctx,)), DMA((n_ctx,)),
+            pltpu.VMEM((n_ctx - 1, count, mix_width), BF), pltpu.VMEM((n_ctx - 1, count, mix_width), BF),
+            pltpu.VMEM((n_ctx // 2, count, mix_width), F32), DMA((groups,)), DMA((groups, n_shard - 1)), DMA((groups, n_shard - 1)),
+            DMA((n_ctx,)), DMA((n_ctx,)), DMA((n_ctx,)), DMA((n_ctx,)),
         ],
-        ident, (rows, picks), mib=56, out_specs=[VMEM],
-    )[0]
+        ident, (rows, mix, picks), mib=60, out_specs=[VMEM, VMEM],
+    )
 
 
 QUERY_HEADS = 32
@@ -622,10 +784,6 @@
 
 def gather_ctx(x):
     return lax.all_gather(x, "ctx", axis=0, tiled=False)
-
-
-def scatter_ctx(x):
-    return lax.psum_scatter(x, "ctx", scatter_dimension=0, tiled=False)
 
 
 def shards(
@@ -728,7 +886,7 @@
         "nkr,nrd->nkd", picks, upstream_z.reshape(groups, group * rows, width), preferred_element_type=F32
     ).astype(BF)
     sent_up = jnp.swapaxes(sent_up.reshape((groups, shard_count, group * capacity, width)), 0, 1)
-    upstream_rows = exchange_shard(sent_up).reshape(slot_rows, width).astype(F32)
+    upstream_rows = exchange_shard(sent_up).reshape(slot_rows, width)
 
     qkv = dot(normed_all, w_mine)
     query_pre = qkv[:, :head_cols].reshape(shard_count, rows, heads, HEAD_DIM)
@@ -793,15 +951,11 @@
     hidden_b = (activated * up_pre).astype(BF)
     expert_out = dot(hidden_b, w_down[0]).astype(BF)
     expert_out_f = expert_out.astype(F32)
-    mix_back = exchange_shard((slot_gates * expert_out_f).astype(BF).reshape(block_shape + (width,)))
-    mix_part = jnp.einsum(
-        "nrsk,snkd->nrd",
-        picks_t.reshape(groups, group * rows, shard_count, group * capacity),
-        mix_back,
-        preferred_element_type=F32,
-    ).astype(BF)
-    mixture = scatter_ctx(mix_part.reshape(ctx_count, rows, width)).astype(F32)
-    mixed = (middle + mixture).astype(BF)
+    mix_sent = (slot_gates * expert_out_f).astype(BF)
+    mix_sent, upstream_rows, expert_out = lax.optimization_barrier((mix_sent, upstream_rows, expert_out))
+    expert_out_f = expert_out.astype(F32)
+    mix_back = exchange_shard(mix_sent.reshape(block_shape + (width,)))
+    upstream_rows = upstream_rows.astype(F32)
     slot_dot = jnp.sum(expert_out_f * upstream_rows, axis=1, keepdims=True)
     grad_expert = (slot_gates * upstream_rows).astype(BF)
     grad_w_down = contract_rows(hidden_b, grad_expert)
@@ -822,9 +976,11 @@
         column == experts + my_expert, fine, 0.0
     )
     back_rows = jnp.concatenate([grad_received, tail], axis=1).astype(BF)
-    back = combine_rows(
-        ctx_count, shard_count, group, back_rows.reshape(block_shape + (width + tail_cols,)), picks_t, 4
-    )
+    back, mixture = combine_rows(
+        ctx_count, shard_count, group, back_rows.reshape(block_shape + (width + tail_cols,)), mix_back,
+        picks_t, 4,
+    )
+    mixed = (middle + mixture).astype(BF)
     grad_second = back[:, :width]
     grad_gates = back[:, width : width + experts] + back[:, width + experts : width + 2 * experts]
     grad_logits_b = (
@@ -838,8 +994,9 @@
     grad_proj_b = grad_middle.astype(BF)
 
     grad_proj_all = spread(shard_count, grad_proj_b, 5).reshape(plane, width)
+    out_part = contract_rows(attn_rows, grad_proj_all).astype(BF)
+    out_part, grad_proj_all = lax.optimization_barrier((out_part, grad_proj_all))
     grad_attn = contract_cols(grad_proj_all, w_out).astype(BF)
-    grad_w_out = lax.psum(contract_rows(attn_rows, grad_proj_all).astype(BF), "ctx").astype(F32)
     grad_heads = grad_attn.reshape(shard_count, rows, heads, HEAD_DIM)
     delta = jnp.transpose(jnp.sum(grad_heads.astype(F32) * attn_f32, axis=-1), (0, 2, 1))[..., None]
     grad_probs = jnp.einsum("sthd,spd->shtp", grad_heads, values, preferred_element_type=F32)
@@ -867,24 +1024,27 @@
     grad_pre = jnp.concatenate(
         [grad_query_pre.reshape(plane, head_cols).astype(BF), grad_kv_full], axis=1
     )
-    grad_normed = product_scatter(shard_count, grad_pre, w_mine, True, 7)
-    unused, norm_one_back = jax.vjp(rms_scale, inputs, attn_gain)
-    grad_input_part, grad_attn_gain = norm_one_back(grad_normed)
-    grad_tokens = grad_middle + grad_input_part
-    gains = jnp.concatenate([grad_attn_gain, grad_ffn_gain, grad_query_gain, grad_key_gain])
-    gain_rows = -(-gains.shape[0] // 1024) * 8
-    gains = jnp.pad(gains, (0, gain_rows * 128 - gains.shape[0])).reshape(gain_rows, 128)
-
+    gains = jnp.concatenate(
+        [
+            jnp.zeros((1, width), F32),
+            grad_ffn_gain[None],
+            jnp.pad(
+                jnp.concatenate([grad_query_gain, grad_key_gain])[None],
+                ((0, 6 - 1), (0, width - 2 * HEAD_DIM)),
+            ),
+        ]
+    )
     grad_w = contract_rows(normed_all, grad_pre).astype(BF).reshape(shard_count, wrows, -1)
     router_parts = jnp.swapaxes(router_part.reshape(experts, shard_count, wrows), 0, 1)
-    q_sum, kv_sum, router_sum, gains = finish(
-        ctx_count, shard_count, head_cols, grad_w, router_parts, gains, 8
-    )
-    gains = gains.reshape(-1)
-    grad_attn_gain, grad_ffn_gain = gains[:width], gains[width : 2 * width]
-    grad_query_gain = gains[2 * width : 2 * width + HEAD_DIM]
-    grad_key_gain = gains[2 * width + HEAD_DIM : 2 * width + 2 * HEAD_DIM]
+    q_sum, kv_sum, out_sum, router_sum, gains, grad_input_part = finish(
+        ctx_count, shard_count, head_cols, grad_w, out_part.reshape(8, -1, width), router_parts, gains, grad_pre, w_mine,
+        tokens[0], attn_gain[None], 8,
+    )
+    grad_tokens = grad_middle + grad_input_part
+    grad_attn_gain, grad_ffn_gain = gains[0], gains[1]
+    grad_query_gain, grad_key_gain = gains[2, :HEAD_DIM], gains[2, HEAD_DIM : 2 * HEAD_DIM]
     grad_w_query = q_sum.astype(F32)
+    grad_w_out = out_sum.reshape(head_cols, width).astype(F32)
     kinds = kv_sum.astype(F32).reshape(KEY_VALUE_HEADS, part_count, 2, wrows, HEAD_DIM)
     kinds = jnp.transpose(jnp.sum(kinds, axis=1), (1, 2, 0, 3)).reshape(2, wrows, -1)
     grad_w_key, grad_w_value = kinds[0], kinds[1]

time: 865 us -> 800 us (0.925)
  Pallas kernels: 580 us -> 509 us
  waiting for transfers between devices: 0.04 us -> 25 us
  between operations: 15.5 us -> 2.27 us
    pallas_call x9 -> x8, Pallas kernels: 580 us -> 509 us  [call(): pl.pallas_call(body, out_shape=outs, in_specs=in_specs, out_specs=out_spe...]
    all_to_all x2, waiting for transfers between devices: 0.01 us -> 25 us  [exchange_shard(): return lax.all_to_all(x, 'shard', split_axis=0, concat_axis=0, tiled=True)]
    unnamed x162 -> x188, local copies, waits for them, and re-layouts: 18.4 us -> 17.3 us
  transfers between devices with their start and end apart: 4 -> 2, of which waited for: 0 -> 1; matrix products, arithmetic and copies ran while one was open for 22% -> 16% of each run, Pallas kernels for 61% -> 18%
where the time goes in v3:
time: 800 us; the launch traced here: 793 us
  Pallas kernels  509 us (64%)
  matrix products  124 us (16%)
  other arithmetic  65.6 us (8%)
  local copies, waits for them, and re-layouts  56.8 us (7%)
  waiting for transfers between devices  25 us (3%)
  starting transfers between devices  9.85 us (1%)
    pallas_call x8, Pallas kernels, call(): pl.pallas_call(body, out_shape=outs, in_specs=in_specs, out_specs=out_spe...  509 us
    dot_general x6, matrix products, contract_rows(): lax.dot_general(left, right, (((0,), (0,)), ((), ())), preferred_element_...  34 us
    dot_general x6, matrix products, dot(): return jnp.dot(left, right, preferred_element_type=F32)  32.7 us
    dot_general x5, matrix products, contract_cols(): lax.dot_general(left, right, (((1,), (1,)), ((), ())), preferred_element_...  30.8 us
    all_to_all x2, waiting for transfers between devices, exchange_shard(): return lax.all_to_all(x, 'shard', split_axis=0, concat_axis=0, tiled=True)  25 us
    unnamed x188, local copies, waits for them, and re-layouts  17.3 us
  transfers between devices with their start and end apart: 2, of which 1 were waited for; matrix products, arithmetic and copies ran while one was open for 16% of the time, Pallas kernels for 18%

profile of v3, /device:TPU:0, one launch (start us, length us, event | category | flops | bytes accessed | tf_op | source)
XLA Modules:
  0.0 793.1 jit_solution(15729895329451505803)
XLA Ops:
  13.6 58.2 %shard_map.263 = (bf16[8,128,2048]{2,1,0:T(8,128)(2,1)}, bf16[8,256,640]{2,1,0:T(8,128)(2,1)S(1)}, s32[4,8,8,128]{3,2,1,0:T(8,128)S(1)}, bf16[8,32,256]{2,1,0:T(8,128)(2,1)S(1)}, bf16[4,128,2048]{2,1,0:T(8,128)(2,1)S(1)}) custom-call(bf16[128,2048]{1,0:T(8,128)(2,1)S(1)} %fusion.33.rows, bf16[8,256,640]{2,1,0:T(8,128)(2,1)} %copy-done.24, ...), custom_call_target="tpu_custom_call" | custom-call | tf_op jit(solution)/shard_map/pallas_call | solution.py:108
  85.8 3.4 convolution_convert_fusion.1
  92.0 4.8 all-to-all-start
  96.9 6.0 fusion.93
  111.7 23.4 %shard_map.264 = bf16[2,8,4,128,128]{4,3,2,1,0:T(8,128)(2,1)S(1)} custom-call(bf16[8,128,128]{2,1,0:T(8,128)(2,1)S(1)} %bitcast.298), custom_call_target="tpu_custom_call" | custom-call | tf_op jit(solution)/shard_map/pallas_call | solution.py:108
  139.6 3.6 multiply_reduce_fusion.2
  149.4 8.4 %fusion.90 = (f32[8,4,128]{2,1,0:T(4,128)S(1)}, f32[8,4,128,512]{2,3,1,0:T(8,128)}) fusion(pred[128,512]{0,1:T(8,128)(4,1)S(1)} %broadcast_compare_fusion, bf16[8,512,128,1]{2,1,3,0:T(8,128)(2,1)} %bitcast.318, bf16[8,128,4,64]{3,1,2,0:T(8,128)(2,1)} %get-tuple-element.71, bf16[8,128,4,64]{3,1,2,0:T(8,128)(2,1)} %get-tuple-element.70), kind=kOutput, calls=%fused_computation.223 | convolution fusion | flops 547357184 | bytes 10567680 | tf_op jit(solution)/shard_map/sub | solution.py:919
  157.8 4.5 fusion.11
  170.1 35.0 %shard_map.265 = f32[128,2048]{1,0:T(8,128)} custom-call(bf16[1024,512]{1,0:T(8,128)(2,1)} %bitcast.325, bf16[512,2048]{1,0:T(8,128)(2,1)} %right.1), custom_call_target="tpu_custom_call" | custom-call | tf_op jit(solution)/shard_map/pallas_call | solution.py:108
  215.3 87.1 %shard_map.266 = bf16[8,2,80,2048]{3,2,1,0:T(8,128)(2,1)} custom-call(bf16[128,2048]{1,0:T(8,128)(2,1)} %multiply_convert_fusion.4.rows, bf16[2,640,256]{2,1,0:T(8,128)(2,1)} %copy.200.picks), custom_call_target="tpu_custom_call" | custom-call | tf_op jit(solution)/shard_map/pallas_call | solution.py:108
  302.4 4.2 fusion.91
  315.9 7.2 fusion.20
  323.2 6.7 multiply_convert_fusion.3
  331.2 7.2 multiply_convert_fusion
  338.4 5.5 fusion.2
  344.0 11.6 %multiply_convert_fusion.1 = (bf16[1280,768]{1,0:T(8,128)(2,1)}, bf16[1280,768]{1,0:T(8,128)(2,1)S(1)}) fusion(f32[1280,768]{1,0:T(8,128)} %copy-done.82, f32[1280,768]{1,0:T(8,128)} %get-tuple-element.111, bf16[1,768,2048]{2,1,0:T(8,128)(2,1)S(1)} %copy-done, bf16[1280,2048]{1,0:T(8,128)(2,1)} %bitcast.44, f32[1280]{0:T(1024)S(1)} %copy-done.66), kind=kOutput, calls=%fused_computation.23 | convolution fusion | flops 4047175680 | bytes 20190208 | tf_op jit(solution)/shard_map/dot_general | solution.py:778
  355.6 6.9 fusion.18
  362.6 5.0 all-to-all-start.1
  368.1 8.0 %add_convert_fusion = bf16[1280,2048]{1,0:T(8,128)(2,1)S(1)} fusion(f32[1280,2048]{1,0:T(8,128)} %fusion.18, bf16[1280,768]{1,0:T(8,128)(2,1)S(1)} %copy-done.85, bf16[1,2048,768]{2,1,0:T(8,128)(2,1)} %param.30), kind=kOutput, calls=%fused_computation.5 | convolution fusion | flops 4031774720 | bytes 20840448 | tf_op jit(solution)/shard_map/dot_general | solution.py:778
  379.1 8.8 %convolution_bitcast_fusion.2 = f32[1,2048,768]{2,1,0:T(8,128)} fusion(bf16[1280,2048]{1,0:T(8,128)(2,1)} %bitcast.306, bf16[1280,768]{1,0:T(8,128)(2,1)S(1)} %copy-done.84), kind=kOutput, calls=%fused_computation.30 | convolution fusion | flops 4026531840 | bytes 13500416 | tf_op jit(solution)/shard_map/dot_general | solution.py:774
  387.9 6.4 convolution_bitcast_fusion.1
  394.4 8.9 %convolution_bitcast_fusion = f32[1,768,2048]{2,1,0:T(8,128)} fusion(bf16[1280,768]{1,0:T(8,128)(2,1)S(1)} %copy-done.81, bf16[1280,2048]{1,0:T(8,128)(2,1)} %bitcast.44, f32[1280]{0:T(1024)S(1)} %copy-done.66), kind=kOutput, calls=%fused_computation.28 | convolution fusion | flops 4034396160 | bytes 13505536 | tf_op jit(solution)/shard_map/dot_general | solution.py:774
  403.2 25.0 %all-to-all-done.1.mix = bf16[8,2,80,2048]{3,2,1,0:T(8,128)(2,1)} async-done(((bf16[8,2,80,2048]{3,2,1,0:T(8,128)(2,1)}), bf16[8,2,80,2048]{3,2,1,0:T(8,128)(2,1)}, u32[]{:S(2)}, u32[]{:S(2)}) %all-to-all-start.1) | async-done | bytes 5242912 | tf_op jit(solution)/shard_map/all_to_all | solution.py:782
  428.2 88.2 %shard_map.267 = (f32[128,2176]{1,0:T(8,128)}, f32[128,2048]{1,0:T(8,128)}) custom-call(bf16[8,2,80,2176]{3,2,1,0:T(8,128)(2,1)} %pad_maximum_fusion.rows, bf16[8,2,80,2048]{3,2,1,0:T(8,128)(2,1)} %all-to-all-done.1.mix, bf16[2,256,640]{2,1,0:T(8,128)(2,1)} %fusion.129.picks), custom_call_target="tpu_custom_call" | custom-call | tf_op jit(solution)/shard_map/pallas_call | solution.py:108
  519.8 35.2 %shard_map.268 = bf16[8,128,2048]{2,1,0:T(8,128)(2,1)S(1)} custom-call(bf16[128,2048]{1,0:T(8,128)(2,1)S(1)} %fusion.78.rows), custom_call_target="tpu_custom_call" | custom-call | tf_op jit(solution)/shard_map/pallas_call | solution.py:108
  555.0 3.7 convolution_convert_fusion.3
  562.1 3.6 bitcast_convert_fusion.1
  566.9 4.9 fusion.4
  576.3 24.3 %shard_map.269 = f32[8,128,128]{2,1,0:T(8,128)S(1)} custom-call(bf16[2,8,4,128,128]{4,3,2,1,0:T(8,128)(2,1)S(1)} %pad_maximum_fusion.1.parts), custom_call_target="tpu_custom_call" | custom-call | tf_op jit(solution)/shard_map/pallas_call | solution.py:108
  611.8 5.0 convolution_convert_fusion.2
  619.3 158.1 %shard_map.270 = (bf16[256,4096]{1,0:T(8,128)(2,1)}, bf16[8,256,128]{2,1,0:T(8,128)(2,1)}, bf16[8,64,2048]{2,1,0:T(8,128)(2,1)}, f32[32,256]{1,0:T(8,128)}, f32[8,2048]{1,0:T(8,128)}, /*index=5*/f32[128,2048]{1,0:T(8,128)}) custom-call(bf16[8,256,640]{2,1,0:T(8,128)(2,1)} %bitcast.328, bf16[8,64,2048]{2,1,0:T(8,128)(2,1)} %bitcast.332, ...), custom_call_target="tpu_custom_call" | custom-call | tf_op jit(solution)/shard_map/pallas_call | solution.py:108
  780.2 4.2 convert_element_type.198
  (304 shorter events, 117.9 us)
Async XLA Ops:
  0.6 330.5 %copy-start = (bf16[1,768,2048]{2,1,0:T(8,128)(2,1)S(1)}, bf16[1,768,2048]{2,1,0:T(8,128)(2,1)}, u32[]{:S(2)}) copy-start(bf16[1,768,2048]{2,1,0:T(8,128)(2,1)} %param.31) | copy-start | bytes 9437188
  75.2 9.4 %copy-start.36 = (bf16[4,8,128,32]{2,3,1,0:T(8,128)(2,1)}, bf16[4,8,128,32]{2,3,1,0:T(8,128)(2,1)S(1)}, u32[]{:S(2)}) copy-start(bf16[4,8,128,32]{2,3,1,0:T(8,128)(2,1)S(1)} %fusion.25) | copy-start | bytes 786436
  92.0 246.3 %all-to-all-start = ((bf16[8,2,80,2048]{3,2,1,0:T(8,128)(2,1)}), bf16[8,2,80,2048]{3,2,1,0:T(8,128)(2,1)}, u32[]{:S(2)}, u32[]{:S(2)}) async-start(bf16[8,2,80,2048]{3,2,1,0:T(8,128)(2,1)} %bitcast.313), calls=%async_computation | async-start | bytes 10485760 | tf_op jit(solution)/shard_map/all_to_all | solution.py:782
  110.1 36.9 %copy-start.30 = (f32[128,64]{1,0:T(8,128)}, f32[128,64]{1,0:T(8,128)S(1)}, u32[]{:S(2)}) copy-start(f32[128,64]{1,0:T(8,128)S(1)} %get-tuple-element.104) | copy-start | bytes 98308
  110.1 36.9 %copy-start.32 = (f32[128,64]{1,0:T(8,128)}, f32[128,64]{1,0:T(8,128)S(1)}, u32[]{:S(2)}) copy-start(f32[128,64]{1,0:T(8,128)S(1)} %get-tuple-element.105) | copy-start | bytes 98308
  170.1 35.0 %copy-start.15 = (bf16[1,128,2048]{2,1,0:T(8,128)(2,1)S(1)}, bf16[1,128,2048]{2,1,0:T(8,128)(2,1)}, u32[]{:S(2)}) copy-start(bf16[1,128,2048]{2,1,0:T(8,128)(2,1)} %param.16) | copy-start | bytes 1572868
  170.1 38.6 %copy-start.37 = (bf16[4,8,128,32]{2,3,1,0:T(8,128)(2,1)S(1)}, bf16[4,8,128,32]{2,3,1,0:T(8,128)(2,1)}, u32[]{:S(2)}) copy-start(bf16[4,8,128,32]{2,3,1,0:T(8,128)(2,1)} %copy-done.36) | copy-start | bytes 786436
  205.1 8.0 %copy-start.56 = (f32[2048]{0:T(1024)S(1)}, f32[2048]{0:T(1024)}, u32[]{:S(2)}) copy-start(f32[2048]{0:T(1024)} %param.27) | copy-start | bytes 24580
  215.3 87.1 %copy-start.29 = (f32[1280,32]{0,1:T(8,128)S(1)}, f32[1280,32]{0,1:T(8,128)}, u32[]{:S(2)}) copy-start(f32[1280,32]{0,1:T(8,128)} %reshape.457) | copy-start | bytes 491524
  215.3 87.1 %copy-start.34 = (bf16[8,4,8,256]{3,2,0,1:T(8,128)(2,1)S(1)}, bf16[8,4,8,256]{3,2,0,1:T(8,128)(2,1)}, u32[]{:S(2)}) copy-start(bf16[8,4,8,256]{3,2,0,1:T(8,128)(2,1)} %copy.243) | copy-start | bytes 393220
  302.4 11.4 %copy-start.25 = (bf16[640,256]{0,1:T(8,128)(2,1)S(1)}, bf16[640,256]{0,1:T(8,128)(2,1)}, u32[]{:S(2)}) copy-start(bf16[640,256]{0,1:T(8,128)(2,1)} %copy.198) | copy-start | bytes 983044
  311.3 18.6 %copy-start.65 = (f32[1280]{0:T(1024)}, f32[1280]{0:T(1024)S(1)}, u32[]{:S(2)}) copy-start(f32[1280]{0:T(1024)S(1)} %divide_reduce_fusion) | copy-start | bytes 15364
  313.8 9.4 %slice-start = ((s8[5242880]{0:T(1024)(128)(4,1)}), s8[4194304]{0:T(1024)(128)(4,1)S(1)}, s32[]{:S(2)}) async-start(s8[5242880]{0:T(1024)(128)(4,1)} %bitcast.307), calls=%async_computation.2 | async-start | bytes 8388608
  315.9 7.3 slice-start.1
  315.9 7.3 copy-start.79
  323.2 6.7 copy-start.82
  344.0 11.7 %copy-start.78 = (bf16[1,2048,768]{2,1,0:T(8,128)(2,1)S(1)}, bf16[1,2048,768]{2,1,0:T(8,128)(2,1)}, u32[]{:S(2)}) copy-start(bf16[1,2048,768]{2,1,0:T(8,128)(2,1)} %param.29) | copy-start | bytes 9437188
  355.6 6.9 copy-start.83
  362.6 65.6 %all-to-all-start.1 = ((bf16[8,2,80,2048]{3,2,1,0:T(8,128)(2,1)}), bf16[8,2,80,2048]{3,2,1,0:T(8,128)(2,1)}, u32[]{:S(2)}, u32[]{:S(2)}) async-start(bf16[8,2,80,2048]{3,2,1,0:T(8,128)(2,1)} %bitcast.316), calls=%async_computation.1 | async-start | bytes 10485760 | tf_op jit(solution)/shard_map/all_to_all | solution.py:782
  376.0 11.8 %slice-start.2 = ((s8[5242880]{0:T(1024)(128)(4,1)}), s8[1048576]{0:T(1024)(128)(4,1)S(1)}, s32[]{:S(2)}) async-start(s8[5242880]{0:T(1024)(128)(4,1)} %bitcast.310), calls=%async_computation.4 | async-start | bytes 2097152
  379.1 8.8 %slice-start.3 = ((s8[5242880]{0:T(1024)(128)(4,1)}), s8[4194304]{0:T(1024)(128)(4,1)S(1)}, s32[]{:S(2)}) async-start(s8[5242880]{0:T(1024)(128)(4,1)} %bitcast.310), calls=%async_computation.5 | async-start | bytes 8388608
  379.1 8.8 %copy-start.86 = (bf16[1280,768]{1,0:T(8,128)(2,1)S(1)}, bf16[1280,768]{1,0:T(8,128)(2,1)}, u32[]{:S(2)}) copy-start(bf16[1280,768]{1,0:T(8,128)(2,1)} %get-tuple-element.64) | copy-start | bytes 5898244
  403.2 114.3 %copy-start.11 = (f32[128,2048]{1,0:T(8,128)S(1)}, f32[128,2048]{1,0:T(8,128)}, u32[]{:S(2)}) copy-start(f32[128,2048]{1,0:T(8,128)} %get-tuple-element.61) | copy-start | bytes 3145732
  403.2 114.3 %copy-start.35 = (bf16[8,4,8,256]{3,2,0,1:T(8,128)(2,1)S(1)}, bf16[8,4,8,256]{3,2,0,1:T(8,128)(2,1)}, u32[]{:S(2)}) copy-start(bf16[8,4,8,256]{3,2,0,1:T(8,128)(2,1)} %copy.243) | copy-start | bytes 393220
  403.2 116.2 %copy-start.76 = (f32[128]{0:T(128)S(1)}, f32[128]{0:T(128)}, u32[]{:S(2)}) copy-start(f32[128]{0:T(128)} %copy-done.75) | copy-start | bytes 1540
  519.4 35.6 %copy-start.20 = (f32[128,2048]{1,0:T(8,128)}, f32[128,2048]{1,0:T(8,128)S(1)}, u32[]{:S(2)}) copy-start(f32[128,2048]{1,0:T(8,128)S(1)} %get-tuple-element.118) | copy-start | bytes 3145732
  519.8 35.2 %copy-start.19 = (bf16[8,128,4,128]{3,2,1,0:T(4,128)(2,1)S(1)}, bf16[8,128,4,128]{3,2,1,0:T(4,128)(2,1)}, u32[]{:S(2)}) copy-start(bf16[8,128,4,128]{3,2,1,0:T(4,128)(2,1)} %copy.192) | copy-start | bytes 3145732
  576.0 24.6 %copy-start.31 = (f32[128,64]{1,0:T(8,128)S(1)}, f32[128,64]{1,0:T(8,128)}, u32[]{:S(2)}) copy-start(f32[128,64]{1,0:T(8,128)} %copy-done.30) | copy-start | bytes 98308
  576.0 24.6 %copy-start.33 = (f32[128,64]{1,0:T(8,128)S(1)}, f32[128,64]{1,0:T(8,128)}, u32[]{:S(2)}) copy-start(f32[128,64]{1,0:T(8,128)} %copy-done.32) | copy-start | bytes 98308
  576.3 24.7 %copy-start.28 = (f32[1024,128]{1,0:T(8,128)S(1)}, f32[1024,128]{1,0:T(8,128)}, u32[]{:S(2)}) copy-start(f32[1024,128]{1,0:T(8,128)} %get-tuple-element.66) | copy-start | bytes 1572868
  576.3 24.7 %copy-start.58 = (f32[8,128]{1,0:T(8,128)S(1)}, f32[8,128]{1,0:T(8,128)}, u32[]{:S(2)}) copy-start(f32[8,128]{1,0:T(8,128)} %copy-done.57) | copy-start | bytes 12292
  576.3 24.7 %copy-start.68 = (f32[128]{0:T(128)S(1)}, f32[128]{0:T(128)}, u32[]{:S(2)}) copy-start(f32[128]{0:T(128)} %param.25) | copy-start | bytes 1540
  (61 other events, 204.8 us)

commit v4 on v3

--- a/solution.py
+++ b/solution.py
@@ -14,6 +14,10 @@
 VMEM = pl.BlockSpec(memory_space=pltpu.VMEM)
 DMA = pltpu.SemaphoreType.DMA
 epsilon = 1e-06
+rope_base = 1000000.0
+QUERY_HEADS = 32
+KEY_VALUE_HEADS = 4
+HEAD_DIM = 128
 
 
 def push(src, dst, send_sem, recv_sem, **where):
@@ -117,78 +121,285 @@
     )(*args)
 
 
-def start_body(n_ctx, n_shard, rows, wsend, routes, router, cot,
-               rows_all, w_all, routes_all, router_all, cot_all,
-               local, ss_row, rs_row, ss_fwd, rs_fwd, ss_w, rs_w, ss_rt, rs_rt, ss_ro, rs_ro,
-               ss_z, rs_z, ss_rz, rs_rz):
+def slot_table(code, slots):
+    places = lax.broadcasted_iota(jnp.int32, (slots, code.shape[1]), 0).astype(F32)
+    return jnp.concatenate(
+        [(places == code[e : e + 1, :]).astype(BF) for e in range(code.shape[0])], axis=0
+    )
+
+
+def turn(value, cosine, sine):
+    return value * cosine + pltpu.roll(value, HEAD_DIM // 2, 1) * sine
+
+
+def unit_rows(value):
+    scale = lax.rsqrt(jnp.mean(value * value, axis=-1, keepdims=True) + epsilon)
+    return value * scale, scale
+
+
+def front_body(n_ctx, n_shard, group, capacity, heads, kv_heads, tile,
+               tokens, gain, w_query, key_w, value_w, routes, router, cot, cosine, sine, bias, q_gain, k_gain, w_out,
+               rows_out, w_all_out, router_all, code, cot_rows, qpre_out, kvpre, q_out, kv_out, attn_out, mid,
+               own_rows, rows_all, w_all, zroutes, zcot, ready, qpre, q, kv, attn,
+               own_part, pair, to_sib, sib, to_chip, got,
+               local, ss_row, rs_row, ss_fwd, rs_fwd, ss_w, rs_w, ss_k, rs_k, ss_rt, rs_rt, ss_ro, rs_ro, ss_z, rs_z,
+               ss_x, rs_x, ss_kz, rs_kz, ss_kf, rs_kf, ss_s, rs_s, ss_c, rs_c, out_sem):
     c, s, parity, sibling, others, layers = here(n_ctx, n_shard)
+    chips = n_shard // 2
+    chip = lax.div(s, 2)
+    count, width = tokens.shape
+    wr = w_query.shape[0]
+    cols = heads * HEAD_DIM
+    sharers = n_shard // kv_heads
+    groups = n_ctx // group
+    slots = group * capacity
+    keys = n_ctx * count
+    mates = [lax.rem(s + 2 * d, n_shard) for d in range(1, chips)]
+    x = tokens[...].astype(F32)
+    unit, unused = unit_rows(x)
+    own_rows[...] = (unit * gain[...]).astype(BF)
     greet(others, layers)
-    chips = n_shard // 2
+
+    route_fan = Fan(n_ctx, c, lambda d: zroutes.at[flip_bits(c, d)], ss_ro, rs_ro, False)
+    route_fan.send(0, routes)
+    cot_fan = Fan(n_ctx, c, lambda d: zcot.at[flip_bits(c, d)], ss_z, rs_z, False)
+    cot_fan.send(0, cot)
+    first, waits = [], []
+    for d in range(1, chips):
+        item = push(own_rows, rows_all.at[s], ss_row.at[d], rs_row.at[d], shard=mates[d - 1])
+        item.start()
+        first.append(item)
+    item = push(own_rows, rows_all.at[s], ss_fwd.at[0], rs_fwd.at[0], shard=sibling)
+    item.start()
+    waits.append(item)
+    w_waits = []
+    for i, peer in enumerate(others):
+        from_q = w_query.at[:, pl.ds(pl.multiple_of(peer * cols, cols), cols)]
+        item = push(from_q, w_all.at[s, :, pl.ds(0, cols)], ss_w.at[i], rs_w.at[i], shard=peer)
+        item.start()
+        w_waits.append(item)
+        head = pl.ds(pl.multiple_of(lax.div(peer, sharers) * HEAD_DIM, HEAD_DIM), HEAD_DIM)
+        for kind, ref in enumerate((key_w, value_w)):
+            item = push(ref.at[:, head], w_all.at[s, :, pl.ds(cols, HEAD_DIM)], ss_k.at[i], rs_k.at[i], shard=peer)
+
+            @pl.when(lax.rem(peer, 2) == kind)
+            def _(item=item):
+                item.start()
+
+        w_waits.append(item)
+        item = push(router, router_all.at[:, pl.ds(pl.multiple_of(s * wr, wr), wr)], ss_rt.at[i], rs_rt.at[i], shard=peer)
+        item.start()
+        waits.append(item)
     copies = [
-        pltpu.make_async_copy(rows, rows_all.at[s], local.at[0]),
-        pltpu.make_async_copy(wsend.at[s], w_all.at[s], local.at[1]),
-        pltpu.make_async_copy(routes, routes_all.at[c, s], local.at[2]),
-        pltpu.make_async_copy(router, router_all.at[s], local.at[3]),
-        pltpu.make_async_copy(cot, cot_all.at[c], local.at[4]),
+        pltpu.make_async_copy(own_rows, rows_all.at[s], local.at[0]),
+        pltpu.make_async_copy(w_query.at[:, pl.ds(pl.multiple_of(s * cols, cols), cols)],
+                              w_all.at[s, :, pl.ds(0, cols)], local.at[1]),
+        pltpu.make_async_copy(routes, zroutes.at[c], local.at[2]),
+        pltpu.make_async_copy(router, router_all.at[:, pl.ds(pl.multiple_of(s * wr, wr), wr)], local.at[3]),
+        pltpu.make_async_copy(cot, zcot.at[c], local.at[4]),
     ]
     for item in copies:
         item.start()
-    waits = []
-    near = []
-    for i, peer in enumerate(others):
-        item = push(routes, routes_all.at[c, s], ss_ro.at[i], rs_ro.at[i], shard=peer)
-        item.start()
-        near.append(item)
-    first = []
-    for d in range(1, chips):
-        item = push(rows, rows_all.at[s], ss_row.at[d], rs_row.at[d], shard=lax.rem(s + 2 * d, n_shard))
-        item.start()
-        first.append(item)
-    item = push(rows, rows_all.at[s], ss_fwd.at[0], rs_fwd.at[0], shard=sibling)
-    item.start()
-    waits.append(item)
-    fan = Fan(n_ctx, c, lambda d: cot_all.at[flip_bits(c, d)], ss_z, rs_z, False)
-    fan.send(0, cot)
-    for i, peer in enumerate(others):
-        item = push(wsend.at[peer], w_all.at[s], ss_w.at[i], rs_w.at[i], shard=peer)
-        item.start()
-        waits.append(item)
-        item = push(router, router_all.at[s], ss_rt.at[i], rs_rt.at[i], shard=peer)
-        item.start()
-        waits.append(item)
+    head = pl.ds(pl.multiple_of(lax.div(s, sharers) * HEAD_DIM, HEAD_DIM), HEAD_DIM)
+    for kind, ref in enumerate((key_w, value_w)):
+        own_head = pltpu.make_async_copy(ref.at[:, head], w_all.at[s, :, pl.ds(cols, HEAD_DIM)], local.at[5])
+
+        @pl.when(parity == kind)
+        def _(own_head=own_head):
+            own_head.start()
+
     copies[2].wait()
-    for item in near:
-        item.wait()
-    for i, layer in enumerate(layers):
-        item = push(routes_all.at[c], routes_all.at[c], ss_rz.at[i], rs_rz.at[i], ctx=layer)
-        item.start()
-        waits.append(item)
+    for d in route_fan.order():
+        route_fan.arrival(d)
+    before = (
+        lax.broadcasted_iota(jnp.int32, (count, count), 0) < lax.broadcasted_iota(jnp.int32, (count, count), 1)
+    ).astype(BF)
+    for layer in range(n_ctx):
+        named = zroutes[layer]
+        mask = jnp.concatenate(
+            [jnp.max((named == c * n_shard + e).astype(F32), axis=0, keepdims=True) for e in range(n_shard)], axis=0
+        )
+        rank = jnp.dot(mask.astype(BF), before, preferred_element_type=F32)
+        at = layer % group
+        code[layer // group, :, at * count : (at + 1) * count] = jnp.where(
+            mask > 0, rank + float(at * capacity), -1.0
+        )
+
     for d in range(1, chips):
         first[d - 1].wait()
         origin = lax.rem(s + n_shard - 2 * d, n_shard)
         item = push(rows_all.at[origin], rows_all.at[origin], ss_fwd.at[d], rs_fwd.at[d], shard=sibling)
         item.start()
         waits.append(item)
+    for d in cot_fan.order():
+        cot_fan.arrival(d)
+    copies[4].wait()
+    for k in range(groups):
+        table = slot_table(code[k], slots)
+
+        @pl.loop(0, width // tile)
+        def _(j):
+            part = pl.ds(pl.multiple_of(j * tile, tile), tile)
+            block = zcot[k * group : (k + 1) * group, :, part].reshape(group * count, tile)
+            value = jnp.dot(table, block, preferred_element_type=F32).astype(BF)
+            ready[k, :, :, part] = value.reshape(n_shard, slots, tile)
+
+    for item in waits + w_waits:
+        item.wait()
+    copies[0].wait()
+    copies[1].wait()
+    copies[3].wait()
+    own_head.wait()
+    outs = [
+        pltpu.make_async_copy(rows_all, rows_out, out_sem.at[0]),
+        pltpu.make_async_copy(w_all, w_all_out, out_sem.at[1]),
+    ]
+    outs[0].start()
+    outs[1].start()
+
+    right = w_all[:, :, pl.ds(cols, HEAD_DIM)].reshape(width, HEAD_DIM)
+
+    @pl.loop(0, n_shard)
+    def _(b):
+        pre = jnp.dot(rows_all[b], right, preferred_element_type=F32)
+        kvpre[b] = pre
+        keyed, unused = unit_rows(pre)
+        keyed = turn(keyed * k_gain[...], cosine[...], sine[...])
+        kv[parity, b, c] = jnp.where(parity == 0, keyed, pre).astype(BF)
+
+    fan = Fan(n_ctx, c, lambda d: kv.at[parity, :, flip_bits(c, d)], ss_kz, rs_kz, False)
+    fan.send(0, kv.at[parity, :, c])
+    kv_waits = []
+    item = push(kv.at[parity, :, c], kv.at[parity, :, c], ss_kf.at[0], rs_kf.at[0], shard=sibling)
+    item.start()
+    kv_waits.append(item)
+
+    cot_waits = []
+    for k in range(groups):
+        for i, peer in enumerate(others):
+            item = push(ready.at[k, peer], cot_rows.at[s, k], ss_x.at[k, i], rs_x.at[k, i], shard=peer)
+            item.start()
+            cot_waits.append(item)
+        item = pltpu.make_async_copy(ready.at[k, s], cot_rows.at[s, k], local.at[6 + k])
+        item.start()
+        cot_waits.append(item)
+
+    @pl.loop(0, n_shard // 2)
+    def _(b):
+        left = rows_all[pl.ds(b * 2, 2)].reshape(2 * count, width)
+        pre = jnp.dot(left, w_all[:, :, pl.ds(0, cols)].reshape(width, cols), preferred_element_type=F32)
+        qpre[pl.ds(b * 2, 2)] = pre.reshape(2, count, cols)
+        for i in range(2):
+            for h in range(heads):
+                part = pre[i * count : (i + 1) * count, h * HEAD_DIM : (h + 1) * HEAD_DIM]
+                unit, unused = unit_rows(part)
+                q[b * 2 + i, :, h * HEAD_DIM : (h + 1) * HEAD_DIM] = turn(
+                    unit * q_gain[...], cosine[...], sine[...]
+                ).astype(BF)
+
     for d in fan.order():
         fan.arrival(d)
+        block = kv.at[parity, :, flip_bits(c, d)]
+        item = push(block, block, ss_kf.at[d], rs_kf.at[d], shard=sibling)
+        item.start()
+        kv_waits.append(item)
+    outs += [pltpu.make_async_copy(qpre, qpre_out, out_sem.at[2]), pltpu.make_async_copy(q, q_out, out_sem.at[3])]
+    outs[2].start()
+    outs[3].start()
+    for item in kv_waits:
+        item.wait()
     fan.drain()
-    for i in (0, 1, 3, 4):
-        copies[i].wait()
-    for item in waits:
+    outs.append(pltpu.make_async_copy(kv, kv_out, out_sem.at[4]))
+    outs[4].start()
+
+    near, far = {}, {}
+    order = list(range(1, chips)) + [0]
+
+    def product(at):
+        d = order[at]
+        first_seq = 2 * lax.rem(chip + d, chips)
+
+        @pl.loop(0, 2)
+        def _(i):
+            b = first_seq + i
+            k_all = kv[0, b].reshape(keys, HEAD_DIM)
+            v_all = kv[1, b].reshape(keys, HEAD_DIM)
+            for h in range(heads):
+                hs = slice(h * HEAD_DIM, (h + 1) * HEAD_DIM)
+                scores = lax.dot_general(q[b, :, hs], k_all, (((1,), (1,)), ((), ())), preferred_element_type=F32)
+                scores = scores * (HEAD_DIM ** -0.5) + bias[...]
+                raised = jnp.exp(scores - jnp.max(scores, axis=-1, keepdims=True))
+                probs = raised / jnp.sum(raised, axis=-1, keepdims=True)
+                attn[b, :, hs] = jnp.dot(probs.astype(BF), v_all, preferred_element_type=F32).astype(BF)
+
+        left = attn[pl.ds(first_seq, 2)].reshape(2 * count, cols)
+
+        @pl.loop(0, width // tile)
+        def _(j):
+            part = pl.ds(pl.multiple_of(j * tile, tile), tile)
+            value = jnp.dot(left, w_out[:, part], preferred_element_type=F32)
+            pair[...] = value.reshape(2, count, tile)
+            own_part[at % 2, :, part] = pair[parity]
+            to_sib[at, :, part] = pair[1 - parity].astype(BF)
+
+        near[at] = push(to_sib.at[at], sib.at[at], ss_s.at[at], rs_s.at[at], shard=sibling)
+        near[at].start()
+
+    def chip_sum(at):
+        near[at].wait()
+        to_chip[at] = (own_part[at % 2] + sib[at].astype(F32)).astype(BF)
+        far[at] = push(to_chip.at[at], got.at[at], ss_c.at[at], rs_c.at[at], shard=mates[order[at] - 1])
+        far[at].start()
+
+    for at in range(chips):
+        product(at)
+        if at:
+            chip_sum(at - 1)
+    outs.append(pltpu.make_async_copy(attn, attn_out, out_sem.at[5]))
+    outs[5].start()
+    near[chips - 1].wait()
+    mid[...] = tokens[...].astype(F32) + own_part[(chips - 1) % 2] + sib[chips - 1].astype(F32)
+    for at in range(chips - 1):
+        far[at].wait()
+        mid[...] += got[at].astype(F32)
+    cot_fan.drain()
+    route_fan.drain()
+    for item in cot_waits + outs:
         item.wait()
 
 
-def start(n_ctx, n_shard, rows, wsend, routes, router, cot):
+def front(n_ctx, n_shard, group, capacity, kv_heads, args, ident):
+    tokens, gain, w_query, key_w, value_w, routes, router, cot = args[:8]
     n, z = n_shard, n_ctx
-    shapes = [
-        (n,) + rows.shape, wsend.shape, (z, n) + routes.shape, (n,) + router.shape, (z,) + cot.shape,
-    ]
-    kinds = [rows.dtype, wsend.dtype, routes.dtype, router.dtype, cot.dtype]
-    sems = [DMA((5,))] + [DMA((n // 2,))] * 4 + [DMA((n - 1,))] * 6 + [DMA((z,))] * 4
+    count, width = tokens.shape
+    wr, chips, groups, slots = w_query.shape[0], n_shard // 2, n_ctx // group, group * capacity
+    cols = w_query.shape[1] // n
+    heads = cols // HEAD_DIM
+    sds = jax.ShapeDtypeStruct
+    dma = lambda *shape: DMA(shape)
     return call(
-        functools.partial(start_body, z, n),
-        [jax.ShapeDtypeStruct(a, b) for a, b in zip(shapes, kinds)],
-        [ANY] * 5, sems, 0, (rows, wsend, routes, router, cot),
+        functools.partial(front_body, z, n, group, capacity, heads, kv_heads, 512),
+        [
+            sds((n, count, width), BF), sds((n, wr, cols + HEAD_DIM), BF), sds((router.shape[0], width), BF),
+            sds((groups, n, group * count), F32), sds((n, groups, slots, width), BF), sds((n, count, cols), F32),
+            sds((n, count, HEAD_DIM), F32), sds((n, count, cols), BF), sds((2, n, z, count, HEAD_DIM), BF),
+            sds((n, count, cols), BF), sds((count, width), F32),
+        ],
+        [VMEM, VMEM, ANY, ANY, ANY, VMEM, ANY, ANY] + [VMEM] * 6,
+        [
+            pltpu.VMEM((count, width), BF), pltpu.VMEM((n, count, width), BF), pltpu.VMEM((n, wr, cols + HEAD_DIM), BF),
+            pltpu.VMEM((z,) + routes.shape, jnp.int32), pltpu.VMEM((z, count, width), BF),
+            pltpu.VMEM((groups, n, slots, width), BF), pltpu.VMEM((n, count, cols), F32),
+            pltpu.VMEM((n, count, cols), BF), pltpu.VMEM((2, n, z, count, HEAD_DIM), BF),
+            pltpu.VMEM((n, count, cols), BF), pltpu.VMEM((2, count, width), F32), pltpu.VMEM((2, count, 512), F32),
+            pltpu.VMEM((chips, count, width), BF), pltpu.VMEM((chips, count, width), BF),
+            pltpu.VMEM((chips - 1, count, width), BF), pltpu.VMEM((chips - 1, count, width), BF),
+            dma(6 + groups), dma(chips), dma(chips), dma(chips), dma(chips), dma(n - 1), dma(n - 1), dma(n - 1), dma(n - 1),
+            dma(n - 1), dma(n - 1), dma(z), dma(z), dma(z), dma(z), dma(groups, n - 1), dma(groups, n - 1),
+            dma(z), dma(z), dma(z), dma(z), dma(chips), dma(chips), dma(chips - 1), dma(chips - 1), dma(6),
+        ],
+        ident, args, mib=60,
+        out_specs=[ANY, ANY, ANY, VMEM, ANY, ANY, VMEM, ANY, ANY, ANY, VMEM],
     )
 
 
@@ -223,38 +434,6 @@
         functools.partial(spread_body, n_shard),
         [jax.ShapeDtypeStruct((n_shard,) + rows.shape, rows.dtype)],
         [ANY], [DMA] + [DMA((n_shard // 2,))] * 4, ident, (rows,),
-    )[0]
-
-
-def key_body(n_ctx, n_shard, mine, kv, local, ss_z, rs_z, ss_f, rs_f):
-    c, s, parity, sibling, others, layers = here(n_ctx, n_shard)
-    greet([sibling], layers)
-    own = pltpu.make_async_copy(mine, kv.at[parity, :, c], local)
-    own.start()
-    fan = Fan(n_ctx, c, lambda d: kv.at[parity, :, flip_bits(c, d)], ss_z, rs_z, False)
-    fan.send(0, mine)
-    waits = []
-    item = push(mine, kv.at[parity, :, c], ss_f.at[0], rs_f.at[0], shard=sibling)
-    item.start()
-    waits.append(item)
-    for d in fan.order():
-        fan.arrival(d)
-        block = kv.at[parity, :, flip_bits(c, d)]
-        item = push(block, block, ss_f.at[d], rs_f.at[d], shard=sibling)
-        item.start()
-        waits.append(item)
-    fan.drain()
-    own.wait()
-    for item in waits:
-        item.wait()
-
-
-def key_exchange(n_ctx, n_shard, mine, ident):
-    n, rows, width = mine.shape
-    return call(
-        functools.partial(key_body, n_ctx, n_shard),
-        [jax.ShapeDtypeStruct((2, n, n_ctx, rows, width), mine.dtype)],
-        [ANY], [DMA] + [DMA((n_ctx,))] * 4, ident, (mine,),
     )[0]
 
 
@@ -293,64 +472,6 @@
             pltpu.VMEM((n_ctx - 1,) + block, BF),
         ] + [DMA((n_ctx,))] * 4,
         ident, (parts,), out_specs=[VMEM],
-    )[0]
-
-
-def product_body(n_shard, tile, flip, left, right, out, part, to_sib, sib, to_chip, got,
-                 ss_s, rs_s, ss_c, rs_c):
-    c, s, parity, sibling, others, layers = here(1, n_shard)
-    chips = n_shard // 2
-    chip = lax.div(s, 2)
-    mates = [lax.rem(s + 2 * d, n_shard) for d in range(1, chips)]
-    greet(mates + [sibling], [])
-    rows, width = out.shape
-    order = list(range(1, chips)) + [0]
-    near = [None] * chips
-    for d in order:
-        first = pl.multiple_of(lax.rem(chip + d, chips) * (2 * rows), 2 * rows)
-
-        @pl.loop(0, width // tile)
-        def _(j):
-            cols = pl.ds(pl.multiple_of(j * tile, tile), tile)
-            if flip:
-                value = lax.dot_general(left[pl.ds(first, 2 * rows), :], right[cols, :],
-                                        (((1,), (1,)), ((), ())), preferred_element_type=F32)
-            else:
-                value = jnp.dot(left[pl.ds(first, 2 * rows), :], right[:, cols],
-                                preferred_element_type=F32)
-            part[d, :, :, cols] = value.reshape(2, rows, tile)
-
-        to_sib[d] = part[d, 1 - parity].astype(BF)
-        near[d] = push(to_sib.at[d], sib.at[d], ss_s.at[d], rs_s.at[d], shard=sibling)
-        near[d].start()
-    far = []
-    for d in range(1, chips):
-        near[d].wait()
-        to_chip[d - 1] = (part[d, parity] + sib[d].astype(F32)).astype(BF)
-        item = push(to_chip.at[d - 1], got.at[d - 1], ss_c.at[d - 1], rs_c.at[d - 1], shard=mates[d - 1])
-        item.start()
-        far.append(item)
-    near[0].wait()
-    out[...] = part[0, parity] + sib[0].astype(F32)
-    for d in range(1, chips):
-        far[d - 1].wait()
-        out[...] += got[d - 1].astype(F32)
-
-
-def product_scatter(n_shard, left, right, flip, ident):
-    rows = left.shape[0] // n_shard
-    width = right.shape[0] if flip else right.shape[1]
-    chips = n_shard // 2
-    return call(
-        functools.partial(product_body, n_shard, 512, flip),
-        [jax.ShapeDtypeStruct((rows, width), F32)],
-        [VMEM, VMEM],
-        [
-            pltpu.VMEM((chips, 2, rows, width), F32), pltpu.VMEM((chips, rows, width), BF),
-            pltpu.VMEM((chips, rows, width), BF), pltpu.VMEM((chips - 1, rows, width), BF),
-            pltpu.VMEM((chips - 1, rows, width), BF),
-        ] + [DMA((chips,))] * 2 + [DMA((chips - 1,))] * 2,
-        ident, (left, right), mib=56, out_specs=[VMEM],
     )[0]
 
 
@@ -593,70 +714,93 @@
     )
 
 
-def dispatch_body(n_ctx, n_shard, group, tile, rows, picks, recv, zrows, ready, local,
-                  ss_z, rs_z, ss_x, rs_x):
+def dispatch_body(n_ctx, n_shard, group, tile, rows, tail, code, recv, tail_recv,
+                  zrows, ztail, ready, tail_ready, local, ss_z, rs_z, ss_t, rs_t, ss_x, rs_x, ss_y, rs_y):
     c, s, parity, sibling, others, layers = here(n_ctx, n_shard)
     greet(others, layers)
     count, width = rows.shape
     groups = n_ctx // group
-    own = pltpu.make_async_copy(rows, zrows.at[c], local.at[0])
-    own.start()
-    fan = Fan(n_ctx, c, lambda d: zrows.at[flip_bits(c, d)], ss_z, rs_z, True)
-    fan.send(0, rows)
+    slots = recv.shape[2]
+    own = [pltpu.make_async_copy(rows, zrows.at[c], local.at[0]), pltpu.make_async_copy(tail, ztail.at[c], local.at[1])]
+    fans = [
+        Fan(n_ctx, c, lambda d: ztail.at[flip_bits(c, d)], ss_t, rs_t, True),
+        Fan(n_ctx, c, lambda d: zrows.at[flip_bits(c, d)], ss_z, rs_z, True),
+    ]
+    fans[0].send(0, tail)
+    fans[1].send(0, rows)
+    for item in own:
+        item.start()
     waits = []
     seen = set()
     for k in range(groups):
         at = flip_bits(lax.div(c, group), k)
         if k == 0:
-            own.wait()
-        for d in fan.order():
+            for item in own:
+                item.wait()
+        table = slot_table(code[at], slots)
+        for d in fans[0].order():
             if d < (k + 1) * group and d not in seen:
-                fan.arrival(d)
+                fans[0].arrival(d)
+                fans[1].arrival(d)
                 seen.add(d)
         first = pl.multiple_of(at * group, group)
+        block = ztail[pl.ds(first, group)].reshape(group * count, -1)
+        tail_ready[k] = jnp.dot(table, block, preferred_element_type=F32).astype(BF).reshape(n_shard, slots, -1)
 
         @pl.loop(0, width // tile)
         def _(j):
             cols = pl.ds(pl.multiple_of(j * tile, tile), tile)
             block = zrows[pl.ds(first, group), :, cols].reshape(group * count, tile)
-            value = jnp.dot(picks[at], block, preferred_element_type=F32).astype(BF)
-            ready[k, :, :, cols] = value.reshape(n_shard, -1, tile)
+            value = jnp.dot(table, block, preferred_element_type=F32).astype(BF)
+            ready[k, :, :, cols] = value.reshape(n_shard, slots, tile)
 
         for i, peer in enumerate(others):
             item = push(ready.at[k, peer], recv.at[s, at], ss_x.at[k, i], rs_x.at[k, i], shard=peer)
             item.start()
             waits.append(item)
-        item = pltpu.make_async_copy(ready.at[k, s], recv.at[s, at], local.at[k + 1])
+            item = push(tail_ready.at[k, peer], tail_recv.at[s, at], ss_y.at[k, i], rs_y.at[k, i], shard=peer)
+            item.start()
+            waits.append(item)
+        item = pltpu.make_async_copy(ready.at[k, s], recv.at[s, at], local.at[2 * k + 2])
         item.start()
         waits.append(item)
-    fan.drain()
+        item = pltpu.make_async_copy(tail_ready.at[k, s], tail_recv.at[s, at], local.at[2 * k + 3])
+        item.start()
+        waits.append(item)
+    for fan in fans:
+        fan.drain()
     for item in waits:
         item.wait()
 
 
-def dispatch_rows(n_ctx, n_shard, group, rows, picks, ident):
-    groups, slots = picks.shape[0], picks.shape[1] // n_shard
+def dispatch_rows(n_ctx, n_shard, group, capacity, rows, tail, code, ident):
+    groups, slots = code.shape[0], group * capacity
     count, width = rows.shape
+    few = tail.shape[1]
     return call(
         functools.partial(dispatch_body, n_ctx, n_shard, group, 512),
-        [jax.ShapeDtypeStruct((n_shard, groups, slots, width), BF)],
-        [VMEM, VMEM],
         [
-            pltpu.VMEM((n_ctx, count, width), BF), pltpu.VMEM((groups, n_shard, slots, width), BF),
-            DMA((groups + 1,)), DMA((n_ctx,)), DMA((n_ctx,)),
-            DMA((groups, n_shard - 1)), DMA((groups, n_shard - 1)),
+            jax.ShapeDtypeStruct((n_shard, groups, slots, width), BF),
+            jax.ShapeDtypeStruct((n_shard, groups, slots, few), BF),
         ],
-        ident, (rows, picks), mib=56,
-    )[0]
-
-
-def combine_body(n_ctx, n_shard, group, tile, rows, mix, picks, out, mix_out, land, value, zsend, zrecv,
-                 msend, mrecv, mix_kept, local, ss_x, rs_x, ss_z, rs_z, ss_m, rs_m):
+        [VMEM, VMEM, VMEM],
+        [
+            pltpu.VMEM((n_ctx, count, width), BF), pltpu.VMEM((n_ctx, count, few), BF),
+            pltpu.VMEM((groups, n_shard, slots, width), BF), pltpu.VMEM((groups, n_shard, slots, few), BF),
+            DMA((2 * groups + 2,)), DMA((n_ctx,)), DMA((n_ctx,)), DMA((n_ctx,)), DMA((n_ctx,)),
+        ] + [DMA((groups, n_shard - 1))] * 4,
+        ident, (rows, tail, code), mib=56,
+    )
+
+
+def combine_body(n_ctx, n_shard, group, tile, rows, tail, mix, code, out, tail_out, mix_out,
+                 land, tail_land, value, tail_value, zsend, zrecv, tsend, trecv, msend, mrecv, mix_kept, table, local,
+                 ss_x, rs_x, ss_y, rs_y, ss_z, rs_z, ss_t, rs_t, ss_m, rs_m):
     c, s, parity, sibling, others, layers = here(n_ctx, n_shard)
     greet(others, layers)
     count, width = out.shape
-    mix_width = mix_out.shape[1]
     groups = n_ctx // group
+    slots = rows.shape[2]
     near = {}
     for k in reversed(range(groups)):
         at = flip_bits(lax.div(c, group), k)
@@ -665,79 +809,87 @@
             item = push(rows.at[peer, at], land.at[k, s], ss_x.at[k, i], rs_x.at[k, i], shard=peer)
             item.start()
             near[k].append(item)
-        item = pltpu.make_async_copy(rows.at[s, at], land.at[k, s], local.at[k])
+            item = push(tail.at[peer, at], tail_land.at[k, s], ss_y.at[k, i], rs_y.at[k, i], shard=peer)
+            item.start()
+            near[k].append(item)
+        item = pltpu.make_async_copy(rows.at[s, at], land.at[k, s], local.at[k, 0])
         item.start()
         near[k].append(item)
-
-    def local_sums(k, block_of, step, last):
-        at = flip_bits(lax.div(c, group), k)
-
-        @pl.loop(0, last // step)
+        item = pltpu.make_async_copy(tail.at[s, at], tail_land.at[k, s], local.at[k, 1])
+        item.start()
+        near[k].append(item)
+    for k in range(groups):
+        table[k] = slot_table(code[flip_bits(lax.div(c, group), k)], slots).T
+
+    def local_sums(k, block_of):
+        @pl.loop(0, width // tile)
         def _(j):
-            cols = pl.ds(pl.multiple_of(j * step, step), step)
-            value[:, cols] = jnp.dot(picks[at], block_of(at, cols), preferred_element_type=F32)
-
-    def part(d, last):
+            cols = pl.ds(pl.multiple_of(j * tile, tile), tile)
+            value[:, cols] = jnp.dot(table[k], block_of(cols), preferred_element_type=F32)
+
+    def part(ref, d):
         place = lax.rem(flip_bits(c, d), group)
-        return value[pl.ds(pl.multiple_of(place * count, count), count), pl.ds(0, last)]
+        return ref[pl.ds(pl.multiple_of(place * count, count), count), :]
 
     def in_group(k):
         return sorted(range(k * group, (k + 1) * group), key=lambda d: (lowest(d) or n_ctx, d))
 
     mix_fold = Fold(c, msend, mrecv, ss_m, rs_m)
     for k in reversed(range(groups)):
-        local_sums(k, lambda at, cols: mix[:, at, :, cols].reshape(picks.shape[2], -1), 512, mix_width)
+        at = flip_bits(lax.div(c, group), k)
+        local_sums(k, lambda cols: mix[:, at, :, cols].reshape(n_shard * slots, tile))
         for d in in_group(k):
             if lowest(d) == 1:
-                mix_fold.give(d, part(d, mix_width))
+                mix_fold.give(d, part(value, d))
             else:
-                mix_kept[d // 2] = part(d, mix_width)
+                mix_kept[d // 2] = part(value, d)
     fold = Fold(c, zsend, zrecv, ss_z, rs_z)
+    tail_fold = Fold(c, tsend, trecv, ss_t, rs_t)
     for k in reversed(range(groups)):
         for item in near[k]:
             item.wait()
-        local_sums(k, lambda at, cols: land[k, :, :, cols].reshape(picks.shape[2], -1), tile, width)
+        local_sums(k, lambda cols: land[k, :, :, cols].reshape(n_shard * slots, tile))
+        tail_value[...] = jnp.dot(
+            table[k], tail_land[k].reshape(n_shard * slots, -1), preferred_element_type=F32
+        )
         for d in in_group(k):
             if lowest(d) == 1:
-                fold.give(d, part(d, width))
+                fold.give(d, part(value, d))
+                tail_fold.give(d, part(tail_value, d))
         for d in in_group(k):
             if lowest(d) != 1:
                 if d:
                     mix_fold.give(d, mix_fold.take(d, mix_kept[d // 2]))
-                    fold.give(d, fold.take(d, part(d, width)))
+                    fold.give(d, fold.take(d, part(value, d)))
+                    tail_fold.give(d, tail_fold.take(d, part(tail_value, d)))
                 else:
                     mix_out[...] = mix_fold.take(0, mix_kept[0])
-                    out[...] = fold.take(0, part(0, width))
-    mix_fold.drain()
-    fold.drain()
-
-
-def combine_rows(n_ctx, n_shard, group, rows, mix, picks, ident):
+                    out[...] = fold.take(0, part(value, 0))
+                    tail_out[...] = tail_fold.take(0, part(tail_value, 0))
+    for item in (mix_fold, fold, tail_fold):
+        item.drain()
+
+
+def combine_rows(n_ctx, n_shard, group, rows, tail, mix, code, ident):
     groups, slots, width = rows.shape[1:]
-    mix_width = mix.shape[3]
-    count = picks.shape[1] // group
-    tile = 128 * max(t for t in range(1, 9) if (width // 128) % t == 0)
+    few = tail.shape[3]
+    count = code.shape[2] // group
+    sds = jax.ShapeDtypeStruct
     return call(
-        functools.partial(combine_body, n_ctx, n_shard, group, tile),
-        [jax.ShapeDtypeStruct((count, width), F32), jax.ShapeDtypeStruct((count, mix_width), F32)],
-        [VMEM, VMEM, VMEM],
+        functools.partial(combine_body, n_ctx, n_shard, group, 512),
+        [sds((count, width), F32), sds((count, few), F32), sds((count, width), F32)],
+        [VMEM] * 4,
         [
-            pltpu.VMEM((groups, n_shard, slots, width), BF), pltpu.VMEM((group * count, width), F32),
+            pltpu.VMEM((groups, n_shard, slots, width), BF), pltpu.VMEM((groups, n_shard, slots, few), BF),
+            pltpu.VMEM((group * count, width), F32), pltpu.VMEM((group * count, few), F32),
             pltpu.VMEM((n_ctx - 1, count, width), BF), pltpu.VMEM((n_ctx - 1, count, width), BF),
-            pltpu.VMEM((n_ctx - 1, count, mix_width), BF), pltpu.VMEM((n_ctx - 1, count, mix_width), BF),
-            pltpu.VMEM((n_ctx // 2, count, mix_width), F32), DMA((groups,)), DMA((groups, n_shard - 1)), DMA((groups, n_shard - 1)),
-            DMA((n_ctx,)), DMA((n_ctx,)), DMA((n_ctx,)), DMA((n_ctx,)),
-        ],
-        ident, (rows, mix, picks), mib=60, out_specs=[VMEM, VMEM],
-    )
-
-
-QUERY_HEADS = 32
-KEY_VALUE_HEADS = 4
-HEAD_DIM = 128
-
-epsilon = 1e-06
-rope_base = 1000000.0
+            pltpu.VMEM((n_ctx - 1, count, few), BF), pltpu.VMEM((n_ctx - 1, count, few), BF),
+            pltpu.VMEM((n_ctx - 1, count, width), BF), pltpu.VMEM((n_ctx - 1, count, width), BF),
+            pltpu.VMEM((n_ctx // 2, count, width), F32), pltpu.VMEM((groups, group * count, n_shard * slots), BF),
+            DMA((groups, 2)),
+        ] + [DMA((groups, n_shard - 1))] * 4 + [DMA((n_ctx,))] * 6,
+        ident, (rows, tail, mix, code), mib=60, out_specs=[VMEM] * 3,
+    )
 
 
 def rms_scale(hidden, gain):
@@ -826,108 +978,50 @@
     upstream_b = cotangent[0]
     upstream = upstream_b.astype(F32)
 
-    kv_kind = [key_weight, value_weight]
-    extra = [
-        kv_kind[(s % sharers) % 2][:, (s // sharers) * HEAD_DIM : (s // sharers + 1) * HEAD_DIM]
-        for s in range(shard_count)
-    ]
-    send_w = jnp.stack(
-        [
-            jnp.concatenate([w_query[:, s * head_cols : (s + 1) * head_cols], extra[s]], axis=1)
-            for s in range(shard_count)
-        ]
-    )
-    normed = rms_scale(inputs, attn_gain)
-    normed_b = normed.astype(BF)
-    normed_all, w_mine, routes_all, router_all, upstream_z = start(
-        ctx_count, shard_count, normed_b, send_w, routes[0].T, w_router.T, upstream_b
-    )
-    normed_all = normed_all.reshape(plane, width)
-    w_mine = w_mine.reshape(width, head_cols + HEAD_DIM)
-    routes_all = jnp.swapaxes(routes_all, 2, 3)
-    router_all = jnp.swapaxes(router_all, 1, 2).reshape(width, experts)
-
-    named = jnp.sum(
-        (routes_all[..., None] == jnp.arange(experts, dtype=jnp.int32)).astype(BF), axis=3
-    )
-    earlier = (
-        jnp.arange(rows, dtype=jnp.int32)[:, None] > jnp.arange(rows, dtype=jnp.int32)[None, :]
-    ).astype(BF)
-    slots = jnp.arange(capacity, dtype=F32)
-
-    def places_in(mask):
-        rank = jnp.einsum("tu,...un->...tn", earlier, mask, preferred_element_type=F32)
-        pick = jnp.where(mask > 0, rank, -1.0)
-        return (jnp.swapaxes(pick, -1, -2)[..., None, :] == slots[:, None]).astype(BF)
-
-    my_rows = lax.dynamic_index_in_dim(named, my_shard, 1, keepdims=False)
-    my_rows = lax.dynamic_slice_in_dim(my_rows, my_ctx * shard_count, shard_count, 2)
-    pick_send = places_in(my_rows)
-    mine = lax.dynamic_slice_in_dim(named, my_ctx * shard_count + my_shard, 1, 3)
-    pick_here = places_in(mine)[:, :, 0]
-    chosen_here = jnp.einsum(
-        "cbqt,cbte->bcqe", pick_here, named, preferred_element_type=F32
-    ).reshape(-1, experts)
-
     group = 1
     while group * capacity % 16:
         group *= 2
     groups = ctx_count // group
-    by_group = jnp.swapaxes(pick_send.reshape(groups, group, shard_count, capacity, rows), 1, 2)
-    same = jnp.eye(group, dtype=BF)
-    picks = (by_group[:, :, :, :, None, :] * same[None, None, :, None, :, None]).reshape(
-        groups, shard_count * group * capacity, group * rows
-    )
-    picks_t = jnp.swapaxes(picks, 1, 2)
     slot_rows = shard_count * ctx_count * capacity
     block_shape = (shard_count, groups, group * capacity)
-
-    sent_up = jnp.einsum(
-        "nkr,nrd->nkd", picks, upstream_z.reshape(groups, group * rows, width), preferred_element_type=F32
-    ).astype(BF)
-    sent_up = jnp.swapaxes(sent_up.reshape((groups, shard_count, group * capacity, width)), 0, 1)
-    upstream_rows = exchange_shard(sent_up).reshape(slot_rows, width)
-
-    qkv = dot(normed_all, w_mine)
-    query_pre = qkv[:, :head_cols].reshape(shard_count, rows, heads, HEAD_DIM)
     row_ids = my_ctx * rows + jnp.arange(rows, dtype=jnp.int32)
     q_places = place_of(row_ids, block_order, block_rows)
     k_places = place_of(jnp.arange(sequence, dtype=jnp.int32), block_order, block_rows)
-    sees = k_places[None, :] <= q_places[:, None]
+    bias = jnp.where(k_places[None, :] <= q_places[:, None], 0.0, -1e30).astype(F32)
+    frequency = rope_base ** (-jnp.arange(HEAD_DIM // 2, dtype=F32) * 2.0 / HEAD_DIM)
+    angles = q_places.astype(F32)[:, None] * frequency[None, :]
+    cosine = jnp.concatenate([jnp.cos(angles)] * 2, axis=1)
+    sine = jnp.concatenate([-jnp.sin(angles), jnp.sin(angles)], axis=1)
+    (
+        normed_all, w_mine, router_all, code, upstream_rows, query_pre, kv_pre, queries, kv_all, attn_rows, middle,
+    ) = front(
+        ctx_count, shard_count, group, capacity, KEY_VALUE_HEADS,
+        (
+            tokens[0], attn_gain[None], w_query, key_weight, value_weight, routes[0].T, w_router.T, upstream_b,
+            cosine, sine, bias, query_gain[None], key_gain[None], w_out,
+        ),
+        0,
+    )
+    normed_all = normed_all.reshape(plane, width)
+    w_mine = w_mine.reshape(width, head_cols + HEAD_DIM)
+    upstream_rows = upstream_rows.reshape(slot_rows, width)
+    query_pre = query_pre.reshape(shard_count, rows, heads, HEAD_DIM)
+    kv_pre = kv_pre.reshape(plane, HEAD_DIM)
+    queries = queries.reshape(shard_count, rows, heads, HEAD_DIM)
+    kv_all = kv_all.reshape(2, shard_count, sequence, HEAD_DIM)
+    keys, values = kv_all[0], kv_all[1]
+    attn_rows = attn_rows.reshape(plane, head_cols)
+    is_key = lax.rem(my_shard, 2) == 0
+    part_count = sharers // 2
 
     def prep(pre, gain):
         shape = pre.shape
         flat = pre.reshape(-1, rows, shape[-2], HEAD_DIM)
         return jax.vmap(lambda v: rotate(rms_scale(v, gain), q_places))(flat).reshape(shape)
 
-    queries = prep(query_pre, query_gain).astype(BF)
-    my_place = lax.rem(my_shard, sharers)
-    is_key = lax.rem(my_place, 2) == 0
-    part_count = sharers // 2
-    kv_pre = qkv[:, head_cols:]
-    key_roped = prep(kv_pre.reshape(shard_count, rows, 1, HEAD_DIM), key_gain).reshape(plane, HEAD_DIM)
-    kv_b = jnp.where(is_key, key_roped, kv_pre).astype(BF)
-    kv_all = key_exchange(ctx_count, shard_count, kv_b.reshape(shard_count, rows, HEAD_DIM), 1)
-    kv_all = kv_all.reshape(2, shard_count, sequence, HEAD_DIM)
-    keys, values = kv_all[0], kv_all[1]
-
-    scores = (
-        jnp.einsum("sthd,spd->shtp", queries, keys, preferred_element_type=F32) * score_scale
-    )
-    scores = jnp.where(sees, scores, -1e30)
-    top = jnp.max(scores, axis=-1, keepdims=True)
-    raised = jnp.exp(scores - top)
-    total = jnp.sum(raised, axis=-1, keepdims=True)
-    probs = raised / total
-    probs_b = probs.astype(BF)
-    attn_f32 = jnp.einsum("shtp,spd->sthd", probs_b, values, preferred_element_type=F32)
-    attn_b = attn_f32.astype(BF)
-    attn_rows = attn_b.reshape(plane, head_cols)
-    middle = inputs + product_scatter(shard_count, attn_rows, w_out, False, 2)
-
     normed_two = rms_scale(middle, ffn_gain)
     second_b = normed_two.astype(BF)
-    logits = dot(second_b, router_all)
+    logits = contract_cols(second_b, router_all)
     chosen = jnp.sum(
         (routes[0][:, :, None] == jnp.arange(experts, dtype=jnp.int32)).astype(F32), axis=1
     )
@@ -940,11 +1034,21 @@
 
     gates = gates_of(logits, chosen)
 
-    received = dispatch_rows(ctx_count, shard_count, group, second_b, picks, 3).reshape(slot_rows, width)
+    tail_cols = -(-2 * experts // 128) * 128
+
+    def two_parts(value):
+        coarse = value.astype(BF).astype(F32)
+        return coarse.astype(BF), (value - coarse).astype(BF)
+
+    gates_two = jnp.concatenate(two_parts(gates), axis=1)
+    gates_two = jnp.pad(gates_two, ((0, 0), (0, tail_cols - 2 * experts)))
+    received, gate_tail = dispatch_rows(ctx_count, shard_count, group, capacity, second_b, gates_two, code, 3)
+    received = received.reshape(slot_rows, width)
     my_expert = my_ctx * shard_count + my_shard
-    slot_gates = lax.dynamic_slice_in_dim(
-        gates_of(dot(received, router_all), chosen_here), my_expert, 1, 1
-    )
+    column = jnp.arange(tail_cols, dtype=jnp.int32)[None, :]
+    mine_column = (column == my_expert) | (column == experts + my_expert)
+    gate_tail = gate_tail.reshape(slot_rows, tail_cols).astype(F32)
+    slot_gates = jnp.sum(jnp.where(mine_column, gate_tail, 0.0), axis=1, keepdims=True)
     gate_pre = dot(received, w_gate[0])
     up_pre = dot(received, w_up[0])
     activated = jax.nn.silu(gate_pre)
@@ -968,26 +1072,19 @@
     grad_w_up = contract_rows(received, grad_up_pre)
     grad_received = contract_cols(grad_gate_pre, w_gate[0]) + contract_cols(grad_up_pre, w_up[0])
 
-    tail_cols = -(-2 * experts // 128) * 128
-    coarse = slot_dot.astype(BF).astype(F32)
-    fine = slot_dot - coarse
-    column = jnp.arange(tail_cols, dtype=jnp.int32)[None, :]
-    tail = jnp.where(column == my_expert, coarse, 0.0) + jnp.where(
-        column == experts + my_expert, fine, 0.0
-    )
-    back_rows = jnp.concatenate([grad_received, tail], axis=1).astype(BF)
-    back, mixture = combine_rows(
-        ctx_count, shard_count, group, back_rows.reshape(block_shape + (width + tail_cols,)), mix_back,
-        picks_t, 4,
+    coarse, fine = two_parts(slot_dot)
+    tail = jnp.where(column == my_expert, coarse, jnp.where(column == experts + my_expert, fine, jnp.zeros((), BF)))
+    grad_second, back_tail, mixture = combine_rows(
+        ctx_count, shard_count, group, grad_received.astype(BF).reshape(block_shape + (width,)),
+        tail.reshape(block_shape + (tail_cols,)), mix_back, code, 4,
     )
     mixed = (middle + mixture).astype(BF)
-    grad_second = back[:, :width]
-    grad_gates = back[:, width : width + experts] + back[:, width + experts : width + 2 * experts]
+    grad_gates = back_tail[:, :experts] + back_tail[:, experts : 2 * experts]
     grad_logits_b = (
         gates * (grad_gates - jnp.sum(gates * grad_gates, axis=-1, keepdims=True))
     ).astype(BF)
     router_part = contract_rows(grad_logits_b, second_b).astype(BF)
-    grad_second = grad_second + contract_cols(grad_logits_b, router_all)
+    grad_second = grad_second + dot(grad_logits_b, router_all)
     unused, norm_two_back = jax.vjp(rms_scale, middle, ffn_gain)
     grad_middle_part, grad_ffn_gain = norm_two_back(grad_second)
     grad_middle = upstream + grad_middle_part
@@ -998,8 +1095,15 @@
     out_part, grad_proj_all = lax.optimization_barrier((out_part, grad_proj_all))
     grad_attn = contract_cols(grad_proj_all, w_out).astype(BF)
     grad_heads = grad_attn.reshape(shard_count, rows, heads, HEAD_DIM)
-    delta = jnp.transpose(jnp.sum(grad_heads.astype(F32) * attn_f32, axis=-1), (0, 2, 1))[..., None]
+    scores = (
+        jnp.einsum("sthd,spd->shtp", queries, keys, preferred_element_type=F32) * score_scale
+    )
+    scores = scores + bias
+    raised = jnp.exp(scores - jnp.max(scores, axis=-1, keepdims=True))
+    probs = raised / jnp.sum(raised, axis=-1, keepdims=True)
+    probs_b = probs.astype(BF)
     grad_probs = jnp.einsum("sthd,spd->shtp", grad_heads, values, preferred_element_type=F32)
+    delta = jnp.sum(probs * grad_probs, axis=-1, keepdims=True)
     grad_scores = (probs * (grad_probs - delta)).astype(BF)
     grad_query = score_scale * jnp.einsum(
         "shtp,spd->sthd", grad_scores, keys, preferred_element_type=F32

time: 800 us -> 720 us (0.900)
  local copies, waits for them, and re-layouts: 56.8 us -> 24 us
  Pallas kernels: 509 us -> 540 us
  matrix products: 124 us -> 94.7 us
  waiting for transfers between devices: 25 us -> 0.01 us
  other arithmetic: 65.6 us -> 45.5 us
    pallas_call x8 -> x6, Pallas kernels: 509 us -> 540 us  [call(): pl.pallas_call(body, out_shape=outs, in_specs=in_specs, out_specs=out_spe...]
    all_to_all x2 -> x1, waiting for transfers between devices: 25 us -> 0.01 us  [exchange_shard(): return lax.all_to_all(x, 'shard', split_axis=0, concat_axis=0, tiled=True)]
    mul x6 -> x1, local copies, waits for them, and re-layouts: 10.5 us -> 0.08 us  [shards(): grad_expert = (slot_gates * upstream_rows).astype(BF)]
    unnamed x188 -> x132, local copies, waits for them, and re-layouts: 17.3 us -> 7.86 us
    dot_general x6 -> x4, matrix products: 32.7 us -> 23.5 us  [dot(): return jnp.dot(left, right, preferred_element_type=F32)]
    sub x1 -> x0, matrix products: 8.4 us -> none  [shards(): raised = jnp.exp(scores - top)]
  transfers between devices with their start and end apart: 2 -> 1, of which waited for: 1 -> 0; matrix products, arithmetic and copies ran while one was open for 16% -> 10% of each run, Pallas kernels for 18% -> 0%
where the time goes in v4:
time: 720 us; the launch traced here: 711 us
  Pallas kernels  540 us (75%)
  matrix products  94.7 us (13%)
  other arithmetic  45.5 us (6%)
  local copies, waits for them, and re-layouts  24 us (3%)
    pallas_call x6, Pallas kernels, call(): pl.pallas_call(body, out_shape=outs, in_specs=in_specs, out_specs=out_spe...  540 us
    dot_general x5, matrix products, contract_cols(): lax.dot_general(left, right, (((1,), (1,)), ((), ())), preferred_element_...  31.7 us
    dot_general x6, matrix products, contract_rows(): lax.dot_general(left, right, (((0,), (0,)), ((), ())), preferred_element_...  27.9 us
    dot_general x4, matrix products, dot(): return jnp.dot(left, right, preferred_element_type=F32)  23.5 us
  transfers between devices with their start and end apart: 1, of which 0 were waited for; matrix products, arithmetic and copies ran while one was open for 10% of the time, Pallas kernels for 0%

profile of v4, /device:TPU:0, one launch (start us, length us, event | category | flops | bytes accessed | tf_op | source)
XLA Modules:
  0.0 711.0 jit_solution(12876393915734814601)
XLA Ops:
  4.2 146.2 %shard_map.263 = (bf16[8,128,2048]{2,1,0:T(8,128)(2,1)}, bf16[8,256,640]{2,1,0:T(8,128)(2,1)}, bf16[32,2048]{1,0:T(8,128)(2,1)}, f32[2,8,256]{2,1,0:T(8,128)}, b...) custom-call(bf16[128,2048]{1,0:T(8,128)(2,1)} %bitcast.217, ...), custom_call_target="tpu_custom_call" | custom-call | tf_op jit(solution)/shard_map/pallas_call | solution.py:112
  157.1 91.0 %shard_map.264 = (bf16[8,2,80,2048]{3,2,1,0:T(8,128)(2,1)}, bf16[8,2,80,128]{3,2,1,0:T(8,128)(2,1)}) custom-call(bf16[128,2048]{1,0:T(8,128)(2,1)} %copy-done.7, bf16[128,128]{1,0:T(8,128)(2,1)} %fusion.43.tail, f32[2,8,256]{2,1,0:T(8,128)} %get-tuple-element.43.code), custom_call_target="tpu_custom_call" | custom-call | tf_op jit(solution)/shard_map/pallas_call | solution.py:112
  249.4 7.7 %fusion.20 = f32[1280,768]{1,0:T(8,128)S(1)} fusion(bf16[1280,2048]{1,0:T(8,128)(2,1)} %bitcast.239, bf16[1,2048,768]{2,1,0:T(8,128)(2,1)} %param.29), kind=kOutput, calls=%fused_computation.39 | convolution fusion | flops 4026531840 | bytes 12320768 | tf_op jit(solution)/shard_map/dot_general | solution.py:922
  257.2 6.7 multiply_convert_fusion.3
  263.8 6.8 multiply_convert_fusion
  270.7 4.8 all-to-all-start
  277.0 2.9 reshape.398
  279.9 3.6 multiply_reduce_fusion.2
  283.5 2.9 copy.151
  286.4 5.5 fusion.2
  292.0 11.6 %multiply_convert_fusion.1 = (bf16[1280,768]{1,0:T(8,128)(2,1)}, bf16[1280,768]{1,0:T(8,128)(2,1)S(1)}) fusion(f32[1280,768]{1,0:T(8,128)} %copy-done.54, f32[1280,768]{1,0:T(8,128)} %get-tuple-element.103, bf16[1,768,2048]{2,1,0:T(8,128)(2,1)S(1)} %copy-done, bf16[1280,2048]{1,0:T(8,128)(2,1)} %bitcast.204, f32[1280]{0:T(1024)S(1)} %mul.381), kind=kOutput, calls=%fused_computation.22 | convolution fusion | flops 4047175680 | bytes 20190208 | tf_op jit(solution)/shard_map/dot_general | solution.py:930
  303.7 7.0 fusion.18
  313.9 4.7 fusion.68
  320.3 6.4 convolution_bitcast_fusion.2
  326.7 6.4 convolution_bitcast_fusion.1
  333.1 6.5 convolution_bitcast_fusion
  339.6 8.5 %add_convert_fusion = bf16[1280,2048]{1,0:T(8,128)(2,1)} fusion(f32[1280,2048]{1,0:T(8,128)} %fusion.18, bf16[1280,768]{1,0:T(8,128)(2,1)S(1)} %copy-done.57, bf16[1,2048,768]{2,1,0:T(8,128)(2,1)S(1)} %copy-done.50), kind=kOutput, calls=%fused_computation.5 | convolution fusion | flops 4031774720 | bytes 20840448 | tf_op jit(solution)/shard_map/dot_general | solution.py:930
  348.2 96.4 %shard_map.265 = (f32[128,2048]{1,0:T(8,128)}, f32[128,128]{1,0:T(8,128)}, f32[128,2048]{1,0:T(8,128)}) custom-call(bf16[8,2,80,2048]{3,2,1,0:T(8,128)(2,1)} %bitcast.202, bf16[8,2,80,128]{3,2,1,0:T(8,128)(2,1)} %select_select_fusion.tail, bf16[8,2,80,2048]{3,2,1,0:T(8,128)(2,1)} %all-to-all-done.mix, f32[2,8,256]{2,1,0:T(8,128)} %get-tuple-element.43.code), custom_call_target="tpu_custom_call" | custom-call | tf_op jit(solution)/shard_map/pallas_call | solution.py:112
  446.8 2.3 multiply_reduce_fusion.3
  450.4 28.3 %shard_map.266 = bf16[8,128,2048]{2,1,0:T(8,128)(2,1)S(1)} custom-call(bf16[128,2048]{1,0:T(8,128)(2,1)S(1)} %fusion.61.rows), custom_call_target="tpu_custom_call" | custom-call | tf_op jit(solution)/shard_map/pallas_call | solution.py:112
  478.8 3.7 bitcast_convert_fusion
  482.5 3.3 convolution_convert_fusion.3
  487.2 4.9 fusion.3
  493.8 2.0 fusion.5
  497.0 2.3 fusion.25
  499.2 2.3 bitcast_convert_fusion.2
  507.6 1.8 pad_maximum_fusion.parts
  509.4 23.3 %shard_map.267 = f32[8,128,128]{2,1,0:T(8,128)S(1)} custom-call(bf16[2,8,4,128,128]{4,3,2,1,0:T(8,128)(2,1)S(1)} %pad_maximum_fusion.parts), custom_call_target="tpu_custom_call" | custom-call | tf_op jit(solution)/shard_map/pallas_call | solution.py:112
  535.3 4.8 convolution_convert_fusion.1
  541.4 155.0 %shard_map.268 = (bf16[256,4096]{1,0:T(8,128)(2,1)}, bf16[8,256,128]{2,1,0:T(8,128)(2,1)}, bf16[8,64,2048]{2,1,0:T(8,128)(2,1)}, f32[32,256]{1,0:T(8,128)}, f32[8,2048]{1,0:T(8,128)}, /*index=5*/f32[128,2048]{1,0:T(8,128)}) custom-call(bf16[8,256,640]{2,1,0:T(8,128)(2,1)} %bitcast.213, bf16[8,64,2048]{2,1,0:T(8,128)(2,1)} %bitcast.216, ...), custom_call_target="tpu_custom_call" | custom-call | tf_op jit(solution)/shard_map/pallas_call | solution.py:112
  699.3 4.1 bitcast_convert_fusion.1
  703.4 2.5 convert_element_type.175
  (204 shorter events, 43.1 us)
Async XLA Ops:
  0.6 263.2 %copy-start = (bf16[1,768,2048]{2,1,0:T(8,128)(2,1)S(1)}, bf16[1,768,2048]{2,1,0:T(8,128)(2,1)}, u32[]{:S(2)}) copy-start(bf16[1,768,2048]{2,1,0:T(8,128)(2,1)} %param.31) | copy-start | bytes 9437188
  2.7 149.2 %copy-start.31 = (s32[1,128,8]{1,2,0:T(8,128)S(1)}, s32[1,128,8]{1,2,0:T(8,128)}, u32[]{:S(2)}) copy-start(s32[1,128,8]{1,2,0:T(8,128)} %param.19) | copy-start | bytes 12292
  2.7 149.3 %copy-start.28 = (f32[2048]{0:T(1024)S(1)}, f32[2048]{0:T(1024)}, u32[]{:S(2)}) copy-start(f32[2048]{0:T(1024)} %param.27) | copy-start | bytes 24580
  249.4 42.6 %copy-start.32 = (f32[1280]{0:T(1024)}, f32[1280]{0:T(1024)S(1)}, u32[]{:S(2)}) copy-start(f32[1280]{0:T(1024)S(1)} %mul.381) | copy-start | bytes 15364
  249.4 7.7 %copy-start.46 = (bf16[8,2,80,2048]{3,2,1,0:T(8,128)(2,1)S(1)}, bf16[8,2,80,2048]{3,2,1,0:T(8,128)(2,1)}, u32[]{:S(2)}) copy-start(bf16[8,2,80,2048]{3,2,1,0:T(8,128)(2,1)} %get-tuple-element.45) | copy-start | bytes 15728644
  249.4 7.7 %copy-start.49 = (bf16[1,2048,768]{2,1,0:T(8,128)(2,1)S(1)}, bf16[1,2048,768]{2,1,0:T(8,128)(2,1)}, u32[]{:S(2)}) copy-start(bf16[1,2048,768]{2,1,0:T(8,128)(2,1)} %param.30) | copy-start | bytes 9437188
  257.2 6.7 copy-start.54
  263.8 6.8 copy-start.52
  270.7 77.5 %all-to-all-start = ((bf16[8,2,80,2048]{3,2,1,0:T(8,128)(2,1)}), bf16[8,2,80,2048]{3,2,1,0:T(8,128)(2,1)}, u32[]{:S(2)}, u32[]{:S(2)}) async-start(bf16[8,2,80,2048]{3,2,1,0:T(8,128)(2,1)} %bitcast.201), calls=%async_computation | async-start | bytes 10485760 | tf_op jit(solution)/shard_map/all_to_all | solution.py:934
  292.0 11.7 %copy-start.48 = (bf16[1,2048,768]{2,1,0:T(8,128)(2,1)S(1)}, bf16[1,2048,768]{2,1,0:T(8,128)(2,1)}, u32[]{:S(2)}) copy-start(bf16[1,2048,768]{2,1,0:T(8,128)(2,1)} %param.29) | copy-start | bytes 9437188
  303.6 7.0 copy-start.55
  303.6 7.0 copy-start.17
  312.6 7.7 %slice-start.4 = ((s8[5242880]{0:T(1024)(128)(4,1)}), s8[4194304]{0:T(1024)(128)(4,1)S(1)}, s32[]{:S(2)}) async-start(s8[5242880]{0:T(1024)(128)(4,1)} %bitcast.241), calls=%async_computation.5 | async-start | bytes 8388608
  313.9 6.4 slice-start.5
  313.9 6.4 copy-start.56
  320.3 6.4 copy-start.57
  320.3 12.8 %slice-start.2 = ((s8[5242880]{0:T(1024)(128)(4,1)}), s8[4194304]{0:T(1024)(128)(4,1)S(1)}, s32[]{:S(2)}) async-start(s8[5242880]{0:T(1024)(128)(4,1)} %bitcast.205), calls=%async_computation.3 | async-start | bytes 8388608
  326.7 6.4 slice-start.3
  326.7 6.4 copy-start.33
  326.7 6.4 copy-start.53
  333.1 6.5 copy-start.50
  348.1 96.5 %copy-start.25 = (f32[128,32]{1,0:T(8,128)S(1)}, f32[128,32]{1,0:T(8,128)}, u32[]{:S(2)}) copy-start(f32[128,32]{1,0:T(8,128)} %get-tuple-element.78) | copy-start | bytes 49156
  348.1 98.6 %copy-start.2 = (f32[128,2048]{1,0:T(8,128)S(1)}, f32[128,2048]{1,0:T(8,128)}, u32[]{:S(2)}) copy-start(f32[128,2048]{1,0:T(8,128)} %get-tuple-element.41) | copy-start | bytes 3145732
  348.1 98.6 %copy-start.27 = (bf16[32,2048]{1,0:T(8,128)(2,1)S(1)}, bf16[32,2048]{1,0:T(8,128)(2,1)}, u32[]{:S(2)}) copy-start(bf16[32,2048]{1,0:T(8,128)(2,1)} %get-tuple-element.42) | copy-start | bytes 393220
  348.1 98.6 %copy-start.35 = (f32[128]{0:T(128)S(1)}, f32[128]{0:T(128)}, u32[]{:S(2)}) copy-start(f32[128]{0:T(128)} %copy-done.34) | copy-start | bytes 1540
  348.2 100.9 %copy-start.44 = (f32[128]{0:T(128)S(1)}, f32[128]{0:T(128)}, u32[]{:S(2)}) copy-start(f32[128]{0:T(128)} %copy-done.43) | copy-start | bytes 1540
  449.1 29.7 %copy-start.41 = (f32[128]{0:T(128)}, f32[128]{0:T(128)S(1)}, u32[]{:S(2)}) copy-start(f32[128]{0:T(128)S(1)} %multiply_multiply_fusion.1) | copy-start | bytes 1540
  450.1 28.7 %copy-start.51 = (bf16[8,128,512]{2,1,0:T(8,128)(2,1)S(1)}, bf16[8,128,512]{2,1,0:T(8,128)(2,1)}, u32[]{:S(2)}) copy-start(bf16[8,128,512]{2,1,0:T(8,128)(2,1)} %get-tuple-element.56) | copy-start | bytes 3145732
  487.2 6.6 slice-start.1
  507.6 25.4 %copy-start.10 = (f32[8,128,128]{2,1,0:T(8,128)S(1)}, f32[8,128,128]{2,1,0:T(8,128)}, u32[]{:S(2)}) copy-start(f32[8,128,128]{2,1,0:T(8,128)} %get-tuple-element.59) | copy-start | bytes 1572868
  507.6 25.4 %copy-start.37 = (f32[128]{0:T(128)S(1)}, f32[128]{0:T(128)}, u32[]{:S(2)}) copy-start(f32[128]{0:T(128)} %param.25) | copy-start | bytes 1540
  696.4 7.0 copy-start.14
  (33 other events, 94.8 us)

commit v5 on v4

--- a/solution.py
+++ b/solution.py
@@ -714,6 +714,380 @@
     )
 
 
+def back_body(n_ctx, n_shard, heads, wides,
+              grad_out, q, kv, attn, qpre, kvpre, w_out, rows_in, w_all, cosine, sine, bias, q_gain, k_gain,
+              tokens, gain, gains, router,
+              q_out, kv_out, wide_out, router_out, gains_out, rows_out,
+              grads, rows_all, attn_t, grad_heads, ds_all, p_all, parts, pre, q_sum, k_sum, wide, weights,
+              sibk, zsend, zrecv, wide_landing, pieces, landing,
+              own_part, pair, to_sib, sib, to_chip, got, router_in, router_mid, router_far,
+              gains_own, gains_in, gains_mid, gains_far, local,
+              ss_row, rs_row, ss_fwd, rs_fwd, ss_sk, rs_sk, ss_zk, rs_zk,
+              ss_wi, rs_wi, ss_wo, ss_wc, ss_w, rs_w, ss_i, rs_i, ss_o, ss_q, ss_k,
+              ss_r, rs_r, ss_g, rs_g, ss_h, rs_h, ss_t, rs_t, ss_s, rs_s, ss_c, rs_c):
+    c, s, parity, sibling, others, layers = here(n_ctx, n_shard)
+    half = n_ctx // 2
+    chips = n_shard // 2
+    chip = lax.div(s, 2)
+    mates = [lax.rem(s + 2 * d, n_shard) for d in range(1, chips)]
+    left_side = c < half
+    depth = jnp.where(left_side, c, n_ctx - 1 - c)
+    inner = jnp.where(left_side, c + 1, c - 1)
+    outer = jnp.clip(jnp.where(left_side, c - 1, c + 1), 0, n_ctx - 1)
+    middle = depth == half - 1
+    inside = depth > 0
+    count, width = tokens.shape
+    wr = w_all.shape[1]
+    cols = heads * HEAD_DIM
+    keys = n_ctx * count
+    scaling = HEAD_DIM ** -0.5
+    own_copies = [
+        pltpu.make_async_copy(grad_out, grads.at[s], local.at[0]),
+        pltpu.make_async_copy(rows_in, rows_all, local.at[1]),
+    ]
+    for item in own_copies:
+        item.start()
+    greet(others, layers)
+
+    first, forwards = {}, {}
+    for d in range(1, chips):
+        first[d] = push(grad_out, grads.at[s], ss_row.at[d], rs_row.at[d], shard=mates[d - 1])
+        first[d].start()
+    forwards[0] = push(grad_out, grads.at[s], ss_fwd.at[0], rs_fwd.at[0], shard=sibling)
+    forwards[0].start()
+    small = []
+    for i, peer in enumerate(others):
+        item = push(router.at[peer], router_in.at[i], ss_r.at[i], rs_r.at[i], shard=peer)
+        item.start()
+        small.append(item)
+    q_sum[...] = jnp.zeros_like(q_sum)
+    k_sum[...] = jnp.zeros_like(k_sum)
+
+    def norm_back(grad, value, norm_gain, total):
+        unit, scale = unit_rows(value)
+        grad = grad * cosine[...] + pltpu.roll(grad * sine[...], HEAD_DIM // 2, 1)
+        total[...] += jnp.sum(grad * unit, axis=0, keepdims=True)
+        scaled = grad * norm_gain[...]
+        return scale * (scaled - unit * jnp.mean(scaled * unit, axis=-1, keepdims=True))
+
+    near, far = {}, {}
+
+    def seqs_of(d):
+        return 2 * lax.rem(chip + chips - d, chips)
+
+    def attention_back(d):
+        fs = seqs_of(d)
+        grad = lax.dot_general(grads[pl.ds(fs, 2)].reshape(2 * count, width), w_out[...],
+                               (((1,), (1,)), ((), ())), preferred_element_type=F32)
+        grad_heads[...] = grad.reshape(2, count, cols).astype(BF)
+
+        @pl.loop(0, 2)
+        def _(i):
+            b = fs + i
+            k_all = kv[0, b].reshape(keys, HEAD_DIM)
+            v_all = kv[1, b].reshape(keys, HEAD_DIM)
+            for h in range(heads):
+                hs = slice(h * HEAD_DIM, (h + 1) * HEAD_DIM)
+                rs = slice(h * count, (h + 1) * count)
+                scores = lax.dot_general(q[b, :, hs], k_all, (((1,), (1,)), ((), ())), preferred_element_type=F32)
+                scores = scores * scaling + bias[...]
+                raised = jnp.exp(scores - jnp.max(scores, axis=-1, keepdims=True))
+                probs = raised / jnp.sum(raised, axis=-1, keepdims=True)
+                grad_p = lax.dot_general(grad_heads[i, :, hs], v_all, (((1,), (1,)), ((), ())),
+                                         preferred_element_type=F32)
+                delta = jnp.sum(probs * grad_p, axis=-1, keepdims=True)
+                ds = (probs * (grad_p - delta)).astype(BF)
+                ds_all[rs, :] = ds
+                p_all[rs, :] = probs.astype(BF)
+                grad_q = jnp.dot(ds, k_all, preferred_element_type=F32) * scaling
+                pre[b, :, hs] = norm_back(grad_q, qpre[b, :, hs], q_gain, q_sum).astype(BF)
+            grad_k, grad_v = jnp.zeros((keys, HEAD_DIM), F32), jnp.zeros((keys, HEAD_DIM), F32)
+            stacked_q = jnp.concatenate([q[b, :, h * HEAD_DIM : (h + 1) * HEAD_DIM] for h in range(heads)], axis=0)
+            stacked_g = jnp.concatenate(
+                [grad_heads[i, :, h * HEAD_DIM : (h + 1) * HEAD_DIM] for h in range(heads)], axis=0
+            )
+            grad_k = lax.dot_general(ds_all[...], stacked_q, (((0,), (0,)), ((), ())), preferred_element_type=F32)
+            grad_v = lax.dot_general(p_all[...], stacked_g, (((0,), (0,)), ((), ())), preferred_element_type=F32)
+            parts[0, b] = (grad_k * scaling).astype(BF).reshape(n_ctx, count, HEAD_DIM)
+            parts[1, b] = grad_v.astype(BF).reshape(n_ctx, count, HEAD_DIM)
+
+        near[d] = push(parts.at[1 - parity, pl.ds(fs, 2)], sibk.at[d], ss_sk.at[d], rs_sk.at[d], shard=sibling)
+        near[d].start()
+
+    def key_sum(d):
+        fs = seqs_of(d)
+        near[d].wait()
+        for i, layer in enumerate(layers):
+            zsend[d, i] = (
+                parts[parity, pl.ds(fs, 2), layer].astype(F32) + sibk[d, :, layer].astype(F32)
+            ).astype(BF)
+            far[d, i] = push(zsend.at[d, i], zrecv.at[d, i], ss_zk.at[d, i], rs_zk.at[d, i], ctx=layer)
+            far[d, i].start()
+
+    for d in range(chips):
+        if d:
+            first[d].wait()
+            origin = lax.rem(s + n_shard - 2 * d, n_shard)
+            forwards[d] = push(grads.at[origin], grads.at[origin], ss_fwd.at[d], rs_fwd.at[d], shard=sibling)
+            forwards[d].start()
+        else:
+            own_copies[0].wait()
+        forwards[d].wait()
+        attention_back(d)
+        if d:
+            key_sum(d - 1)
+    key_sum(chips - 1)
+
+    def out_copies(j, ref):
+        source = lax.rem(s + n_shard - j, n_shard)
+        to = pl.ds(pl.multiple_of(source * cols, cols), cols)
+        return (
+            pltpu.make_async_copy(ref.at[:, pl.ds(0, cols)], q_out.at[:, to], ss_q.at[j]),
+            pltpu.make_async_copy(ref.at[:, pl.ds(cols, HEAD_DIM)], kv_out.at[source], ss_k.at[j]),
+        )
+
+    def wide_copies(j, ref):
+        step = wide.shape[2]
+        return (pltpu.make_async_copy(ref, wide_out.at[:, pl.ds(j * step, step)], ss_wc.at[j]),)
+
+    class Line:
+        def __init__(self, ready, own, landing, ss_i, rs_i, ss_o, copies):
+            self.ready, self.own, self.landing = ready, own, landing
+            self.ss_i, self.rs_i, self.ss_o, self.copies = ss_i, rs_i, ss_o, copies
+
+        def inward(self, j, ref):
+            at = jnp.where(middle, 1, 0)
+            return push(ref, self.landing.at[at, j], self.ss_i.at[j], self.rs_i.at[at, j], ctx=inner)
+
+        def outward(self, j):
+            return push(self.landing.at[1, j], self.landing.at[1, j], self.ss_o.at[j], self.rs_i.at[1, j], ctx=outer)
+
+        def arrived(self, which, j):
+            push(self.landing.at[0, j], self.landing.at[which, j], self.ss_i.at[j], self.rs_i.at[which, j],
+                 ctx=inner).wait_recv()
+
+        def outermost(self, j):
+            @pl.when(jnp.logical_not(inside))
+            def _():
+                self.ready(j)
+                self.inward(j, self.own(j)).start()
+
+        def first_half(self, j):
+            @pl.when(inside)
+            def _():
+                self.ready(j)
+                self.arrived(0, j)
+                self.landing[0, j] = (self.own(j)[...].astype(F32) + self.landing[0, j].astype(F32)).astype(BF)
+                self.inward(j, self.landing.at[0, j]).start()
+
+        def second_half(self, j):
+            self.arrived(1, j)
+
+            @pl.when(middle)
+            def _():
+                self.landing[1, j] = (self.landing[0, j].astype(F32) + self.landing[1, j].astype(F32)).astype(BF)
+
+            @pl.when(inside)
+            def _():
+                self.outward(j).start()
+
+            for item in self.copies(j, self.landing.at[1, j]):
+                item.start()
+
+        def drain(self, j):
+            self.inward(j, self.landing.at[0, j]).wait_send()
+
+            @pl.when(inside)
+            def _():
+                self.outward(j).wait_send()
+
+            for item in self.copies(j, self.landing.at[1, j]):
+                item.wait()
+
+    sends = [None]
+    line = Line(lambda j: sends[j].wait() if j else None, lambda j: pieces.at[j] if j else weights.at[s],
+                landing, ss_i, rs_i, ss_o, out_copies)
+    wide_line = Line(lambda j: None, lambda j: wide.at[j], wide_landing, ss_wi, rs_wi, ss_wo, wide_copies)
+    steps = [(wide_line, j) for j in range(wides)] + [(line, j) for j in range(n_shard)]
+    lag, ahead = 2, 6
+
+    attn_t[...] = attn[...].reshape(n_shard * count, cols).T
+    step = width // wides
+    for j in range(wides):
+        block = grads[:, :, j * step : (j + 1) * step].reshape(n_shard * count, step)
+        wide[j] = jnp.dot(attn_t[...], block, preferred_element_type=F32).astype(BF)
+        if j < ahead:
+            wide_line.outermost(j)
+
+    own_copies[1].wait()
+
+    @pl.loop(0, n_shard)
+    def _(e):
+        block = rows_all[:, :, pl.ds(pl.multiple_of(e * wr, wr), wr)].reshape(n_shard * count, wr)
+        right = pre[:, :, pl.ds(0, cols)].reshape(n_shard * count, cols)
+        weights[e, :, pl.ds(0, cols)] = lax.dot_general(
+            block, right, (((0,), (0,)), ((), ())), preferred_element_type=F32).astype(BF)
+
+    wide_line.first_half(0)
+    for d in range(chips):
+        fs = seqs_of(d)
+        total = parts[parity, pl.ds(fs, 2), c].astype(F32) + sibk[d, :, c].astype(F32)
+        for i in range(n_ctx - 1):
+            far[d, i].wait()
+            total = total + zrecv[d, i].astype(F32)
+        for i in range(2):
+            keyed = norm_back(total[i], kvpre[fs + i], k_gain, k_sum)
+            pre[fs + i, :, pl.ds(cols, HEAD_DIM)] = jnp.where(parity == 0, keyed, total[i]).astype(BF)
+
+    @pl.loop(0, n_shard)
+    def _(e):
+        block = rows_all[:, :, pl.ds(pl.multiple_of(e * wr, wr), wr)].reshape(n_shard * count, wr)
+        right = pre[:, :, pl.ds(cols, HEAD_DIM)].reshape(n_shard * count, HEAD_DIM)
+        weights[e, :, pl.ds(cols, HEAD_DIM)] = lax.dot_general(
+            block, right, (((0,), (0,)), ((), ())), preferred_element_type=F32).astype(BF)
+
+    for i, peer in enumerate(others):
+        item = push(weights.at[peer], pieces.at[i + 1], ss_w.at[i], rs_w.at[i], shard=peer)
+        item.start()
+        sends.append(item)
+
+    order = list(range(1, chips)) + [0]
+    to_sibling, to_mate = {}, {}
+
+    def product(at):
+        fs = 2 * lax.rem(chip + order[at], chips)
+        left = pre[pl.ds(fs, 2)].reshape(2 * count, cols + HEAD_DIM)
+
+        @pl.loop(0, n_shard)
+        def _(j):
+            part = pl.ds(pl.multiple_of(j * wr, wr), wr)
+            value = lax.dot_general(left, w_all[j], (((1,), (1,)), ((), ())), preferred_element_type=F32)
+            pair[...] = value.reshape(2, count, wr)
+            own_part[at % 2, :, part] = pair[parity]
+            to_sib[at, :, part] = pair[1 - parity].astype(BF)
+
+        to_sibling[at] = push(to_sib.at[at], sib.at[at], ss_s.at[at], rs_s.at[at], shard=sibling)
+        to_sibling[at].start()
+
+    def chip_sum(at):
+        to_sibling[at].wait()
+        to_chip[at] = (own_part[at % 2] + sib[at].astype(F32)).astype(BF)
+        to_mate[at] = push(to_chip.at[at], got.at[at], ss_c.at[at], rs_c.at[at], shard=mates[order[at] - 1])
+        to_mate[at].start()
+
+    gain_sends = []
+
+    def last_sum():
+        to_sibling[chips - 1].wait()
+        grad = own_part[(chips - 1) % 2] + sib[chips - 1].astype(F32)
+        for at in range(chips - 1):
+            to_mate[at].wait()
+            grad = grad + got[at].astype(F32)
+        unit, scale = unit_rows(tokens[...].astype(F32))
+        scaled = grad * gain[...]
+        rows_out[...] = scale * (scaled - unit * jnp.mean(scaled * unit, axis=-1, keepdims=True))
+        gains_own[...] = gains[...]
+        gains_own[0:1] = jnp.sum(grad * unit, axis=0, keepdims=True)
+        gains_own[2:3, 0:HEAD_DIM] = q_sum[...]
+        gains_own[2:3, HEAD_DIM : 2 * HEAD_DIM] = jnp.where(parity == 0, k_sum[...], jnp.zeros_like(k_sum))
+        mine = pltpu.make_async_copy(gains_own, gains_in.at[s], local.at[2])
+        mine.start()
+        gain_sends.append(mine)
+        for i, peer in enumerate(others):
+            item = push(gains_own, gains_in.at[s], ss_g.at[i], rs_g.at[i], shard=peer)
+            item.start()
+            gain_sends.append(item)
+
+    def small_plane():
+        for item in small + gain_sends:
+            item.wait()
+        gains_mid[...] = gains_in[0]
+        for i in range(1, n_shard):
+            gains_mid[...] += gains_in[i]
+        router_mid[...] = router[s].astype(F32)
+        for i in range(n_shard - 1):
+            router_mid[...] += router_in[i].astype(F32)
+        for i, layer in enumerate(layers):
+            push(gains_mid, gains_far.at[c], ss_h.at[i], rs_h.at[i], ctx=layer).start()
+            push(router_mid, router_far.at[c], ss_t.at[i], rs_t.at[i], ctx=layer).start()
+        pltpu.make_async_copy(gains_mid, gains_far.at[c], local.at[3]).start()
+        pltpu.make_async_copy(router_mid, router_far.at[c], local.at[4]).start()
+
+    def small_all():
+        pltpu.make_async_copy(gains_mid, gains_far.at[c], local.at[3]).wait()
+        pltpu.make_async_copy(router_mid, router_far.at[c], local.at[4]).wait()
+        for i, layer in enumerate(layers):
+            push(gains_mid, gains_far.at[c], ss_h.at[i], rs_h.at[i], ctx=layer).wait()
+            push(router_mid, router_far.at[c], ss_t.at[i], rs_t.at[i], ctx=layer).wait()
+        gains_out[...] = gains_far[0]
+        router_out[...] = router_far[0]
+        for i in range(1, n_ctx):
+            gains_out[...] += gains_far[i]
+            router_out[...] += router_far[i]
+
+    side = []
+    for at in range(chips):
+        side.append(functools.partial(product, at))
+        if at:
+            side.append(functools.partial(chip_sum, at - 1))
+    side += [last_sum, small_plane]
+    for n in range(1, len(steps) + lag):
+        if n + ahead - 1 < len(steps):
+            steps[n + ahead - 1][0].outermost(steps[n + ahead - 1][1])
+        if n < len(steps):
+            steps[n][0].first_half(steps[n][1])
+        if n >= lag:
+            steps[n - lag][0].second_half(steps[n - lag][1])
+        if side:
+            side.pop(0)()
+    for job in side:
+        job()
+    small_all()
+    for which, j in steps:
+        which.drain(j)
+
+
+def back(n_ctx, n_shard, heads, args, ident):
+    count, width = args[0].shape
+    rows_in, w_all, router, gains = args[7], args[8], args[17], args[16]
+    n, z, chips, wides = n_shard, n_ctx, n_shard // 2, 8
+    wr, cols = w_all.shape[1], heads * HEAD_DIM
+    keys = z * count
+    sds, scratch = jax.ShapeDtypeStruct, pltpu.VMEM
+    router_shape = router.shape[1:]
+    dma = lambda *shape: DMA(shape)
+    wide_block, block = (cols, width // wides), (wr, cols + HEAD_DIM)
+    return call(
+        functools.partial(back_body, z, n, heads, wides),
+        [
+            sds((wr, n * cols), BF), sds((n, wr, HEAD_DIM), BF), sds((cols, width), BF), sds(router_shape, F32),
+            sds(gains.shape, F32), sds((count, width), F32),
+        ],
+        [VMEM] * 7 + [ANY] + [VMEM] * 10,
+        [
+            scratch((n, count, width), BF), scratch((n, count, width), BF), scratch((cols, n * count), BF),
+            scratch((2, count, cols), BF), scratch((heads * count, keys), BF), scratch((heads * count, keys), BF),
+            scratch((2, n, z, count, HEAD_DIM), BF), scratch((n, count, cols + HEAD_DIM), BF),
+            scratch((1, HEAD_DIM), F32), scratch((1, HEAD_DIM), F32),
+            scratch((wides,) + wide_block, BF), scratch((n,) + block, BF),
+            scratch((chips, 2, z, count, HEAD_DIM), BF), scratch((chips, z - 1, 2, count, HEAD_DIM), BF),
+            scratch((chips, z - 1, 2, count, HEAD_DIM), BF), scratch((2, wides) + wide_block, BF),
+            scratch((n,) + block, BF), scratch((2, n) + block, BF),
+            scratch((2, count, width), F32), scratch((2, count, wr), F32), scratch((chips, count, width), BF),
+            scratch((chips, count, width), BF), scratch((chips - 1, count, width), BF),
+            scratch((chips - 1, count, width), BF),
+            scratch((n - 1,) + router_shape, BF), scratch(router_shape, F32), scratch((z,) + router_shape, F32),
+            scratch(gains.shape, F32), scratch((n,) + gains.shape, F32), scratch(gains.shape, F32),
+            scratch((z,) + gains.shape, F32), dma(5),
+            dma(chips), dma(chips), dma(chips), dma(chips), dma(chips), dma(chips), dma(chips, z - 1), dma(chips, z - 1),
+            dma(wides), dma(2, wides), dma(wides), dma(wides), dma(n - 1), dma(n - 1), dma(n), dma(2, n), dma(n), dma(n),
+            dma(n), dma(n - 1), dma(n - 1), dma(n - 1), dma(n - 1), dma(z - 1), dma(z - 1), dma(z - 1), dma(z - 1),
+            dma(chips), dma(chips), dma(chips - 1), dma(chips - 1),
+        ],
+        ident, args, mib=62, out_specs=[ANY, ANY, ANY, VMEM, VMEM, VMEM],
+    )
+
+
 def dispatch_body(n_ctx, n_shard, group, tile, rows, tail, code, recv, tail_recv,
                   zrows, ztail, ready, tail_ready, local, ss_z, rs_z, ss_t, rs_t, ss_x, rs_x, ss_y, rs_y):
     c, s, parity, sibling, others, layers = here(n_ctx, n_shard)
@@ -1002,15 +1376,7 @@
         ),
         0,
     )
-    normed_all = normed_all.reshape(plane, width)
-    w_mine = w_mine.reshape(width, head_cols + HEAD_DIM)
     upstream_rows = upstream_rows.reshape(slot_rows, width)
-    query_pre = query_pre.reshape(shard_count, rows, heads, HEAD_DIM)
-    kv_pre = kv_pre.reshape(plane, HEAD_DIM)
-    queries = queries.reshape(shard_count, rows, heads, HEAD_DIM)
-    kv_all = kv_all.reshape(2, shard_count, sequence, HEAD_DIM)
-    keys, values = kv_all[0], kv_all[1]
-    attn_rows = attn_rows.reshape(plane, head_cols)
     is_key = lax.rem(my_shard, 2) == 0
     part_count = sharers // 2
 
@@ -1090,60 +1456,79 @@
     grad_middle = upstream + grad_middle_part
     grad_proj_b = grad_middle.astype(BF)
 
-    grad_proj_all = spread(shard_count, grad_proj_b, 5).reshape(plane, width)
-    out_part = contract_rows(attn_rows, grad_proj_all).astype(BF)
-    out_part, grad_proj_all = lax.optimization_barrier((out_part, grad_proj_all))
-    grad_attn = contract_cols(grad_proj_all, w_out).astype(BF)
-    grad_heads = grad_attn.reshape(shard_count, rows, heads, HEAD_DIM)
-    scores = (
-        jnp.einsum("sthd,spd->shtp", queries, keys, preferred_element_type=F32) * score_scale
-    )
-    scores = scores + bias
-    raised = jnp.exp(scores - jnp.max(scores, axis=-1, keepdims=True))
-    probs = raised / jnp.sum(raised, axis=-1, keepdims=True)
-    probs_b = probs.astype(BF)
-    grad_probs = jnp.einsum("sthd,spd->shtp", grad_heads, values, preferred_element_type=F32)
-    delta = jnp.sum(probs * grad_probs, axis=-1, keepdims=True)
-    grad_scores = (probs * (grad_probs - delta)).astype(BF)
-    grad_query = score_scale * jnp.einsum(
-        "shtp,spd->sthd", grad_scores, keys, preferred_element_type=F32
-    )
-    grad_keys = score_scale * jnp.einsum(
-        "shtp,sthd->spd", grad_scores, queries, preferred_element_type=F32
-    )
-    grad_values = jnp.einsum("shtp,sthd->spd", probs_b, grad_heads, preferred_element_type=F32)
-    grad_kv = jnp.stack([grad_keys, grad_values]).astype(BF)
-    grad_kv = key_back(
-        ctx_count, shard_count, grad_kv.reshape(2, shard_count, ctx_count, rows, HEAD_DIM), 6
-    )
-    unused, query_back = jax.vjp(prep, query_pre, query_gain)
-    grad_query_pre, grad_query_gain = query_back(grad_query)
-    kv_shape = (shard_count, rows, 1, HEAD_DIM)
-    unused, key_prep_back = jax.vjp(prep, kv_pre.reshape(kv_shape), key_gain)
-    grad_key_pre, grad_key_gain = key_prep_back(grad_kv.reshape(kv_shape))
-    grad_key_gain = jnp.where(is_key, grad_key_gain, 0.0)
-    grad_kv_full = jnp.where(
-        is_key, grad_key_pre.reshape(plane, HEAD_DIM), grad_kv.reshape(plane, HEAD_DIM)
-    ).astype(BF)
-    grad_pre = jnp.concatenate(
-        [grad_query_pre.reshape(plane, head_cols).astype(BF), grad_kv_full], axis=1
-    )
-    gains = jnp.concatenate(
-        [
-            jnp.zeros((1, width), F32),
-            grad_ffn_gain[None],
-            jnp.pad(
-                jnp.concatenate([grad_query_gain, grad_key_gain])[None],
-                ((0, 6 - 1), (0, width - 2 * HEAD_DIM)),
+    router_parts = jnp.swapaxes(router_part.reshape(experts, shard_count, wrows), 0, 1)
+    if plane * width <= 2**21:
+        gains = jnp.concatenate([jnp.zeros((1, width), F32), grad_ffn_gain[None], jnp.zeros((6, width), F32)])
+        q_sum, kv_sum, out_sum, router_sum, gains, grad_input_part = back(
+            ctx_count, shard_count, heads,
+            (
+                grad_proj_b, queries, kv_all, attn_rows, query_pre, kv_pre, w_out, normed_all, w_mine,
+                cosine, sine, bias, query_gain[None], key_gain[None], tokens[0], attn_gain[None], gains, router_parts,
             ),
-        ]
-    )
-    grad_w = contract_rows(normed_all, grad_pre).astype(BF).reshape(shard_count, wrows, -1)
-    router_parts = jnp.swapaxes(router_part.reshape(experts, shard_count, wrows), 0, 1)
-    q_sum, kv_sum, out_sum, router_sum, gains, grad_input_part = finish(
-        ctx_count, shard_count, head_cols, grad_w, out_part.reshape(8, -1, width), router_parts, gains, grad_pre, w_mine,
-        tokens[0], attn_gain[None], 8,
-    )
+            5,
+        )
+    else:
+        normed_all = normed_all.reshape(plane, width)
+        w_mine = w_mine.reshape(width, head_cols + HEAD_DIM)
+        query_pre = query_pre.reshape(shard_count, rows, heads, HEAD_DIM)
+        kv_pre = kv_pre.reshape(plane, HEAD_DIM)
+        queries = queries.reshape(shard_count, rows, heads, HEAD_DIM)
+        kv_all = kv_all.reshape(2, shard_count, sequence, HEAD_DIM)
+        keys, values = kv_all[0], kv_all[1]
+        attn_rows = attn_rows.reshape(plane, head_cols)
+        grad_proj_all = spread(shard_count, grad_proj_b, 5).reshape(plane, width)
+        out_part = contract_rows(attn_rows, grad_proj_all).astype(BF)
+        out_part, grad_proj_all = lax.optimization_barrier((out_part, grad_proj_all))
+        grad_attn = contract_cols(grad_proj_all, w_out).astype(BF)
+        grad_heads = grad_attn.reshape(shard_count, rows, heads, HEAD_DIM)
+        scores = (
+            jnp.einsum("sthd,spd->shtp", queries, keys, preferred_element_type=F32) * score_scale
+        )
+        scores = scores + bias
+        raised = jnp.exp(scores - jnp.max(scores, axis=-1, keepdims=True))
+        probs = raised / jnp.sum(raised, axis=-1, keepdims=True)
+        probs_b = probs.astype(BF)
+        grad_probs = jnp.einsum("sthd,spd->shtp", grad_heads, values, preferred_element_type=F32)
+        delta = jnp.sum(probs * grad_probs, axis=-1, keepdims=True)
+        grad_scores = (probs * (grad_probs - delta)).astype(BF)
+        grad_query = score_scale * jnp.einsum(
+            "shtp,spd->sthd", grad_scores, keys, preferred_element_type=F32
+        )
+        grad_keys = score_scale * jnp.einsum(
+            "shtp,sthd->spd", grad_scores, queries, preferred_element_type=F32
+        )
+        grad_values = jnp.einsum("shtp,sthd->spd", probs_b, grad_heads, preferred_element_type=F32)
+        grad_kv = jnp.stack([grad_keys, grad_values]).astype(BF)
+        grad_kv = key_back(
+            ctx_count, shard_count, grad_kv.reshape(2, shard_count, ctx_count, rows, HEAD_DIM), 6
+        )
+        unused, query_back = jax.vjp(prep, query_pre, query_gain)
+        grad_query_pre, grad_query_gain = query_back(grad_query)
+        kv_shape = (shard_count, rows, 1, HEAD_DIM)
+        unused, key_prep_back = jax.vjp(prep, kv_pre.reshape(kv_shape), key_gain)
+        grad_key_pre, grad_key_gain = key_prep_back(grad_kv.reshape(kv_shape))
+        grad_key_gain = jnp.where(is_key, grad_key_gain, 0.0)
+        grad_kv_full = jnp.where(
+            is_key, grad_key_pre.reshape(plane, HEAD_DIM), grad_kv.reshape(plane, HEAD_DIM)
+        ).astype(BF)
+        grad_pre = jnp.concatenate(
+            [grad_query_pre.reshape(plane, head_cols).astype(BF), grad_kv_full], axis=1
+        )
+        gains = jnp.concatenate(
+            [
+                jnp.zeros((1, width), F32),
+                grad_ffn_gain[None],
+                jnp.pad(
+                    jnp.concatenate([grad_query_gain, grad_key_gain])[None],
+                    ((0, 6 - 1), (0, width - 2 * HEAD_DIM)),
+                ),
+            ]
+        )
+        grad_w = contract_rows(normed_all, grad_pre).astype(BF).reshape(shard_count, wrows, -1)
+        q_sum, kv_sum, out_sum, router_sum, gains, grad_input_part = finish(
+            ctx_count, shard_count, head_cols, grad_w, out_part.reshape(8, -1, width), router_parts, gains, grad_pre, w_mine,
+            tokens[0], attn_gain[None], 8,
+        )
     grad_tokens = grad_middle + grad_input_part
     grad_attn_gain, grad_ffn_gain = gains[0], gains[1]
     grad_query_gain, grad_key_gain = gains[2, :HEAD_DIM], gains[2, HEAD_DIM : 2 * HEAD_DIM]

time: 720 us -> 663 us (0.921)
  other arithmetic: 45.5 us -> 23.6 us
  local copies, waits for them, and re-layouts: 24 us -> 7.47 us
  Pallas kernels: 540 us -> 527 us
    pallas_call x6 -> x4, Pallas kernels: 540 us -> 527 us  [call(): pl.pallas_call(body, out_shape=outs, in_specs=in_specs, out_specs=out_spe...]
    dot_general x5 -> x0, matrix products: 11.5 us -> none  [the longest x1 4.93 us: shards(): jnp.einsum('sthd,spd->shtp', grad_heads, values, preferred_element_type=F32)]
    dot_general x6 -> x4, matrix products: 27.9 us -> 32.7 us  [contract_rows(): lax.dot_general(left, right, (((0,), (0,)), ((), ())), preferred_element_...]
    dot_general x5 -> x4, matrix products: 31.7 us -> 34.1 us  [contract_cols(): lax.dot_general(left, right, (((1,), (1,)), ((), ())), preferred_element_...]
where the time goes in v5:
time: 663 us; the launch traced here: 654 us
  Pallas kernels  527 us (79%)
  matrix products  89.5 us (13%)
  other arithmetic  23.6 us (4%)
  local copies, waits for them, and re-layouts  7.47 us (1%)
    pallas_call x4, Pallas kernels, call(): pl.pallas_call(body, out_shape=outs, in_specs=in_specs, out_specs=out_spe...  527 us
    dot_general x4, matrix products, contract_cols(): lax.dot_general(left, right, (((1,), (1,)), ((), ())), preferred_element_...  34.1 us
    dot_general x4, matrix products, contract_rows(): lax.dot_general(left, right, (((0,), (0,)), ((), ())), preferred_element_...  32.7 us
    dot_general x4, matrix products, dot(): return jnp.dot(left, right, preferred_element_type=F32)  22.8 us
  transfers between devices with their start and end apart: 1, of which 0 were waited for; matrix products, arithmetic and copies ran while one was open for 10% of the time, Pallas kernels for 0%

profile of v5, /device:TPU:0, one launch (start us, length us, event | category | flops | bytes accessed | tf_op | source)
XLA Modules:
  0.0 654.1 jit_solution(3494978205785730839)
XLA Ops:
  4.9 146.3 %shard_map.263 = (bf16[8,128,2048]{2,1,0:T(8,128)(2,1)}, bf16[8,256,640]{2,1,0:T(8,128)(2,1)}, bf16[32,2048]{1,0:T(8,128)(2,1)}, f32[2,8,256]{2,1,0:T(8,128)}, b...) custom-call(bf16[128,2048]{1,0:T(8,128)(2,1)} %bitcast.105, ...), custom_call_target="tpu_custom_call" | custom-call | tf_op jit(solution)/shard_map/pallas_call | solution.py:112
  151.2 1.4 multiply_reduce_fusion.2
  152.6 1.4 multiply_convert_fusion.4.rows
  154.0 1.4 fusion.38
  156.4 90.9 %shard_map.264 = (bf16[8,2,80,2048]{3,2,1,0:T(8,128)(2,1)}, bf16[8,2,80,128]{3,2,1,0:T(8,128)(2,1)}) custom-call(bf16[128,2048]{1,0:T(8,128)(2,1)} %copy-done.3, bf16[128,128]{1,0:T(8,128)(2,1)} %fusion.19.tail, f32[2,8,256]{2,1,0:T(8,128)} %get-tuple-element.41.code), custom_call_target="tpu_custom_call" | custom-call | tf_op jit(solution)/shard_map/pallas_call | solution.py:112
  247.4 1.2 select_reduce_fusion
  248.7 7.5 %fusion.11 = f32[1280,768]{1,0:T(8,128)S(1)} fusion(bf16[1280,2048]{1,0:T(8,128)(2,1)} %bitcast.127, bf16[1,2048,768]{2,1,0:T(8,128)(2,1)} %param.29), kind=kOutput, calls=%fused_computation.23 | convolution fusion | flops 4026531840 | bytes 12320768 | tf_op jit(solution)/shard_map/dot_general | solution.py:1296
  256.2 6.7 %multiply_convert_fusion.3 = (bf16[1280,768]{1,0:T(8,128)(2,1)S(1)}, f32[1280,768]{1,0:T(8,128)}) fusion(f32[1280,768]{1,0:T(8,128)S(1)} %fusion.11, bf16[1280,2048]{1,0:T(8,128)(2,1)S(1)} %bitcast.130, bf16[1,2048,768]{2,1,0:T(8,128)(2,1)S(1)} %copy-done.16), kind=kOutput, calls=%fused_computation.9 | convolution fusion | flops 4032430080 | bytes 18219008 | tf_op jit(solution)/shard_map/dot_general | solution.py:1296
  262.9 6.9 %multiply_convert_fusion = (bf16[1280,2048]{1,0:T(8,128)(2,1)}, bf16[1280,2048]{1,0:T(8,128)(2,1)}) fusion(f32[1280]{0:T(1024)S(1)} %mul.165, bf16[1280,768]{1,0:T(8,128)(2,1)S(1)} %get-tuple-element.88, bf16[1,768,2048]{2,1,0:T(8,128)(2,1)S(1)} %copy-done.15), kind=kOutput, calls=%fused_computation.5 | convolution fusion | flops 4037017600 | bytes 15602688 | tf_op jit(solution)/shard_map/dot_general | solution.py:1296
  269.8 4.8 all-to-all-start
  274.7 13.2 %multiply_convert_fusion.1 = (bf16[1280,768]{1,0:T(8,128)(2,1)}, bf16[1280,768]{1,0:T(8,128)(2,1)}) fusion(f32[1280,768]{1,0:T(8,128)} %copy-done.20, f32[1280,768]{1,0:T(8,128)} %get-tuple-element.89, bf16[1,768,2048]{2,1,0:T(8,128)(2,1)} %param.31, bf16[1280,2048]{1,0:T(8,128)(2,1)} %bitcast.97, f32[1280]{0:T(1024)S(1)} %mul.165), kind=kOutput, calls=%fused_computation.7 | convolution fusion | flops 4047175680 | bytes 20190208 | tf_op jit(solution)/shard_map/dot_general | solution.py:1304
  287.9 1.5 fusion.1
  289.5 10.9 %fusion.9 = f32[1280,2048]{1,0:T(8,128)} fusion(bf16[1280,768]{1,0:T(8,128)(2,1)} %get-tuple-element.74, bf16[1,2048,768]{2,1,0:T(8,128)(2,1)} %param.29), kind=kOutput, calls=%fused_computation.21 | convolution fusion | flops 4026531840 | bytes 15597568 | tf_op jit(solution)/shard_map/dot_general | solution.py:1304
  300.4 1.1 select_select_fusion.tail
  301.5 8.8 %convolution_bitcast_fusion.2 = f32[1,2048,768]{2,1,0:T(8,128)} fusion(bf16[1280,2048]{1,0:T(8,128)(2,1)} %bitcast.128, bf16[1280,768]{1,0:T(8,128)(2,1)S(1)} %copy-done.21), kind=kOutput, calls=%fused_computation.14 | convolution fusion | flops 4026531840 | bytes 13500416 | tf_op jit(solution)/shard_map/dot_general | solution.py:1300
  310.3 17.3 %convolution_bitcast_fusion.1 = f32[1,2048,768]{2,1,0:T(8,128)} fusion(bf16[1280,2048]{1,0:T(8,128)(2,1)} %bitcast.129, bf16[1280,768]{1,0:T(8,128)(2,1)S(1)} %copy-done.22), kind=kOutput, calls=%fused_computation.13 | convolution fusion | flops 4026531840 | bytes 13500416 | tf_op jit(solution)/shard_map/dot_general | solution.py:1300
  327.6 6.5 convolution_bitcast_fusion
  334.1 8.6 %add_convert_fusion = bf16[1280,2048]{1,0:T(8,128)(2,1)} fusion(f32[1280,2048]{1,0:T(8,128)} %fusion.9, bf16[1280,768]{1,0:T(8,128)(2,1)S(1)} %copy-done.22, bf16[1,2048,768]{2,1,0:T(8,128)(2,1)S(1)} %copy-done.17), kind=kOutput, calls=%fused_computation.4 | convolution fusion | flops 4031774720 | bytes 20840448 | tf_op jit(solution)/shard_map/dot_general | solution.py:1304
  342.7 95.9 %shard_map.265 = (f32[128,2048]{1,0:T(8,128)}, f32[128,128]{1,0:T(8,128)}, f32[128,2048]{1,0:T(8,128)}) custom-call(bf16[8,2,80,2048]{3,2,1,0:T(8,128)(2,1)} %bitcast.96, bf16[8,2,80,128]{3,2,1,0:T(8,128)(2,1)} %select_select_fusion.tail, bf16[8,2,80,2048]{3,2,1,0:T(8,128)(2,1)} %all-to-all-done.mix, f32[2,8,256]{2,1,0:T(8,128)} %get-tuple-element.41.code), custom_call_target="tpu_custom_call" | custom-call | tf_op jit(solution)/shard_map/pallas_call | solution.py:112
  438.6 1.1 multiply_reduce_fusion.3
  439.7 1.0 multiply_convert_fusion.5
  441.0 1.7 multiply_reduce_fusion
  443.8 1.2 fusion.33.grad_out
  445.6 194.0 %shard_map.266 = (bf16[256,4096]{1,0:T(8,128)(2,1)}, bf16[8,256,128]{2,1,0:T(8,128)(2,1)}, bf16[512,2048]{1,0:T(8,128)(2,1)}, f32[32,256]{1,0:T(8,128)}, f32[8,2048]{1,0:T(8,128)}, /*index=5*/f32[128,2048]{1,0:T(8,128)}) custom-call(bf16[128,2048]{1,0:T(8,128)(2,1)} %fusion.33.grad_out, bf16[8,128,512]{2,1,0:T(8,128)(2,1)} %get-tuple-element.51.q, ...), custom_call_target="tpu_custom_call" | custom-call | tf_op jit(solution)/shard_map/pallas_call | solution.py:112
  639.6 1.2 slice_bitcast_fusion
  640.8 1.5 fusion.37
  642.4 1.3 convert_bitcast_fusion
  644.0 0.8 copy.52
  645.2 0.8 copy.53
  646.1 2.5 convert_element_type.134
  648.6 2.5 convert_element_type.135
  651.4 1.6 add_bitcast_fusion
  (90 shorter events, 9.2 us)
Async XLA Ops:
  3.3 149.2 %copy-start.12 = (f32[2048]{0:T(1024)S(1)}, f32[2048]{0:T(1024)}, u32[]{:S(2)}) copy-start(f32[2048]{0:T(1024)} %param.27) | copy-start | bytes 24580
  154.0 2.4 copy-start.3
  248.6 7.5 %copy-start.14 = (bf16[8,2,80,2048]{3,2,1,0:T(8,128)(2,1)S(1)}, bf16[8,2,80,2048]{3,2,1,0:T(8,128)(2,1)}, u32[]{:S(2)}) copy-start(bf16[8,2,80,2048]{3,2,1,0:T(8,128)(2,1)} %get-tuple-element.43) | copy-start | bytes 15728644
  248.6 7.5 %copy-start.16 = (bf16[1,2048,768]{2,1,0:T(8,128)(2,1)S(1)}, bf16[1,2048,768]{2,1,0:T(8,128)(2,1)}, u32[]{:S(2)}) copy-start(bf16[1,2048,768]{2,1,0:T(8,128)(2,1)} %param.30) | copy-start | bytes 9437188
  256.2 6.7 %copy-start.20 = (f32[1280,768]{1,0:T(8,128)}, f32[1280,768]{1,0:T(8,128)S(1)}, u32[]{:S(2)}) copy-start(f32[1280,768]{1,0:T(8,128)S(1)} %fusion.11) | copy-start | bytes 11796484
  256.2 6.7 %copy-start.15 = (bf16[1,768,2048]{2,1,0:T(8,128)(2,1)S(1)}, bf16[1,768,2048]{2,1,0:T(8,128)(2,1)}, u32[]{:S(2)}) copy-start(bf16[1,768,2048]{2,1,0:T(8,128)(2,1)} %param.31) | copy-start | bytes 9437188
  262.9 6.9 %copy-start.18 = (bf16[1280,768]{1,0:T(8,128)(2,1)}, bf16[1280,768]{1,0:T(8,128)(2,1)S(1)}, u32[]{:S(2)}) copy-start(bf16[1280,768]{1,0:T(8,128)(2,1)S(1)} %get-tuple-element.88) | copy-start | bytes 5898244
  269.8 18.1 %slice-start = ((s8[5242880]{0:T(1024)(128)(4,1)}), s8[1048576]{0:T(1024)(128)(4,1)S(1)}, s32[]{:S(2)}) async-start(s8[5242880]{0:T(1024)(128)(4,1)} %bitcast.98), calls=%async_computation.1 | async-start | bytes 2097152
  269.8 72.9 %all-to-all-start = ((bf16[8,2,80,2048]{3,2,1,0:T(8,128)(2,1)}), bf16[8,2,80,2048]{3,2,1,0:T(8,128)(2,1)}, u32[]{:S(2)}, u32[]{:S(2)}) async-start(bf16[8,2,80,2048]{3,2,1,0:T(8,128)(2,1)} %bitcast.95), calls=%async_computation | async-start | bytes 10485760 | tf_op jit(solution)/shard_map/all_to_all | solution.py:1308
  274.7 13.2 %slice-start.1 = ((s8[5242880]{0:T(1024)(128)(4,1)}), s8[4194304]{0:T(1024)(128)(4,1)S(1)}, s32[]{:S(2)}) async-start(s8[5242880]{0:T(1024)(128)(4,1)} %bitcast.98), calls=%async_computation.2 | async-start | bytes 8388608
  274.7 13.2 %copy-start.5 = (bf16[1280,2048]{1,0:T(8,128)(2,1)S(1)}, bf16[1280,2048]{1,0:T(8,128)(2,1)}, u32[]{:S(2)}) copy-start(bf16[1280,2048]{1,0:T(8,128)(2,1)} %get-tuple-element.46) | copy-start | bytes 15728644
  289.5 12.1 %copy-start.21 = (bf16[1280,768]{1,0:T(8,128)(2,1)S(1)}, bf16[1280,768]{1,0:T(8,128)(2,1)}, u32[]{:S(2)}) copy-start(bf16[1280,768]{1,0:T(8,128)(2,1)} %get-tuple-element.74) | copy-start | bytes 5898244
  301.5 8.8 %copy-start.22 = (bf16[1280,768]{1,0:T(8,128)(2,1)S(1)}, bf16[1280,768]{1,0:T(8,128)(2,1)}, u32[]{:S(2)}) copy-start(bf16[1280,768]{1,0:T(8,128)(2,1)} %get-tuple-element.73) | copy-start | bytes 5898244
  301.5 26.0 %slice-start.2 = ((s8[5242880]{0:T(1024)(128)(4,1)}), s8[4194304]{0:T(1024)(128)(4,1)S(1)}, s32[]{:S(2)}) async-start(s8[5242880]{0:T(1024)(128)(4,1)} %bitcast.101), calls=%async_computation.3 | async-start | bytes 8388608
  310.3 17.3 %slice-start.3 = ((s8[5242880]{0:T(1024)(128)(4,1)}), s8[1048576]{0:T(1024)(128)(4,1)S(1)}, s32[]{:S(2)}) async-start(s8[5242880]{0:T(1024)(128)(4,1)} %bitcast.101), calls=%async_computation.4 | async-start | bytes 2097152
  310.3 17.3 %copy-start.19 = (bf16[1280,768]{1,0:T(8,128)(2,1)S(1)}, bf16[1280,768]{1,0:T(8,128)(2,1)}, u32[]{:S(2)}) copy-start(bf16[1280,768]{1,0:T(8,128)(2,1)} %copy-done.18) | copy-start | bytes 5898244
  327.6 6.5 copy-start.17
  342.7 98.1 %copy-start.4 = (bf16[128,2048]{1,0:T(8,128)(2,1)S(1)}, bf16[128,2048]{1,0:T(8,128)(2,1)}, u32[]{:S(2)}) copy-start(bf16[128,2048]{1,0:T(8,128)(2,1)} %copy-done.3) | copy-start | bytes 1572868
  342.7 98.4 %copy-start = (f32[128,2048]{1,0:T(8,128)S(1)}, f32[128,2048]{1,0:T(8,128)}, u32[]{:S(2)}) copy-start(f32[128,2048]{1,0:T(8,128)} %get-tuple-element.39) | copy-start | bytes 3145732
  342.7 98.4 %copy-start.11 = (bf16[32,2048]{1,0:T(8,128)(2,1)S(1)}, bf16[32,2048]{1,0:T(8,128)(2,1)}, u32[]{:S(2)}) copy-start(bf16[32,2048]{1,0:T(8,128)(2,1)} %get-tuple-element.40) | copy-start | bytes 393220
  438.6 5.1 copy-start.6
  442.7 1.0 copy-start.1
  642.4 3.7 copy-start.8
  645.2 3.4 copy-start.7
  648.6 2.6 copy-start.2
  648.6 2.6 copy-start.9
  648.6 2.8 copy-start.10
  651.1 1.9 copy-start.13

commit v6 on v5

--- a/solution.py
+++ b/solution.py
@@ -85,9 +85,10 @@
 
 
 class Fold:
-    def __init__(self, c, sent, received, ss, rs):
+    def __init__(self, c, sent, received, ss, rs, slots=None, after=None):
         self.c, self.sent, self.received, self.ss, self.rs = c, sent, received, ss, rs
-        self.items = {}
+        self.slots, self.after = slots or {}, after or {}
+        self.items, self.left = {}, set()
 
     def take(self, d, value):
         for b in (1, 2, 4, 8, 16):
@@ -97,15 +98,21 @@
         return value
 
     def give(self, d, value):
-        self.sent[d - 1] = value.astype(BF)
-        item = push(self.sent.at[d - 1], self.received.at[d - 1], self.ss.at[d], self.rs.at[d],
+        slot = self.slots.get(d, d - 1)
+        if d in self.after:
+            other, which = self.after[d]
+            other.items[which].wait_send()
+            other.left.add(which)
+        self.sent[slot] = value.astype(BF)
+        item = push(self.sent.at[slot], self.received.at[d - 1], self.ss.at[d], self.rs.at[d],
                     ctx=flip_bits(self.c, lowest(d)))
         item.start()
         self.items[d] = item
 
     def drain(self):
-        for item in self.items.values():
-            item.wait_send()
+        for d, item in self.items.items():
+            if d not in self.left:
+                item.wait_send()
 
 
 def call(body, outs, in_specs, scratch, ident, args, mib=48, out_specs=None):
@@ -277,10 +284,10 @@
     cot_waits = []
     for k in range(groups):
         for i, peer in enumerate(others):
-            item = push(ready.at[k, peer], cot_rows.at[s, k], ss_x.at[k, i], rs_x.at[k, i], shard=peer)
+            item = push(ready.at[k, peer], cot_rows.at[k, s], ss_x.at[k, i], rs_x.at[k, i], shard=peer)
             item.start()
             cot_waits.append(item)
-        item = pltpu.make_async_copy(ready.at[k, s], cot_rows.at[s, k], local.at[6 + k])
+        item = pltpu.make_async_copy(ready.at[k, s], cot_rows.at[k, s], local.at[6 + k])
         item.start()
         cot_waits.append(item)
 
@@ -381,7 +388,7 @@
         functools.partial(front_body, z, n, group, capacity, heads, kv_heads, 512),
         [
             sds((n, count, width), BF), sds((n, wr, cols + HEAD_DIM), BF), sds((router.shape[0], width), BF),
-            sds((groups, n, group * count), F32), sds((n, groups, slots, width), BF), sds((n, count, cols), F32),
+            sds((groups, n, group * count), F32), sds((groups, n, slots, width), BF), sds((n, count, cols), F32),
             sds((n, count, HEAD_DIM), F32), sds((n, count, cols), BF), sds((2, n, z, count, HEAD_DIM), BF),
             sds((n, count, cols), BF), sds((count, width), F32),
         ],
@@ -1266,6 +1273,272 @@
     )
 
 
+def expert_body(n_ctx, n_shard, group, half, tile,
+                rows, tail, code, w_gate, w_up, w_down, cot_in,
+                out, tail_out, mix_out, g_gate, g_up, g_down,
+                zrows, ztail, ready, tail_ready, recv, tail_recv, cot, back_rows, back_tail, land, tail_land, mix_land,
+                hidden, grad_gate, grad_up, work, slot_dot, table, tail_value,
+                zrecv, tsend, trecv, mrecv, stage, stage_d, local,
+                ss_z, rs_z, ss_t, rs_t, ss_x, rs_x, ss_y, rs_y, ss_d, rs_d, ss_e, rs_e, ss_m, rs_m,
+                ss_fz, rs_fz, ss_ft, rs_ft, ss_fm, rs_fm, ss_st, ss_sd):
+    c, s, parity, sibling, others, layers = here(n_ctx, n_shard)
+    count, width = rows.shape
+    few = tail.shape[1]
+    inner = w_gate.shape[1]
+    groups = n_ctx // group
+    slots = recv.shape[2]
+    chunk = half * slots
+    experts = n_ctx * n_shard
+    expert = c * n_shard + s
+    loads = [
+        pltpu.make_async_copy(rows, zrows.at[c], local.at[0]),
+        pltpu.make_async_copy(tail, ztail.at[c], local.at[1]),
+    ] + [
+        pltpu.make_async_copy(cot_in.at[flip_bits(lax.div(c, group), k)], cot.at[k], local.at[2 + 2 * groups + k])
+        for k in range(groups)
+    ]
+    for item in loads:
+        item.start()
+    greet(others, layers)
+    fans = [
+        Fan(n_ctx, c, lambda d: ztail.at[flip_bits(c, d)], ss_t, rs_t, True),
+        Fan(n_ctx, c, lambda d: zrows.at[flip_bits(c, d)], ss_z, rs_z, True),
+    ]
+    fans[0].send(0, tail)
+    fans[1].send(0, rows)
+
+    sent = {}
+    seen = set()
+    loads[0].wait()
+    loads[1].wait()
+    for k in range(groups):
+        at = flip_bits(lax.div(c, group), k)
+        picks = slot_table(code[at], slots)
+        table[k] = picks.T
+        for d in fans[0].order():
+            if d < (k + 1) * group and d not in seen:
+                fans[0].arrival(d)
+                fans[1].arrival(d)
+                seen.add(d)
+        first = pl.multiple_of(at * group, group)
+        block = ztail[pl.ds(first, group)].reshape(group * count, few)
+        tail_ready[k] = jnp.dot(picks, block, preferred_element_type=F32).astype(BF).reshape(n_shard, slots, few)
+
+        @pl.loop(0, width // tile)
+        def _(j):
+            cols = pl.ds(pl.multiple_of(j * tile, tile), tile)
+            block = zrows[pl.ds(first, group), :, cols].reshape(group * count, tile)
+            moved = jnp.dot(picks, block, preferred_element_type=F32).astype(BF)
+            ready[k, :, :, cols] = moved.reshape(n_shard, slots, tile)
+
+        sent[k] = []
+        for i, peer in enumerate(others):
+            sent[k].append(push(ready.at[k, peer], recv.at[k, s], ss_x.at[k, i], rs_x.at[k, i], shard=peer))
+            sent[k].append(push(tail_ready.at[k, peer], tail_recv.at[k, s], ss_y.at[k, i], rs_y.at[k, i], shard=peer))
+        sent[k].append(pltpu.make_async_copy(ready.at[k, s], recv.at[k, s], local.at[2 + 2 * k]))
+        sent[k].append(pltpu.make_async_copy(tail_ready.at[k, s], tail_recv.at[k, s], local.at[3 + 2 * k]))
+        for item in sent[k]:
+            item.start()
+    for fan in fans:
+        fan.drain()
+    for item in loads[2:]:
+        item.wait()
+
+    gate_pre, up_pre = work.at[0:chunk, 0:inner], work.at[0:chunk, inner : 2 * inner]
+    value = work.at[0 : group * count, 0:width]
+    column = lax.broadcasted_iota(jnp.int32, (1, few), 1)
+    is_coarse, is_fine = column == expert, column == experts + expert
+
+    def send_back(src, dst, k, e, ss, rs):
+        @pl.when(s != e)
+        def _():
+            push(src.at[k, e], dst.at[k, s], ss.at[k, e], rs.at[k, s], shard=e).start()
+
+        @pl.when(s == e)
+        def _():
+            pltpu.make_async_copy(src.at[k, e], dst.at[k, e], rs.at[k, e]).start()
+
+    def wait_back(src, dst, k, ss, rs):
+        for e in range(n_shard):
+            @pl.when(s != e)
+            def _():
+                push(src.at[k, e], dst.at[k, e], ss.at[k, e], rs.at[k, e], shard=e).wait()
+
+            @pl.when(s == e)
+            def _():
+                pltpu.make_async_copy(src.at[k, e], dst.at[k, e], rs.at[k, e]).wait()
+
+    def experts_part(k, h):
+        of = slice(h * half, (h + 1) * half)
+        r = pl.ds((k * n_shard + h * half) * slots, chunk)
+        gates = jnp.sum(
+            jnp.where(is_coarse | is_fine, tail_recv[k, of].reshape(chunk, few).astype(F32), 0.0), axis=1, keepdims=True
+        )
+
+        @pl.loop(0, inner // 256)
+        def _(j):
+            cols = pl.ds(pl.multiple_of(j * 256, 256), 256)
+            x = recv[k, of].reshape(chunk, width)
+            g = jnp.dot(x, w_gate[:, cols], preferred_element_type=F32)
+            u = jnp.dot(x, w_up[:, cols], preferred_element_type=F32)
+            gate_pre[:, cols] = g
+            up_pre[:, cols] = u
+            hidden[r, cols] = (g * jax.nn.sigmoid(g) * u).astype(BF)
+
+        slot_dot[...] = jnp.zeros_like(slot_dot)
+
+        @pl.loop(0, width // tile)
+        def _(j):
+            cols = pl.ds(pl.multiple_of(j * tile, tile), tile)
+            o = jnp.dot(hidden[r, :], w_down[:, cols], preferred_element_type=F32).astype(BF).astype(F32)
+            up_row = cot[k, of, :, cols].reshape(chunk, tile).astype(F32)
+            slot_dot[...] += jnp.sum(o * up_row, axis=1, keepdims=True)
+            ready[k, of, :, cols] = (gates * o).astype(BF).reshape(half, slots, tile)
+            cot[k, of, :, cols] = (gates * up_row).astype(BF).reshape(half, slots, tile)
+
+        coarse = slot_dot[...].astype(BF).astype(F32)
+        fine = slot_dot[...] - coarse
+        back_tail[k, of] = jnp.where(is_coarse, coarse, jnp.where(is_fine, fine, 0.0)).astype(BF).reshape(half, slots, few)
+
+        @pl.loop(0, inner // 256)
+        def _(j):
+            cols = pl.ds(pl.multiple_of(j * 256, 256), 256)
+            gh = lax.dot_general(cot[k, of].reshape(chunk, width), w_down[cols, :], (((1,), (1,)), ((), ())),
+                                 preferred_element_type=F32)
+            g, u = gate_pre[:, cols], up_pre[:, cols]
+            sig = jax.nn.sigmoid(g)
+            grad_gate[r, cols] = (gh * u * (sig * (1.0 + g * (1.0 - sig)))).astype(BF)
+            grad_up[r, cols] = (gh * (g * sig)).astype(BF)
+
+        @pl.loop(0, width // tile)
+        def _(j):
+            cols = pl.ds(pl.multiple_of(j * tile, tile), tile)
+            gx = lax.dot_general(grad_gate[r, :], w_gate[cols, :], (((1,), (1,)), ((), ())), preferred_element_type=F32)
+            gx += lax.dot_general(grad_up[r, :], w_up[cols, :], (((1,), (1,)), ((), ())), preferred_element_type=F32)
+            back_rows[k, of, :, cols] = gx.astype(BF).reshape(half, slots, tile)
+
+        for e in range(h * half, (h + 1) * half):
+            send_back(back_rows, land, k, e, ss_d, rs_d)
+            send_back(back_tail, tail_land, k, e, ss_e, rs_e)
+
+    for k in range(groups):
+        for item in sent[k]:
+            item.wait()
+        for h in range(n_shard // half):
+            experts_part(k, h)
+    for k in reversed(range(groups)):
+        for e in range(n_shard):
+            send_back(ready, mix_land, k, e, ss_m, rs_m)
+
+    everything = groups * n_shard * slots
+
+    def stage_out(j, which):
+        at = pl.ds(pl.multiple_of(j * 256, 256), 256)
+        return pltpu.make_async_copy(stage.at[which], (g_gate, g_up)[which].at[at], ss_st.at[which])
+
+    @pl.loop(0, width // 256)
+    def _(j):
+        x = recv[:, :, :, pl.ds(pl.multiple_of(j * 256, 256), 256)].reshape(everything, 256)
+        for which, grad in enumerate((grad_gate, grad_up)):
+            total = lax.dot_general(x, grad[...], (((0,), (0,)), ((), ())), preferred_element_type=F32).astype(BF)
+
+            @pl.when(j >= 1)
+            def _():
+                stage_out(j - 1, which).wait()
+
+            stage[which] = total
+            stage_out(j, which).start()
+
+    def down_out(j):
+        return pltpu.make_async_copy(stage_d, g_down.at[:, pl.ds(pl.multiple_of(j * 256, 256), 256)], ss_sd)
+
+    @pl.loop(0, width // 256)
+    def _(j):
+        grad = cot[:, :, :, pl.ds(pl.multiple_of(j * 256, 256), 256)].reshape(everything, 256)
+        total = lax.dot_general(
+            hidden[...], grad, (((0,), (0,)), ((), ())), preferred_element_type=F32).astype(BF)
+
+        @pl.when(j >= 1)
+        def _():
+            down_out(j - 1).wait()
+
+        stage_d[...] = total
+        down_out(j).start()
+
+    last = width // 256 - 1
+    stage_out(last, 0).wait()
+    stage_out(last, 1).wait()
+    down_out(last).wait()
+
+    def local_sums(k, ref):
+        @pl.loop(0, width // tile)
+        def _(j):
+            cols = pl.ds(pl.multiple_of(j * tile, tile), tile)
+            block = ref[k, :, :, cols].reshape(n_shard * slots, tile)
+            value[:, cols] = jnp.dot(table[k], block, preferred_element_type=F32)
+
+    def part(ref, d):
+        place = lax.rem(flip_bits(c, d), group)
+        return ref[pl.ds(pl.multiple_of(place * count, count), count), :]
+
+    def fold_group(k, fold, ref, into):
+        for d in sorted(range(k * group, (k + 1) * group), key=lambda d: (lowest(d) or n_ctx, d)):
+            if d:
+                fold.give(d, fold.take(d, part(ref, d)) if lowest(d) > 1 else part(ref, d))
+            else:
+                into[...] = part(ref, 0)
+
+    fold = Fold(c, zrows, zrecv, ss_fz, rs_fz)
+    tail_fold = Fold(c, tsend, trecv, ss_ft, rs_ft)
+    mix_fold = Fold(c, zrows, mrecv, ss_fm, rs_fm, {3: 3, 2: 0, 1: 2}, {2: (fold, 1), 1: (fold, 3)})
+    for k in range(groups):
+        wait_back(back_rows, land, k, ss_d, rs_d)
+        wait_back(back_tail, tail_land, k, ss_e, rs_e)
+        local_sums(k, land)
+        tail_value[...] = jnp.dot(table[k], tail_land[k].reshape(n_shard * slots, few), preferred_element_type=F32)
+        fold_group(k, tail_fold, tail_value, tail_out)
+        fold_group(k, fold, value, out)
+    for k in reversed(range(groups)):
+        wait_back(ready, mix_land, k, ss_m, rs_m)
+        local_sums(k, mix_land)
+        fold_group(k, mix_fold, value, mix_out)
+    out[...] = fold.take(0, out[...])
+    tail_out[...] = tail_fold.take(0, tail_out[...])
+    mix_out[...] = mix_fold.take(0, mix_out[...])
+    for item in (fold, tail_fold, mix_fold):
+        item.drain()
+
+
+def run_experts(n_ctx, n_shard, group, capacity, rows, tail, code, w_gate, w_up, w_down, cot_rows, ident):
+    n, z, groups, slots = n_shard, n_ctx, code.shape[0], group * capacity
+    count, width = rows.shape
+    few, inner, half = tail.shape[1], w_gate.shape[1], n_shard // 2
+    everything, chunk = groups * n * slots, half * slots
+    sds, scratch = jax.ShapeDtypeStruct, pltpu.VMEM
+    dma = lambda *shape: DMA(shape)
+    wide, thin = (groups, n, slots, width), (groups, n, slots, few)
+    return call(
+        functools.partial(expert_body, z, n, group, half, 512),
+        [
+            sds((count, width), F32), sds((count, few), F32), sds((count, width), F32),
+            sds((width, inner), BF), sds((width, inner), BF), sds((inner, width), BF),
+        ],
+        [VMEM] * 6 + [ANY],
+        [
+            scratch((z, count, width), BF), scratch((z, count, few), BF), scratch(wide, BF), scratch(thin, BF),
+            scratch(wide, BF), scratch(thin, BF), scratch(wide, BF), scratch(wide, BF), scratch(thin, BF),
+            scratch(wide, BF), scratch(thin, BF), scratch(wide, BF),
+            scratch((everything, inner), BF), scratch((everything, inner), BF), scratch((everything, inner), BF),
+            scratch((max(chunk, group * count), max(2 * inner, width)), F32), scratch((chunk, 1), F32),
+            scratch((groups, group * count, n * slots), BF),
+            scratch((group * count, few), F32), scratch((z - 1, count, width), BF),
+            scratch((z - 1, count, few), BF), scratch((z - 1, count, few), BF), scratch((z - 1, count, width), BF),
+            scratch((2, 256, inner), BF), scratch((inner, 256), BF), dma(2 + 3 * groups),
+        ] + [dma(z)] * 4 + [dma(groups, n - 1)] * 4 + [dma(groups, n)] * 6 + [dma(z)] * 6 + [dma(2), DMA],
+        ident, (rows, tail, code, w_gate, w_up, w_down, cot_rows), mib=63, out_specs=[VMEM] * 3 + [ANY] * 3,
+    )
+
+
 def rms_scale(hidden, gain):
     return hidden * lax.rsqrt(jnp.mean(hidden * hidden, axis=-1, keepdims=True) + epsilon) * gain
 
@@ -1376,7 +1649,6 @@
         ),
         0,
     )
-    upstream_rows = upstream_rows.reshape(slot_rows, width)
     is_key = lax.rem(my_shard, 2) == 0
     part_count = sharers // 2
 
@@ -1408,42 +1680,53 @@
 
     gates_two = jnp.concatenate(two_parts(gates), axis=1)
     gates_two = jnp.pad(gates_two, ((0, 0), (0, tail_cols - 2 * experts)))
-    received, gate_tail = dispatch_rows(ctx_count, shard_count, group, capacity, second_b, gates_two, code, 3)
-    received = received.reshape(slot_rows, width)
-    my_expert = my_ctx * shard_count + my_shard
-    column = jnp.arange(tail_cols, dtype=jnp.int32)[None, :]
-    mine_column = (column == my_expert) | (column == experts + my_expert)
-    gate_tail = gate_tail.reshape(slot_rows, tail_cols).astype(F32)
-    slot_gates = jnp.sum(jnp.where(mine_column, gate_tail, 0.0), axis=1, keepdims=True)
-    gate_pre = dot(received, w_gate[0])
-    up_pre = dot(received, w_up[0])
-    activated = jax.nn.silu(gate_pre)
-    hidden_b = (activated * up_pre).astype(BF)
-    expert_out = dot(hidden_b, w_down[0]).astype(BF)
-    expert_out_f = expert_out.astype(F32)
-    mix_sent = (slot_gates * expert_out_f).astype(BF)
-    mix_sent, upstream_rows, expert_out = lax.optimization_barrier((mix_sent, upstream_rows, expert_out))
-    expert_out_f = expert_out.astype(F32)
-    mix_back = exchange_shard(mix_sent.reshape(block_shape + (width,)))
-    upstream_rows = upstream_rows.astype(F32)
-    slot_dot = jnp.sum(expert_out_f * upstream_rows, axis=1, keepdims=True)
-    grad_expert = (slot_gates * upstream_rows).astype(BF)
-    grad_w_down = contract_rows(hidden_b, grad_expert)
-    grad_hidden = contract_cols(grad_expert, w_down[0])
-    sigmoid_g = jax.nn.sigmoid(gate_pre)
-    silu_slope = sigmoid_g * (1.0 + gate_pre * (1.0 - sigmoid_g))
-    grad_gate_pre = (grad_hidden * up_pre * silu_slope).astype(BF)
-    grad_up_pre = (grad_hidden * activated).astype(BF)
-    grad_w_gate = contract_rows(received, grad_gate_pre)
-    grad_w_up = contract_rows(received, grad_up_pre)
-    grad_received = contract_cols(grad_gate_pre, w_gate[0]) + contract_cols(grad_up_pre, w_up[0])
-
-    coarse, fine = two_parts(slot_dot)
-    tail = jnp.where(column == my_expert, coarse, jnp.where(column == experts + my_expert, fine, jnp.zeros((), BF)))
-    grad_second, back_tail, mixture = combine_rows(
-        ctx_count, shard_count, group, grad_received.astype(BF).reshape(block_shape + (width,)),
-        tail.reshape(block_shape + (tail_cols,)), mix_back, code, 4,
-    )
+    small = plane * width <= 2**21 and ctx_count == 4
+    if small:
+        grad_second, back_tail, mixture, grad_w_gate, grad_w_up, grad_w_down = run_experts(
+            ctx_count, shard_count, group, capacity, second_b, gates_two, code, w_gate[0], w_up[0], w_down[0],
+            upstream_rows, 3,
+        )
+        grad_w_gate, grad_w_up, grad_w_down = (
+            grad_w_gate.astype(F32), grad_w_up.astype(F32), grad_w_down.astype(F32),
+        )
+    else:
+        received, gate_tail = dispatch_rows(ctx_count, shard_count, group, capacity, second_b, gates_two, code, 3)
+        received = received.reshape(slot_rows, width)
+        my_expert = my_ctx * shard_count + my_shard
+        upstream_rows = jnp.swapaxes(upstream_rows, 0, 1).reshape(slot_rows, width)
+        column = jnp.arange(tail_cols, dtype=jnp.int32)[None, :]
+        mine_column = (column == my_expert) | (column == experts + my_expert)
+        gate_tail = gate_tail.reshape(slot_rows, tail_cols).astype(F32)
+        slot_gates = jnp.sum(jnp.where(mine_column, gate_tail, 0.0), axis=1, keepdims=True)
+        gate_pre = dot(received, w_gate[0])
+        up_pre = dot(received, w_up[0])
+        activated = jax.nn.silu(gate_pre)
+        hidden_b = (activated * up_pre).astype(BF)
+        expert_out = dot(hidden_b, w_down[0]).astype(BF)
+        expert_out_f = expert_out.astype(F32)
+        mix_sent = (slot_gates * expert_out_f).astype(BF)
+        mix_sent, upstream_rows, expert_out = lax.optimization_barrier((mix_sent, upstream_rows, expert_out))
+        expert_out_f = expert_out.astype(F32)
+        mix_back = exchange_shard(mix_sent.reshape(block_shape + (width,)))
+        upstream_rows = upstream_rows.astype(F32)
+        slot_dot = jnp.sum(expert_out_f * upstream_rows, axis=1, keepdims=True)
+        grad_expert = (slot_gates * upstream_rows).astype(BF)
+        grad_w_down = contract_rows(hidden_b, grad_expert)
+        grad_hidden = contract_cols(grad_expert, w_down[0])
+        sigmoid_g = jax.nn.sigmoid(gate_pre)
+        silu_slope = sigmoid_g * (1.0 + gate_pre * (1.0 - sigmoid_g))
+        grad_gate_pre = (grad_hidden * up_pre * silu_slope).astype(BF)
+        grad_up_pre = (grad_hidden * activated).astype(BF)
+        grad_w_gate = contract_rows(received, grad_gate_pre)
+        grad_w_up = contract_rows(received, grad_up_pre)
+        grad_received = contract_cols(grad_gate_pre, w_gate[0]) + contract_cols(grad_up_pre, w_up[0])
+
+        coarse, fine = two_parts(slot_dot)
+        tail = jnp.where(column == my_expert, coarse, jnp.where(column == experts + my_expert, fine, jnp.zeros((), BF)))
+        grad_second, back_tail, mixture = combine_rows(
+            ctx_count, shard_count, group, grad_received.astype(BF).reshape(block_shape + (width,)),
+            tail.reshape(block_shape + (tail_cols,)), mix_back, code, 4,
+        )
     mixed = (middle + mixture).astype(BF)
     grad_gates = back_tail[:, :experts] + back_tail[:, experts : 2 * experts]
     grad_logits_b = (
@@ -1457,7 +1740,7 @@
     grad_proj_b = grad_middle.astype(BF)
 
     router_parts = jnp.swapaxes(router_part.reshape(experts, shard_count, wrows), 0, 1)
-    if plane * width <= 2**21:
+    if small:
         gains = jnp.concatenate([jnp.zeros((1, width), F32), grad_ffn_gain[None], jnp.zeros((6, width), F32)])
         q_sum, kv_sum, out_sum, router_sum, gains, grad_input_part = back(
             ctx_count, shard_count, heads,

time: 663 us -> 635 us (0.958)
  matrix products: 89.5 us -> 4.69 us
  Pallas kernels: 527 us -> 586 us
  other arithmetic: 23.6 us -> 30.4 us
    pallas_call x4 -> x3, Pallas kernels: 527 us -> 586 us  [call(): pl.pallas_call(body, out_shape=outs, in_specs=in_specs, out_specs=out_spe...]
    dot_general x4 -> x1, matrix products: 34.1 us -> 1.41 us  [contract_cols(): lax.dot_general(left, right, (((1,), (1,)), ((), ())), preferred_element_...]
    dot_general x4 -> x1, matrix products: 32.7 us -> 1.27 us  [contract_rows(): lax.dot_general(left, right, (((0,), (0,)), ((), ())), preferred_element_...]
    dot_general x4 -> x1, matrix products: 22.8 us -> 2.01 us  [dot(): return jnp.dot(left, right, preferred_element_type=F32)]
    broadcast_in_dim x0 -> x3, other arithmetic: none -> 9.93 us  [the longest x1 3.55 us: shards(): grad_w_down[None]]
  transfers between devices with their start and end apart: 1 -> 0, of which waited for: 0 -> 0; matrix products, arithmetic and copies ran while one was open for 10% -> 0% of each run, Pallas kernels for 0% -> 0%
where the time goes in v6:
time: 635 us; the launch traced here: 629 us
  Pallas kernels  586 us (92%)
  other arithmetic  30.4 us (5%)
  local copies, waits for them, and re-layouts  7.06 us (1%)
    pallas_call x3, Pallas kernels, call(): pl.pallas_call(body, out_shape=outs, in_specs=in_specs, out_specs=out_spe...  586 us

profile of v6, /device:TPU:0, one launch (start us, length us, event | category | flops | bytes accessed | tf_op | source)
XLA Modules:
  0.0 629.2 jit_solution(11837017109963996338)
XLA Ops:
  0.7 0.7 select_reduce_fusion.1
  1.5 0.7 select_reduce_fusion
  2.3 0.7 convert_reduce_fusion
  3.4 0.8 pad_maximum_fusion
  4.2 0.8 compare_select_fusion.bias
  5.0 146.3 %shard_map.263 = (bf16[8,128,2048]{2,1,0:T(8,128)(2,1)}, bf16[8,256,640]{2,1,0:T(8,128)(2,1)}, bf16[32,2048]{1,0:T(8,128)(2,1)}, f32[2,8,256]{2,1,0:T(8,128)}, b...) custom-call(bf16[128,2048]{1,0:T(8,128)(2,1)} %bitcast.70, ...), custom_call_target="tpu_custom_call" | custom-call | tf_op jit(solution)/shard_map/pallas_call | solution.py:119
  151.2 1.4 multiply_reduce_fusion.2
  152.6 1.4 multiply_convert_fusion.rows
  154.0 1.4 fusion.22
  155.7 0.7 fusion.4.tail
  156.5 228.4 %shard_map.264 = (f32[128,2048]{1,0:T(8,128)}, f32[128,128]{1,0:T(8,128)}, f32[128,2048]{1,0:T(8,128)}, bf16[2048,768]{1,0:T(8,128)(2,1)}, bf16[2048,768]{1,0:T(8,128)(2,1)}, /*index=5*/bf16[768,2048]{1,0:T(8,128)(2,1)}) custom-call(bf16[128,2048]{1,0:T(8,128)(2,1)} %copy-done.2, bf16[128,128]{1,0:T(8,128)(2,1)} %fusion.4.tail, ...), custom_call_target="tpu_custom_call" | custom-call | tf_op jit(solution)/shard_map/pallas_call | solution.py:119
  384.9 1.2 multiply_reduce_fusion.3
  386.1 1.0 multiply_convert_fusion.1
  387.1 1.3 convolution_convert_fusion
  388.4 2.0 multiply_reduce_fusion
  390.4 0.7 copy.54
  391.1 0.7 maximum_maximum_fusion.gains
  391.9 1.2 fusion.17.grad_out
  393.0 211.3 %shard_map.265 = (bf16[256,4096]{1,0:T(8,128)(2,1)}, bf16[8,256,128]{2,1,0:T(8,128)(2,1)}, bf16[512,2048]{1,0:T(8,128)(2,1)}, f32[32,256]{1,0:T(8,128)}, f32[8,2048]{1,0:T(8,128)}, /*index=5*/f32[128,2048]{1,0:T(8,128)}) custom-call(bf16[128,2048]{1,0:T(8,128)(2,1)} %fusion.17.grad_out, bf16[8,128,512]{2,1,0:T(8,128)(2,1)} %get-tuple-element.44.q, ...), custom_call_target="tpu_custom_call" | custom-call | tf_op jit(solution)/shard_map/pallas_call | solution.py:119
  604.3 3.5 add_bitcast_fusion
  607.8 1.2 slice_bitcast_fusion
  609.0 1.5 fusion.21
  610.7 0.3 copy.44
  611.1 0.8 copy.52
  612.2 0.8 copy.53
  613.1 2.5 convert_element_type.61
  615.6 2.5 convert_element_type.62
  618.1 0.3 copy-done.6
  618.5 3.2 bitcast_convert_fusion.2
  621.6 3.2 bitcast_convert_fusion.1
  624.8 3.6 bitcast_convert_fusion
  628.4 0.6 copy.56
  (43 shorter events, 1.4 us)
Async XLA Ops:
  4.9 147.7 %copy-start.11 = (f32[2048]{0:T(1024)S(1)}, f32[2048]{0:T(1024)}, u32[]{:S(2)}) copy-start(f32[2048]{0:T(1024)} %param.27) | copy-start | bytes 24580
  154.0 2.4 copy-start.2
  156.5 231.9 %copy-start.10 = (bf16[32,2048]{1,0:T(8,128)(2,1)S(1)}, bf16[32,2048]{1,0:T(8,128)(2,1)}, u32[]{:S(2)}) copy-start(bf16[32,2048]{1,0:T(8,128)(2,1)} %get-tuple-element.38) | copy-start | bytes 393220
  384.9 7.0 %copy-start = (f32[128,2048]{1,0:T(8,128)S(1)}, f32[128,2048]{1,0:T(8,128)}, u32[]{:S(2)}) copy-start(f32[128,2048]{1,0:T(8,128)} %get-tuple-element.37) | copy-start | bytes 3145732
  384.9 7.0 %copy-start.3 = (bf16[1,128,2048]{2,1,0:T(8,128)(2,1)S(1)}, bf16[1,128,2048]{2,1,0:T(8,128)(2,1)}, u32[]{:S(2)}) copy-start(bf16[1,128,2048]{2,1,0:T(8,128)(2,1)} %param.17) | copy-start | bytes 1572868
  390.4 1.5 copy-start.1
  604.3 6.2 copy-start.9
  610.6 2.4 copy-start.8
  613.1 2.5 copy-start.7
  615.6 2.9 copy-start.6
  618.5 3.2 copy-start.5
  621.6 3.2 copy-start.4
  624.8 3.6 copy-start.12

commit v7 on v6

--- a/solution.py
+++ b/solution.py
@@ -251,6 +251,16 @@
             value = jnp.dot(table, block, preferred_element_type=F32).astype(BF)
             ready[k, :, :, part] = value.reshape(n_shard, slots, tile)
 
+    cot_waits = []
+    for k in range(groups):
+        for i, peer in enumerate(others):
+            item = push(ready.at[k, peer], cot_rows.at[k, s], ss_x.at[k, i], rs_x.at[k, i], shard=peer)
+            item.start()
+            cot_waits.append(item)
+        item = pltpu.make_async_copy(ready.at[k, s], cot_rows.at[k, s], local.at[6 + k])
+        item.start()
+        cot_waits.append(item)
+
     for item in waits + w_waits:
         item.wait()
     copies[0].wait()
@@ -280,16 +290,6 @@
     item = push(kv.at[parity, :, c], kv.at[parity, :, c], ss_kf.at[0], rs_kf.at[0], shard=sibling)
     item.start()
     kv_waits.append(item)
-
-    cot_waits = []
-    for k in range(groups):
-        for i, peer in enumerate(others):
-            item = push(ready.at[k, peer], cot_rows.at[k, s], ss_x.at[k, i], rs_x.at[k, i], shard=peer)
-            item.start()
-            cot_waits.append(item)
-        item = pltpu.make_async_copy(ready.at[k, s], cot_rows.at[k, s], local.at[6 + k])
-        item.start()
-        cot_waits.append(item)
 
     @pl.loop(0, n_shard // 2)
     def _(b):
@@ -721,17 +721,17 @@
     )
 
 
-def back_body(n_ctx, n_shard, heads, wides,
+def back_body(n_ctx, n_shard, group, heads, wides,
               grad_out, q, kv, attn, qpre, kvpre, w_out, rows_in, w_all, cosine, sine, bias, q_gain, k_gain,
-              tokens, gain, gains, router,
-              q_out, kv_out, wide_out, router_out, gains_out, rows_out,
-              grads, rows_all, attn_t, grad_heads, ds_all, p_all, parts, pre, q_sum, k_sum, wide, weights,
+              tokens, gain, gains, router, mix_near, mix_far, code,
+              q_out, kv_out, wide_out, router_out, gains_out, rows_out, mix_out, mix_land,
+              grads, attn_t, grad_heads, ds_all, p_all, parts, pre, q_sum, k_sum, wide, weights,
               sibk, zsend, zrecv, wide_landing, pieces, landing,
               own_part, pair, to_sib, sib, to_chip, got, router_in, router_mid, router_far,
-              gains_own, gains_in, gains_mid, gains_far, local,
+              gains_own, gains_in, gains_mid, gains_far, mix_rows, mix_sent, mix_recv, local,
               ss_row, rs_row, ss_fwd, rs_fwd, ss_sk, rs_sk, ss_zk, rs_zk,
               ss_wi, rs_wi, ss_wo, ss_wc, ss_w, rs_w, ss_i, rs_i, ss_o, ss_q, ss_k,
-              ss_r, rs_r, ss_g, rs_g, ss_h, rs_h, ss_t, rs_t, ss_s, rs_s, ss_c, rs_c):
+              ss_r, rs_r, ss_g, rs_g, ss_h, rs_h, ss_t, rs_t, ss_s, rs_s, ss_c, rs_c, ss_m, rs_m, ss_f, rs_f, ss_v, rs_v):
     c, s, parity, sibling, others, layers = here(n_ctx, n_shard)
     half = n_ctx // 2
     chips = n_shard // 2
@@ -750,10 +750,9 @@
     scaling = HEAD_DIM ** -0.5
     own_copies = [
         pltpu.make_async_copy(grad_out, grads.at[s], local.at[0]),
-        pltpu.make_async_copy(rows_in, rows_all, local.at[1]),
+        pltpu.make_async_copy(rows_in, grads, local.at[1]),
     ]
-    for item in own_copies:
-        item.start()
+    own_copies[0].start()
     greet(others, layers)
 
     first, forwards = {}, {}
@@ -777,6 +776,40 @@
         scaled = grad * norm_gain[...]
         return scale * (scaled - unit * jnp.mean(scaled * unit, axis=-1, keepdims=True))
 
+    slots = mix_near.shape[1]
+    mix_fold = Fold(c, mix_sent, mix_recv, ss_f, rs_f)
+    tile = mix_rows.shape[2]
+
+    def mix_sums(k, ref):
+        table = slot_table(code[flip_bits(lax.div(c, group), k)], slots).T
+
+        @pl.loop(0, width // tile)
+        def _(j):
+            part = pl.ds(pl.multiple_of(j * tile, tile), tile)
+            item = pltpu.make_async_copy(ref.at[:, :, part], mix_rows, local.at[5])
+            item.start()
+            item.wait()
+            value = jnp.dot(table, mix_rows[...].reshape(n_shard * slots, tile), preferred_element_type=F32)
+            own_part[:, :, part] = value.reshape(2, count, tile)
+
+    def mix_part(d):
+        return own_part[lax.rem(flip_bits(c, d), group)]
+
+    def mix_send():
+        for i, peer in enumerate(others):
+            push(mix_near.at[peer], mix_land.at[s], ss_m.at[i], rs_m.at[i], shard=peer).start()
+        pltpu.make_async_copy(mix_near.at[s], mix_land.at[s], local.at[6]).start()
+
+    def mix_last():
+        for i, peer in enumerate(others):
+            push(mix_near.at[peer], mix_land.at[s], ss_m.at[i], rs_m.at[i], shard=peer).wait()
+        pltpu.make_async_copy(mix_near.at[s], mix_land.at[s], local.at[6]).wait()
+        mix_sums(0, mix_land)
+        mix_fold.give(1, mix_part(1))
+        mix_out[...] = mix_part(0)
+
+    mix_sums(1, mix_far)
+    mix_fold.give(3, mix_part(3))
     near, far = {}, {}
 
     def seqs_of(d):
@@ -831,6 +864,93 @@
             far[d, i] = push(zsend.at[d, i], zrecv.at[d, i], ss_zk.at[d, i], rs_zk.at[d, i], ctx=layer)
             far[d, i].start()
 
+    def half_rows(j):
+        return pl.ds((j % 2) * (wr // 2), wr // 2)
+
+    def out_copies(j, ref):
+        source = lax.rem(s + n_shard - j // 2, n_shard)
+        to = pl.ds(pl.multiple_of(source * cols, cols), cols)
+        return (
+            pltpu.make_async_copy(ref.at[:, pl.ds(0, cols)], q_out.at[half_rows(j), to], ss_q.at[j]),
+            pltpu.make_async_copy(ref.at[:, pl.ds(cols, HEAD_DIM)], kv_out.at[source, half_rows(j)], ss_k.at[j]),
+        )
+
+    def wide_copies(j, ref):
+        step = wide.shape[2]
+        return (pltpu.make_async_copy(ref, wide_out.at[:, pl.ds(j * step, step)], ss_wc.at[j]),)
+
+    class Line:
+        def __init__(self, ready, own, landing, ss_i, rs_i, ss_o, copies):
+            self.ready, self.own, self.landing = ready, own, landing
+            self.ss_i, self.rs_i, self.ss_o, self.copies = ss_i, rs_i, ss_o, copies
+
+        def inward(self, j, ref):
+            at = jnp.where(middle, 1, 0)
+            return push(ref, self.landing.at[at, j], self.ss_i.at[j], self.rs_i.at[at, j], ctx=inner)
+
+        def outward(self, j):
+            return push(self.landing.at[1, j], self.landing.at[1, j], self.ss_o.at[j], self.rs_i.at[1, j], ctx=outer)
+
+        def arrived(self, which, j):
+            push(self.landing.at[0, j], self.landing.at[which, j], self.ss_i.at[j], self.rs_i.at[which, j],
+                 ctx=inner).wait_recv()
+
+        def outermost(self, j):
+            @pl.when(jnp.logical_not(inside))
+            def _():
+                self.ready(j)
+                self.inward(j, self.own(j)).start()
+
+        def first_half(self, j):
+            @pl.when(inside)
+            def _():
+                self.ready(j)
+                self.arrived(0, j)
+                self.landing[0, j] = (self.own(j)[...].astype(F32) + self.landing[0, j].astype(F32)).astype(BF)
+                self.inward(j, self.landing.at[0, j]).start()
+
+        def second_half(self, j):
+            self.arrived(1, j)
+
+            @pl.when(middle)
+            def _():
+                self.landing[1, j] = (self.landing[0, j].astype(F32) + self.landing[1, j].astype(F32)).astype(BF)
+
+            @pl.when(inside)
+            def _():
+                self.outward(j).start()
+
+            for item in self.copies(j, self.landing.at[1, j]):
+                item.start()
+
+        def drain(self, j):
+            self.inward(j, self.landing.at[0, j]).wait_send()
+
+            @pl.when(inside)
+            def _():
+                self.outward(j).wait_send()
+
+            for item in self.copies(j, self.landing.at[1, j]):
+                item.wait()
+
+    sends = [[] for j in range(n_shard)]
+    line = Line(lambda j: [item.wait() for item in sends[j // 2]] if j % 2 == 0 else None,
+                lambda j: pieces.at[j // 2, half_rows(j)] if j >= 2 else weights.at[s, half_rows(j)],
+                landing, ss_i, rs_i, ss_o, out_copies)
+    wide_line = Line(lambda j: None, lambda j: wide.at[j], wide_landing, ss_wi, rs_wi, ss_wo, wide_copies)
+    steps = [(wide_line, j) for j in range(wides)] + [(line, j) for j in range(2 * n_shard)]
+    lag, ahead = 2, 6
+
+    def advance(n):
+        if n + ahead < len(steps):
+            steps[n + ahead][0].outermost(steps[n + ahead][1])
+        if n < len(steps):
+            steps[n][0].first_half(steps[n][1])
+        if n >= lag:
+            steps[n - lag][0].second_half(steps[n - lag][1])
+
+    attn_t[...] = attn[...].reshape(n_shard * count, cols).T
+    step = width // wides
     for d in range(chips):
         if d:
             first[d].wait()
@@ -840,92 +960,23 @@
         else:
             own_copies[0].wait()
         forwards[d].wait()
+        if d + 1 == chips:
+            mix_send()
+            for j in range(wides):
+                block = grads[:, :, j * step : (j + 1) * step].reshape(n_shard * count, step)
+                wide[j] = jnp.dot(attn_t[...], block, preferred_element_type=F32).astype(BF)
+                if j < ahead:
+                    wide_line.outermost(j)
         attention_back(d)
+        if d == 0:
+            mix_fold.give(2, mix_fold.take(2, mix_part(2)))
         if d:
             key_sum(d - 1)
+
+    rows_all = grads
+    own_copies[1].start()
     key_sum(chips - 1)
-
-    def out_copies(j, ref):
-        source = lax.rem(s + n_shard - j, n_shard)
-        to = pl.ds(pl.multiple_of(source * cols, cols), cols)
-        return (
-            pltpu.make_async_copy(ref.at[:, pl.ds(0, cols)], q_out.at[:, to], ss_q.at[j]),
-            pltpu.make_async_copy(ref.at[:, pl.ds(cols, HEAD_DIM)], kv_out.at[source], ss_k.at[j]),
-        )
-
-    def wide_copies(j, ref):
-        step = wide.shape[2]
-        return (pltpu.make_async_copy(ref, wide_out.at[:, pl.ds(j * step, step)], ss_wc.at[j]),)
-
-    class Line:
-        def __init__(self, ready, own, landing, ss_i, rs_i, ss_o, copies):
-            self.ready, self.own, self.landing = ready, own, landing
-            self.ss_i, self.rs_i, self.ss_o, self.copies = ss_i, rs_i, ss_o, copies
-
-        def inward(self, j, ref):
-            at = jnp.where(middle, 1, 0)
-            return push(ref, self.landing.at[at, j], self.ss_i.at[j], self.rs_i.at[at, j], ctx=inner)
-
-        def outward(self, j):
-            return push(self.landing.at[1, j], self.landing.at[1, j], self.ss_o.at[j], self.rs_i.at[1, j], ctx=outer)
-
-        def arrived(self, which, j):
-            push(self.landing.at[0, j], self.landing.at[which, j], self.ss_i.at[j], self.rs_i.at[which, j],
-                 ctx=inner).wait_recv()
-
-        def outermost(self, j):
-            @pl.when(jnp.logical_not(inside))
-            def _():
-                self.ready(j)
-                self.inward(j, self.own(j)).start()
-
-        def first_half(self, j):
-            @pl.when(inside)
-            def _():
-                self.ready(j)
-                self.arrived(0, j)
-                self.landing[0, j] = (self.own(j)[...].astype(F32) + self.landing[0, j].astype(F32)).astype(BF)
-                self.inward(j, self.landing.at[0, j]).start()
-
-        def second_half(self, j):
-            self.arrived(1, j)
-
-            @pl.when(middle)
-            def _():
-                self.landing[1, j] = (self.landing[0, j].astype(F32) + self.landing[1, j].astype(F32)).astype(BF)
-
-            @pl.when(inside)
-            def _():
-                self.outward(j).start()
-
-            for item in self.copies(j, self.landing.at[1, j]):
-                item.start()
-
-        def drain(self, j):
-            self.inward(j, self.landing.at[0, j]).wait_send()
-
-            @pl.when(inside)
-            def _():
-                self.outward(j).wait_send()
-
-            for item in self.copies(j, self.landing.at[1, j]):
-                item.wait()
-
-    sends = [None]
-    line = Line(lambda j: sends[j].wait() if j else None, lambda j: pieces.at[j] if j else weights.at[s],
-                landing, ss_i, rs_i, ss_o, out_copies)
-    wide_line = Line(lambda j: None, lambda j: wide.at[j], wide_landing, ss_wi, rs_wi, ss_wo, wide_copies)
-    steps = [(wide_line, j) for j in range(wides)] + [(line, j) for j in range(n_shard)]
-    lag, ahead = 2, 6
-
-    attn_t[...] = attn[...].reshape(n_shard * count, cols).T
-    step = width // wides
-    for j in range(wides):
-        block = grads[:, :, j * step : (j + 1) * step].reshape(n_shard * count, step)
-        wide[j] = jnp.dot(attn_t[...], block, preferred_element_type=F32).astype(BF)
-        if j < ahead:
-            wide_line.outermost(j)
-
+    advance(0)
     own_copies[1].wait()
 
     @pl.loop(0, n_shard)
@@ -935,7 +986,12 @@
         weights[e, :, pl.ds(0, cols)] = lax.dot_general(
             block, right, (((0,), (0,)), ((), ())), preferred_element_type=F32).astype(BF)
 
-    wide_line.first_half(0)
+    for i, peer in enumerate(others):
+        item = push(weights.at[peer, :, pl.ds(0, cols)], pieces.at[i + 1, :, pl.ds(0, cols)],
+                    ss_w.at[i], rs_w.at[i], shard=peer)
+        item.start()
+        sends[i + 1].append(item)
+    advance(1)
     for d in range(chips):
         fs = seqs_of(d)
         total = parts[parity, pl.ds(fs, 2), c].astype(F32) + sibk[d, :, c].astype(F32)
@@ -954,9 +1010,11 @@
             block, right, (((0,), (0,)), ((), ())), preferred_element_type=F32).astype(BF)
 
     for i, peer in enumerate(others):
-        item = push(weights.at[peer], pieces.at[i + 1], ss_w.at[i], rs_w.at[i], shard=peer)
-        item.start()
-        sends.append(item)
+        item = push(weights.at[peer, :, pl.ds(cols, HEAD_DIM)], pieces.at[i + 1, :, pl.ds(cols, HEAD_DIM)],
+                    ss_v.at[i], rs_v.at[i], shard=peer)
+        item.start()
+        sends[i + 1].append(item)
+    advance(2)
 
     order = list(range(1, chips)) + [0]
     to_sibling, to_mate = {}, {}
@@ -1037,27 +1095,27 @@
         side.append(functools.partial(product, at))
         if at:
             side.append(functools.partial(chip_sum, at - 1))
-    side += [last_sum, small_plane]
-    for n in range(1, len(steps) + lag):
-        if n + ahead - 1 < len(steps):
-            steps[n + ahead - 1][0].outermost(steps[n + ahead - 1][1])
-        if n < len(steps):
-            steps[n][0].first_half(steps[n][1])
-        if n >= lag:
-            steps[n - lag][0].second_half(steps[n - lag][1])
+    count_steps = len(steps) + lag
+    late = {16: last_sum, 18: mix_last, 21: small_plane}
+    for n in range(3, count_steps):
+        advance(n)
         if side:
             side.pop(0)()
+        if n in late:
+            late[n]()
     for job in side:
         job()
     small_all()
+    mix_out[...] = mix_fold.take(0, mix_out[...])
+    mix_fold.drain()
     for which, j in steps:
         which.drain(j)
 
 
-def back(n_ctx, n_shard, heads, args, ident):
+def back(n_ctx, n_shard, group, heads, args, ident):
     count, width = args[0].shape
-    rows_in, w_all, router, gains = args[7], args[8], args[17], args[16]
-    n, z, chips, wides = n_shard, n_ctx, n_shard // 2, 8
+    rows_in, w_all, router, gains, mix_near = args[7], args[8], args[17], args[16], args[18]
+    n, z, chips, wides = n_shard, n_ctx, n_shard // 2, 16
     wr, cols = w_all.shape[1], heads * HEAD_DIM
     keys = z * count
     sds, scratch = jax.ShapeDtypeStruct, pltpu.VMEM
@@ -1065,33 +1123,34 @@
     dma = lambda *shape: DMA(shape)
     wide_block, block = (cols, width // wides), (wr, cols + HEAD_DIM)
     return call(
-        functools.partial(back_body, z, n, heads, wides),
+        functools.partial(back_body, z, n, group, heads, wides),
         [
             sds((wr, n * cols), BF), sds((n, wr, HEAD_DIM), BF), sds((cols, width), BF), sds(router_shape, F32),
-            sds(gains.shape, F32), sds((count, width), F32),
+            sds(gains.shape, F32), sds((count, width), F32), sds((count, width), F32), sds(mix_near.shape, BF),
         ],
-        [VMEM] * 7 + [ANY] + [VMEM] * 10,
+        [VMEM] * 7 + [ANY] + [VMEM] * 10 + [ANY, ANY, VMEM],
         [
-            scratch((n, count, width), BF), scratch((n, count, width), BF), scratch((cols, n * count), BF),
+            scratch((n, count, width), BF), scratch((cols, n * count), BF),
             scratch((2, count, cols), BF), scratch((heads * count, keys), BF), scratch((heads * count, keys), BF),
             scratch((2, n, z, count, HEAD_DIM), BF), scratch((n, count, cols + HEAD_DIM), BF),
             scratch((1, HEAD_DIM), F32), scratch((1, HEAD_DIM), F32),
             scratch((wides,) + wide_block, BF), scratch((n,) + block, BF),
             scratch((chips, 2, z, count, HEAD_DIM), BF), scratch((chips, z - 1, 2, count, HEAD_DIM), BF),
             scratch((chips, z - 1, 2, count, HEAD_DIM), BF), scratch((2, wides) + wide_block, BF),
-            scratch((n,) + block, BF), scratch((2, n) + block, BF),
+            scratch((n,) + block, BF), scratch((2, 2 * n, wr // 2, cols + HEAD_DIM), BF),
             scratch((2, count, width), F32), scratch((2, count, wr), F32), scratch((chips, count, width), BF),
             scratch((chips, count, width), BF), scratch((chips - 1, count, width), BF),
             scratch((chips - 1, count, width), BF),
             scratch((n - 1,) + router_shape, BF), scratch(router_shape, F32), scratch((z,) + router_shape, F32),
             scratch(gains.shape, F32), scratch((n,) + gains.shape, F32), scratch(gains.shape, F32),
-            scratch((z,) + gains.shape, F32), dma(5),
+            scratch((z,) + gains.shape, F32), scratch((n, mix_near.shape[1], 512), BF),
+            scratch((z - 1, count, width), BF), scratch((z - 1, count, width), BF), dma(7),
             dma(chips), dma(chips), dma(chips), dma(chips), dma(chips), dma(chips), dma(chips, z - 1), dma(chips, z - 1),
-            dma(wides), dma(2, wides), dma(wides), dma(wides), dma(n - 1), dma(n - 1), dma(n), dma(2, n), dma(n), dma(n),
-            dma(n), dma(n - 1), dma(n - 1), dma(n - 1), dma(n - 1), dma(z - 1), dma(z - 1), dma(z - 1), dma(z - 1),
-            dma(chips), dma(chips), dma(chips - 1), dma(chips - 1),
+            dma(wides), dma(2, wides), dma(wides), dma(wides), dma(n - 1), dma(n - 1), dma(2 * n), dma(2, 2 * n), dma(2 * n),
+            dma(2 * n), dma(2 * n), dma(n - 1), dma(n - 1), dma(n - 1), dma(n - 1), dma(z - 1), dma(z - 1), dma(z - 1), dma(z - 1),
+            dma(chips), dma(chips), dma(chips - 1), dma(chips - 1), dma(n - 1), dma(n - 1), dma(z), dma(z), dma(n - 1), dma(n - 1),
         ],
-        ident, args, mib=62, out_specs=[ANY, ANY, ANY, VMEM, VMEM, VMEM],
+        ident, args, mib=62, out_specs=[ANY, ANY, ANY, VMEM, VMEM, VMEM, VMEM, ANY],
     )
 
 
@@ -1275,12 +1334,12 @@
 
 def expert_body(n_ctx, n_shard, group, half, tile,
                 rows, tail, code, w_gate, w_up, w_down, cot_in,
-                out, tail_out, mix_out, g_gate, g_up, g_down,
-                zrows, ztail, ready, tail_ready, recv, tail_recv, cot, back_rows, back_tail, land, tail_land, mix_land,
+                out, tail_out, mix_near, mix_far, g_gate, g_up, g_down,
+                zrows, ztail, ready, tail_ready, recv, tail_recv, cot, back_rows, back_tail, land, tail_land,
                 hidden, grad_gate, grad_up, work, slot_dot, table, tail_value,
-                zrecv, tsend, trecv, mrecv, stage, stage_d, local,
+                zrecv, tsend, trecv, stage, stage_d, local, ss_a, rs_a,
                 ss_z, rs_z, ss_t, rs_t, ss_x, rs_x, ss_y, rs_y, ss_d, rs_d, ss_e, rs_e, ss_m, rs_m,
-                ss_fz, rs_fz, ss_ft, rs_ft, ss_fm, rs_fm, ss_st, ss_sd):
+                ss_fz, rs_fz, ss_ft, rs_ft, ss_st, ss_sd):
     c, s, parity, sibling, others, layers = here(n_ctx, n_shard)
     count, width = rows.shape
     few = tail.shape[1]
@@ -1300,47 +1359,93 @@
     for item in loads:
         item.start()
     greet(others, layers)
-    fans = [
-        Fan(n_ctx, c, lambda d: ztail.at[flip_bits(c, d)], ss_t, rs_t, True),
-        Fan(n_ctx, c, lambda d: zrows.at[flip_bits(c, d)], ss_z, rs_z, True),
-    ]
-    fans[0].send(0, tail)
-    fans[1].send(0, rows)
-
-    sent = {}
-    seen = set()
+    fan = Fan(n_ctx, c, lambda d: ztail.at[flip_bits(c, d)], ss_t, rs_t, True)
+    fan.send(0, tail)
+    near_layer, far_layer = flip_bits(c, 1), flip_bits(c, 2)
+    sides = [slice(0, width // 2), slice(width // 2, width)]
+    near = push(rows, zrows.at[c], ss_z.at[0], rs_z.at[0], ctx=near_layer)
+    near.start()
+    away = [push(rows.at[:, side], zrows.at[c, :, side], ss_z.at[1 + n], rs_z.at[1 + n], ctx=far_layer)
+            for n, side in enumerate(sides)]
+    passed = [push(zrows.at[far_layer, :, side], zrows.at[far_layer, :, side], ss_z.at[3 + n], rs_z.at[3 + n],
+                   ctx=near_layer) for n, side in enumerate(sides)]
+
+    sent = {0: [], 1: []}
+    early = (slots // group) // 16 * 16
+    place = lax.rem(c, group)
+    early_at = pl.multiple_of(place * (slots - early), 16)
+    late_at = pl.multiple_of((1 - place) * early, 16)
+
+    def some_slots(rows_code, first, amount):
+        places = (lax.broadcasted_iota(jnp.int32, (amount, rows_code.shape[1]), 0) + first).astype(F32)
+        return jnp.concatenate(
+            [(places == rows_code[e : e + 1, :]).astype(BF) for e in range(n_shard)], axis=0
+        )
+
+    own_code = code[lax.div(c, group), :, pl.ds(pl.multiple_of(place * count, count), count)]
+    early_picks = some_slots(own_code, early_at, early)
+
+    @pl.loop(0, width // tile)
+    def _(j):
+        cols = pl.ds(pl.multiple_of(j * tile, tile), tile)
+        moved = jnp.dot(early_picks, rows[:, cols], preferred_element_type=F32).astype(BF)
+        ready[0, :, pl.ds(early_at, early), cols] = moved.reshape(n_shard, early, tile)
+
+    for i, peer in enumerate(others):
+        sent[0].append(push(ready.at[0, peer, pl.ds(early_at, early)], recv.at[0, s, pl.ds(early_at, early)],
+                            ss_a.at[i], rs_a.at[i], shard=peer))
+        sent[0][-1].start()
     loads[0].wait()
     loads[1].wait()
+    near.wait_send()
+    away[0].start()
+    near.wait_recv()
     for k in range(groups):
         at = flip_bits(lax.div(c, group), k)
-        picks = slot_table(code[at], slots)
-        table[k] = picks.T
-        for d in fans[0].order():
-            if d < (k + 1) * group and d not in seen:
-                fans[0].arrival(d)
-                fans[1].arrival(d)
-                seen.add(d)
+        whole = slot_table(code[at], slots)
+        table[k] = whole.T
+        for d in (2, 3) if k else (1,):
+            fan.arrival(d)
         first = pl.multiple_of(at * group, group)
         block = ztail[pl.ds(first, group)].reshape(group * count, few)
-        tail_ready[k] = jnp.dot(picks, block, preferred_element_type=F32).astype(BF).reshape(n_shard, slots, few)
-
-        @pl.loop(0, width // tile)
-        def _(j):
-            cols = pl.ds(pl.multiple_of(j * tile, tile), tile)
-            block = zrows[pl.ds(first, group), :, cols].reshape(group * count, tile)
-            moved = jnp.dot(picks, block, preferred_element_type=F32).astype(BF)
-            ready[k, :, :, cols] = moved.reshape(n_shard, slots, tile)
-
-        sent[k] = []
-        for i, peer in enumerate(others):
-            sent[k].append(push(ready.at[k, peer], recv.at[k, s], ss_x.at[k, i], rs_x.at[k, i], shard=peer))
-            sent[k].append(push(tail_ready.at[k, peer], tail_recv.at[k, s], ss_y.at[k, i], rs_y.at[k, i], shard=peer))
-        sent[k].append(pltpu.make_async_copy(ready.at[k, s], recv.at[k, s], local.at[2 + 2 * k]))
-        sent[k].append(pltpu.make_async_copy(tail_ready.at[k, s], tail_recv.at[k, s], local.at[3 + 2 * k]))
-        for item in sent[k]:
-            item.start()
-    for fan in fans:
-        fan.drain()
+        tail_ready[k] = jnp.dot(whole, block, preferred_element_type=F32).astype(BF).reshape(n_shard, slots, few)
+        amount = slots if k else slots - early
+        begin = 0 if k else late_at
+        span = pl.ds(begin, amount)
+        picks = some_slots(code[at], begin, amount)
+        for n, side in enumerate(sides if k else [slice(0, width)]):
+            if k:
+                if n == 0:
+                    away[0].wait_send()
+                    away[1].start()
+                away[n].wait_recv()
+                passed[n].start()
+                passed[n].wait_recv()
+
+            @pl.loop(side.start // tile, side.stop // tile)
+            def _(j):
+                cols = pl.ds(pl.multiple_of(j * tile, tile), tile)
+                block = zrows[pl.ds(first, group), :, cols].reshape(group * count, tile)
+                moved = jnp.dot(picks, block, preferred_element_type=F32).astype(BF)
+                ready[k, :, span, cols] = moved.reshape(n_shard, amount, tile)
+
+            fresh = []
+            for i, peer in enumerate(others):
+                fresh.append(push(ready.at[k, peer, span, side], recv.at[k, s, span, side],
+                                  ss_x.at[k + n, i], rs_x.at[k + n, i], shard=peer))
+            if n == 0:
+                for i, peer in enumerate(others):
+                    fresh.append(push(tail_ready.at[k, peer], tail_recv.at[k, s], ss_y.at[k, i], rs_y.at[k, i], shard=peer))
+                fresh.append(pltpu.make_async_copy(tail_ready.at[k, s], tail_recv.at[k, s], local.at[3 + 2 * k]))
+            if n == k:
+                fresh.append(pltpu.make_async_copy(ready.at[k, s], recv.at[k, s], local.at[2 + 2 * k]))
+            for item in fresh:
+                item.start()
+            sent[k] += fresh
+    fan.drain()
+    away[1].wait_send()
+    for item in passed:
+        item.wait_send()
     for item in loads[2:]:
         item.wait()
 
@@ -1349,24 +1454,24 @@
     column = lax.broadcasted_iota(jnp.int32, (1, few), 1)
     is_coarse, is_fine = column == expert, column == experts + expert
 
-    def send_back(src, dst, k, e, ss, rs):
+    def send_back(src, dst, e, ss, rs):
         @pl.when(s != e)
         def _():
-            push(src.at[k, e], dst.at[k, s], ss.at[k, e], rs.at[k, s], shard=e).start()
+            push(src.at[e], dst.at[s], ss.at[e], rs.at[s], shard=e).start()
 
         @pl.when(s == e)
         def _():
-            pltpu.make_async_copy(src.at[k, e], dst.at[k, e], rs.at[k, e]).start()
-
-    def wait_back(src, dst, k, ss, rs):
+            pltpu.make_async_copy(src.at[e], dst.at[e], rs.at[e]).start()
+
+    def wait_back(src, dst, ss, rs):
         for e in range(n_shard):
             @pl.when(s != e)
             def _():
-                push(src.at[k, e], dst.at[k, e], ss.at[k, e], rs.at[k, e], shard=e).wait()
+                push(src.at[e], dst.at[e], ss.at[e], rs.at[e], shard=e).wait()
 
             @pl.when(s == e)
             def _():
-                pltpu.make_async_copy(src.at[k, e], dst.at[k, e], rs.at[k, e]).wait()
+                pltpu.make_async_copy(src.at[e], dst.at[e], rs.at[e]).wait()
 
     def experts_part(k, h):
         of = slice(h * half, (h + 1) * half)
@@ -1417,18 +1522,24 @@
             gx += lax.dot_general(grad_up[r, :], w_up[cols, :], (((1,), (1,)), ((), ())), preferred_element_type=F32)
             back_rows[k, of, :, cols] = gx.astype(BF).reshape(half, slots, tile)
 
+    def send_part(k, h):
         for e in range(h * half, (h + 1) * half):
-            send_back(back_rows, land, k, e, ss_d, rs_d)
-            send_back(back_tail, tail_land, k, e, ss_e, rs_e)
-
+            send_back(back_rows.at[k], land.at[k], e, ss_d.at[k], rs_d.at[k])
+            send_back(back_tail.at[k], tail_land.at[k], e, ss_e.at[k], rs_e.at[k])
+
+    halves = n_shard // half
     for k in range(groups):
         for item in sent[k]:
             item.wait()
-        for h in range(n_shard // half):
+        for h in range(halves):
             experts_part(k, h)
-    for k in reversed(range(groups)):
-        for e in range(n_shard):
-            send_back(ready, mix_land, k, e, ss_m, rs_m)
+            if k or h + 1 < halves:
+                send_part(k, h)
+    send_part(0, halves - 1)
+    for e in range(n_shard):
+        send_back(ready.at[groups - 1], mix_far, e, ss_m, rs_m)
+    keep = pltpu.make_async_copy(ready.at[0], mix_near, local.at[0])
+    keep.start()
 
     everything = groups * n_shard * slots
 
@@ -1481,32 +1592,33 @@
         place = lax.rem(flip_bits(c, d), group)
         return ref[pl.ds(pl.multiple_of(place * count, count), count), :]
 
-    def fold_group(k, fold, ref, into):
-        for d in sorted(range(k * group, (k + 1) * group), key=lambda d: (lowest(d) or n_ctx, d)):
-            if d:
-                fold.give(d, fold.take(d, part(ref, d)) if lowest(d) > 1 else part(ref, d))
-            else:
-                into[...] = part(ref, 0)
-
-    fold = Fold(c, zrows, zrecv, ss_fz, rs_fz)
+    folds = [Fold(c, zrows.at[:, :, side], zrecv.at[:, :, side], ss_fz.at[n], rs_fz.at[n]) for n, side in enumerate(sides)]
     tail_fold = Fold(c, tsend, trecv, ss_ft, rs_ft)
-    mix_fold = Fold(c, zrows, mrecv, ss_fm, rs_fm, {3: 3, 2: 0, 1: 2}, {2: (fold, 1), 1: (fold, 3)})
-    for k in range(groups):
-        wait_back(back_rows, land, k, ss_d, rs_d)
-        wait_back(back_tail, tail_land, k, ss_e, rs_e)
+    for k in reversed(range(groups)):
+        wait_back(back_rows.at[k], land.at[k], ss_d.at[k], rs_d.at[k])
+        wait_back(back_tail.at[k], tail_land.at[k], ss_e.at[k], rs_e.at[k])
         local_sums(k, land)
         tail_value[...] = jnp.dot(table[k], tail_land[k].reshape(n_shard * slots, few), preferred_element_type=F32)
-        fold_group(k, tail_fold, tail_value, tail_out)
-        fold_group(k, fold, value, out)
-    for k in reversed(range(groups)):
-        wait_back(ready, mix_land, k, ss_m, rs_m)
-        local_sums(k, mix_land)
-        fold_group(k, mix_fold, value, mix_out)
-    out[...] = fold.take(0, out[...])
-    tail_out[...] = tail_fold.take(0, tail_out[...])
-    mix_out[...] = mix_fold.take(0, mix_out[...])
-    for item in (fold, tail_fold, mix_fold):
-        item.drain()
+        if k:
+            tail_fold.give(3, part(tail_value, 3))
+            folds[0].give(3, part(value, 3)[:, sides[0]])
+            folds[0].items[3].wait_send()
+            folds[0].left.add(3)
+            folds[1].give(3, part(value, 3)[:, sides[1]])
+            for fold, side in zip(folds, sides):
+                fold.give(2, fold.take(2, part(value, 2)[:, side]))
+            tail_fold.give(2, tail_fold.take(2, part(tail_value, 2)))
+        else:
+            tail_fold.give(1, part(tail_value, 1))
+            for fold, side in zip(folds, sides):
+                fold.give(1, part(value, 1)[:, side])
+    for fold, side in zip(folds, sides):
+        out[:, side] = fold.take(0, part(value, 0)[:, side])
+    tail_out[...] = tail_fold.take(0, part(tail_value, 0))
+    for fold in folds + [tail_fold]:
+        fold.drain()
+    wait_back(ready.at[groups - 1], mix_far, ss_m, rs_m)
+    keep.wait()
 
 
 def run_experts(n_ctx, n_shard, group, capacity, rows, tail, code, w_gate, w_up, w_down, cot_rows, ident):
@@ -1520,22 +1632,23 @@
     return call(
         functools.partial(expert_body, z, n, group, half, 512),
         [
-            sds((count, width), F32), sds((count, few), F32), sds((count, width), F32),
+            sds((count, width), F32), sds((count, few), F32), sds((n, slots, width), BF), sds((n, slots, width), BF),
             sds((width, inner), BF), sds((width, inner), BF), sds((inner, width), BF),
         ],
         [VMEM] * 6 + [ANY],
         [
             scratch((z, count, width), BF), scratch((z, count, few), BF), scratch(wide, BF), scratch(thin, BF),
             scratch(wide, BF), scratch(thin, BF), scratch(wide, BF), scratch(wide, BF), scratch(thin, BF),
-            scratch(wide, BF), scratch(thin, BF), scratch(wide, BF),
+            scratch(wide, BF), scratch(thin, BF),
             scratch((everything, inner), BF), scratch((everything, inner), BF), scratch((everything, inner), BF),
             scratch((max(chunk, group * count), max(2 * inner, width)), F32), scratch((chunk, 1), F32),
             scratch((groups, group * count, n * slots), BF),
             scratch((group * count, few), F32), scratch((z - 1, count, width), BF),
-            scratch((z - 1, count, few), BF), scratch((z - 1, count, few), BF), scratch((z - 1, count, width), BF),
-            scratch((2, 256, inner), BF), scratch((inner, 256), BF), dma(2 + 3 * groups),
-        ] + [dma(z)] * 4 + [dma(groups, n - 1)] * 4 + [dma(groups, n)] * 6 + [dma(z)] * 6 + [dma(2), DMA],
-        ident, (rows, tail, code, w_gate, w_up, w_down, cot_rows), mib=63, out_specs=[VMEM] * 3 + [ANY] * 3,
+            scratch((z - 1, count, few), BF), scratch((z - 1, count, few), BF),
+            scratch((2, 256, inner), BF), scratch((inner, 256), BF), dma(2 + 3 * groups), dma(n - 1), dma(n - 1),
+        ] + [dma(5)] * 2 + [dma(z)] * 2 + [dma(groups + 1, n - 1)] * 2 + [dma(groups, n - 1)] * 2 + [dma(groups, n)] * 4
+        + [dma(n)] * 2 + [dma(2, z)] * 2 + [dma(z)] * 2 + [dma(2), DMA],
+        ident, (rows, tail, code, w_gate, w_up, w_down, cot_rows), mib=62, out_specs=[VMEM] * 2 + [ANY] * 5,
     )
 
 
@@ -1680,9 +1793,9 @@
 
     gates_two = jnp.concatenate(two_parts(gates), axis=1)
     gates_two = jnp.pad(gates_two, ((0, 0), (0, tail_cols - 2 * experts)))
-    small = plane * width <= 2**21 and ctx_count == 4
+    small = plane * width <= 2**21 and ctx_count == 4 and group == 2
     if small:
-        grad_second, back_tail, mixture, grad_w_gate, grad_w_up, grad_w_down = run_experts(
+        grad_second, back_tail, mix_near, mix_far, grad_w_gate, grad_w_up, grad_w_down = run_experts(
             ctx_count, shard_count, group, capacity, second_b, gates_two, code, w_gate[0], w_up[0], w_down[0],
             upstream_rows, 3,
         )
@@ -1727,7 +1840,6 @@
             ctx_count, shard_count, group, grad_received.astype(BF).reshape(block_shape + (width,)),
             tail.reshape(block_shape + (tail_cols,)), mix_back, code, 4,
         )
-    mixed = (middle + mixture).astype(BF)
     grad_gates = back_tail[:, :experts] + back_tail[:, experts : 2 * experts]
     grad_logits_b = (
         gates * (grad_gates - jnp.sum(gates * grad_gates, axis=-1, keepdims=True))
@@ -1742,11 +1854,12 @@
     router_parts = jnp.swapaxes(router_part.reshape(experts, shard_count, wrows), 0, 1)
     if small:
         gains = jnp.concatenate([jnp.zeros((1, width), F32), grad_ffn_gain[None], jnp.zeros((6, width), F32)])
-        q_sum, kv_sum, out_sum, router_sum, gains, grad_input_part = back(
-            ctx_count, shard_count, heads,
+        q_sum, kv_sum, out_sum, router_sum, gains, grad_input_part, mixture, unused = back(
+            ctx_count, shard_count, group, heads,
             (
                 grad_proj_b, queries, kv_all, attn_rows, query_pre, kv_pre, w_out, normed_all, w_mine,
                 cosine, sine, bias, query_gain[None], key_gain[None], tokens[0], attn_gain[None], gains, router_parts,
+                mix_near, mix_far, code,
             ),
             5,
         )
@@ -1812,6 +1925,7 @@
             ctx_count, shard_count, head_cols, grad_w, out_part.reshape(8, -1, width), router_parts, gains, grad_pre, w_mine,
             tokens[0], attn_gain[None], 8,
         )
+    mixed = (middle + mixture).astype(BF)
     grad_tokens = grad_middle + grad_input_part
     grad_attn_gain, grad_ffn_gain = gains[0], gains[1]
     grad_query_gain, grad_key_gain = gains[2, :HEAD_DIM], gains[2, HEAD_DIM : 2 * HEAD_DIM]

time: 635 us -> 602 us (0.948)
  Pallas kernels: 586 us -> 554 us
    pallas_call x3, Pallas kernels: 586 us -> 554 us  [call(): pl.pallas_call(body, out_shape=outs, in_specs=in_specs, out_specs=out_spe...]
where the time goes in v7:
time: 602 us; the launch traced here: 597 us
  Pallas kernels  554 us (92%)
  other arithmetic  30.4 us (5%)
  local copies, waits for them, and re-layouts  7.03 us (1%)
    pallas_call x3, Pallas kernels, call(): pl.pallas_call(body, out_shape=outs, in_specs=in_specs, out_specs=out_spe...  554 us

profile of v7, /device:TPU:0, one launch (start us, length us, event | category | flops | bytes accessed | tf_op | source)
XLA Modules:
  0.0 596.8 jit_solution(5434474184225054259)
XLA Ops:
  0.7 0.7 select_reduce_fusion.1
  1.5 0.7 select_reduce_fusion
  2.3 0.7 convert_reduce_fusion
  3.4 0.8 pad_maximum_fusion
  4.2 0.8 compare_select_fusion.bias
  5.0 142.6 %shard_map.263 = (bf16[8,128,2048]{2,1,0:T(8,128)(2,1)}, bf16[8,256,640]{2,1,0:T(8,128)(2,1)}, bf16[32,2048]{1,0:T(8,128)(2,1)}, f32[2,8,256]{2,1,0:T(8,128)}, b...) custom-call(bf16[128,2048]{1,0:T(8,128)(2,1)} %bitcast.70, ...), custom_call_target="tpu_custom_call" | custom-call | tf_op jit(solution)/shard_map/pallas_call | solution.py:119
  147.6 1.4 multiply_reduce_fusion.2
  149.0 1.4 multiply_convert_fusion.rows
  150.4 1.4 fusion.22
  152.1 0.7 fusion.4.tail
  152.8 199.9 %shard_map.264 = (f32[128,2048]{1,0:T(8,128)}, f32[128,128]{1,0:T(8,128)}, bf16[8,80,2048]{2,1,0:T(8,128)(2,1)}, bf16[8,80,2048]{2,1,0:T(8,128)(2,1)}, bf16[2048...) custom-call(bf16[128,2048]{1,0:T(8,128)(2,1)} %copy-done.2, bf16[128,128]{1,0:T(8,128)(2,1)} %fusion.4.tail, ...), custom_call_target="tpu_custom_call" | custom-call | tf_op jit(solution)/shard_map/pallas_call | solution.py:119
  352.7 1.1 multiply_reduce_fusion.3
  353.8 1.0 multiply_convert_fusion.1
  354.8 1.3 convolution_convert_fusion
  356.1 1.7 multiply_reduce_fusion
  357.9 0.7 copy.54
  358.6 0.7 maximum_maximum_fusion.gains
  359.3 1.2 fusion.17.grad_out
  360.5 211.4 %shard_map.265 = (bf16[256,4096]{1,0:T(8,128)(2,1)}, bf16[8,256,128]{2,1,0:T(8,128)(2,1)}, bf16[512,2048]{1,0:T(8,128)(2,1)}, f32[32,256]{1,0:T(8,128)}, f32[8,2...) custom-call(bf16[128,2048]{1,0:T(8,128)(2,1)} %fusion.17.grad_out, ...), custom_call_target="tpu_custom_call" | custom-call | tf_op jit(solution)/shard_map/pallas_call | solution.py:119
  571.9 3.5 add_bitcast_fusion
  575.4 1.2 slice_bitcast_fusion
  576.6 1.5 fusion.21
  578.3 0.3 copy.44
  578.6 0.8 copy.52
  579.8 0.8 copy.53
  580.6 2.5 convert_element_type.61
  583.1 2.5 convert_element_type.62
  585.7 0.3 copy-done.6
  586.0 3.2 bitcast_convert_fusion.2
  589.2 3.2 bitcast_convert_fusion.1
  592.4 3.6 bitcast_convert_fusion
  596.0 0.6 copy.56
  (43 shorter events, 1.4 us)
Async XLA Ops:
  4.9 144.0 %copy-start.11 = (f32[2048]{0:T(1024)S(1)}, f32[2048]{0:T(1024)}, u32[]{:S(2)}) copy-start(f32[2048]{0:T(1024)} %param.27) | copy-start | bytes 24580
  150.3 2.4 copy-start.2
  152.8 203.3 %copy-start = (f32[128,2048]{1,0:T(8,128)S(1)}, f32[128,2048]{1,0:T(8,128)}, u32[]{:S(2)}) copy-start(f32[128,2048]{1,0:T(8,128)} %get-tuple-element.39) | copy-start | bytes 3145732
  152.8 203.3 %copy-start.10 = (bf16[32,2048]{1,0:T(8,128)(2,1)S(1)}, bf16[32,2048]{1,0:T(8,128)(2,1)}, u32[]{:S(2)}) copy-start(bf16[32,2048]{1,0:T(8,128)(2,1)} %get-tuple-element.40) | copy-start | bytes 393220
  352.7 6.6 %copy-start.3 = (bf16[1,128,2048]{2,1,0:T(8,128)(2,1)S(1)}, bf16[1,128,2048]{2,1,0:T(8,128)(2,1)}, u32[]{:S(2)}) copy-start(bf16[1,128,2048]{2,1,0:T(8,128)(2,1)} %param.17) | copy-start | bytes 1572868
  357.8 1.5 copy-start.1
  571.9 6.2 %copy-start.9 = (bf16[8,256,128]{2,1,0:T(8,128)(2,1)S(1)}, bf16[8,256,128]{2,1,0:T(8,128)(2,1)}, u32[]{:S(2)}) copy-start(bf16[8,256,128]{2,1,0:T(8,128)(2,1)} %get-tuple-element.58) | copy-start | bytes 1572868
  578.2 2.4 copy-start.8
  580.6 2.5 copy-start.7
  583.1 2.9 copy-start.6
  586.0 3.2 copy-start.5
  589.2 3.2 copy-start.4
  592.4 3.6 copy-start.12

commit v8 on v7

--- a/solution.py
+++ b/solution.py
@@ -109,6 +109,11 @@
         item.start()
         self.items[d] = item
 
+    def give_as_is(self, d, ref):
+        self.items[d] = push(ref, self.received.at[d - 1], self.ss.at[d], self.rs.at[d],
+                             ctx=flip_bits(self.c, lowest(d)))
+        self.items[d].start()
+
     def drain(self):
         for d, item in self.items.items():
             if d not in self.left:
@@ -128,6 +133,14 @@
     )(*args)
 
 
+def by_core(s, n_shard):
+    return lax.rem(s, 2) * (n_shard // 2) + lax.div(s, 2)
+
+
+def from_core(place, n_shard):
+    return place % (n_shard // 2) * 2 + place // (n_shard // 2)
+
+
 def slot_table(code, slots):
     places = lax.broadcasted_iota(jnp.int32, (slots, code.shape[1]), 0).astype(F32)
     return jnp.concatenate(
@@ -144,7 +157,7 @@
     return value * scale, scale
 
 
-def front_body(n_ctx, n_shard, group, capacity, heads, kv_heads, tile,
+def front_body(n_ctx, n_shard, group, capacity, heads, kv_heads, paired, tile,
                tokens, gain, w_query, key_w, value_w, routes, router, cot, cosine, sine, bias, q_gain, k_gain, w_out,
                rows_out, w_all_out, router_all, code, cot_rows, qpre_out, kvpre, q_out, kv_out, attn_out, mid,
                own_rows, rows_all, w_all, zroutes, zcot, ready, qpre, q, kv, attn,
@@ -251,13 +264,14 @@
             value = jnp.dot(table, block, preferred_element_type=F32).astype(BF)
             ready[k, :, :, part] = value.reshape(n_shard, slots, tile)
 
+    place = by_core(s, n_shard) if paired else s
     cot_waits = []
     for k in range(groups):
         for i, peer in enumerate(others):
-            item = push(ready.at[k, peer], cot_rows.at[k, s], ss_x.at[k, i], rs_x.at[k, i], shard=peer)
+            item = push(ready.at[k, peer], cot_rows.at[k, place], ss_x.at[k, i], rs_x.at[k, i], shard=peer)
             item.start()
             cot_waits.append(item)
-        item = pltpu.make_async_copy(ready.at[k, s], cot_rows.at[k, s], local.at[6 + k])
+        item = pltpu.make_async_copy(ready.at[k, s], cot_rows.at[k, place], local.at[6 + k])
         item.start()
         cot_waits.append(item)
 
@@ -375,7 +389,7 @@
         item.wait()
 
 
-def front(n_ctx, n_shard, group, capacity, kv_heads, args, ident):
+def front(n_ctx, n_shard, group, capacity, kv_heads, paired, args, ident):
     tokens, gain, w_query, key_w, value_w, routes, router, cot = args[:8]
     n, z = n_shard, n_ctx
     count, width = tokens.shape
@@ -385,7 +399,7 @@
     sds = jax.ShapeDtypeStruct
     dma = lambda *shape: DMA(shape)
     return call(
-        functools.partial(front_body, z, n, group, capacity, heads, kv_heads, 512),
+        functools.partial(front_body, z, n, group, capacity, heads, kv_heads, paired, 512),
         [
             sds((n, count, width), BF), sds((n, wr, cols + HEAD_DIM), BF), sds((router.shape[0], width), BF),
             sds((groups, n, group * count), F32), sds((groups, n, slots, width), BF), sds((n, count, cols), F32),
@@ -722,10 +736,10 @@
 
 
 def back_body(n_ctx, n_shard, group, heads, wides,
-              grad_out, q, kv, attn, qpre, kvpre, w_out, rows_in, w_all, cosine, sine, bias, q_gain, k_gain,
-              tokens, gain, gains, router, mix_near, mix_far, code,
+              grad_out, q_in, kv_in, attn_in, qpre_in, kvpre_in, w_out_in, rows_in, w_all_in, cosine, sine, bias, q_gain, k_gain,
+              tokens, gain, gains, router, mix_near, mix_part, code,
               q_out, kv_out, wide_out, router_out, gains_out, rows_out, mix_out, mix_land,
-              grads, attn_t, grad_heads, ds_all, p_all, parts, pre, q_sum, k_sum, wide, weights,
+              q, kv, attn, qpre, kvpre, w_out, w_all, loads, grads, attn_t, grad_heads, ds_all, p_all, parts, pre, q_sum, k_sum, wide, weights,
               sibk, zsend, zrecv, wide_landing, pieces, landing,
               own_part, pair, to_sib, sib, to_chip, got, router_in, router_mid, router_far,
               gains_own, gains_in, gains_mid, gains_far, mix_rows, mix_sent, mix_recv, local,
@@ -753,6 +767,11 @@
         pltpu.make_async_copy(rows_in, grads, local.at[1]),
     ]
     own_copies[0].start()
+    load = [
+        pltpu.make_async_copy(a, b, loads.at[n])
+        for n, (a, b) in enumerate(((q_in, q), (kv_in, kv), (w_out_in, w_out), (qpre_in, qpre), (attn_in, attn),
+                                    (kvpre_in, kvpre), (w_all_in, w_all)))
+    ]
     greet(others, layers)
 
     first, forwards = {}, {}
@@ -761,6 +780,8 @@
         first[d].start()
     forwards[0] = push(grad_out, grads.at[s], ss_fwd.at[0], rs_fwd.at[0], shard=sibling)
     forwards[0].start()
+    for item in load:
+        item.start()
     small = []
     for i, peer in enumerate(others):
         item = push(router.at[peer], router_in.at[i], ss_r.at[i], rs_r.at[i], shard=peer)
@@ -792,24 +813,23 @@
             value = jnp.dot(table, mix_rows[...].reshape(n_shard * slots, tile), preferred_element_type=F32)
             own_part[:, :, part] = value.reshape(2, count, tile)
 
-    def mix_part(d):
+    def near_part(d):
         return own_part[lax.rem(flip_bits(c, d), group)]
 
     def mix_send():
         for i, peer in enumerate(others):
-            push(mix_near.at[peer], mix_land.at[s], ss_m.at[i], rs_m.at[i], shard=peer).start()
-        pltpu.make_async_copy(mix_near.at[s], mix_land.at[s], local.at[6]).start()
+            push(mix_near.at[by_core(peer, n_shard)], mix_land.at[s], ss_m.at[i], rs_m.at[i], shard=peer).start()
+        pltpu.make_async_copy(mix_near.at[by_core(s, n_shard)], mix_land.at[s], local.at[6]).start()
 
     def mix_last():
         for i, peer in enumerate(others):
-            push(mix_near.at[peer], mix_land.at[s], ss_m.at[i], rs_m.at[i], shard=peer).wait()
-        pltpu.make_async_copy(mix_near.at[s], mix_land.at[s], local.at[6]).wait()
+            push(mix_near.at[by_core(peer, n_shard)], mix_land.at[s], ss_m.at[i], rs_m.at[i], shard=peer).wait()
+        pltpu.make_async_copy(mix_near.at[by_core(s, n_shard)], mix_land.at[s], local.at[6]).wait()
         mix_sums(0, mix_land)
-        mix_fold.give(1, mix_part(1))
-        mix_out[...] = mix_part(0)
-
-    mix_sums(1, mix_far)
-    mix_fold.give(3, mix_part(3))
+        mix_fold.give(1, near_part(1))
+        mix_out[...] = near_part(0)
+
+    mix_fold.give_as_is(3, mix_part.at[1])
     near, far = {}, {}
 
     def seqs_of(d):
@@ -949,8 +969,9 @@
         if n >= lag:
             steps[n - lag][0].second_half(steps[n - lag][1])
 
-    attn_t[...] = attn[...].reshape(n_shard * count, cols).T
     step = width // wides
+    for item in load[:4]:
+        item.wait()
     for d in range(chips):
         if d:
             first[d].wait()
@@ -962,6 +983,9 @@
         forwards[d].wait()
         if d + 1 == chips:
             mix_send()
+            for item in load[4:]:
+                item.wait()
+            attn_t[...] = attn[...].reshape(n_shard * count, cols).T
             for j in range(wides):
                 block = grads[:, :, j * step : (j + 1) * step].reshape(n_shard * count, step)
                 wide[j] = jnp.dot(attn_t[...], block, preferred_element_type=F32).astype(BF)
@@ -969,7 +993,7 @@
                     wide_line.outermost(j)
         attention_back(d)
         if d == 0:
-            mix_fold.give(2, mix_fold.take(2, mix_part(2)))
+            mix_fold.give(2, mix_fold.take(2, mix_part[0].astype(F32)))
         if d:
             key_sum(d - 1)
 
@@ -1052,9 +1076,13 @@
         scaled = grad * gain[...]
         rows_out[...] = scale * (scaled - unit * jnp.mean(scaled * unit, axis=-1, keepdims=True))
         gains_own[...] = gains[...]
-        gains_own[0:1] = jnp.sum(grad * unit, axis=0, keepdims=True)
-        gains_own[2:3, 0:HEAD_DIM] = q_sum[...]
-        gains_own[2:3, HEAD_DIM : 2 * HEAD_DIM] = jnp.where(parity == 0, k_sum[...], jnp.zeros_like(k_sum))
+        summed = jnp.sum(grad * unit, axis=0, keepdims=True)
+        lanes = gains.shape[1]
+        for n in range(width // lanes):
+            gains_own[n : n + 1] = summed[:, n * lanes : (n + 1) * lanes]
+        n = 2 * width // lanes
+        gains_own[n : n + 1] = q_sum[...]
+        gains_own[n + 1 : n + 2] = jnp.where(parity == 0, k_sum[...], jnp.zeros_like(k_sum))
         mine = pltpu.make_async_copy(gains_own, gains_in.at[s], local.at[2])
         mine.start()
         gain_sends.append(mine)
@@ -1069,9 +1097,10 @@
         gains_mid[...] = gains_in[0]
         for i in range(1, n_shard):
             gains_mid[...] += gains_in[i]
-        router_mid[...] = router[s].astype(F32)
+        total = router[s].astype(F32)
         for i in range(n_shard - 1):
-            router_mid[...] += router_in[i].astype(F32)
+            total = total + router_in[i].astype(F32)
+        router_mid[...] = total.astype(BF)
         for i, layer in enumerate(layers):
             push(gains_mid, gains_far.at[c], ss_h.at[i], rs_h.at[i], ctx=layer).start()
             push(router_mid, router_far.at[c], ss_t.at[i], rs_t.at[i], ctx=layer).start()
@@ -1085,10 +1114,10 @@
             push(gains_mid, gains_far.at[c], ss_h.at[i], rs_h.at[i], ctx=layer).wait()
             push(router_mid, router_far.at[c], ss_t.at[i], rs_t.at[i], ctx=layer).wait()
         gains_out[...] = gains_far[0]
-        router_out[...] = router_far[0]
+        router_out[...] = router_far[0].astype(F32)
         for i in range(1, n_ctx):
             gains_out[...] += gains_far[i]
-            router_out[...] += router_far[i]
+            router_out[...] += router_far[i].astype(F32)
 
     side = []
     for at in range(chips):
@@ -1096,7 +1125,7 @@
         if at:
             side.append(functools.partial(chip_sum, at - 1))
     count_steps = len(steps) + lag
-    late = {16: last_sum, 18: mix_last, 21: small_plane}
+    late = {21: last_sum, 23: mix_last, 26: small_plane}
     for n in range(3, count_steps):
         advance(n)
         if side:
@@ -1128,8 +1157,8 @@
             sds((wr, n * cols), BF), sds((n, wr, HEAD_DIM), BF), sds((cols, width), BF), sds(router_shape, F32),
             sds(gains.shape, F32), sds((count, width), F32), sds((count, width), F32), sds(mix_near.shape, BF),
         ],
-        [VMEM] * 7 + [ANY] + [VMEM] * 10 + [ANY, ANY, VMEM],
-        [
+        [VMEM] + [ANY] * 8 + [VMEM] * 9 + [ANY, VMEM, VMEM],
+        [scratch(item.shape, item.dtype) for item in args[1:7] + args[8:9]] + [dma(7)] + [
             scratch((n, count, width), BF), scratch((cols, n * count), BF),
             scratch((2, count, cols), BF), scratch((heads * count, keys), BF), scratch((heads * count, keys), BF),
             scratch((2, n, z, count, HEAD_DIM), BF), scratch((n, count, cols + HEAD_DIM), BF),
@@ -1141,7 +1170,7 @@
             scratch((2, count, width), F32), scratch((2, count, wr), F32), scratch((chips, count, width), BF),
             scratch((chips, count, width), BF), scratch((chips - 1, count, width), BF),
             scratch((chips - 1, count, width), BF),
-            scratch((n - 1,) + router_shape, BF), scratch(router_shape, F32), scratch((z,) + router_shape, F32),
+            scratch((n - 1,) + router_shape, BF), scratch(router_shape, BF), scratch((z,) + router_shape, BF),
             scratch(gains.shape, F32), scratch((n,) + gains.shape, F32), scratch(gains.shape, F32),
             scratch((z,) + gains.shape, F32), scratch((n, mix_near.shape[1], 512), BF),
             scratch((z - 1, count, width), BF), scratch((z - 1, count, width), BF), dma(7),
@@ -1333,9 +1362,9 @@
 
 
 def expert_body(n_ctx, n_shard, group, half, tile,
-                rows, tail, code, w_gate, w_up, w_down, cot_in,
-                out, tail_out, mix_near, mix_far, g_gate, g_up, g_down,
-                zrows, ztail, ready, tail_ready, recv, tail_recv, cot, back_rows, back_tail, land, tail_land,
+                rows, tail, code, gate_in, up_in, down_in, cot_in,
+                out, tail_out, mix_near, mix_far, mix_part, g_gate, g_up, g_down,
+                w_gate, w_up, w_down, loaded, zrows, ztail, ready, tail_ready, recv, tail_recv, cot, back_rows, back_tail, land, tail_land,
                 hidden, grad_gate, grad_up, work, slot_dot, table, tail_value,
                 zrecv, tsend, trecv, stage, stage_d, local, ss_a, rs_a,
                 ss_z, rs_z, ss_t, rs_t, ss_x, rs_x, ss_y, rs_y, ss_d, rs_d, ss_e, rs_e, ss_m, rs_m,
@@ -1349,6 +1378,7 @@
     chunk = half * slots
     experts = n_ctx * n_shard
     expert = c * n_shard + s
+    mine = by_core(s, n_shard)
     loads = [
         pltpu.make_async_copy(rows, zrows.at[c], local.at[0]),
         pltpu.make_async_copy(tail, ztail.at[c], local.at[1]),
@@ -1356,8 +1386,6 @@
         pltpu.make_async_copy(cot_in.at[flip_bits(lax.div(c, group), k)], cot.at[k], local.at[2 + 2 * groups + k])
         for k in range(groups)
     ]
-    for item in loads:
-        item.start()
     greet(others, layers)
     fan = Fan(n_ctx, c, lambda d: ztail.at[flip_bits(c, d)], ss_t, rs_t, True)
     fan.send(0, tail)
@@ -1365,10 +1393,23 @@
     sides = [slice(0, width // 2), slice(width // 2, width)]
     near = push(rows, zrows.at[c], ss_z.at[0], rs_z.at[0], ctx=near_layer)
     near.start()
+    edge = jnp.logical_or(c == 0, c == n_ctx - 1)
     away = [push(rows.at[:, side], zrows.at[c, :, side], ss_z.at[1 + n], rs_z.at[1 + n], ctx=far_layer)
             for n, side in enumerate(sides)]
     passed = [push(zrows.at[far_layer, :, side], zrows.at[far_layer, :, side], ss_z.at[3 + n], rs_z.at[3 + n],
                    ctx=near_layer) for n, side in enumerate(sides)]
+
+    @pl.when(jnp.logical_not(edge))
+    def _():
+        for item in away:
+            item.start()
+
+    loads += [
+        pltpu.make_async_copy(a, b, loaded.at[n])
+        for n, (a, b) in enumerate(((gate_in, w_gate), (up_in, w_up), (down_in, w_down)))
+    ]
+    loads[0].start()
+    loads[1].start()
 
     sent = {0: [], 1: []}
     early = (slots // group) // 16 * 16
@@ -1392,13 +1433,20 @@
         ready[0, :, pl.ds(early_at, early), cols] = moved.reshape(n_shard, early, tile)
 
     for i, peer in enumerate(others):
-        sent[0].append(push(ready.at[0, peer, pl.ds(early_at, early)], recv.at[0, s, pl.ds(early_at, early)],
+        sent[0].append(push(ready.at[0, peer, pl.ds(early_at, early)], recv.at[0, mine, pl.ds(early_at, early)],
                             ss_a.at[i], rs_a.at[i], shard=peer))
         sent[0][-1].start()
+    for item in loads[2:]:
+        item.start()
     loads[0].wait()
     loads[1].wait()
     near.wait_send()
-    away[0].start()
+
+    @pl.when(edge)
+    def _():
+        for item in away:
+            item.start()
+
     near.wait_recv()
     for k in range(groups):
         at = flip_bits(lax.div(c, group), k)
@@ -1416,10 +1464,9 @@
         for n, side in enumerate(sides if k else [slice(0, width)]):
             if k:
                 if n == 0:
-                    away[0].wait_send()
-                    away[1].start()
-                away[n].wait_recv()
-                passed[n].start()
+                    for m in range(2):
+                        away[m].wait_recv()
+                        passed[m].start()
                 passed[n].wait_recv()
 
             @pl.loop(side.start // tile, side.stop // tile)
@@ -1431,20 +1478,19 @@
 
             fresh = []
             for i, peer in enumerate(others):
-                fresh.append(push(ready.at[k, peer, span, side], recv.at[k, s, span, side],
+                fresh.append(push(ready.at[k, peer, span, side], recv.at[k, mine, span, side],
                                   ss_x.at[k + n, i], rs_x.at[k + n, i], shard=peer))
             if n == 0:
                 for i, peer in enumerate(others):
-                    fresh.append(push(tail_ready.at[k, peer], tail_recv.at[k, s], ss_y.at[k, i], rs_y.at[k, i], shard=peer))
-                fresh.append(pltpu.make_async_copy(tail_ready.at[k, s], tail_recv.at[k, s], local.at[3 + 2 * k]))
+                    fresh.append(push(tail_ready.at[k, peer], tail_recv.at[k, mine], ss_y.at[k, i], rs_y.at[k, i], shard=peer))
+                fresh.append(pltpu.make_async_copy(tail_ready.at[k, s], tail_recv.at[k, mine], local.at[3 + 2 * k]))
             if n == k:
-                fresh.append(pltpu.make_async_copy(ready.at[k, s], recv.at[k, s], local.at[2 + 2 * k]))
+                fresh.append(pltpu.make_async_copy(ready.at[k, s], recv.at[k, mine], local.at[2 + 2 * k]))
             for item in fresh:
                 item.start()
             sent[k] += fresh
     fan.drain()
-    away[1].wait_send()
-    for item in passed:
+    for item in away + passed:
         item.wait_send()
     for item in loads[2:]:
         item.wait()
@@ -1454,24 +1500,28 @@
     column = lax.broadcasted_iota(jnp.int32, (1, few), 1)
     is_coarse, is_fine = column == expert, column == experts + expert
 
-    def send_back(src, dst, e, ss, rs):
+    def send_back(src, dst, p, ss, rs):
+        e = from_core(p, n_shard)
+
         @pl.when(s != e)
         def _():
-            push(src.at[e], dst.at[s], ss.at[e], rs.at[s], shard=e).start()
+            push(src.at[p], dst.at[s], ss.at[e], rs.at[s], shard=e).start()
 
         @pl.when(s == e)
         def _():
-            pltpu.make_async_copy(src.at[e], dst.at[e], rs.at[e]).start()
+            pltpu.make_async_copy(src.at[p], dst.at[e], rs.at[e]).start()
 
     def wait_back(src, dst, ss, rs):
-        for e in range(n_shard):
+        for p in range(n_shard):
+            e = from_core(p, n_shard)
+
             @pl.when(s != e)
             def _():
-                push(src.at[e], dst.at[e], ss.at[e], rs.at[e], shard=e).wait()
+                push(src.at[p], dst.at[e], ss.at[e], rs.at[e], shard=e).wait()
 
             @pl.when(s == e)
             def _():
-                pltpu.make_async_copy(src.at[e], dst.at[e], rs.at[e]).wait()
+                pltpu.make_async_copy(src.at[p], dst.at[e], rs.at[e]).wait()
 
     def experts_part(k, h):
         of = slice(h * half, (h + 1) * half)
@@ -1523,9 +1573,9 @@
             back_rows[k, of, :, cols] = gx.astype(BF).reshape(half, slots, tile)
 
     def send_part(k, h):
-        for e in range(h * half, (h + 1) * half):
-            send_back(back_rows.at[k], land.at[k], e, ss_d.at[k], rs_d.at[k])
-            send_back(back_tail.at[k], tail_land.at[k], e, ss_e.at[k], rs_e.at[k])
+        for p in range(h * half, (h + 1) * half):
+            send_back(back_rows.at[k], land.at[k], p, ss_d.at[k], rs_d.at[k])
+            send_back(back_tail.at[k], tail_land.at[k], p, ss_e.at[k], rs_e.at[k])
 
     halves = n_shard // half
     for k in range(groups):
@@ -1536,8 +1586,8 @@
             if k or h + 1 < halves:
                 send_part(k, h)
     send_part(0, halves - 1)
-    for e in range(n_shard):
-        send_back(ready.at[groups - 1], mix_far, e, ss_m, rs_m)
+    for p in range(n_shard):
+        send_back(ready.at[groups - 1], mix_far, p, ss_m, rs_m)
     keep = pltpu.make_async_copy(ready.at[0], mix_near, local.at[0])
     keep.start()
 
@@ -1612,13 +1662,26 @@
             tail_fold.give(1, part(tail_value, 1))
             for fold, side in zip(folds, sides):
                 fold.give(1, part(value, 1)[:, side])
+    out[...] = part(value, 0)
+    wait_back(ready.at[groups - 1], mix_far, ss_m, rs_m)
+    keep.wait()
+    again = pltpu.make_async_copy(mix_far, ready.at[0], local.at[0])
+    again.start()
+    again.wait()
+
+    @pl.loop(0, width // tile)
+    def _(j):
+        cols = pl.ds(pl.multiple_of(j * tile, tile), tile)
+        block = ready[0, :, :, cols].reshape(n_shard * slots, tile)
+        value[:, cols] = jnp.dot(table[1], block, preferred_element_type=F32)
+
+    for d in (2, 3):
+        mix_part[d - 2] = part(value, d).astype(BF)
     for fold, side in zip(folds, sides):
-        out[:, side] = fold.take(0, part(value, 0)[:, side])
+        out[:, side] = fold.take(0, out[:, side])
     tail_out[...] = tail_fold.take(0, part(tail_value, 0))
     for fold in folds + [tail_fold]:
         fold.drain()
-    wait_back(ready.at[groups - 1], mix_far, ss_m, rs_m)
-    keep.wait()
 
 
 def run_experts(n_ctx, n_shard, group, capacity, rows, tail, code, w_gate, w_up, w_down, cot_rows, ident):
@@ -1633,10 +1696,11 @@
         functools.partial(expert_body, z, n, group, half, 512),
         [
             sds((count, width), F32), sds((count, few), F32), sds((n, slots, width), BF), sds((n, slots, width), BF),
-            sds((width, inner), BF), sds((width, inner), BF), sds((inner, width), BF),
+            sds((2, count, width), BF), sds((width, inner), BF), sds((width, inner), BF), sds((inner, width), BF),
         ],
-        [VMEM] * 6 + [ANY],
-        [
+        [VMEM] * 3 + [ANY] * 4,
+        [scratch(item.shape, BF) for item in (w_gate, w_up, w_down)] + [
+            dma(3),
             scratch((z, count, width), BF), scratch((z, count, few), BF), scratch(wide, BF), scratch(thin, BF),
             scratch(wide, BF), scratch(thin, BF), scratch(wide, BF), scratch(wide, BF), scratch(thin, BF),
             scratch(wide, BF), scratch(thin, BF),
@@ -1648,7 +1712,7 @@
             scratch((2, 256, inner), BF), scratch((inner, 256), BF), dma(2 + 3 * groups), dma(n - 1), dma(n - 1),
         ] + [dma(5)] * 2 + [dma(z)] * 2 + [dma(groups + 1, n - 1)] * 2 + [dma(groups, n - 1)] * 2 + [dma(groups, n)] * 4
         + [dma(n)] * 2 + [dma(2, z)] * 2 + [dma(z)] * 2 + [dma(2), DMA],
-        ident, (rows, tail, code, w_gate, w_up, w_down, cot_rows), mib=62, out_specs=[VMEM] * 2 + [ANY] * 5,
+        ident, (rows, tail, code, w_gate, w_up, w_down, cot_rows), mib=62, out_specs=[VMEM] * 2 + [ANY] * 2 + [VMEM] + [ANY] * 3,
     )
 
 
@@ -1742,6 +1806,7 @@
     while group * capacity % 16:
         group *= 2
     groups = ctx_count // group
+    small = plane * width <= 2**21 and ctx_count == 4 and group == 2
     slot_rows = shard_count * ctx_count * capacity
     block_shape = (shard_count, groups, group * capacity)
     row_ids = my_ctx * rows + jnp.arange(rows, dtype=jnp.int32)
@@ -1755,7 +1820,7 @@
     (
         normed_all, w_mine, router_all, code, upstream_rows, query_pre, kv_pre, queries, kv_all, attn_rows, middle,
     ) = front(
-        ctx_count, shard_count, group, capacity, KEY_VALUE_HEADS,
+        ctx_count, shard_count, group, capacity, KEY_VALUE_HEADS, small,
         (
             tokens[0], attn_gain[None], w_query, key_weight, value_weight, routes[0].T, w_router.T, upstream_b,
             cosine, sine, bias, query_gain[None], key_gain[None], w_out,
@@ -1793,9 +1858,8 @@
 
     gates_two = jnp.concatenate(two_parts(gates), axis=1)
     gates_two = jnp.pad(gates_two, ((0, 0), (0, tail_cols - 2 * experts)))
-    small = plane * width <= 2**21 and ctx_count == 4 and group == 2
     if small:
-        grad_second, back_tail, mix_near, mix_far, grad_w_gate, grad_w_up, grad_w_down = run_experts(
+        grad_second, back_tail, mix_near, unused, mix_part, grad_w_gate, grad_w_up, grad_w_down = run_experts(
             ctx_count, shard_count, group, capacity, second_b, gates_two, code, w_gate[0], w_up[0], w_down[0],
             upstream_rows, 3,
         )
@@ -1853,13 +1917,14 @@
 
     router_parts = jnp.swapaxes(router_part.reshape(experts, shard_count, wrows), 0, 1)
     if small:
-        gains = jnp.concatenate([jnp.zeros((1, width), F32), grad_ffn_gain[None], jnp.zeros((6, width), F32)])
+        gains = jnp.concatenate([jnp.zeros((width,), F32), grad_ffn_gain, jnp.zeros((8 * HEAD_DIM,), F32)])
+        gains = gains.reshape(-1, HEAD_DIM)
         q_sum, kv_sum, out_sum, router_sum, gains, grad_input_part, mixture, unused = back(
             ctx_count, shard_count, group, heads,
             (
                 grad_proj_b, queries, kv_all, attn_rows, query_pre, kv_pre, w_out, normed_all, w_mine,
                 cosine, sine, bias, query_gain[None], key_gain[None], tokens[0], attn_gain[None], gains, router_parts,
-                mix_near, mix_far, code,
+                mix_near, mix_part, code,
             ),
             5,
         )
@@ -1927,8 +1992,10 @@
         )
     mixed = (middle + mixture).astype(BF)
     grad_tokens = grad_middle + grad_input_part
-    grad_attn_gain, grad_ffn_gain = gains[0], gains[1]
-    grad_query_gain, grad_key_gain = gains[2, :HEAD_DIM], gains[2, HEAD_DIM : 2 * HEAD_DIM]
+    gains = gains.reshape(-1)
+    grad_attn_gain, grad_ffn_gain = gains[:width], gains[width : 2 * width]
+    grad_query_gain = gains[2 * width : 2 * width + HEAD_DIM]
+    grad_key_gain = gains[2 * width + HEAD_DIM : 2 * width + 2 * HEAD_DIM]
     grad_w_query = q_sum.astype(F32)
     grad_w_out = out_sum.reshape(head_cols, width).astype(F32)
     kinds = kv_sum.astype(F32).reshape(KEY_VALUE_HEADS, part_count, 2, wrows, HEAD_DIM)

time: 602 us -> 563 us (0.935)
  Pallas kernels: 554 us -> 512 us
    pallas_call x3, Pallas kernels: 554 us -> 512 us  [call(): pl.pallas_call(body, out_shape=outs, in_specs=in_specs, out_specs=out_spe...]
where the time goes in v8:
time: 563 us; the launch traced here: 553 us
  Pallas kernels  512 us (91%)
  other arithmetic  30.4 us (5%)
    pallas_call x3, Pallas kernels, call(): pl.pallas_call(body, out_shape=outs, in_specs=in_specs, out_specs=out_spe...  512 us

profile of v8, /device:TPU:0, one launch (start us, length us, event | category | flops | bytes accessed | tf_op | source)
XLA Modules:
  0.0 553.5 jit_solution(1416603516315923269)
XLA Ops:
  0.7 0.7 select_reduce_fusion.1
  1.4 0.7 select_reduce_fusion
  2.2 0.7 convert_reduce_fusion
  3.3 0.8 pad_maximum_fusion
  4.1 0.8 compare_select_fusion.bias
  4.9 142.6 %shard_map.263 = (bf16[8,128,2048]{2,1,0:T(8,128)(2,1)}, bf16[8,256,640]{2,1,0:T(8,128)(2,1)}, bf16[32,2048]{1,0:T(8,128)(2,1)}, f32[2,8,256]{2,1,0:T(8,128)}, b...) custom-call(bf16[128,2048]{1,0:T(8,128)(2,1)} %bitcast.72, ...), custom_call_target="tpu_custom_call" | custom-call | tf_op jit(solution)/shard_map/pallas_call | solution.py:124
  147.5 1.4 multiply_reduce_fusion.2
  148.9 1.4 multiply_convert_fusion.rows
  150.3 1.4 fusion.21
  152.0 0.7 fusion.4.tail
  152.7 173.0 %shard_map.264 = (f32[128,2048]{1,0:T(8,128)}, f32[128,128]{1,0:T(8,128)}, bf16[8,80,2048]{2,1,0:T(8,128)(2,1)}, bf16[8,80,2048]{2,1,0:T(8,128)(2,1)}, bf16[2,12...) custom-call(bf16[128,2048]{1,0:T(8,128)(2,1)} %copy-done.2, ...), custom_call_target="tpu_custom_call" | custom-call | tf_op jit(solution)/shard_map/pallas_call | solution.py:124
  325.8 1.1 multiply_reduce_fusion.3
  326.9 1.0 multiply_convert_fusion.1
  327.9 1.3 convolution_convert_fusion
  329.2 1.7 multiply_reduce_fusion
  330.9 0.7 maximum_bitcast_fusion.gains
  331.6 0.7 copy.54
  332.3 1.2 fusion.17.grad_out
  333.5 196.7 %shard_map.265 = (bf16[256,4096]{1,0:T(8,128)(2,1)}, bf16[8,256,128]{2,1,0:T(8,128)(2,1)}, bf16[512,2048]{1,0:T(8,128)(2,1)}, f32[32,256]{1,0:T(8,128)}, f32[40,...) custom-call(bf16[128,2048]{1,0:T(8,128)(2,1)} %fusion.17.grad_out, ...), custom_call_target="tpu_custom_call" | custom-call | tf_op jit(solution)/shard_map/pallas_call | solution.py:124
  530.2 3.5 add_bitcast_fusion
  533.7 0.5 slice_bitcast_fusion.2
  534.2 0.6 slice_bitcast_fusion
  535.0 0.3 copy.44
  535.3 0.8 copy.52
  536.5 0.8 copy.53
  537.3 2.5 convert_element_type.61
  539.8 2.5 convert_element_type.62
  542.4 0.3 copy-done.6
  542.7 3.2 bitcast_convert_fusion.2
  545.9 3.2 bitcast_convert_fusion.1
  549.1 3.6 bitcast_convert_fusion
  552.7 0.6 copy.56
  (44 shorter events, 1.3 us)
Async XLA Ops:
  4.9 144.0 %copy-start.11 = (f32[2048]{0:T(1024)S(1)}, f32[2048]{0:T(1024)}, u32[]{:S(2)}) copy-start(f32[2048]{0:T(1024)} %param.27) | copy-start | bytes 24580
  150.3 2.4 copy-start.2
  152.7 176.4 %copy-start = (f32[128,2048]{1,0:T(8,128)S(1)}, f32[128,2048]{1,0:T(8,128)}, u32[]{:S(2)}) copy-start(f32[128,2048]{1,0:T(8,128)} %get-tuple-element.39) | copy-start | bytes 3145732
  152.7 176.4 %copy-start.10 = (bf16[32,2048]{1,0:T(8,128)(2,1)S(1)}, bf16[32,2048]{1,0:T(8,128)(2,1)}, u32[]{:S(2)}) copy-start(bf16[32,2048]{1,0:T(8,128)(2,1)} %get-tuple-element.40) | copy-start | bytes 393220
  325.7 6.5 %copy-start.3 = (bf16[1,128,2048]{2,1,0:T(8,128)(2,1)S(1)}, bf16[1,128,2048]{2,1,0:T(8,128)(2,1)}, u32[]{:S(2)}) copy-start(bf16[1,128,2048]{2,1,0:T(8,128)(2,1)} %param.17) | copy-start | bytes 1572868
  330.9 1.4 copy-start.1
  530.2 3.5 copy-start.13
  530.2 4.6 copy-start.9
  534.9 2.4 copy-start.8
  537.3 2.5 copy-start.7
  539.8 2.9 copy-start.6
  542.7 3.2 copy-start.5
  545.9 3.2 copy-start.4
  549.1 3.6 copy-start.12

commit v9 on v8

--- a/solution.py
+++ b/solution.py
@@ -1716,6 +1716,51 @@
     )
 
 
+def finish_types_body(q, o, g, u, d, kv, tokens, part, mid, mix, gains, router,
+                      q_out, o_out, g_out, u_out, d_out, k_out, v_out, tokens_out, mixed_out,
+                      attn_gain, ffn_gain, q_gain, k_gain, router_out):
+    for source, target in ((q, q_out), (o, o_out), (g, g_out), (u, u_out), (d, d_out)):
+        target[...] = source[...].astype(F32)
+    for head in range(kv.shape[0] // 2):
+        lanes = slice(head * HEAD_DIM, (head + 1) * HEAD_DIM)
+        k_out[:, lanes] = kv[2 * head].astype(F32)
+        v_out[:, lanes] = kv[2 * head + 1].astype(F32)
+    tokens_out[...] = tokens[...] + part[...]
+    mixed_out[...] = (mid[...] + mix[...]).astype(BF)
+    n = attn_gain.shape[0]
+    attn_gain[...] = gains[0:n]
+    ffn_gain[...] = gains[n : 2 * n]
+    q_gain[...] = gains[2 * n : 2 * n + 1]
+    k_gain[...] = gains[2 * n + 1 : 2 * n + 2]
+    router_out[...] = router[...].T
+
+
+def finish_types(q, o, g, u, d, kv, tokens, part, mid, mix, gains, router):
+    steps = 8
+    sds = jax.ShapeDtypeStruct
+    heads, wr, lanes = kv.shape
+    width = tokens.shape[1]
+    by_rows = lambda shape: pl.BlockSpec((shape[0] // steps,) + shape[1:], lambda i: (i, 0))
+    whole = lambda shape: pl.BlockSpec(shape, lambda i: (0, 0))
+    kv_shape, gain_shape, one = (wr, heads // 2 * lanes), (width // lanes, lanes), (1, lanes)
+    ins = [q, o, g, u, d, kv, tokens, part, mid, mix, gains, router]
+    in_specs = [by_rows(item.shape) for item in (q, o, g, u, d)]
+    in_specs += [pl.BlockSpec((heads, wr // steps, lanes), lambda i: (0, i, 0))]
+    in_specs += [by_rows(tokens.shape)] * 4 + [whole(gains.shape), whole(router.shape)]
+    outs = [sds(item.shape, F32) for item in (q, o, g, u, d)] + [sds(kv_shape, F32)] * 2
+    outs += [sds(tokens.shape, F32), sds(tokens.shape, BF)]
+    out_specs = [by_rows(item.shape) for item in outs]
+    small = [gain_shape, gain_shape, one, one, router.shape[::-1]]
+    return pl.pallas_call(
+        finish_types_body,
+        grid=(steps,),
+        out_shape=outs + [sds(shape, F32) for shape in small],
+        in_specs=in_specs,
+        out_specs=out_specs + [whole(shape) for shape in small],
+        compiler_params=pltpu.CompilerParams(vmem_limit_bytes=62 * 2**20),
+    )(*ins)
+
+
 def rms_scale(hidden, gain):
     return hidden * lax.rsqrt(jnp.mean(hidden * hidden, axis=-1, keepdims=True) + epsilon) * gain
 
@@ -1863,9 +1908,6 @@
             ctx_count, shard_count, group, capacity, second_b, gates_two, code, w_gate[0], w_up[0], w_down[0],
             upstream_rows, 3,
         )
-        grad_w_gate, grad_w_up, grad_w_down = (
-            grad_w_gate.astype(F32), grad_w_up.astype(F32), grad_w_down.astype(F32),
-        )
     else:
         received, gate_tail = dispatch_rows(ctx_count, shard_count, group, capacity, second_b, gates_two, code, 3)
         received = received.reshape(slot_rows, width)
@@ -1928,6 +1970,15 @@
             ),
             5,
         )
+        (
+            grad_w_query, grad_w_out, grad_w_gate, grad_w_up, grad_w_down, grad_w_key, grad_w_value, grad_tokens, mixed,
+            grad_attn_gain, grad_ffn_gain, grad_query_gain, grad_key_gain, grad_w_router,
+        ) = finish_types(
+            q_sum, out_sum, grad_w_gate, grad_w_up, grad_w_down, kv_sum, grad_middle, grad_input_part, middle, mixture,
+            gains, router_sum,
+        )
+        grad_attn_gain, grad_ffn_gain = grad_attn_gain.reshape(-1), grad_ffn_gain.reshape(-1)
+        grad_query_gain, grad_key_gain = grad_query_gain.reshape(-1), grad_key_gain.reshape(-1)
     else:
         normed_all = normed_all.reshape(plane, width)
         w_mine = w_mine.reshape(width, head_cols + HEAD_DIM)
@@ -1990,18 +2041,18 @@
             ctx_count, shard_count, head_cols, grad_w, out_part.reshape(8, -1, width), router_parts, gains, grad_pre, w_mine,
             tokens[0], attn_gain[None], 8,
         )
-    mixed = (middle + mixture).astype(BF)
-    grad_tokens = grad_middle + grad_input_part
-    gains = gains.reshape(-1)
-    grad_attn_gain, grad_ffn_gain = gains[:width], gains[width : 2 * width]
-    grad_query_gain = gains[2 * width : 2 * width + HEAD_DIM]
-    grad_key_gain = gains[2 * width + HEAD_DIM : 2 * width + 2 * HEAD_DIM]
-    grad_w_query = q_sum.astype(F32)
-    grad_w_out = out_sum.reshape(head_cols, width).astype(F32)
-    kinds = kv_sum.astype(F32).reshape(KEY_VALUE_HEADS, part_count, 2, wrows, HEAD_DIM)
-    kinds = jnp.transpose(jnp.sum(kinds, axis=1), (1, 2, 0, 3)).reshape(2, wrows, -1)
-    grad_w_key, grad_w_value = kinds[0], kinds[1]
-    grad_w_router = router_sum.T
+        mixed = (middle + mixture).astype(BF)
+        grad_tokens = grad_middle + grad_input_part
+        gains = gains.reshape(-1)
+        grad_attn_gain, grad_ffn_gain = gains[:width], gains[width : 2 * width]
+        grad_query_gain = gains[2 * width : 2 * width + HEAD_DIM]
+        grad_key_gain = gains[2 * width + HEAD_DIM : 2 * width + 2 * HEAD_DIM]
+        grad_w_query = q_sum.astype(F32)
+        grad_w_out = out_sum.reshape(head_cols, width).astype(F32)
+        kinds = kv_sum.astype(F32).reshape(KEY_VALUE_HEADS, part_count, 2, wrows, HEAD_DIM)
+        kinds = jnp.transpose(jnp.sum(kinds, axis=1), (1, 2, 0, 3)).reshape(2, wrows, -1)
+        grad_w_key, grad_w_value = kinds[0], kinds[1]
+        grad_w_router = router_sum.T
     return (
         mixed[None],
         grad_tokens[None],

time: 563 us -> 563 us (level)
  Pallas kernels: 512 us -> 538 us
  other arithmetic: 30.4 us -> 12.1 us
    pallas_call x0 -> x1, Pallas kernels: none -> 17.6 us  [finish_types(): pl.pallas_call(finish_types_body, grid=(steps,), out_shape=outs + [sds(sh...]
    broadcast_in_dim x4 -> x0, other arithmetic: 13.4 us -> none  [the longest x1 3.55 us: shards(): grad_w_down[None]]
    pallas_call x3, Pallas kernels: 512 us -> 521 us  [call(): pl.pallas_call(body, out_shape=outs, in_specs=in_specs, out_specs=out_spe...]
where the time goes in v9:
time: 563 us; the launch traced here: 558 us
  Pallas kernels  538 us (96%)
  other arithmetic  12.1 us (2%)
    pallas_call x3, Pallas kernels, call(): pl.pallas_call(body, out_shape=outs, in_specs=in_specs, out_specs=out_spe...  521 us
    pallas_call x1, Pallas kernels, finish_types(): pl.pallas_call(finish_types_body, grid=(steps,), out_shape=outs + [sds(sh...  17.6 us

profile of v9, /device:TPU:0, one launch (start us, length us, event | category | flops | bytes accessed | tf_op | source)
XLA Modules:
  0.0 558.1 jit_solution(14224595349030522666)
XLA Ops:
  0.7 0.7 select_reduce_fusion.1
  1.4 0.7 select_reduce_fusion
  2.2 0.7 convert_reduce_fusion
  2.9 0.1 copy.37
  3.0 0.3 fusion.4
  3.3 0.8 pad_maximum_fusion
  4.1 0.8 compare_select_fusion.bias
  4.9 142.6 %shard_map.263 = (bf16[8,128,2048]{2,1,0:T(8,128)(2,1)}, bf16[8,256,640]{2,1,0:T(8,128)(2,1)}, bf16[32,2048]{1,0:T(8,128)(2,1)}, f32[2,8,256]{2,1,0:T(8,128)}, b...) custom-call(bf16[128,2048]{1,0:T(8,128)(2,1)} %bitcast.42, ...), custom_call_target="tpu_custom_call" | custom-call | tf_op jit(solution)/shard_map/pallas_call | solution.py:124
  147.5 1.4 multiply_reduce_fusion.2
  148.9 0.0 copy-done.4
  148.9 1.4 multiply_convert_fusion.rows
  150.3 0.0 copy-start.1
  150.3 1.4 fusion.20
  151.7 0.2 fusion.5
  151.9 0.1 subtract_convert_fusion
  152.0 0.7 fusion.3.tail
  152.7 0.0 copy-done.1
  152.7 173.2 %shard_map.264 = (f32[128,2048]{1,0:T(8,128)}, f32[128,128]{1,0:T(8,128)}, bf16[8,80,2048]{2,1,0:T(8,128)(2,1)}, bf16[8,80,2048]{2,1,0:T(8,128)(2,1)}, bf16[2,12...) custom-call(bf16[128,2048]{1,0:T(8,128)(2,1)} %copy-done.1, ...), custom_call_target="tpu_custom_call" | custom-call | tf_op jit(solution)/shard_map/pallas_call | solution.py:124
  325.9 0.0 copy-start.2
  325.9 1.1 multiply_reduce_fusion.3
  327.1 1.0 multiply_convert_fusion.1
  328.1 1.3 convolution_convert_fusion
  329.4 0.0 copy-done
  329.4 0.0 copy-done.3
  329.4 1.7 multiply_reduce_fusion
  331.1 0.6 maximum_bitcast_fusion.gains
  331.7 0.7 copy.45
  332.4 0.0 copy-done.2
  332.4 1.5 fusion.16
  333.9 204.8 %shard_map.265 = (bf16[256,4096]{1,0:T(8,128)(2,1)}, bf16[8,256,128]{2,1,0:T(8,128)(2,1)}, bf16[512,2048]{1,0:T(8,128)(2,1)}, f32[32,256]{1,0:T(8,128)}, f32[40,...) custom-call(bf16[128,2048]{1,0:T(8,128)(2,1)} %get-tuple-element.136.grad_out, ...), custom_call_target="tpu_custom_call" | custom-call | tf_op jit(solution)/shard_map/pallas_call | solution.py:124
  538.7 17.6 %shard_map.266 = (f32[256,4096]{1,0:T(8,128)}, f32[512,2048]{1,0:T(8,128)}, f32[2048,768]{1,0:T(8,128)}, f32[2048,768]{1,0:T(8,128)}, f32[768,2048]{1,0:T(8,128)...) custom-call(bf16[256,4096]{1,0:T(8,128)(2,1)} %get-tuple-element.68., ...), custom_call_target="tpu_custom_call" | custom-call | tf_op jit(solution)/shard_map/pallas_call | solution.py:1754
  556.3 1.6 copy.41
  (13 shorter events, 0.1 us)
Async XLA Ops:
  4.9 144.0 %copy-start.4 = (f32[2048]{0:T(1024)S(1)}, f32[2048]{0:T(1024)}, u32[]{:S(2)}) copy-start(f32[2048]{0:T(1024)} %param.27) | copy-start | bytes 24580
  150.3 2.4 copy-start.1
  152.7 176.6 %copy-start = (f32[128,2048]{1,0:T(8,128)S(1)}, f32[128,2048]{1,0:T(8,128)}, u32[]{:S(2)}) copy-start(f32[128,2048]{1,0:T(8,128)} %get-tuple-element.53.mid) | copy-start | bytes 3145732
  152.7 176.6 %copy-start.3 = (bf16[32,2048]{1,0:T(8,128)(2,1)S(1)}, bf16[32,2048]{1,0:T(8,128)(2,1)}, u32[]{:S(2)}) copy-start(bf16[32,2048]{1,0:T(8,128)(2,1)} %get-tuple-element.54) | copy-start | bytes 393220
  325.9 6.5 %copy-start.2 = (bf16[1,128,2048]{2,1,0:T(8,128)(2,1)S(1)}, bf16[1,128,2048]{2,1,0:T(8,128)(2,1)}, u32[]{:S(2)}) copy-start(bf16[1,128,2048]{2,1,0:T(8,128)(2,1)} %param.17) | copy-start | bytes 1572868

commit v10 on v9

--- a/solution.py
+++ b/solution.py
@@ -158,8 +158,8 @@
 
 
 def front_body(n_ctx, n_shard, group, capacity, heads, kv_heads, paired, tile,
-               tokens, gain, w_query, key_w, value_w, routes, router, cot, cosine, sine, bias, q_gain, k_gain, w_out,
-               rows_out, w_all_out, router_all, code, cot_rows, qpre_out, kvpre, q_out, kv_out, attn_out, mid,
+               tokens, gain, w_query, key_w, value_w, routes, router, cot, cosine, sine, bias, q_gain, k_gain, w_out, second_gain,
+               rows_out, w_all_out, router_all, code, cot_rows, qpre_out, kvpre, q_out, kv_out, attn_out, mid, second,
                own_rows, rows_all, w_all, zroutes, zcot, ready, qpre, q, kv, attn,
                own_part, pair, to_sib, sib, to_chip, got,
                local, ss_row, rs_row, ss_fwd, rs_fwd, ss_w, rs_w, ss_k, rs_k, ss_rt, rs_rt, ss_ro, rs_ro, ss_z, rs_z,
@@ -383,6 +383,8 @@
     for at in range(chips - 1):
         far[at].wait()
         mid[...] += got[at].astype(F32)
+    unit, unused = unit_rows(mid[...])
+    second[...] = (unit * second_gain[...]).astype(BF)
     cot_fan.drain()
     route_fan.drain()
     for item in cot_waits + outs:
@@ -404,9 +406,9 @@
             sds((n, count, width), BF), sds((n, wr, cols + HEAD_DIM), BF), sds((router.shape[0], width), BF),
             sds((groups, n, group * count), F32), sds((groups, n, slots, width), BF), sds((n, count, cols), F32),
             sds((n, count, HEAD_DIM), F32), sds((n, count, cols), BF), sds((2, n, z, count, HEAD_DIM), BF),
-            sds((n, count, cols), BF), sds((count, width), F32),
+            sds((n, count, cols), BF), sds((count, width), F32), sds((count, width), BF),
         ],
-        [VMEM, VMEM, ANY, ANY, ANY, VMEM, ANY, ANY] + [VMEM] * 6,
+        [VMEM, VMEM, ANY, ANY, ANY, VMEM, ANY, ANY] + [VMEM] * 7,
         [
             pltpu.VMEM((count, width), BF), pltpu.VMEM((n, count, width), BF), pltpu.VMEM((n, wr, cols + HEAD_DIM), BF),
             pltpu.VMEM((z,) + routes.shape, jnp.int32), pltpu.VMEM((z, count, width), BF),
@@ -420,7 +422,7 @@
             dma(z), dma(z), dma(z), dma(z), dma(chips), dma(chips), dma(chips - 1), dma(chips - 1), dma(6),
         ],
         ident, args, mib=60,
-        out_specs=[ANY, ANY, ANY, VMEM, ANY, ANY, VMEM, ANY, ANY, ANY, VMEM],
+        out_specs=[ANY, ANY, ANY, VMEM, ANY, ANY, VMEM, ANY, ANY, ANY, VMEM, VMEM],
     )
 
 
@@ -1732,7 +1734,7 @@
     ffn_gain[...] = gains[n : 2 * n]
     q_gain[...] = gains[2 * n : 2 * n + 1]
     k_gain[...] = gains[2 * n + 1 : 2 * n + 2]
-    router_out[...] = router[...].T
+    router_out[...] = router[...]
 
 
 def finish_types(q, o, g, u, d, kv, tokens, part, mid, mix, gains, router):
@@ -1750,7 +1752,7 @@
     outs = [sds(item.shape, F32) for item in (q, o, g, u, d)] + [sds(kv_shape, F32)] * 2
     outs += [sds(tokens.shape, F32), sds(tokens.shape, BF)]
     out_specs = [by_rows(item.shape) for item in outs]
-    small = [gain_shape, gain_shape, one, one, router.shape[::-1]]
+    small = [gain_shape, gain_shape, one, one, router.shape]
     return pl.pallas_call(
         finish_types_body,
         grid=(steps,),
@@ -1864,11 +1866,12 @@
     sine = jnp.concatenate([-jnp.sin(angles), jnp.sin(angles)], axis=1)
     (
         normed_all, w_mine, router_all, code, upstream_rows, query_pre, kv_pre, queries, kv_all, attn_rows, middle,
+        second_b,
     ) = front(
         ctx_count, shard_count, group, capacity, KEY_VALUE_HEADS, small,
         (
             tokens[0], attn_gain[None], w_query, key_weight, value_weight, routes[0].T, w_router.T, upstream_b,
-            cosine, sine, bias, query_gain[None], key_gain[None], w_out,
+            cosine, sine, bias, query_gain[None], key_gain[None], w_out, ffn_gain[None],
         ),
         0,
     )
@@ -1880,8 +1883,6 @@
         flat = pre.reshape(-1, rows, shape[-2], HEAD_DIM)
         return jax.vmap(lambda v: rotate(rms_scale(v, gain), q_places))(flat).reshape(shape)
 
-    normed_two = rms_scale(middle, ffn_gain)
-    second_b = normed_two.astype(BF)
     logits = contract_cols(second_b, router_all)
     chosen = jnp.sum(
         (routes[0][:, :, None] == jnp.arange(experts, dtype=jnp.int32)).astype(F32), axis=1
@@ -1979,6 +1980,7 @@
         )
         grad_attn_gain, grad_ffn_gain = grad_attn_gain.reshape(-1), grad_ffn_gain.reshape(-1)
         grad_query_gain, grad_key_gain = grad_query_gain.reshape(-1), grad_key_gain.reshape(-1)
+        grad_w_router = grad_w_router.T
     else:
         normed_all = normed_all.reshape(plane, width)
         w_mine = w_mine.reshape(width, head_cols + HEAD_DIM)

time: 563 us -> 559 us (level)
  no operation moved by 1% of the time
where the time goes in v10:
time: 559 us; the launch traced here: 555 us
  Pallas kernels  539 us (96%)
  other arithmetic  10.8 us (2%)
    pallas_call x3, Pallas kernels, call(): pl.pallas_call(body, out_shape=outs, in_specs=in_specs, out_specs=out_spe...  521 us
    pallas_call x1, Pallas kernels, finish_types(): pl.pallas_call(finish_types_body, grid=(steps,), out_shape=outs + [sds(sh...  17.6 us

profile of v10, /device:TPU:0, one launch (start us, length us, event | category | flops | bytes accessed | tf_op | source)
XLA Modules:
  0.0 554.6 jit_solution(17680425493959685208)
XLA Ops:
  0.7 0.7 select_reduce_fusion.1
  1.4 0.7 select_reduce_fusion
  2.2 0.7 convert_reduce_fusion
  2.9 0.1 copy.35
  3.0 0.3 fusion.4
  3.3 0.8 pad_maximum_fusion
  4.1 0.8 compare_select_fusion.bias
  4.9 143.0 %shard_map.263 = (bf16[8,128,2048]{2,1,0:T(8,128)(2,1)}, bf16[8,256,640]{2,1,0:T(8,128)(2,1)}, bf16[32,2048]{1,0:T(8,128)(2,1)}, f32[2,8,256]{2,1,0:T(8,128)}, b...) custom-call(bf16[128,2048]{1,0:T(8,128)(2,1)} %bitcast.44, ...), custom_call_target="tpu_custom_call" | custom-call | tf_op jit(solution)/shard_map/pallas_call | solution.py:124
  147.9 1.4 multiply_reduce_fusion.2
  149.2 1.4 fusion.20
  150.7 0.2 fusion.5
  150.9 0.1 subtract_convert_fusion
  151.0 0.7 fusion.3.tail
  151.7 0.0 copy-start.1
  151.7 0.0 copy-start
  151.7 0.0 copy-start.4
  151.7 173.3 %shard_map.264 = (f32[128,2048]{1,0:T(8,128)}, f32[128,128]{1,0:T(8,128)}, bf16[8,80,2048]{2,1,0:T(8,128)(2,1)}, bf16[8,80,2048]{2,1,0:T(8,128)(2,1)}, bf16[2,12...) custom-call(bf16[128,2048]{1,0:T(8,128)(2,1)} %get-tuple-element.54.row, ...), custom_call_target="tpu_custom_call" | custom-call | tf_op jit(solution)/shard_map/pallas_call | solution.py:124
  325.0 0.0 copy-start.2
  325.0 1.1 multiply_reduce_fusion.3
  326.1 1.0 multiply_convert_fusion
  327.1 0.0 copy-done.1
  327.1 0.2 convolution_convert_fusion
  327.4 0.0 copy-done
  327.4 0.0 copy-done.3
  327.4 0.0 copy-done.4
  327.4 1.7 multiply_reduce_fusion
  329.1 0.6 maximum_bitcast_fusion.gains
  329.7 0.7 copy.42
  330.4 0.0 copy-done.2
  330.4 1.5 fusion.16
  331.9 204.8 %shard_map.265 = (bf16[256,4096]{1,0:T(8,128)(2,1)}, bf16[8,256,128]{2,1,0:T(8,128)(2,1)}, bf16[512,2048]{1,0:T(8,128)(2,1)}, f32[32,256]{1,0:T(8,128)}, f32[40,...) custom-call(bf16[128,2048]{1,0:T(8,128)(2,1)} %get-tuple-element.96.grad_out, ...), custom_call_target="tpu_custom_call" | custom-call | tf_op jit(solution)/shard_map/pallas_call | solution.py:124
  536.8 17.6 %shard_map.266 = (f32[256,4096]{1,0:T(8,128)}, f32[512,2048]{1,0:T(8,128)}, f32[2048,768]{1,0:T(8,128)}, f32[2048,768]{1,0:T(8,128)}, f32[768,2048]{1,0:T(8,128)...) custom-call(bf16[256,4096]{1,0:T(8,128)(2,1)} %get-tuple-element.70., ...), custom_call_target="tpu_custom_call" | custom-call | tf_op jit(solution)/shard_map/pallas_call | solution.py:1756
  (11 shorter events, 0.1 us)
Async XLA Ops:
  151.7 175.4 %copy-start.1 = (bf16[128,2048]{1,0:T(8,128)(2,1)S(1)}, bf16[128,2048]{1,0:T(8,128)(2,1)}, u32[]{:S(2)}) copy-start(bf16[128,2048]{1,0:T(8,128)(2,1)} %get-tuple-element.54.rows) | copy-start | bytes 1572868
  151.7 175.7 %copy-start = (f32[128,2048]{1,0:T(8,128)S(1)}, f32[128,2048]{1,0:T(8,128)}, u32[]{:S(2)}) copy-start(f32[128,2048]{1,0:T(8,128)} %get-tuple-element.60.mid) | copy-start | bytes 3145732
  151.7 175.7 %copy-start.3 = (bf16[32,2048]{1,0:T(8,128)(2,1)S(1)}, bf16[32,2048]{1,0:T(8,128)(2,1)}, u32[]{:S(2)}) copy-start(bf16[32,2048]{1,0:T(8,128)(2,1)} %get-tuple-element.55) | copy-start | bytes 393220
  151.7 175.7 %copy-start.4 = (f32[2048]{0:T(1024)S(1)}, f32[2048]{0:T(1024)}, u32[]{:S(2)}) copy-start(f32[2048]{0:T(1024)} %param.27) | copy-start | bytes 24580
  325.0 5.4 copy-start.2

commit v11 on v10

--- a/solution.py
+++ b/solution.py
@@ -961,7 +961,7 @@
                 landing, ss_i, rs_i, ss_o, out_copies)
     wide_line = Line(lambda j: None, lambda j: wide.at[j], wide_landing, ss_wi, rs_wi, ss_wo, wide_copies)
     steps = [(wide_line, j) for j in range(wides)] + [(line, j) for j in range(2 * n_shard)]
-    lag, ahead = 2, 6
+    lag, ahead = 2, 4
 
     def advance(n):
         if n + ahead < len(steps):
@@ -1127,7 +1127,7 @@
         if at:
             side.append(functools.partial(chip_sum, at - 1))
     count_steps = len(steps) + lag
-    late = {21: last_sum, 23: mix_last, 26: small_plane}
+    late = {24: last_sum, 26: mix_last, 29: small_plane}
     for n in range(3, count_steps):
         advance(n)
         if side:

time: 559 us -> 556 us (level)
  no operation moved by 1% of the time
where the time goes in v11:
time: 556 us; the launch traced here: 550 us
  Pallas kernels  535 us (96%)
  other arithmetic  10.8 us (2%)
    pallas_call x3, Pallas kernels, call(): pl.pallas_call(body, out_shape=outs, in_specs=in_specs, out_specs=out_spe...  517 us
    pallas_call x1, Pallas kernels, finish_types(): pl.pallas_call(finish_types_body, grid=(steps,), out_shape=outs + [sds(sh...  17.6 us

profile of v11, /device:TPU:0, one launch (start us, length us, event | category | flops | bytes accessed | tf_op | source)
XLA Modules:
  0.0 550.5 jit_solution(8157687435574074146)
XLA Ops:
  0.7 0.7 select_reduce_fusion.1
  1.4 0.7 select_reduce_fusion
  2.2 0.7 convert_reduce_fusion
  2.9 0.1 copy.35
  3.0 0.3 fusion.4
  3.3 0.8 pad_maximum_fusion
  4.1 0.8 compare_select_fusion.bias
  4.9 143.0 %shard_map.263 = (bf16[8,128,2048]{2,1,0:T(8,128)(2,1)}, bf16[8,256,640]{2,1,0:T(8,128)(2,1)}, bf16[32,2048]{1,0:T(8,128)(2,1)}, f32[2,8,256]{2,1,0:T(8,128)}, b...) custom-call(bf16[128,2048]{1,0:T(8,128)(2,1)} %bitcast.44, ...), custom_call_target="tpu_custom_call" | custom-call | tf_op jit(solution)/shard_map/pallas_call | solution.py:124
  147.9 1.4 multiply_reduce_fusion.2
  149.2 1.4 fusion.20
  150.7 0.2 fusion.5
  150.9 0.1 subtract_convert_fusion
  151.0 0.7 fusion.3.tail
  151.7 0.0 copy-start.1
  151.7 0.0 copy-start
  151.7 0.0 copy-start.3
  151.7 173.3 %shard_map.264 = (f32[128,2048]{1,0:T(8,128)}, f32[128,128]{1,0:T(8,128)}, bf16[8,80,2048]{2,1,0:T(8,128)(2,1)}, bf16[8,80,2048]{2,1,0:T(8,128)(2,1)}, bf16[2,12...) custom-call(bf16[128,2048]{1,0:T(8,128)(2,1)} %get-tuple-element.54.row, ...), custom_call_target="tpu_custom_call" | custom-call | tf_op jit(solution)/shard_map/pallas_call | solution.py:124
  325.0 0.0 copy-start.2
  325.0 1.1 multiply_reduce_fusion.3
  326.1 1.0 multiply_convert_fusion
  327.1 0.0 copy-done.1
  327.1 0.2 convolution_convert_fusion
  327.4 0.0 copy-done
  327.4 0.0 copy-done.3
  327.4 0.0 copy-done.4
  327.4 1.7 multiply_reduce_fusion
  329.1 0.6 maximum_bitcast_fusion.gains
  329.7 0.7 copy.42
  330.4 0.0 copy-done.2
  330.4 1.5 fusion.16
  331.9 200.7 %shard_map.265 = (bf16[256,4096]{1,0:T(8,128)(2,1)}, bf16[8,256,128]{2,1,0:T(8,128)(2,1)}, bf16[512,2048]{1,0:T(8,128)(2,1)}, f32[32,256]{1,0:T(8,128)}, f32[40,...) custom-call(bf16[128,2048]{1,0:T(8,128)(2,1)} %get-tuple-element.96.grad_out, ...), custom_call_target="tpu_custom_call" | custom-call | tf_op jit(solution)/shard_map/pallas_call | solution.py:124
  532.7 17.6 %shard_map.266 = (f32[256,4096]{1,0:T(8,128)}, f32[512,2048]{1,0:T(8,128)}, f32[2048,768]{1,0:T(8,128)}, f32[2048,768]{1,0:T(8,128)}, f32[768,2048]{1,0:T(8,128)...) custom-call(bf16[256,4096]{1,0:T(8,128)(2,1)} %get-tuple-element.70., ...), custom_call_target="tpu_custom_call" | custom-call | tf_op jit(solution)/shard_map/pallas_call | solution.py:1756
  (11 shorter events, 0.1 us)
Async XLA Ops:
  151.7 175.4 %copy-start.1 = (bf16[128,2048]{1,0:T(8,128)(2,1)S(1)}, bf16[128,2048]{1,0:T(8,128)(2,1)}, u32[]{:S(2)}) copy-start(bf16[128,2048]{1,0:T(8,128)(2,1)} %get-tuple-element.54.rows) | copy-start | bytes 1572868
  151.7 175.7 %copy-start = (f32[128,2048]{1,0:T(8,128)S(1)}, f32[128,2048]{1,0:T(8,128)}, u32[]{:S(2)}) copy-start(f32[128,2048]{1,0:T(8,128)} %get-tuple-element.60.mid) | copy-start | bytes 3145732
  151.7 175.7 %copy-start.3 = (bf16[32,2048]{1,0:T(8,128)(2,1)S(1)}, bf16[32,2048]{1,0:T(8,128)(2,1)}, u32[]{:S(2)}) copy-start(bf16[32,2048]{1,0:T(8,128)(2,1)} %get-tuple-element.55) | copy-start | bytes 393220
  151.7 175.7 %copy-start.4 = (f32[2048]{0:T(1024)S(1)}, f32[2048]{0:T(1024)}, u32[]{:S(2)}) copy-start(f32[2048]{0:T(1024)} %param.27) | copy-start | bytes 24580
  325.0 5.4 copy-start.2
